TPU v7x, 32 devices: a whole 2x2x4 slice. The times are simulated.
32 devices in a mesh: gx: 8 (over y, x, core), gy: 4 (over z).
Axes of the slice: x: 2, y: 2, z: 4, core: 2. Of those that a mesh axis runs over, the one named last changes fastest.
Arguments:
- volume: bfloat16 [64, 16, 64, 128], P(None, 'gx', 'gy'), may hold values from -6 to 6
- kernel: bfloat16 [4, 4, 4, 32, 64], replicated, may hold values from -0.25 to 0.25
- cotangent: bfloat16 [2, 2, 2, 32, 16, 64, 128], P(None, None, None, None, 'gx', 'gy'), may hold values from -6 to 6
Outputs:
- activation: bfloat16 [2, 2, 2, 32, 16, 64, 128], P(None, None, None, None, 'gx', 'gy')
- input_grad: bfloat16 [64, 16, 64, 128], P(None, 'gx', 'gy')
- weight_grad: float32 [4, 4, 4, 32, 64], replicated
All inputs are finite; a program needn't handle non-finite values.
Results may differ from a plain program's by a relative error of at most 0.0049.
Values may be sent and summed in bfloat16 or wider, within the bound.
No kernel may reach another device: no remote copies, remote signals or barrier semaphores. Data moves between devices by JAX's collectives and lax.ppermute only.
A program may use at most 192 MiB of HBM per device.

v0:
```python
import math

import jax
import jax.numpy as jnp
from jax import lax
from jax.sharding import PartitionSpec as P

FORWARD_TAPS = (((1, 0), (3, -1)), ((2, 0), (0, 1)))
PHASE_TAPS = (((1, 0), (3, 1)), ((0, -1), (2, 0)))


def padded_2(block, sides, width):
    for axis, dim in sides:
        count = lax.axis_size(axis)
        forward = [(i, i + 1) for i in range(count - 1)]
        backward = [(target, source) for source, target in forward]
        low = lax.ppermute(
            lax.slice_in_dim(block, block.shape[dim] - width, None, axis=dim), axis, forward
        )
        high = lax.ppermute(lax.slice_in_dim(block, 0, width, axis=dim), axis, backward)
        block = jnp.concatenate([low, block, high], axis=dim)
    return block


def silu_pair(before):
    sigmoid = jax.nn.sigmoid(before)
    return (before * sigmoid, sigmoid * (1.0 + before * (1.0 - sigmoid)))


def phase_product(padded, kernel, phase_x, phase_y, phase_z, span_x, span_y, depth_cells):
    total = None
    for tap_x, shift_x in FORWARD_TAPS[phase_x]:
        for tap_y, shift_y in FORWARD_TAPS[phase_y]:
            for tap_z, shift_z in FORWARD_TAPS[phase_z]:
                piece = lax.slice(
                    padded,
                    (0, 1 + shift_x, 1 + shift_y, 1 + shift_z),
                    (
                        padded.shape[0],
                        1 + shift_x + span_x,
                        1 + shift_y + span_y,
                        1 + shift_z + depth_cells,
                    ),
                )
                term = lax.dot_general(
                    kernel[tap_x, tap_y, tap_z],
                    piece,
                    (((1,), (0,)), ((), ())),
                    preferred_element_type=jnp.float32,
                )
                total = term if total is None else total + term
    return total


def all_phases(padded, kernel, span_x, span_y, depth_cells):
    results = []
    for phase_x in range(2):
        for phase_y in range(2):
            for phase_z in range(2):
                results.append(
                    phase_product(
                        padded, kernel, phase_x, phase_y, phase_z, span_x, span_y, depth_cells
                    )
                )
    chans_out = results[0].shape[0]
    return jnp.stack(results).reshape(2, 2, 2, chans_out, span_x, span_y, depth_cells)


def on_device(volume, kernel, cotangent):
    cells_x = volume.shape[1]
    cells_y = volume.shape[2]
    depth_cells = volume.shape[3]
    rim_cells = padded_2(volume, (("gx", 1), ("gy", 2)), 1)
    padded = jnp.pad(rim_cells, ((0, 0), (0, 0), (0, 0), (1, 1)))
    before = all_phases(padded, kernel, cells_x, cells_y, depth_cells)
    values, slopes = silu_pair(before)
    activation = values.astype(jnp.bfloat16)
    grad_pre = (cotangent.astype(jnp.float32) * slopes).astype(jnp.bfloat16)
    grad_rim = padded_2(grad_pre, (("gx", 4), ("gy", 5)), 1)
    grad_pad = jnp.pad(grad_rim, ((0, 0), (0, 0), (0, 0), (0, 0), (0, 0), (0, 0), (1, 1)))
    chans_out = grad_pad.shape[3]
    back_sum = None
    weight_parts = [None] * 64
    for phase_x in range(2):
        for phase_y in range(2):
            for phase_z in range(2):
                source = grad_pad[phase_x, phase_y, phase_z]
                group_list = []
                group_slots = []
                for tap_x, shift_x in PHASE_TAPS[phase_x]:
                    for tap_y, shift_y in PHASE_TAPS[phase_y]:
                        for tap_z, shift_z in PHASE_TAPS[phase_z]:
                            piece = lax.slice(
                                source,
                                (0, 1 + shift_x, 1 + shift_y, 1 + shift_z),
                                (
                                    chans_out,
                                    1 + shift_x + cells_x,
                                    1 + shift_y + cells_y,
                                    1 + shift_z + depth_cells,
                                ),
                            )
                            product = lax.dot_general(
                                kernel[tap_x, tap_y, tap_z],
                                piece,
                                (((0,), (0,)), ((), ())),
                                preferred_element_type=jnp.float32,
                            )
                            back_sum = product if back_sum is None else back_sum + product
                            group_list.append(
                                lax.dot_general(
                                    piece,
                                    volume,
                                    (((1, 2, 3), (1, 2, 3)), ((), ())),
                                    preferred_element_type=jnp.float32,
                                )
                            )
                            group_slots.append(16 * tap_x + 4 * tap_y + tap_z)
                group_terms = jnp.stack(group_list)
                for position, flat_index in enumerate(group_slots):
                    weight_parts[flat_index] = group_terms[position]
    input_grad = back_sum.astype(jnp.bfloat16)
    stacked_grad = jnp.stack(weight_parts).reshape(4, 4, 4, chans_out, volume.shape[0])
    stacked_grad = lax.psum(stacked_grad, ("gx", "gy"))
    scaling = 1.0 / math.sqrt(
        cells_x * lax.axis_size("gx") * cells_y * lax.axis_size("gy") * depth_cells
    )
    return (activation, input_grad, stacked_grad * scaling)


def solution(mesh):
    placed = (P(None, "gx", "gy", None), P(), P(None, None, None, None, "gx", "gy", None))
    return jax.shard_map(
        on_device,
        mesh=mesh,
        in_specs=placed,
        out_specs=(P(None, None, None, None, "gx", "gy", None), P(None, "gx", "gy", None), P()),
        check_vma=False,
    )
```

profile of v0, /device:TPU:1, one launch (start us, length us, event | category | flops | bytes accessed | tf_op | source)
XLA Modules:
  0.0 316.4 jit_solution(11962142027953839589)
XLA Ops:
  8.6 4.5 %collective-permute-start = (bf16[64,1,16,128]{3,0,2,1:T(8,128)(2,1)S(1)}, bf16[64,1,16,128]{3,0,2,1:T(8,128)(2,1)S(1)}, u32[]{:S(2)}, u32[]{:S(2)}) collective-permute-start(bf16[64,1,16,128]{3,0,2,1:T(8,128)(2,1)S(1)} %get-tuple-element.25), channel_id=1, source_target_pairs={{0,4},{4,8},{8,12},{12,16},{16,20},{20,24},{24,28},{1,5},{5,9},{9,... | collective-permute-start | bytes 786440 | tf_op jit(solution)/shard_map/ppermute | solution.py:17
  13.1 1.9 collective-permute-start.1
  17.6 3.2 %collective-permute-done.1 = bf16[64,1,16,128]{3,0,2,1:T(8,128)(2,1)S(1)} collective-permute-done((bf16[64,1,16,128]{3,0,2,1:T(8,128)(2,1)S(1)}, bf16[64,1,16,128]{3,0,2,1:T(8,128)(2,1)S(1)}, u32[]{:S(2)}, u32[]{:S(2)}) %collective-permute-start.1) | collective-permute-done | bytes 262176 | tf_op jit(solution)/shard_map/ppermute | solution.py:20
  20.9 3.2 %collective-permute-start.2 = (bf16[64,4,1,128]{3,0,2,1:T(8,128)(2,1)S(1)}, bf16[64,4,1,128]{3,0,2,1:T(8,128)(2,1)S(1)}, u32[]{:S(2)}, u32[]{:S(2)}) collective-permute-start(bf16[64,4,1,128]{3,0,2,1:T(8,128)(2,1)S(1)} %get-tuple-element.22), channel_id=1, source_target_pairs={{0,1},{1,2},{2,3},{4,5},{5,6},{6,7},{8,9},{9,10},{10,11},{12,13},{... | collective-permute-start | bytes 196616 | tf_op jit(solution)/shard_map/ppermute | solution.py:17
  27.2 2.0 collective-permute-done.3
  29.2 1.8 fusion.11
  45.4 2.5 multiply_convert_fusion
  48.3 3.2 %collective-permute-start.4 = (bf16[2,2,2,32,1,16,128]{6,3,5,4,2,1,0:T(8,128)(2,1)S(1)}, bf16[2,2,2,32,1,16,128]{6,3,5,4,2,1,0:T(8,128)(2,1)S(1)}, u32[]{:S(2)}, u32[]{:S(2)}) collective-permute-start(bf16[2,2,2,32,1,16,128]{6,3,5,4,2,1,0:T(8,128)(2,1)S(1)} %get-tuple-element.18), channel_id=1, source_target_pairs={{0,4},{4,8},{8,12},{12,16},{16,20},{20,24},{24,28},{1,5},{5,9},{9,... | collective-permute-start | bytes 3145736 | tf_op jit(solution)/shard_map/ppermute | solution.py:17
  51.5 1.9 collective-permute-start.5
  53.4 9.8 %collective-permute-done.4 = bf16[2,2,2,32,1,16,128]{6,3,5,4,2,1,0:T(8,128)(2,1)S(1)} collective-permute-done((bf16[2,2,2,32,1,16,128]{6,3,5,4,2,1,0:T(8,128)(2,1)S(1)}, bf16[2,2,2,32,1,16,128]{6,3,5,4,2,1,0:T(8,128)(2,1)S(1)}, u32[]{:S(2)}, u32[]{:S(2)}) %collective-permute-start.4) | collective-permute-done | bytes 1048608 | tf_op jit(solution)/shard_map/ppermute | solution.py:17
  63.2 14.0 %collective-permute-done.5 = bf16[2,2,2,32,1,16,128]{6,3,5,4,2,1,0:T(8,128)(2,1)S(1)} collective-permute-done((bf16[2,2,2,32,1,16,128]{6,3,5,4,2,1,0:T(8,128)(2,1)S(1)}, bf16[2,2,2,32,1,16,128]{6,3,5,4,2,1,0:T(8,128)(2,1)S(1)}, u32[]{:S(2)}, u32[]{:S(2)}) %collective-permute-start.5) | collective-permute-done | bytes 1048608 | tf_op jit(solution)/shard_map/ppermute | solution.py:20
  77.3 3.2 %collective-permute-start.6 = (bf16[2,2,2,32,4,1,128]{6,3,5,4,2,1,0:T(8,128)(2,1)S(1)}, bf16[2,2,2,32,4,1,128]{6,3,5,4,2,1,0:T(8,128)(2,1)S(1)}, u32[]{:S(2)}, u32[]{:S(2)}) collective-permute-start(bf16[2,2,2,32,4,1,128]{6,3,5,4,2,1,0:T(8,128)(2,1)S(1)} %get-tuple-element.14), channel_id=1, source_target_pairs={{0,1},{1,2},{2,3},{4,5},{5,6},{6,7},{8,9},{9,10},{10,11},{12,13},{... | collective-permute-start | bytes 786440 | tf_op jit(solution)/shard_map/ppermute | solution.py:17
  81.8 2.1 copy.84
  84.0 3.7 %collective-permute-done.7 = bf16[2,2,2,32,4,1,128]{6,3,5,4,2,1,0:T(8,128)(2,1)S(1)} collective-permute-done((bf16[2,2,2,32,4,1,128]{6,3,5,4,2,1,0:T(8,128)(2,1)S(1)}, bf16[2,2,2,32,4,1,128]{6,3,5,4,2,1,0:T(8,128)(2,1)S(1)}, u32[]{:S(2)}, u32[]{:S(2)}) %collective-permute-start.7) | collective-permute-done | bytes 262176 | tf_op jit(solution)/shard_map/ppermute | solution.py:20
  87.7 8.8 %select_maximum_fusion = bf16[2,2,2,32,4,18,130]{6,3,5,4,2,1,0:T(8,128)(2,1)S(1)} fusion(bf16[2,2,2,32,4,1,128]{6,3,5,4,2,1,0:T(8,128)(2,1)S(1)} %collective-permute-done.7, bf16[2,2,2,32,4,1,128]{6,3,5,4,2,1,0:T(8,128)(2,1)S(1)} %collective-permute-done.6, bf16[2,2,2,32,1,16,128]{6,3,5,4,2,1,0:T(8,128)(2,1)S(1)} %collective-permute-done.5, ...), kind=kLoop, calls=%fused_computation.3 | loop fusion | flops 43130880 | bytes 9510912 | tf_op jit(solution)/shard_map/concatenate | solution.py:21
  97.7 1.8 convolution_bitcast_fusion.40
  99.5 1.8 convolution_bitcast_fusion.41
  101.2 1.4 convolution_bitcast_fusion.42
  104.0 1.4 convolution_bitcast_fusion.44
  110.7 1.4 convolution_bitcast_fusion.34
  116.1 1.4 convolution_bitcast_fusion.31
  127.0 1.4 convolution_bitcast_fusion.16
  132.3 1.4 convolution_bitcast_fusion.20
  148.9 1.5 convolution_bitcast_fusion.2
  178.0 1.9 convolution_add_fusion.15
  186.1 1.8 fusion.54
  188.5 1.9 fusion.59
  191.8 1.9 fusion.58
  195.1 1.9 fusion.57
  198.4 1.9 fusion.56
  206.4 100.6 %all-reduce.4.cloned.1.call-done = f32[4,4,4,32,64]{4,3,2,1,0:T(8,128)} async-done(((f32[4,4,4,32,64]{4,3,2,1,0:T(8,128)}), f32[4,4,4,32,64]{4,3,2,1,0:T(8,128)}) %all-reduce.4.cloned.1.call-update) | async-done | bytes 524304 | tf_op jit(solution)/shard_map/psum | solution.py:124
  307.0 2.3 broadcast_multiply_fusion
  (301 shorter events, 107.6 us)
Async XLA Ops:
  7.2 7.9 %copy-start = (bf16[64,2,16,128]{3,2,1,0:T(8,128)(2,1)S(1)}, bf16[64,2,16,128]{3,2,1,0:T(8,128)(2,1)}, u32[]{:S(2)}) copy-start(bf16[64,2,16,128]{3,2,1,0:T(8,128)(2,1)} %param.3) | copy-start | bytes 1572868
  7.2 7.9 %copy-start.51 = (bf16[4,4,4,32,64]{4,3,2,1,0:T(8,128)(2,1)S(1)}, bf16[4,4,4,32,64]{4,3,2,1,0:T(8,128)(2,1)}, u32[]{:S(2)}) copy-start(bf16[4,4,4,32,64]{4,3,2,1,0:T(8,128)(2,1)} %param.4) | copy-start | bytes 786436
  7.2 299.8 %all-reduce.4.cloned.1.call-start = ((), (), s32[]{:S(2)}) async-start(), calls=%async_computation | async-start | bytes 2097152 | tf_op jit(solution)/shard_map/psum | solution.py:124
  8.6 8.7 %collective-permute-start = (bf16[64,1,16,128]{3,0,2,1:T(8,128)(2,1)S(1)}, bf16[64,1,16,128]{3,0,2,1:T(8,128)(2,1)S(1)}, u32[]{:S(2)}, u32[]{:S(2)}) collective-permute-start(bf16[64,1,16,128]{3,0,2,1:T(8,128)(2,1)S(1)} %get-tuple-element.25), channel_id=1, source_target_pairs={{0,4},{4,8},{8,12},{12,16},{16,20},{20,24},{24,28},{1,5},{5,9},{9,... | collective-permute-start | bytes 786440 | tf_op jit(solution)/shard_map/ppermute | solution.py:17
  13.1 7.8 %collective-permute-start.1 = (bf16[64,1,16,128]{3,0,2,1:T(8,128)(2,1)S(1)}, bf16[64,1,16,128]{3,0,2,1:T(8,128)(2,1)S(1)}, u32[]{:S(2)}, u32[]{:S(2)}) collective-permute-start(bf16[64,1,16,128]{3,0,2,1:T(8,128)(2,1)S(1)} %get-tuple-element.24), channel_id=1, source_target_pairs={{4,0},{8,4},{12,8},{16,12},{20,16},{24,20},{28,24},{5,1},{9,5},{13... | collective-permute-start | bytes 786440 | tf_op jit(solution)/shard_map/ppermute | solution.py:20
  20.9 6.2 %collective-permute-start.2 = (bf16[64,4,1,128]{3,0,2,1:T(8,128)(2,1)S(1)}, bf16[64,4,1,128]{3,0,2,1:T(8,128)(2,1)S(1)}, u32[]{:S(2)}, u32[]{:S(2)}) collective-permute-start(bf16[64,4,1,128]{3,0,2,1:T(8,128)(2,1)S(1)} %get-tuple-element.22), channel_id=1, source_target_pairs={{0,1},{1,2},{2,3},{4,5},{5,6},{6,7},{8,9},{9,10},{10,11},{12,13},{... | collective-permute-start | bytes 196616 | tf_op jit(solution)/shard_map/ppermute | solution.py:17
  24.1 5.0 %collective-permute-start.3 = (bf16[64,4,1,128]{3,0,2,1:T(8,128)(2,1)S(1)}, bf16[64,4,1,128]{3,0,2,1:T(8,128)(2,1)S(1)}, u32[]{:S(2)}, u32[]{:S(2)}) collective-permute-start(bf16[64,4,1,128]{3,0,2,1:T(8,128)(2,1)S(1)} %get-tuple-element.23), channel_id=1, source_target_pairs={{1,0},{2,1},{3,2},{5,4},{6,5},{7,6},{9,8},{10,9},{11,10},{13,12},{... | collective-permute-start | bytes 196616 | tf_op jit(solution)/shard_map/ppermute | solution.py:20
  48.3 14.9 %collective-permute-start.4 = (bf16[2,2,2,32,1,16,128]{6,3,5,4,2,1,0:T(8,128)(2,1)S(1)}, bf16[2,2,2,32,1,16,128]{6,3,5,4,2,1,0:T(8,128)(2,1)S(1)}, u32[]{:S(2)}, u32[]{:S(2)}) collective-permute-start(bf16[2,2,2,32,1,16,128]{6,3,5,4,2,1,0:T(8,128)(2,1)S(1)} %get-tuple-element.18), channel_id=1, source_target_pairs={{0,4},{4,8},{8,12},{12,16},{16,20},{20,24},{24,28},{1,5},{5,9},{9,... | collective-permute-start | bytes 3145736 | tf_op jit(solution)/shard_map/ppermute | solution.py:17
  51.5 25.8 %collective-permute-start.5 = (bf16[2,2,2,32,1,16,128]{6,3,5,4,2,1,0:T(8,128)(2,1)S(1)}, bf16[2,2,2,32,1,16,128]{6,3,5,4,2,1,0:T(8,128)(2,1)S(1)}, u32[]{:S(2)}, u32[]{:S(2)}) collective-permute-start(bf16[2,2,2,32,1,16,128]{6,3,5,4,2,1,0:T(8,128)(2,1)S(1)} %get-tuple-element.19), channel_id=1, source_target_pairs={{4,0},{8,4},{12,8},{16,12},{20,16},{24,20},{28,24},{5,1},{9,5},{13... | collective-permute-start | bytes 3145736 | tf_op jit(solution)/shard_map/ppermute | solution.py:20
  77.3 6.7 %collective-permute-start.6 = (bf16[2,2,2,32,4,1,128]{6,3,5,4,2,1,0:T(8,128)(2,1)S(1)}, bf16[2,2,2,32,4,1,128]{6,3,5,4,2,1,0:T(8,128)(2,1)S(1)}, u32[]{:S(2)}, u32[]{:S(2)}) collective-permute-start(bf16[2,2,2,32,4,1,128]{6,3,5,4,2,1,0:T(8,128)(2,1)S(1)} %get-tuple-element.14), channel_id=1, source_target_pairs={{0,1},{1,2},{2,3},{4,5},{5,6},{6,7},{8,9},{9,10},{10,11},{12,13},{... | collective-permute-start | bytes 786440 | tf_op jit(solution)/shard_map/ppermute | solution.py:17
  80.5 7.1 %collective-permute-start.7 = (bf16[2,2,2,32,4,1,128]{6,3,5,4,2,1,0:T(8,128)(2,1)S(1)}, bf16[2,2,2,32,4,1,128]{6,3,5,4,2,1,0:T(8,128)(2,1)S(1)}, u32[]{:S(2)}, u32[]{:S(2)}) collective-permute-start(bf16[2,2,2,32,4,1,128]{6,3,5,4,2,1,0:T(8,128)(2,1)S(1)} %get-tuple-element.15), channel_id=1, source_target_pairs={{1,0},{2,1},{3,2},{5,4},{6,5},{7,6},{9,8},{10,9},{11,10},{13,12},{... | collective-permute-start | bytes 786440 | tf_op jit(solution)/shard_map/ppermute | solution.py:20
  97.7 73.0 %copy-start.1 = (bf16[32,4,18,130]{3,0,2,1:T(8,128)(2,1)}, bf16[32,4,18,130]{3,0,2,1:T(8,128)(2,1)S(1)}, u32[]{:S(2)}) copy-start(bf16[32,4,18,130]{3,0,2,1:T(8,128)(2,1)S(1)} %get-tuple-element.8) | copy-start | bytes 1797124
  97.7 73.3 %copy-start.2 = (bf16[32,4,18,130]{3,0,2,1:T(8,128)(2,1)}, bf16[32,4,18,130]{3,0,2,1:T(8,128)(2,1)S(1)}, u32[]{:S(2)}) copy-start(bf16[32,4,18,130]{3,0,2,1:T(8,128)(2,1)S(1)} %get-tuple-element.9) | copy-start | bytes 1797124
  97.7 77.2 %copy-start.3 = (bf16[32,4,18,130]{3,0,2,1:T(8,128)(2,1)}, bf16[32,4,18,130]{3,0,2,1:T(8,128)(2,1)S(1)}, u32[]{:S(2)}) copy-start(bf16[32,4,18,130]{3,0,2,1:T(8,128)(2,1)S(1)} %get-tuple-element.10) | copy-start | bytes 1797124
  97.7 77.6 %copy-start.4 = (bf16[32,4,18,130]{3,0,2,1:T(8,128)(2,1)}, bf16[32,4,18,130]{3,0,2,1:T(8,128)(2,1)S(1)}, u32[]{:S(2)}) copy-start(bf16[32,4,18,130]{3,0,2,1:T(8,128)(2,1)S(1)} %get-tuple-element.11) | copy-start | bytes 1797124
  97.7 78.6 %copy-start.5 = (bf16[32,4,18,130]{3,0,2,1:T(8,128)(2,1)}, bf16[32,4,18,130]{3,0,2,1:T(8,128)(2,1)S(1)}, u32[]{:S(2)}) copy-start(bf16[32,4,18,130]{3,0,2,1:T(8,128)(2,1)S(1)} %get-tuple-element.6) | copy-start | bytes 1797124
  97.7 78.9 %copy-start.7 = (bf16[32,4,18,130]{3,0,2,1:T(8,128)(2,1)}, bf16[32,4,18,130]{3,0,2,1:T(8,128)(2,1)S(1)}, u32[]{:S(2)}) copy-start(bf16[32,4,18,130]{3,0,2,1:T(8,128)(2,1)S(1)} %get-tuple-element.12) | copy-start | bytes 1797124
  184.9 3.0 copy-start.49
  185.3 2.6 copy-start.47
  188.4 2.7 copy-start.40
  188.5 3.0 copy-start.41
  188.5 3.3 %copy-start.42 = (f32[64,2,16,128]{3,0,2,1:T(8,128)S(1)}, f32[64,2,16,128]{3,0,2,1:T(8,128)}, u32[]{:S(2)}) copy-start(f32[64,2,16,128]{3,0,2,1:T(8,128)} %convolution_bitcast_fusion.31) | copy-start | bytes 3145732
  191.8 2.7 copy-start.33
  191.8 3.0 copy-start.34
  191.8 3.3 %copy-start.35 = (f32[64,2,16,128]{3,0,2,1:T(8,128)S(1)}, f32[64,2,16,128]{3,0,2,1:T(8,128)}, u32[]{:S(2)}) copy-start(f32[64,2,16,128]{3,0,2,1:T(8,128)} %convolution_bitcast_fusion.23) | copy-start | bytes 3145732
  195.1 2.7 copy-start.26
  195.1 3.0 copy-start.27
  195.1 3.3 %copy-start.28 = (f32[64,2,16,128]{3,0,2,1:T(8,128)S(1)}, f32[64,2,16,128]{3,0,2,1:T(8,128)}, u32[]{:S(2)}) copy-start(f32[64,2,16,128]{3,0,2,1:T(8,128)} %convolution_bitcast_fusion.15) | copy-start | bytes 3145732
  198.4 2.7 copy-start.19
  198.4 3.0 copy-start.20
  198.4 3.3 %copy-start.21 = (f32[64,2,16,128]{3,0,2,1:T(8,128)S(1)}, f32[64,2,16,128]{3,0,2,1:T(8,128)}, u32[]{:S(2)}) copy-start(f32[64,2,16,128]{3,0,2,1:T(8,128)} %convolution_bitcast_fusion.9) | copy-start | bytes 3145732
  201.7 2.8 copy-start.14
  (30 other events, 60.1 us)
Sparse Core Ops, SparseCore 0:
  178.1 128.8 all-reduce.3
where the time goes:
time: 322 us; the launch traced here: 316 us
  waiting for transfers between devices  133 us (41%)
  matrix products  114 us (35%)
  starting transfers between devices  20.6 us (6%)
  local copies, waits for them, and re-layouts  17.7 us (5%)
  other arithmetic  15.5 us (5%)
  between operations  15.3 us (5%)
    psum x1, waiting for transfers between devices, on_device(): stacked_grad = lax.psum(stacked_grad, ('gx', 'gy'))  101 us
    dot_general x64, matrix products, on_device(): lax.dot_general(kernel[tap_x, tap_y, tap_z], piece, (((0,), (0,)), ((), (...  75.6 us
    ppermute x4, waiting for transfers between devices, padded_2(): lax.ppermute(lax.slice_in_dim(block, 0, width, axis=dim), axis, backward)  22.9 us
    dot_general x64, matrix products, on_device(): lax.dot_general(piece, volume, (((1, 2, 3), (1, 2, 3)), ((), ())), prefer...  21.3 us
    dot_general x64, matrix products, phase_product(): lax.dot_general(kernel[tap_x, tap_y, tap_z], piece, (((1,), (0,)), ((), (...  17 us
    unnamed x111, local copies, waits for them, and re-layouts  16 us
    ppermute x4, starting transfers between devices, padded_2(): lax.ppermute(lax.slice_in_dim(block, block.shape[dim] - width, None, axis...  14.1 us
    concatenate x3, other arithmetic, padded_2(): block = jnp.concatenate([low, block, high], axis=dim)  10.7 us
  transfers between devices with their start and end apart: 9, of which 6 were waited for; matrix products, arithmetic and copies ran while one was open for 8% of the time, Pallas kernels for 0%

commit v1 on v0

v1 whole, which is shorter than its diff:
```python
import functools
import math

import jax
import jax.numpy as jnp
from jax import lax
from jax.experimental import pallas as pl
from jax.experimental.pallas import tpu as pltpu
from jax.sharding import PartitionSpec as P

F32 = jnp.float32
BF16 = jnp.bfloat16


def forward_kernel(nx, ny, nz, ci, co, chunk, ext, xlo, xhi, w, cot, act, g, wg, vm, ga, gb):
    half = 4 * ci
    rows = 8 * co

    def plain(x, lanes):
        if x == 0:
            return xlo[0, :, lanes]
        if x == nx + 1:
            return xhi[0, :, lanes]
        return ext[x - 1, :, lanes]

    def corners(get, i, j0, j1):
        return jnp.concatenate(
            [
                get(i + 1 - ex, slice((j0 + 1 - ey) * nz, (j1 + 1 - ey) * nz))
                for ex in range(2)
                for ey in range(2)
            ],
            axis=0,
        )

    def rolled(x, lanes):
        return vm[x, :, lanes]

    for x in range(nx + 2):
        for y in range(ny + 2):
            lanes = slice(y * nz, (y + 1) * nz)
            vm[x, :, lanes] = pltpu.roll(plain(x, lanes).astype(F32), 1, 1).astype(BF16)

    first = lax.broadcasted_iota(jnp.int32, (co, nz), 1) == 0
    zeros = jnp.zeros((2 * co, nz), BF16)

    for i in range(nx + 1):
        for j0 in range(0, ny + 1, chunk):
            j1 = min(j0 + chunk, ny + 1)
            back = jnp.dot(w[:, half:], corners(rolled, i, j0, j1), preferred_element_type=F32)
            here = jnp.dot(w[:, :half], corners(plain, i, j0, j1), preferred_element_type=F32)
            for j in range(j0, j1):
                cols = slice((j - j0) * nz, (j - j0 + 1) * nz)
                wide = slice(j * nz, (j + 1) * nz)
                for tx in range(2):
                    for ty in range(2):
                        sx, sy = 1 - tx, 1 - ty
                        m, n = i - sx, j - sy
                        base = (2 * tx + ty) * 2 * co
                        if not (0 <= m < nx and 0 <= n < ny):
                            g[i, base : base + 2 * co, wide] = zeros
                            ga[i, base : base + 2 * co, wide] = zeros
                            gb[i, base : base + 2 * co, wide] = zeros
                            continue
                        out = slice(n * nz, (n + 1) * nz)
                        for tz in range(2):
                            sz = 1 - tz
                            r = slice(base + tz * co, base + (tz + 1) * co)
                            low, high = back[r, cols], here[r, cols]
                            if sz == 1:
                                before = low + jnp.where(first, 0.0, high)
                                before = pltpu.roll(before, nz - 1, 1)
                            else:
                                before = jnp.where(first, 0.0, low) + high
                            q = ((2 * sx + sy) * 2 + sz) * co
                            sig = 0.5 * jnp.tanh(0.5 * before) + 0.5
                            value = before * sig
                            act[m, q : q + co, out] = value.astype(BF16)
                            slope = sig + value * (1.0 - sig)
                            grad = cot[m, q : q + co, out].astype(F32) * slope
                            if sz == 1:
                                grad = pltpu.roll(grad, 1, 1)
                            whole = grad.astype(BF16)
                            cut = jnp.where(first, 0.0, grad).astype(BF16)
                            g[i, r, wide] = whole
                            ga[i, r, wide] = cut if sz == 0 else whole
                            gb[i, r, wide] = cut if sz == 1 else whole

    nt = (((1,), (1,)), ((), ()))
    for part, (grads, get) in enumerate(((gb, plain), (ga, rolled))):
        total = None
        for i in range(nx + 1):
            term = lax.dot_general(
                grads[i], corners(get, i, 0, ny + 1), nt, preferred_element_type=F32
            )
            total = term if total is None else total + term
        wg[:, part * half : (part + 1) * half] = total


def backward_kernel(nx, ny, nz, ci, co, chunk, g, wt, ig, u):
    half = 4 * ci
    rows = 8 * co
    shape = (rows, nz)
    first = lax.broadcasted_iota(jnp.int32, shape, 1) == 0
    phase = (lax.broadcasted_iota(jnp.int32, shape, 0) // co) % 2
    cut_a = first & (phase == 1)
    cut_b = first & (phase == 0)
    for i in range(nx + 1):
        for j0 in range(0, ny + 1, chunk):
            j1 = min(j0 + chunk, ny + 1)
            lefts, rights = [], []
            for j in range(j0, j1):
                piece = g[i, :, j * nz : (j + 1) * nz].astype(F32)
                lefts.append(jnp.where(cut_a, 0.0, piece).astype(BF16))
                rights.append(jnp.where(cut_b, 0.0, piece).astype(BF16))
            back = jnp.dot(wt[half:], jnp.concatenate(lefts, axis=1), preferred_element_type=F32)
            here = jnp.dot(wt[:half], jnp.concatenate(rights, axis=1), preferred_element_type=F32)
            for j in range(j0, j1):
                cols = slice((j - j0) * nz, (j - j0 + 1) * nz)
                u[i, :, j * nz : (j + 1) * nz] = here[:, cols] + pltpu.roll(
                    back[:, cols], nz - 1, 1
                )
    for m in range(-1, nx + 1):
        for y in range(-1, ny + 1):
            total = None
            for ex in range(2):
                for ey in range(2):
                    i, j = m + ex, y + ey
                    if 0 <= i <= nx and 0 <= j <= ny:
                        r = (2 * ex + ey) * ci
                        term = u[i, r : r + ci, j * nz : (j + 1) * nz]
                        total = term if total is None else total + term
            ig[m + 1, :, (y + 1) * nz : (y + 2) * nz] = total


def neighbours(axis):
    count = lax.axis_size(axis)
    up = [(i, i + 1) for i in range(count - 1)]
    return up, [(b, a) for a, b in up]


def on_device(volume, kernel, cotangent):
    ci, nx, ny, nz = volume.shape
    co = kernel.shape[3]
    gx_up, gx_down = neighbours("gx")
    gy_up, gy_down = neighbours("gy")
    devices = lax.axis_size("gx") * lax.axis_size("gy")
    cells = nx * lax.axis_size("gx") * ny * lax.axis_size("gy") * nz

    flat = volume.transpose(1, 0, 2, 3).reshape(nx, ci, ny * nz)
    ylo = lax.ppermute(flat[:, :, (ny - 1) * nz :], "gy", gy_up)
    yhi = lax.ppermute(flat[:, :, :nz], "gy", gy_down)
    ext = jnp.concatenate([ylo, flat, yhi], axis=2)
    xlo = lax.ppermute(ext[nx - 1 :], "gx", gx_up)
    xhi = lax.ppermute(ext[:1], "gx", gx_down)

    taps = kernel.reshape(2, 2, 2, 2, 2, 2, co, ci)
    w = taps.transpose(1, 3, 5, 6, 4, 0, 2, 7).reshape(8 * co, 8 * ci)
    wt = w.T
    cot = (
        cotangent.reshape(8 * co, nx, ny, nz).transpose(1, 0, 2, 3).reshape(nx, 8 * co, ny * nz)
    )

    vmem = pl.BlockSpec(memory_space=pltpu.VMEM)
    chunk = 4
    act, g, wg = pl.pallas_call(
        functools.partial(forward_kernel, nx, ny, nz, ci, co, chunk),
        out_shape=(
            jax.ShapeDtypeStruct((nx, 8 * co, ny * nz), BF16),
            jax.ShapeDtypeStruct((nx + 1, 8 * co, (ny + 1) * nz), BF16),
            jax.ShapeDtypeStruct((8 * co, 8 * ci), F32),
        ),
        in_specs=[vmem] * 5,
        out_specs=(vmem,) * 3,
        scratch_shapes=[
            pltpu.VMEM((nx + 2, ci, (ny + 2) * nz), BF16),
            pltpu.VMEM((nx + 1, 8 * co, (ny + 1) * nz), BF16),
            pltpu.VMEM((nx + 1, 8 * co, (ny + 1) * nz), BF16),
        ],
        compiler_params=pltpu.CompilerParams(vmem_limit_bytes=48 * 1024 * 1024),
    )(ext, xlo, xhi, w, cot)

    shares = wg.astype(BF16).reshape(devices, 8 * co * 8 * ci // devices // 128, 128)
    mine = lax.all_to_all(shares, ("gx", "gy"), 0, 0, tiled=True)
    scale = 1.0 / math.sqrt(cells)
    summed = (jnp.sum(mine.astype(F32), axis=0) * scale).astype(F32)
    spread = jnp.broadcast_to(summed[None], (devices,) + summed.shape)
    gathered = lax.all_to_all(spread, ("gx", "gy"), 0, 0, tiled=True)
    weight_grad = (
        gathered.reshape(2, 2, 2, co, 2, 2, 2, ci)
        .transpose(5, 0, 6, 1, 4, 2, 3, 7)
        .reshape(4, 4, 4, co, ci)
    )

    ig = pl.pallas_call(
        functools.partial(backward_kernel, nx, ny, nz, ci, co, chunk),
        out_shape=jax.ShapeDtypeStruct((nx + 2, ci, (ny + 2) * nz), F32),
        in_specs=[vmem] * 2,
        out_specs=vmem,
        scratch_shapes=[pltpu.VMEM((nx + 1, 4 * ci, (ny + 1) * nz), F32)],
        compiler_params=pltpu.CompilerParams(vmem_limit_bytes=48 * 1024 * 1024),
    )(g, wt)
    from_low = lax.ppermute(ig[nx + 1 :].astype(BF16), "gx", gx_up).astype(F32)
    from_high = lax.ppermute(ig[:1].astype(BF16), "gx", gx_down).astype(F32)
    zero = jnp.zeros((nx - 1,) + from_low.shape[1:], F32)
    mid = (
        ig[1 : nx + 1]
        + jnp.concatenate([from_low, zero], axis=0)
        + jnp.concatenate([zero, from_high], axis=0)
    )
    y_low = lax.ppermute(mid[:, :, (ny + 1) * nz :].astype(BF16), "gy", gy_up).astype(F32)
    y_high = lax.ppermute(mid[:, :, :nz].astype(BF16), "gy", gy_down).astype(F32)
    gap = jnp.zeros((nx, ci, (ny - 1) * nz), F32)
    full = (
        mid[:, :, nz : (ny + 1) * nz]
        + jnp.concatenate([y_low, gap], axis=2)
        + jnp.concatenate([gap, y_high], axis=2)
    )
    input_grad = full.astype(BF16).reshape(nx, ci, ny, nz).transpose(1, 0, 2, 3)
    activation = (
        act.reshape(nx, 8 * co, ny, nz).transpose(1, 0, 2, 3).reshape(cotangent.shape)
    )
    return activation, input_grad, weight_grad


def solution(mesh):
    placed = (P(None, "gx", "gy", None), P(), P(None, None, None, None, "gx", "gy", None))
    return jax.shard_map(
        on_device,
        mesh=mesh,
        in_specs=placed,
        out_specs=(placed[2], placed[0], P()),
        check_vma=False,
    )
```

time: 322 us -> 90.1 us (0.28); the launches traced: 316 us -> 89.2 us
  waiting for transfers between devices: 133 us -> 13.3 us
  matrix products: 114 us -> 0 us
  between operations: 15.3 us -> 0.86 us
  starting transfers between devices: 20.6 us -> 33.9 us
  other arithmetic: 15.5 us -> 2.63 us
  local copies, waits for them, and re-layouts: 17.7 us -> 28.4 us
  Pallas kernels: 0 us -> 10.1 us
    dot_general x192 -> x0, matrix products: 114 us -> none  [the longest x64 75.6 us: on_device(): lax.dot_general(kernel[tap_x, tap_y, tap_z], piece, (((0,), (0,)), ((), (...]
    psum x1 -> x0, waiting for transfers between devices: 101 us -> none  [on_device(): stacked_grad = lax.psum(stacked_grad, ('gx', 'gy'))]
    ppermute x8, waiting for transfers between devices: 32.7 us -> 1.22 us  [the longest x1 0.69 us: on_device(): xhi = lax.ppermute(ext[:1], 'gx', gx_down)]
    all_to_all x0 -> x2, waiting for transfers between devices: none -> 12.1 us  [the longest x1 9.89 us: on_device(): gathered = lax.all_to_all(spread, ('gx', 'gy'), 0, 0, tiled=True)]
    all_to_all x0 -> x2, starting transfers between devices: none -> 10.9 us  [the longest x1 5.94 us: on_device(): mine = lax.all_to_all(shares, ('gx', 'gy'), 0, 0, tiled=True)]
    concatenate x3 -> x0, other arithmetic: 10.7 us -> none  [padded_2(): block = jnp.concatenate([low, block, high], axis=dim)]
    pallas_call x0 -> x2, Pallas kernels: none -> 10.1 us  [the longest x1 7.95 us: on_device(): pl.pallas_call(functools.partial(forward_kernel, nx, ny, nz, ci, co, chun...]
    reshape x0 -> x7, local copies, waits for them, and re-layouts: none -> 10 us  [the longest x1 4.18 us: on_device(): cotangent.reshape(8 * co, nx, ny, nz).transpose(1, 0, 2, 3)]
  transfers between devices with their start and end apart: 9 -> 10, of which waited for: 6 -> 4; matrix products, arithmetic and copies ran while one was open for 8% -> 23% of each run, Pallas kernels for 0% -> 0%
where the time goes in v1:
time: 90.1 us; the launch traced here: 89.2 us
  starting transfers between devices  33.9 us (38%)
  local copies, waits for them, and re-layouts  28.4 us (32%)
  waiting for transfers between devices  13.3 us (15%)
  Pallas kernels  10.1 us (11%)
  other arithmetic  2.63 us (3%)
    all_to_all x1, waiting for transfers between devices, on_device(): gathered = lax.all_to_all(spread, ('gx', 'gy'), 0, 0, tiled=True)  9.89 us
    unnamed x16, local copies, waits for them, and re-layouts  8.5 us
    pallas_call x1, Pallas kernels, on_device(): pl.pallas_call(functools.partial(forward_kernel, nx, ny, nz, ci, co, chun...  7.95 us
    all_to_all x1, starting transfers between devices, on_device(): mine = lax.all_to_all(shares, ('gx', 'gy'), 0, 0, tiled=True)  5.94 us
    ppermute x1, starting transfers between devices, on_device(): xlo = lax.ppermute(ext[nx - 1:], 'gx', gx_up)  5.1 us
    all_to_all x1, starting transfers between devices, on_device(): gathered = lax.all_to_all(spread, ('gx', 'gy'), 0, 0, tiled=True)  4.94 us
    ppermute x1, starting transfers between devices, on_device(): ylo = lax.ppermute(flat[:, :, (ny - 1) * nz:], 'gy', gy_up)  4.64 us
    reshape x1, local copies, waits for them, and re-layouts, on_device(): cotangent.reshape(8 * co, nx, ny, nz).transpose(1, 0, 2, 3)  4.18 us
  transfers between devices with their start and end apart: 10, of which 4 were waited for; matrix products, arithmetic and copies ran while one was open for 23% of the time, Pallas kernels for 0%

profile of v1, /device:TPU:1, one launch (start us, length us, event | category | flops | bytes accessed | tf_op | source)
XLA Modules:
  0.0 89.2 jit_solution(15911716543914808345)
XLA Ops:
  0.6 1.3 %reshape.53 = bf16[2,64,2048]{2,0,1:T(2,128)(2,1)S(1)} reshape(bf16[2,64,16,128]{3,2,0,1:T(8,128)(2,1)} %bitcast.47) | data formatting | bytes 1048576 | tf_op jit(solution)/shard_map/reshape | solution.py:150
  2.0 4.6 %collective-permute-start = (bf16[2,64,128]{2,1,0:T(8,128)(2,1)S(1)}, bf16[2,64,128]{2,1,0:T(8,128)(2,1)}, u32[]{:S(2)}, u32[]{:S(2)}) collective-permute-start(bf16[2,64,128]{2,1,0:T(8,128)(2,1)S(1)} %copy.32), channel_id=1, source_target_pairs={{0,1},{1,2},{2,3},{4,5},{5,6},{6,7},{8,9},{9,10},{10,11},{12,13},{... | collective-permute-start | bytes 98312 | tf_op jit(solution)/shard_map/ppermute | solution.py:151
  6.7 1.3 %collective-permute-start.1 = (bf16[2,64,128]{2,1,0:T(8,128)(2,1)S(1)}, bf16[2,64,128]{2,1,0:T(8,128)(2,1)S(1)}, u32[]{:S(2)}, u32[]{:S(2)}) collective-permute-start(bf16[2,64,128]{2,1,0:T(8,128)(2,1)S(1)} %copy.33), channel_id=1, source_target_pairs={{1,0},{2,1},{3,2},{5,4},{6,5},{7,6},{9,8},{10,9},{11,10},{13,12},{... | collective-permute-start | bytes 98312 | tf_op jit(solution)/shard_map/ppermute | solution.py:152
  8.0 1.6 %copy.34 = bf16[2,2,2,2,2,2,32,64]{7,2,0,4,6,5,3,1:T(2,128)(2,1)S(1)} copy(bf16[2,2,2,2,2,2,32,64]{7,6,5,4,3,2,1,0:T(8,128)(2,1)} %bitcast.48) | data formatting | bytes 524288 | tf_op jit(solution)/shard_map/reshape | solution.py:157
  11.3 0.8 fusion.7
  12.2 5.1 %collective-permute-start.2 = (bf16[1,64,2304]{2,1,0:T(8,128)(2,1)}, bf16[1,64,2304]{2,1,0:T(8,128)(2,1)S(1)}, u32[]{:S(2)}, u32[]{:S(2)}) collective-permute-start(bf16[1,64,2304]{2,1,0:T(8,128)(2,1)} %get-tuple-element.16), channel_id=1, source_target_pairs={{0,4},{4,8},{8,12},{12,16},{16,20},{20,24},{24,28},{1,5},{5,9},{9,... | collective-permute-start | bytes 884744 | tf_op jit(solution)/shard_map/ppermute | solution.py:154
  17.3 1.9 %collective-permute-start.3 = (bf16[1,64,2304]{2,1,0:T(8,128)(2,1)}, bf16[1,64,2304]{2,1,0:T(8,128)(2,1)}, u32[]{:S(2)}, u32[]{:S(2)}) collective-permute-start(bf16[1,64,2304]{2,1,0:T(8,128)(2,1)} %get-tuple-element.15), channel_id=1, source_target_pairs={{4,0},{8,4},{12,8},{16,12},{20,16},{24,20},{28,24},{5,1},{9,5},{13... | collective-permute-start | bytes 884744 | tf_op jit(solution)/shard_map/ppermute | solution.py:155
  19.2 1.8 %copy_bitcast_fusion = bf16[2,256,16,128]{3,2,1,0:T(8,128)(2,1)} fusion(bf16[2,2,2,32,2,16,128]{6,5,4,3,2,1,0:T(8,128)(2,1)S(1)} %copy-done), kind=kLoop, calls=%fused_computation.1 | loop fusion | bytes 4194304 | tf_op jit(solution)/shard_map/transpose | solution.py:161
  21.1 4.2 %reshape.46.cot = bf16[2,256,2048]{2,1,0:T(8,128)(2,1)} reshape(bf16[2,256,16,128]{3,2,1,0:T(8,128)(2,1)} %copy_bitcast_fusion) | data formatting | bytes 4194304 | tf_op jit(solution)/shard_map/reshape | solution.py:161
  26.1 1.6 %copy-done.2 = bf16[2,256,2048]{2,1,0:T(8,128)(2,1)S(1)} copy-done((bf16[2,256,2048]{2,1,0:T(8,128)(2,1)S(1)}, bf16[2,256,2048]{2,1,0:T(8,128)(2,1)}, u32[]{:S(2)}) %copy-start.2) | copy-done | bytes 2097176
  27.7 7.9 %shard_map.58 = (bf16[2,256,2048]{2,1,0:T(8,128)(2,1)S(1)}, bf16[3,256,2176]{2,1,0:T(8,128)(2,1)}, f32[256,512]{1,0:T(8,128)S(1)}) custom-call(bf16[2,64,2304]{2,1,0:T(8,128)(2,1)S(1)} %constant_dynamic-update-slice_fusion.ext, bf16[1,64,2304]{2,1,0:T(8,128)(2,1)S(1)} %collective-permute-done.2.xlo, bf16[1,64,2304]{2,1,0:T(8,128)(2,1)} %collective-permute-done.3.xhi, ...), custom_call_target="tpu_custom_call" | custom-call | tf_op jit(solution)/shard_map/pallas_call | solution.py:166
  35.6 1.9 %copy-done.3 = bf16[3,256,2176]{2,1,0:T(8,128)(2,1)S(1)} copy-done((bf16[3,256,2176]{2,1,0:T(8,128)(2,1)S(1)}, bf16[3,256,2176]{2,1,0:T(8,128)(2,1)}, u32[]{:S(2)}) %copy-start.3) | copy-done | bytes 3342360
  37.6 2.1 %shard_map.59 = f32[4,64,2304]{2,1,0:T(8,128)S(1)} custom-call(bf16[3,256,2176]{2,1,0:T(8,128)(2,1)S(1)} %copy-done.3, bf16[512,256]{1,0:T(8,128)(2,1)S(1)} %bitcast.39), custom_call_target="tpu_custom_call" | custom-call | tf_op jit(solution)/shard_map/pallas_call | solution.py:195
  39.8 1.2 %copy-done.1 = f32[4,64,2304]{2,1,0:T(8,128)} copy-done((f32[4,64,2304]{2,1,0:T(8,128)}, f32[4,64,2304]{2,1,0:T(8,128)S(1)}, u32[]{:S(2)}) %copy-start.1) | copy-done | bytes 2359320
  41.1 2.9 %collective-permute-start.4 = (bf16[1,64,2304]{2,1,0:T(8,128)(2,1)S(1)}, bf16[1,64,2304]{2,1,0:T(8,128)(2,1)S(1)}, u32[]{:S(2)}, u32[]{:S(2)}) collective-permute-start(bf16[1,64,2304]{2,1,0:T(8,128)(2,1)S(1)} %get-tuple-element.11), channel_id=1, source_target_pairs={{0,4},{4,8},{8,12},{12,16},{16,20},{20,24},{24,28},{1,5},{5,9},{9,... | collective-permute-start | bytes 884744 | tf_op jit(solution)/shard_map/ppermute | solution.py:203
  44.0 1.9 %collective-permute-start.5 = (bf16[1,64,2304]{2,1,0:T(8,128)(2,1)S(1)}, bf16[1,64,2304]{2,1,0:T(8,128)(2,1)}, u32[]{:S(2)}, u32[]{:S(2)}) collective-permute-start(bf16[1,64,2304]{2,1,0:T(8,128)(2,1)S(1)} %get-tuple-element.12), channel_id=1, source_target_pairs={{4,0},{8,4},{12,8},{16,12},{20,16},{24,20},{28,24},{5,1},{9,5},{13... | collective-permute-start | bytes 884744 | tf_op jit(solution)/shard_map/ppermute | solution.py:204
  46.0 2.0 %copy.26 = bf16[64,8,16,128]{3,2,1,0:T(8,128)(2,1)} copy(bf16[64,8,16,128]{3,1,2,0:T(8,128)(2,1)S(1)} %bitcast.38) | data formatting | bytes 4194304
  48.0 0.9 reshape.50
  48.8 5.9 %all-to-all-start = ((bf16[32,32,128]{2,1,0:T(8,128)(2,1)}), bf16[32,32,128]{2,1,0:T(8,128)(2,1)S(1)}, u32[]{:S(2)}, u32[]{:S(2)}) async-start(bf16[32,32,128]{2,1,0:T(8,128)(2,1)} %reshape.50), calls=%async_computation | async-start | bytes 524288 | tf_op jit(solution)/shard_map/all_to_all | solution.py:184
  55.5 1.6 %fusion.3 = (bf16[2,64,2304]{2,1,0:T(8,128)(2,1)S(1)}, f32[2,64,2304]{2,1,0:T(8,128)S(1)}) fusion(bf16[1,64,2304]{2,1,0:T(8,128)(2,1)} %collective-permute-done.5, bf16[1,64,2304]{2,1,0:T(8,128)(2,1)} %copy-done.4, f32[4,64,2304]{2,1,0:T(8,128)} %copy-done.1), kind=kLoop, calls=%fused_computation.14 | loop fusion | flops 1474560 | bytes 3538944 | tf_op jit(solution)/shard_map/convert.9
  57.7 3.9 %collective-permute-start.6 = (bf16[2,64,128]{2,1,0:T(8,128)(2,1)}, bf16[2,64,128]{2,1,0:T(8,128)(2,1)}, u32[]{:S(2)}, u32[]{:S(2)}) collective-permute-start(bf16[2,64,128]{2,1,0:T(8,128)(2,1)} %get-tuple-element.13), channel_id=1, source_target_pairs={{0,1},{1,2},{2,3},{4,5},{5,6},{6,7},{8,9},{9,10},{10,11},{12,13},{... | collective-permute-start | bytes 98312 | tf_op jit(solution)/shard_map/ppermute | solution.py:211
  61.6 1.3 %collective-permute-start.7 = (bf16[2,64,128]{2,1,0:T(8,128)(2,1)}, bf16[2,64,128]{2,1,0:T(8,128)(2,1)}, u32[]{:S(2)}, u32[]{:S(2)}) collective-permute-start(bf16[2,64,128]{2,1,0:T(8,128)(2,1)} %get-tuple-element.14), channel_id=1, source_target_pairs={{1,0},{2,1},{3,2},{5,4},{6,5},{7,6},{9,8},{10,9},{11,10},{13,12},{... | collective-permute-start | bytes 98312 | tf_op jit(solution)/shard_map/ppermute | solution.py:212
  62.9 2.2 %all-to-all-done = bf16[32,32,128]{2,1,0:T(8,128)(2,1)S(1)} async-done(((bf16[32,32,128]{2,1,0:T(8,128)(2,1)}), bf16[32,32,128]{2,1,0:T(8,128)(2,1)S(1)}, u32[]{:S(2)}, u32[]{:S(2)}) %all-to-all-start) | async-done | bytes 262176 | tf_op jit(solution)/shard_map/all_to_all | solution.py:184
  65.2 0.9 broadcast_in_dim.2
  66.0 4.9 %all-to-all-start.1 = ((f32[32,32,128]{2,1,0:T(8,128)}), f32[32,32,128]{2,1,0:T(8,128)}, u32[]{:S(2)}, u32[]{:S(2)}) async-start(f32[32,32,128]{2,1,0:T(8,128)} %broadcast_in_dim.2), calls=%async_computation.1 | async-start | bytes 1048576 | tf_op jit(solution)/shard_map/all_to_all | solution.py:188
  71.0 2.0 %bitcast_bitcast_fusion = bf16[256,2,16,128]{3,2,0,1:T(8,128)(2,1)S(1)} fusion(bf16[2,256,16,128]{3,2,1,0:T(8,128)(2,1)} %bitcast.40), kind=kLoop, calls=%fused_computation | loop fusion | bytes 4194304 | tf_op jit(solution)/shard_map/transpose | solution.py:221
  73.0 1.7 %copy.21 = bf16[256,2,16,128]{3,2,1,0:T(8,128)(2,1)} copy(bf16[256,2,16,128]{3,2,0,1:T(8,128)(2,1)S(1)} %bitcast_bitcast_fusion) | data formatting | bytes 4194304 | tf_op jit(solution)/shard_map/transpose | solution.py:221
  74.6 0.8 fusion.2
  75.6 0.8 copy_bitcast_fusion.1
  76.4 9.9 %all-to-all-done.1 = f32[32,32,128]{2,1,0:T(8,128)} async-done(((f32[32,32,128]{2,1,0:T(8,128)}), f32[32,32,128]{2,1,0:T(8,128)}, u32[]{:S(2)}, u32[]{:S(2)}) %all-to-all-start.1) | async-done | bytes 524320 | tf_op jit(solution)/shard_map/all_to_all | solution.py:188
  86.3 1.7 %reshape.51 = f32[2,2,2,32,2,2,2,64]{7,6,5,4,3,2,1,0:T(2,128)S(1)} reshape(f32[32,32,128]{2,1,0:T(8,128)} %all-to-all-done.1) | data formatting | bytes 1048576 | tf_op jit(solution)/shard_map/reshape | solution.py:190
  88.0 1.2 %copy.24 = f32[2,2,2,2,2,2,32,64]{7,6,5,4,3,2,1,0:T(8,128)} copy(f32[2,2,2,2,2,2,32,64]{7,2,0,4,6,5,3,1:T(2,128)S(1)} %bitcast.41) | data formatting | bytes 1048576 | tf_op jit(solution)/shard_map/transpose | solution.py:191
  (30 shorter events, 4.4 us)
Async XLA Ops:
  0.6 18.6 %copy-start = (bf16[2,2,2,32,2,16,128]{6,5,4,3,2,1,0:T(8,128)(2,1)S(1)}, bf16[2,2,2,32,2,16,128]{6,5,4,3,2,1,0:T(8,128)(2,1)}, u32[]{:S(2)}) copy-start(bf16[2,2,2,32,2,16,128]{6,5,4,3,2,1,0:T(8,128)(2,1)} %param.5) | copy-start | bytes 6291460
  2.0 7.8 %collective-permute-start = (bf16[2,64,128]{2,1,0:T(8,128)(2,1)S(1)}, bf16[2,64,128]{2,1,0:T(8,128)(2,1)}, u32[]{:S(2)}, u32[]{:S(2)}) collective-permute-start(bf16[2,64,128]{2,1,0:T(8,128)(2,1)S(1)} %copy.32), channel_id=1, source_target_pairs={{0,1},{1,2},{2,3},{4,5},{5,6},{6,7},{8,9},{9,10},{10,11},{12,13},{... | collective-permute-start | bytes 98312 | tf_op jit(solution)/shard_map/ppermute | solution.py:151
  6.7 4.6 %collective-permute-start.1 = (bf16[2,64,128]{2,1,0:T(8,128)(2,1)S(1)}, bf16[2,64,128]{2,1,0:T(8,128)(2,1)S(1)}, u32[]{:S(2)}, u32[]{:S(2)}) collective-permute-start(bf16[2,64,128]{2,1,0:T(8,128)(2,1)S(1)} %copy.33), channel_id=1, source_target_pairs={{1,0},{2,1},{3,2},{5,4},{6,5},{7,6},{9,8},{10,9},{11,10},{13,12},{... | collective-permute-start | bytes 98312 | tf_op jit(solution)/shard_map/ppermute | solution.py:152
  12.2 13.2 %collective-permute-start.2 = (bf16[1,64,2304]{2,1,0:T(8,128)(2,1)}, bf16[1,64,2304]{2,1,0:T(8,128)(2,1)S(1)}, u32[]{:S(2)}, u32[]{:S(2)}) collective-permute-start(bf16[1,64,2304]{2,1,0:T(8,128)(2,1)} %get-tuple-element.16), channel_id=1, source_target_pairs={{0,4},{4,8},{8,12},{12,16},{16,20},{20,24},{24,28},{1,5},{5,9},{9,... | collective-permute-start | bytes 884744 | tf_op jit(solution)/shard_map/ppermute | solution.py:154
  17.3 8.8 %collective-permute-start.3 = (bf16[1,64,2304]{2,1,0:T(8,128)(2,1)}, bf16[1,64,2304]{2,1,0:T(8,128)(2,1)}, u32[]{:S(2)}, u32[]{:S(2)}) collective-permute-start(bf16[1,64,2304]{2,1,0:T(8,128)(2,1)} %get-tuple-element.15), channel_id=1, source_target_pairs={{4,0},{8,4},{12,8},{16,12},{20,16},{24,20},{28,24},{5,1},{9,5},{13... | collective-permute-start | bytes 884744 | tf_op jit(solution)/shard_map/ppermute | solution.py:155
  26.1 1.6 %copy-start.2 = (bf16[2,256,2048]{2,1,0:T(8,128)(2,1)S(1)}, bf16[2,256,2048]{2,1,0:T(8,128)(2,1)}, u32[]{:S(2)}) copy-start(bf16[2,256,2048]{2,1,0:T(8,128)(2,1)} %reshape.46.cot) | copy-start | bytes 6291460
  35.6 1.9 %copy-start.3 = (bf16[3,256,2176]{2,1,0:T(8,128)(2,1)S(1)}, bf16[3,256,2176]{2,1,0:T(8,128)(2,1)}, u32[]{:S(2)}) copy-start(bf16[3,256,2176]{2,1,0:T(8,128)(2,1)} %get-tuple-element.7.g) | copy-start | bytes 10027012
  39.7 1.4 %copy-start.1 = (f32[4,64,2304]{2,1,0:T(8,128)}, f32[4,64,2304]{2,1,0:T(8,128)S(1)}, u32[]{:S(2)}) copy-start(f32[4,64,2304]{2,1,0:T(8,128)S(1)} %shard_map.59) | copy-start | bytes 7077892
  41.1 13.7 %collective-permute-start.4 = (bf16[1,64,2304]{2,1,0:T(8,128)(2,1)S(1)}, bf16[1,64,2304]{2,1,0:T(8,128)(2,1)S(1)}, u32[]{:S(2)}, u32[]{:S(2)}) collective-permute-start(bf16[1,64,2304]{2,1,0:T(8,128)(2,1)S(1)} %get-tuple-element.11), channel_id=1, source_target_pairs={{0,4},{4,8},{8,12},{12,16},{16,20},{20,24},{24,28},{1,5},{5,9},{9,... | collective-permute-start | bytes 884744 | tf_op jit(solution)/shard_map/ppermute | solution.py:203
  44.0 11.5 %collective-permute-start.5 = (bf16[1,64,2304]{2,1,0:T(8,128)(2,1)S(1)}, bf16[1,64,2304]{2,1,0:T(8,128)(2,1)}, u32[]{:S(2)}, u32[]{:S(2)}) collective-permute-start(bf16[1,64,2304]{2,1,0:T(8,128)(2,1)S(1)} %get-tuple-element.12), channel_id=1, source_target_pairs={{4,0},{8,4},{12,8},{16,12},{20,16},{24,20},{28,24},{5,1},{9,5},{13... | collective-permute-start | bytes 884744 | tf_op jit(solution)/shard_map/ppermute | solution.py:204
  48.8 16.3 %all-to-all-start = ((bf16[32,32,128]{2,1,0:T(8,128)(2,1)}), bf16[32,32,128]{2,1,0:T(8,128)(2,1)S(1)}, u32[]{:S(2)}, u32[]{:S(2)}) async-start(bf16[32,32,128]{2,1,0:T(8,128)(2,1)} %reshape.50), calls=%async_computation | async-start | bytes 524288 | tf_op jit(solution)/shard_map/all_to_all | solution.py:184
  54.8 0.7 copy-start.4
  57.7 16.9 %collective-permute-start.6 = (bf16[2,64,128]{2,1,0:T(8,128)(2,1)}, bf16[2,64,128]{2,1,0:T(8,128)(2,1)}, u32[]{:S(2)}, u32[]{:S(2)}) collective-permute-start(bf16[2,64,128]{2,1,0:T(8,128)(2,1)} %get-tuple-element.13), channel_id=1, source_target_pairs={{0,1},{1,2},{2,3},{4,5},{5,6},{6,7},{8,9},{9,10},{10,11},{12,13},{... | collective-permute-start | bytes 98312 | tf_op jit(solution)/shard_map/ppermute | solution.py:211
  61.6 13.0 %collective-permute-start.7 = (bf16[2,64,128]{2,1,0:T(8,128)(2,1)}, bf16[2,64,128]{2,1,0:T(8,128)(2,1)}, u32[]{:S(2)}, u32[]{:S(2)}) collective-permute-start(bf16[2,64,128]{2,1,0:T(8,128)(2,1)} %get-tuple-element.14), channel_id=1, source_target_pairs={{1,0},{2,1},{3,2},{5,4},{6,5},{7,6},{9,8},{10,9},{11,10},{13,12},{... | collective-permute-start | bytes 98312 | tf_op jit(solution)/shard_map/ppermute | solution.py:212
  66.0 20.3 %all-to-all-start.1 = ((f32[32,32,128]{2,1,0:T(8,128)}), f32[32,32,128]{2,1,0:T(8,128)}, u32[]{:S(2)}, u32[]{:S(2)}) async-start(f32[32,32,128]{2,1,0:T(8,128)} %broadcast_in_dim.2), calls=%async_computation.1 | async-start | bytes 1048576 | tf_op jit(solution)/shard_map/all_to_all | solution.py:188

commit v2 on v1

--- a/solution.py
+++ b/solution.py
@@ -94,7 +94,15 @@
                 grads[i], corners(get, i, 0, ny + 1), nt, preferred_element_type=F32
             )
             total = term if total is None else total + term
-        wg[:, part * half : (part + 1) * half] = total
+        for ex in range(2):
+            for tx in range(2):
+                for ty in range(2):
+                    for tz in range(2):
+                        r = ((2 * tx + ty) * 2 + tz) * co
+                        block = (((2 * ex + tx) * 2 + ty) * 2 + part) * 2 + tz
+                        wg[block] = total[
+                            r : r + co, ex * 2 * ci : (ex + 1) * 2 * ci
+                        ].astype(BF16)
 
 
 def backward_kernel(nx, ny, nz, ci, co, chunk, g, wt, ig, u):
@@ -133,6 +141,30 @@
             ig[m + 1, :, (y + 1) * nz : (y + 2) * nz] = total
 
 
+def sum_kernel(scale, shares, *refs):
+    out = refs[2] if len(refs) > 1 else refs[0]
+    total = shares[0].astype(F32)
+    for k in range(1, shares.shape[0]):
+        total = total + shares[k].astype(F32)
+    rounded = (total * scale).astype(BF16)
+    for k in range(out.shape[0]):
+        out[k] = rounded
+
+
+def unpack_kernel(co, ci, packed, out):
+    for ex in range(2):
+        for tx in range(2):
+            for ty in range(2):
+                for ez in range(2):
+                    for tz in range(2):
+                        block = (((2 * ex + tx) * 2 + ty) * 2 + ez) * 2 + tz
+                        pair = packed[block].astype(F32)
+                        for ey in range(2):
+                            out[2 * ex + tx, 2 * ey + ty, 2 * ez + tz] = pair[
+                                :, ey * ci : (ey + 1) * ci
+                            ]
+
+
 def neighbours(axis):
     count = lax.axis_size(axis)
     up = [(i, i + 1) for i in range(count - 1)]
@@ -162,13 +194,14 @@
     )
 
     vmem = pl.BlockSpec(memory_space=pltpu.VMEM)
+    anywhere = pl.BlockSpec(memory_space=pl.ANY)
     chunk = 4
     act, g, wg = pl.pallas_call(
         functools.partial(forward_kernel, nx, ny, nz, ci, co, chunk),
         out_shape=(
             jax.ShapeDtypeStruct((nx, 8 * co, ny * nz), BF16),
             jax.ShapeDtypeStruct((nx + 1, 8 * co, (ny + 1) * nz), BF16),
-            jax.ShapeDtypeStruct((8 * co, 8 * ci), F32),
+            jax.ShapeDtypeStruct((32, co, 2 * ci), BF16),
         ),
         in_specs=[vmem] * 5,
         out_specs=(vmem,) * 3,
@@ -180,17 +213,11 @@
         compiler_params=pltpu.CompilerParams(vmem_limit_bytes=48 * 1024 * 1024),
     )(ext, xlo, xhi, w, cot)
 
-    shares = wg.astype(BF16).reshape(devices, 8 * co * 8 * ci // devices // 128, 128)
-    mine = lax.all_to_all(shares, ("gx", "gy"), 0, 0, tiled=True)
     scale = 1.0 / math.sqrt(cells)
-    summed = (jnp.sum(mine.astype(F32), axis=0) * scale).astype(F32)
-    spread = jnp.broadcast_to(summed[None], (devices,) + summed.shape)
-    gathered = lax.all_to_all(spread, ("gx", "gy"), 0, 0, tiled=True)
-    weight_grad = (
-        gathered.reshape(2, 2, 2, co, 2, 2, 2, ci)
-        .transpose(5, 0, 6, 1, 4, 2, 3, 7)
-        .reshape(4, 4, 4, co, ci)
-    )
+    wide = lax.axis_size("gx")
+    tall = lax.axis_size("gy")
+    piece = 8 * co * 4 // wide
+    first = lax.all_to_all(wg.reshape(wide, piece, 2 * ci), "gx", 0, 0, tiled=True)
 
     ig = pl.pallas_call(
         functools.partial(backward_kernel, nx, ny, nz, ci, co, chunk),
@@ -200,8 +227,35 @@
         scratch_shapes=[pltpu.VMEM((nx + 1, 4 * ci, (ny + 1) * nz), F32)],
         compiler_params=pltpu.CompilerParams(vmem_limit_bytes=48 * 1024 * 1024),
     )(g, wt)
-    from_low = lax.ppermute(ig[nx + 1 :].astype(BF16), "gx", gx_up).astype(F32)
-    from_high = lax.ppermute(ig[:1].astype(BF16), "gx", gx_down).astype(F32)
+    send_up = ig[nx + 1 :].astype(BF16)
+    send_down = ig[:1].astype(BF16)
+    part, send_up, send_down = pl.pallas_call(
+        functools.partial(sum_kernel, 1.0),
+        out_shape=(
+            jax.ShapeDtypeStruct((tall, piece, 2 * ci), BF16),
+            jax.ShapeDtypeStruct(send_up.shape, BF16),
+            jax.ShapeDtypeStruct(send_down.shape, BF16),
+        ),
+        in_specs=[vmem, anywhere, anywhere],
+        out_specs=(vmem, anywhere, anywhere),
+        input_output_aliases={1: 1, 2: 2},
+    )(first, send_up, send_down)
+    second = lax.all_to_all(part, "gy", 0, 0, tiled=True)
+    from_low = lax.ppermute(send_up, "gx", gx_up).astype(F32)
+    from_high = lax.ppermute(send_down, "gx", gx_down).astype(F32)
+    total = pl.pallas_call(
+        functools.partial(sum_kernel, scale),
+        out_shape=jax.ShapeDtypeStruct((wide, piece, 2 * ci), BF16),
+        in_specs=[vmem],
+        out_specs=vmem,
+    )(second)
+    third = lax.all_to_all(total, "gx", 0, 0, tiled=True)
+    weight_grad = pl.pallas_call(
+        functools.partial(unpack_kernel, co, ci),
+        out_shape=jax.ShapeDtypeStruct((4, 4, 4, co, ci), F32),
+        in_specs=[vmem],
+        out_specs=vmem,
+    )(third.reshape(32, co, 2 * ci))
     zero = jnp.zeros((nx - 1,) + from_low.shape[1:], F32)
     mid = (
         ig[1 : nx + 1]

time: 90.1 us -> 95 us (1.054)
  the two profiles are of different devices: /device:TPU:1 before, /device:TPU:0 now
where the time goes in v2:
time: 95 us; the launch traced here: 93.9 us
  starting transfers between devices  33.9 us (36%)
  local copies, waits for them, and re-layouts  28.3 us (30%)
  Pallas kernels  15.4 us (16%)
  waiting for transfers between devices  12.9 us (14%)
  other arithmetic  2.56 us (3%)
    unnamed x26, local copies, waits for them, and re-layouts  13.7 us
    pallas_call x1, Pallas kernels, on_device(): pl.pallas_call(functools.partial(forward_kernel, nx, ny, nz, ci, co, chun...  8.01 us
    all_to_all x1, starting transfers between devices, on_device(): lax.all_to_all(wg.reshape(wide, piece, 2 * ci), 'gx', 0, 0, tiled=True)  6.7 us
    all_to_all x1, waiting for transfers between devices, on_device(): lax.all_to_all(wg.reshape(wide, piece, 2 * ci), 'gx', 0, 0, tiled=True)  6.09 us
    all_to_all x1, starting transfers between devices, on_device(): third = lax.all_to_all(total, 'gx', 0, 0, tiled=True)  5.7 us
    ppermute x1, starting transfers between devices, on_device(): ylo = lax.ppermute(flat[:, :, (ny - 1) * nz:], 'gy', gy_up)  5.53 us
    all_to_all x1, waiting for transfers between devices, on_device(): third = lax.all_to_all(total, 'gx', 0, 0, tiled=True)  5.11 us
    ppermute x1, starting transfers between devices, on_device(): lax.ppermute(mid[:, :, (ny + 1) * nz:].astype(BF16), 'gy', gy_up)  4.52 us
  transfers between devices with their start and end apart: 11, of which 3 were waited for; matrix products, arithmetic and copies ran while one was open for 21% of the time, Pallas kernels for 2%

profile of v2, /device:TPU:0, one launch (start us, length us, event | category | flops | bytes accessed | tf_op | source)
XLA Modules:
  0.0 93.9 jit_solution(12677491023716617780)
XLA Ops:
  0.6 1.3 %reshape.46 = bf16[2,64,2048]{2,0,1:T(2,128)(2,1)S(1)} reshape(bf16[2,64,16,128]{3,2,0,1:T(8,128)(2,1)} %bitcast.46) | data formatting | bytes 1048576 | tf_op jit(solution)/shard_map/reshape | solution.py:182
  2.0 5.5 %collective-permute-start = (bf16[2,64,128]{2,1,0:T(8,128)(2,1)S(1)}, bf16[2,64,128]{2,1,0:T(8,128)(2,1)}, u32[]{:S(2)}, u32[]{:S(2)}) collective-permute-start(bf16[2,64,128]{2,1,0:T(8,128)(2,1)S(1)} %copy.27), channel_id=1, source_target_pairs={{0,1},{1,2},{2,3},{4,5},{5,6},{6,7},{8,9},{9,10},{10,11},{12,13},{... | collective-permute-start | bytes 98312 | tf_op jit(solution)/shard_map/ppermute | solution.py:183
  7.6 1.3 %collective-permute-start.1 = (bf16[2,64,128]{2,1,0:T(8,128)(2,1)S(1)}, bf16[2,64,128]{2,1,0:T(8,128)(2,1)S(1)}, u32[]{:S(2)}, u32[]{:S(2)}) collective-permute-start(bf16[2,64,128]{2,1,0:T(8,128)(2,1)S(1)} %copy.28), channel_id=1, source_target_pairs={{1,0},{2,1},{3,2},{5,4},{6,5},{7,6},{9,8},{10,9},{11,10},{13,12},{... | collective-permute-start | bytes 98312 | tf_op jit(solution)/shard_map/ppermute | solution.py:184
  8.9 1.6 %copy.29 = bf16[2,2,2,2,2,2,32,64]{7,2,0,4,6,5,3,1:T(2,128)(2,1)S(1)} copy(bf16[2,2,2,2,2,2,32,64]{7,6,5,4,3,2,1,0:T(8,128)(2,1)} %bitcast.47) | data formatting | bytes 524288 | tf_op jit(solution)/shard_map/reshape | solution.py:189
  11.7 1.7 %collective-permute-done.1 = bf16[2,64,128]{2,1,0:T(8,128)(2,1)S(1)} collective-permute-done((bf16[2,64,128]{2,1,0:T(8,128)(2,1)S(1)}, bf16[2,64,128]{2,1,0:T(8,128)(2,1)S(1)}, u32[]{:S(2)}, u32[]{:S(2)}) %collective-permute-start.1) | collective-permute-done | bytes 32800 | tf_op jit(solution)/shard_map/ppermute | solution.py:184
  13.4 0.8 fusion.7
  14.2 1.3 %collective-permute-start.2 = (bf16[1,64,2304]{2,1,0:T(8,128)(2,1)}, bf16[1,64,2304]{2,1,0:T(8,128)(2,1)S(1)}, u32[]{:S(2)}, u32[]{:S(2)}) collective-permute-start(bf16[1,64,2304]{2,1,0:T(8,128)(2,1)} %get-tuple-element.22), channel_id=1, source_target_pairs={{0,4},{4,8},{8,12},{12,16},{16,20},{20,24},{24,28},{1,5},{5,9},{9,... | collective-permute-start | bytes 884744 | tf_op jit(solution)/shard_map/ppermute | solution.py:186
  15.5 1.3 %collective-permute-start.3 = (bf16[1,64,2304]{2,1,0:T(8,128)(2,1)}, bf16[1,64,2304]{2,1,0:T(8,128)(2,1)}, u32[]{:S(2)}, u32[]{:S(2)}) collective-permute-start(bf16[1,64,2304]{2,1,0:T(8,128)(2,1)} %get-tuple-element.21), channel_id=1, source_target_pairs={{4,0},{8,4},{12,8},{16,12},{20,16},{24,20},{28,24},{5,1},{9,5},{13... | collective-permute-start | bytes 884744 | tf_op jit(solution)/shard_map/ppermute | solution.py:187
  16.8 1.8 %copy_bitcast_fusion = bf16[2,256,16,128]{3,2,1,0:T(8,128)(2,1)} fusion(bf16[2,2,2,32,2,16,128]{6,5,4,3,2,1,0:T(8,128)(2,1)S(1)} %copy-done), kind=kLoop, calls=%fused_computation.1 | loop fusion | bytes 4194304 | tf_op jit(solution)/shard_map/transpose | solution.py:193
  18.7 4.2 %reshape.40.cot = bf16[2,256,2048]{2,1,0:T(8,128)(2,1)} reshape(bf16[2,256,16,128]{3,2,1,0:T(8,128)(2,1)} %copy_bitcast_fusion) | data formatting | bytes 4194304 | tf_op jit(solution)/shard_map/reshape | solution.py:193
  23.0 1.6 %copy-done.2 = bf16[2,256,2048]{2,1,0:T(8,128)(2,1)S(1)} copy-done((bf16[2,256,2048]{2,1,0:T(8,128)(2,1)S(1)}, bf16[2,256,2048]{2,1,0:T(8,128)(2,1)}, u32[]{:S(2)}) %copy-start.2) | copy-done | bytes 2097176
  24.6 8.0 %shard_map.58 = (bf16[2,256,2048]{2,1,0:T(8,128)(2,1)S(1)}, bf16[3,256,2176]{2,1,0:T(8,128)(2,1)}, bf16[32,32,128]{2,1,0:T(8,128)(2,1)}) custom-call(bf16[2,64,2304]{2,1,0:T(8,128)(2,1)S(1)} %constant_dynamic-update-slice_fusion.ext, bf16[1,64,2304]{2,1,0:T(8,128)(2,1)S(1)} %collective-permute-done.2.xlo, bf16[1,64,2304]{2,1,0:T(8,128)(2,1)} %collective-permute-done.3.xhi, ...), custom_call_target="tpu_custom_call" | custom-call | tf_op jit(solution)/shard_map/pallas_call | solution.py:199
  32.6 1.3 %copy-done.4 = bf16[2,256,2048]{2,1,0:T(8,128)(2,1)} copy-done((bf16[2,256,2048]{2,1,0:T(8,128)(2,1)}, bf16[2,256,2048]{2,1,0:T(8,128)(2,1)S(1)}, u32[]{:S(2)}) %copy-start.4) | copy-done | bytes 2097176
  33.9 1.9 %copy-done.3 = bf16[3,256,2176]{2,1,0:T(8,128)(2,1)S(1)} copy-done((bf16[3,256,2176]{2,1,0:T(8,128)(2,1)S(1)}, bf16[3,256,2176]{2,1,0:T(8,128)(2,1)}, u32[]{:S(2)}) %copy-start.3) | copy-done | bytes 3342360
  35.9 2.1 %shard_map.59 = f32[4,64,2304]{2,1,0:T(8,128)S(1)} custom-call(bf16[3,256,2176]{2,1,0:T(8,128)(2,1)S(1)} %copy-done.3, bf16[512,256]{1,0:T(8,128)(2,1)S(1)} %bitcast.39), custom_call_target="tpu_custom_call" | custom-call | tf_op jit(solution)/shard_map/pallas_call | solution.py:222
  38.0 1.4 %copy-done.1 = f32[4,64,2304]{2,1,0:T(8,128)} copy-done((f32[4,64,2304]{2,1,0:T(8,128)}, f32[4,64,2304]{2,1,0:T(8,128)S(1)}, u32[]{:S(2)}) %copy-start.1) | copy-done | bytes 2359320
  39.5 6.7 %all-to-all-start = ((bf16[8,128,128]{2,1,0:T(8,128)(2,1)}), bf16[8,128,128]{2,1,0:T(8,128)(2,1)S(1)}, u32[]{:S(2)}, u32[]{:S(2)}) async-start(bf16[8,128,128]{2,1,0:T(8,128)(2,1)} %bitcast.8), calls=%async_computation | async-start | bytes 524288 | tf_op jit(solution)/shard_map/all_to_all | solution.py:220
  46.2 0.8 fusion.5
  47.1 6.1 %all-to-all-done.shares = bf16[8,128,128]{2,1,0:T(8,128)(2,1)S(1)} async-done(((bf16[8,128,128]{2,1,0:T(8,128)(2,1)}), bf16[8,128,128]{2,1,0:T(8,128)(2,1)S(1)}, u32[]{:S(2)}, u32[]{:S(2)}) %all-to-all-start) | async-done | bytes 262176 | tf_op jit(solution)/shard_map/all_to_all | solution.py:220
  53.9 1.6 %shard_map.60 = (bf16[4,128,128]{2,1,0:T(8,128)(2,1)}, bf16[1,64,2304]{2,1,0:T(8,128)(2,1)}, bf16[1,64,2304]{2,1,0:T(8,128)(2,1)}) custom-call(bf16[8,128,128]{2,1,0:T(8,128)(2,1)} %copy-done.7, bf16[1,64,2304]{2,1,0:T(8,128)(2,1)} %get-tuple-element.18.refs_0_, ...), custom_call_target="tpu_custom_call", output_to_operand_aliasing={{1}: (1, {}), {2}: (2, {})} | custom-call | tf_op jit(solution)/shard_map/pallas_call | solution.py:232
  55.5 1.3 %collective-permute-start.4 = (bf16[1,64,2304]{2,1,0:T(8,128)(2,1)}, bf16[1,64,2304]{2,1,0:T(8,128)(2,1)S(1)}, u32[]{:S(2)}, u32[]{:S(2)}) collective-permute-start(bf16[1,64,2304]{2,1,0:T(8,128)(2,1)} %get-tuple-element.12), channel_id=1, source_target_pairs={{0,4},{4,8},{8,12},{12,16},{16,20},{20,24},{24,28},{1,5},{5,9},{9,... | collective-permute-start | bytes 884744 | tf_op jit(solution)/shard_map/ppermute | solution.py:244
  56.8 1.3 %collective-permute-start.5 = (bf16[1,64,2304]{2,1,0:T(8,128)(2,1)}, bf16[1,64,2304]{2,1,0:T(8,128)(2,1)}, u32[]{:S(2)}, u32[]{:S(2)}) collective-permute-start(bf16[1,64,2304]{2,1,0:T(8,128)(2,1)} %get-tuple-element.13), channel_id=1, source_target_pairs={{4,0},{8,4},{12,8},{16,12},{20,16},{24,20},{28,24},{5,1},{9,5},{13... | collective-permute-start | bytes 884744 | tf_op jit(solution)/shard_map/ppermute | solution.py:245
  58.1 3.6 %copy.21 = bf16[64,8,16,128]{3,2,1,0:T(8,128)(2,1)} copy(bf16[64,8,16,128]{3,1,2,0:T(8,128)(2,1)} %bitcast.38) | data formatting | bytes 4194304
  61.7 3.7 %all-to-all-start.1 = ((bf16[4,128,128]{2,1,0:T(8,128)(2,1)}), bf16[4,128,128]{2,1,0:T(8,128)(2,1)S(1)}, u32[]{:S(2)}, u32[]{:S(2)}) async-start(bf16[4,128,128]{2,1,0:T(8,128)(2,1)} %get-tuple-element.14), calls=%async_computation.1 | async-start | bytes 262144 | tf_op jit(solution)/shard_map/all_to_all | solution.py:243
  66.1 1.6 %fusion.3 = (bf16[2,64,2304]{2,1,0:T(8,128)(2,1)S(1)}, f32[2,64,2304]{2,1,0:T(8,128)S(1)}) fusion(bf16[1,64,2304]{2,1,0:T(8,128)(2,1)} %collective-permute-done.5, bf16[1,64,2304]{2,1,0:T(8,128)(2,1)} %copy-done.9, f32[4,64,2304]{2,1,0:T(8,128)} %copy-done.1), kind=kLoop, calls=%fused_computation.12 | loop fusion | flops 1474560 | bytes 3538944 | tf_op jit(solution)/shard_map/convert.9
  68.3 4.5 %collective-permute-start.6 = (bf16[2,64,128]{2,1,0:T(8,128)(2,1)}, bf16[2,64,128]{2,1,0:T(8,128)(2,1)}, u32[]{:S(2)}, u32[]{:S(2)}) collective-permute-start(bf16[2,64,128]{2,1,0:T(8,128)(2,1)} %get-tuple-element.19), channel_id=1, source_target_pairs={{0,1},{1,2},{2,3},{4,5},{5,6},{6,7},{8,9},{9,10},{10,11},{12,13},{... | collective-permute-start | bytes 98312 | tf_op jit(solution)/shard_map/ppermute | solution.py:265
  72.9 1.3 %collective-permute-start.7 = (bf16[2,64,128]{2,1,0:T(8,128)(2,1)}, bf16[2,64,128]{2,1,0:T(8,128)(2,1)}, u32[]{:S(2)}, u32[]{:S(2)}) collective-permute-start(bf16[2,64,128]{2,1,0:T(8,128)(2,1)} %get-tuple-element.20), channel_id=1, source_target_pairs={{1,0},{2,1},{3,2},{5,4},{6,5},{7,6},{9,8},{10,9},{11,10},{13,12},{... | collective-permute-start | bytes 98312 | tf_op jit(solution)/shard_map/ppermute | solution.py:266
  74.5 1.7 %copy.17 = bf16[256,2,16,128]{3,2,1,0:T(8,128)(2,1)} copy(bf16[256,2,16,128]{3,2,0,1:T(8,128)(2,1)S(1)} %bitcast_bitcast_fusion) | data formatting | bytes 4194304 | tf_op jit(solution)/shard_map/transpose | solution.py:275
  76.9 1.6 %shard_map.61 = bf16[8,128,128]{2,1,0:T(8,128)(2,1)} custom-call(bf16[4,128,128]{2,1,0:T(8,128)(2,1)} %copy-done.8), custom_call_target="tpu_custom_call" | custom-call | tf_op jit(solution)/shard_map/pallas_call | solution.py:246
  78.5 5.7 %all-to-all-start.2 = ((bf16[8,128,128]{2,1,0:T(8,128)(2,1)}), bf16[8,128,128]{2,1,0:T(8,128)(2,1)S(1)}, u32[]{:S(2)}, u32[]{:S(2)}) async-start(bf16[8,128,128]{2,1,0:T(8,128)(2,1)} %shard_map.61), calls=%async_computation.2 | async-start | bytes 524288 | tf_op jit(solution)/shard_map/all_to_all | solution.py:252
  86.0 5.1 %all-to-all-done.2 = bf16[8,128,128]{2,1,0:T(8,128)(2,1)S(1)} async-done(((bf16[8,128,128]{2,1,0:T(8,128)(2,1)}), bf16[8,128,128]{2,1,0:T(8,128)(2,1)S(1)}, u32[]{:S(2)}, u32[]{:S(2)}) %all-to-all-start.2) | async-done | bytes 262176 | tf_op jit(solution)/shard_map/all_to_all | solution.py:252
  91.9 2.1 %shard_map.62 = f32[4,4,4,32,64]{4,3,2,1,0:T(8,128)} custom-call(bf16[32,32,128]{2,1,0:T(8,128)(2,1)} %bitcast.45), custom_call_target="tpu_custom_call" | custom-call | tf_op jit(solution)/shard_map/pallas_call | solution.py:253
  (38 shorter events, 7.2 us)
Async XLA Ops:
  0.6 16.2 %copy-start = (bf16[2,2,2,32,2,16,128]{6,5,4,3,2,1,0:T(8,128)(2,1)S(1)}, bf16[2,2,2,32,2,16,128]{6,5,4,3,2,1,0:T(8,128)(2,1)}, u32[]{:S(2)}) copy-start(bf16[2,2,2,32,2,16,128]{6,5,4,3,2,1,0:T(8,128)(2,1)} %param.5) | copy-start | bytes 6291460
  2.0 8.7 %collective-permute-start = (bf16[2,64,128]{2,1,0:T(8,128)(2,1)S(1)}, bf16[2,64,128]{2,1,0:T(8,128)(2,1)}, u32[]{:S(2)}, u32[]{:S(2)}) collective-permute-start(bf16[2,64,128]{2,1,0:T(8,128)(2,1)S(1)} %copy.27), channel_id=1, source_target_pairs={{0,1},{1,2},{2,3},{4,5},{5,6},{6,7},{8,9},{9,10},{10,11},{12,13},{... | collective-permute-start | bytes 98312 | tf_op jit(solution)/shard_map/ppermute | solution.py:183
  7.6 5.8 %collective-permute-start.1 = (bf16[2,64,128]{2,1,0:T(8,128)(2,1)S(1)}, bf16[2,64,128]{2,1,0:T(8,128)(2,1)S(1)}, u32[]{:S(2)}, u32[]{:S(2)}) collective-permute-start(bf16[2,64,128]{2,1,0:T(8,128)(2,1)S(1)} %copy.28), channel_id=1, source_target_pairs={{1,0},{2,1},{3,2},{5,4},{6,5},{7,6},{9,8},{10,9},{11,10},{13,12},{... | collective-permute-start | bytes 98312 | tf_op jit(solution)/shard_map/ppermute | solution.py:184
  14.2 8.8 %collective-permute-start.2 = (bf16[1,64,2304]{2,1,0:T(8,128)(2,1)}, bf16[1,64,2304]{2,1,0:T(8,128)(2,1)S(1)}, u32[]{:S(2)}, u32[]{:S(2)}) collective-permute-start(bf16[1,64,2304]{2,1,0:T(8,128)(2,1)} %get-tuple-element.22), channel_id=1, source_target_pairs={{0,4},{4,8},{8,12},{12,16},{16,20},{20,24},{24,28},{1,5},{5,9},{9,... | collective-permute-start | bytes 884744 | tf_op jit(solution)/shard_map/ppermute | solution.py:186
  15.5 7.5 %collective-permute-start.3 = (bf16[1,64,2304]{2,1,0:T(8,128)(2,1)}, bf16[1,64,2304]{2,1,0:T(8,128)(2,1)}, u32[]{:S(2)}, u32[]{:S(2)}) collective-permute-start(bf16[1,64,2304]{2,1,0:T(8,128)(2,1)} %get-tuple-element.21), channel_id=1, source_target_pairs={{4,0},{8,4},{12,8},{16,12},{20,16},{24,20},{28,24},{5,1},{9,5},{13... | collective-permute-start | bytes 884744 | tf_op jit(solution)/shard_map/ppermute | solution.py:187
  23.0 1.6 %copy-start.2 = (bf16[2,256,2048]{2,1,0:T(8,128)(2,1)S(1)}, bf16[2,256,2048]{2,1,0:T(8,128)(2,1)}, u32[]{:S(2)}) copy-start(bf16[2,256,2048]{2,1,0:T(8,128)(2,1)} %reshape.40.cot) | copy-start | bytes 6291460
  32.6 1.3 %copy-start.4 = (bf16[2,256,2048]{2,1,0:T(8,128)(2,1)}, bf16[2,256,2048]{2,1,0:T(8,128)(2,1)S(1)}, u32[]{:S(2)}) copy-start(bf16[2,256,2048]{2,1,0:T(8,128)(2,1)S(1)} %get-tuple-element.9) | copy-start | bytes 6291460
  33.9 1.9 %copy-start.3 = (bf16[3,256,2176]{2,1,0:T(8,128)(2,1)S(1)}, bf16[3,256,2176]{2,1,0:T(8,128)(2,1)}, u32[]{:S(2)}) copy-start(bf16[3,256,2176]{2,1,0:T(8,128)(2,1)} %get-tuple-element.10.g) | copy-start | bytes 10027012
  38.0 1.4 %copy-start.1 = (f32[4,64,2304]{2,1,0:T(8,128)}, f32[4,64,2304]{2,1,0:T(8,128)S(1)}, u32[]{:S(2)}) copy-start(f32[4,64,2304]{2,1,0:T(8,128)S(1)} %shard_map.59) | copy-start | bytes 7077892
  39.5 13.6 %all-to-all-start = ((bf16[8,128,128]{2,1,0:T(8,128)(2,1)}), bf16[8,128,128]{2,1,0:T(8,128)(2,1)S(1)}, u32[]{:S(2)}, u32[]{:S(2)}) async-start(bf16[8,128,128]{2,1,0:T(8,128)(2,1)} %bitcast.8), calls=%async_computation | async-start | bytes 524288 | tf_op jit(solution)/shard_map/all_to_all | solution.py:220
  53.2 0.7 copy-start.7
  55.5 9.9 %collective-permute-start.4 = (bf16[1,64,2304]{2,1,0:T(8,128)(2,1)}, bf16[1,64,2304]{2,1,0:T(8,128)(2,1)S(1)}, u32[]{:S(2)}, u32[]{:S(2)}) collective-permute-start(bf16[1,64,2304]{2,1,0:T(8,128)(2,1)} %get-tuple-element.12), channel_id=1, source_target_pairs={{0,4},{4,8},{8,12},{12,16},{16,20},{20,24},{24,28},{1,5},{5,9},{9,... | collective-permute-start | bytes 884744 | tf_op jit(solution)/shard_map/ppermute | solution.py:244
  56.8 9.3 %collective-permute-start.5 = (bf16[1,64,2304]{2,1,0:T(8,128)(2,1)}, bf16[1,64,2304]{2,1,0:T(8,128)(2,1)}, u32[]{:S(2)}, u32[]{:S(2)}) collective-permute-start(bf16[1,64,2304]{2,1,0:T(8,128)(2,1)} %get-tuple-element.13), channel_id=1, source_target_pairs={{4,0},{8,4},{12,8},{16,12},{20,16},{24,20},{28,24},{5,1},{9,5},{13... | collective-permute-start | bytes 884744 | tf_op jit(solution)/shard_map/ppermute | solution.py:245
  61.7 14.5 %all-to-all-start.1 = ((bf16[4,128,128]{2,1,0:T(8,128)(2,1)}), bf16[4,128,128]{2,1,0:T(8,128)(2,1)S(1)}, u32[]{:S(2)}, u32[]{:S(2)}) async-start(bf16[4,128,128]{2,1,0:T(8,128)(2,1)} %get-tuple-element.14), calls=%async_computation.1 | async-start | bytes 262144 | tf_op jit(solution)/shard_map/all_to_all | solution.py:243
  65.4 8.8 %copy-start.5 = (bf16[64,8,16,128]{3,2,1,0:T(8,128)(2,1)S(1)}, bf16[64,8,16,128]{3,2,1,0:T(8,128)(2,1)}, u32[]{:S(2)}) copy-start(bf16[64,8,16,128]{3,2,1,0:T(8,128)(2,1)} %copy.21) | copy-start | bytes 6291460
  65.4 0.7 copy-start.9
  68.3 15.9 %collective-permute-start.6 = (bf16[2,64,128]{2,1,0:T(8,128)(2,1)}, bf16[2,64,128]{2,1,0:T(8,128)(2,1)}, u32[]{:S(2)}, u32[]{:S(2)}) collective-permute-start(bf16[2,64,128]{2,1,0:T(8,128)(2,1)} %get-tuple-element.19), channel_id=1, source_target_pairs={{0,1},{1,2},{2,3},{4,5},{5,6},{6,7},{8,9},{9,10},{10,11},{12,13},{... | collective-permute-start | bytes 98312 | tf_op jit(solution)/shard_map/ppermute | solution.py:265
  72.9 11.3 %collective-permute-start.7 = (bf16[2,64,128]{2,1,0:T(8,128)(2,1)}, bf16[2,64,128]{2,1,0:T(8,128)(2,1)}, u32[]{:S(2)}, u32[]{:S(2)}) collective-permute-start(bf16[2,64,128]{2,1,0:T(8,128)(2,1)} %get-tuple-element.20), channel_id=1, source_target_pairs={{1,0},{2,1},{3,2},{5,4},{6,5},{7,6},{9,8},{10,9},{11,10},{13,12},{... | collective-permute-start | bytes 98312 | tf_op jit(solution)/shard_map/ppermute | solution.py:266
  76.2 0.7 copy-start.8
  78.5 12.6 %all-to-all-start.2 = ((bf16[8,128,128]{2,1,0:T(8,128)(2,1)}), bf16[8,128,128]{2,1,0:T(8,128)(2,1)S(1)}, u32[]{:S(2)}, u32[]{:S(2)}) async-start(bf16[8,128,128]{2,1,0:T(8,128)(2,1)} %shard_map.61), calls=%async_computation.2 | async-start | bytes 524288 | tf_op jit(solution)/shard_map/all_to_all | solution.py:252
  91.1 0.7 copy-start.6

commit v3 on v1

v3 whole, which is shorter than its diff:
```python
import functools
import math

import jax
import jax.numpy as jnp
from jax import lax
from jax.experimental import pallas as pl
from jax.experimental.pallas import tpu as pltpu
from jax.sharding import PartitionSpec as P

F32 = jnp.float32
BF16 = jnp.bfloat16
GROUP = 16


def swap_matrix(outer, inner):
    size = outer * inner
    row = lax.broadcasted_iota(jnp.int32, (size, size), 0)
    col = lax.broadcasted_iota(jnp.int32, (size, size), 1)
    return jnp.where(col == (row % outer) * inner + row // outer, 1.0, 0.0).astype(BF16)


def brick_pass(dims, chunk, duals, block, cot, w, wt, act_out, wg_add, ig_add, scratch):
    nx, ny, nz, ci, co = dims
    vm, ga, gb, cots, vals, staged, sems = scratch
    half = 4 * ci
    slot = {i: k for k, i in enumerate(duals)}
    planes = sorted({i + 1 - e for i in duals for e in range(2)})
    place = {x: k for k, x in enumerate(planes)}
    split = co // GROUP

    for x in planes:
        for y in range(ny + 2):
            lanes = slice(y * nz, (y + 1) * nz)
            vm[place[x], :, lanes] = pltpu.roll(block(x, y).astype(F32), 1, 1).astype(BF16)

    def rolled(x, y):
        return vm[place[x], :, y * nz : (y + 1) * nz]

    def corners(get, i, j0, j1):
        return jnp.concatenate(
            [
                jnp.concatenate([get(i + 1 - ex, j + 1 - ey) for j in range(j0, j1)], axis=1)
                for ex in range(2)
                for ey in range(2)
            ],
            axis=0,
        )

    pairs = [
        (i, sx, i - sx, sy, sz)
        for i in duals
        for sx in range(2)
        if 0 <= i - sx < nx
        for sy in range(2)
        for sz in range(2)
    ]

    to_y = swap_matrix(GROUP, ny)
    for i, sx, m, sy, sz in pairs:
        q = (2 * sx + sy) * 2 + sz
        raw = jnp.concatenate(
            [
                cot[q, k * GROUP : (k + 1) * GROUP, m].reshape(GROUP * ny, nz)
                for k in range(split)
            ],
            axis=1,
        )
        moved = jnp.dot(to_y, raw, preferred_element_type=F32).astype(BF16)
        for y in range(ny):
            for k in range(split):
                cots[
                    slot[i],
                    q * co + k * GROUP : q * co + (k + 1) * GROUP,
                    y * nz : (y + 1) * nz,
                ] = moved[y * GROUP : (y + 1) * GROUP, k * nz : (k + 1) * nz]

    first = lax.broadcasted_iota(jnp.int32, (co, nz), 1) == 0
    zeros = jnp.zeros((2 * co, nz), BF16)
    started = set()

    for i in duals:
        s = slot[i]
        for j0 in range(0, ny + 1, chunk):
            j1 = min(j0 + chunk, ny + 1)
            back = jnp.dot(w[:, half:], corners(rolled, i, j0, j1), preferred_element_type=F32)
            here = jnp.dot(w[:, :half], corners(block, i, j0, j1), preferred_element_type=F32)
            for j in range(j0, j1):
                cols = slice((j - j0) * nz, (j - j0 + 1) * nz)
                wide = slice(j * nz, (j + 1) * nz)
                for tx in range(2):
                    for ty in range(2):
                        sx, sy = 1 - tx, 1 - ty
                        m, n = i - sx, j - sy
                        base = (2 * tx + ty) * 2 * co
                        if not (0 <= m < nx and 0 <= n < ny):
                            ga[s, base : base + 2 * co, wide] = zeros
                            gb[s, base : base + 2 * co, wide] = zeros
                            continue
                        out = slice(n * nz, (n + 1) * nz)
                        for tz in range(2):
                            sz = 1 - tz
                            r = slice(base + tz * co, base + (tz + 1) * co)
                            low, high = back[r, cols], here[r, cols]
                            if sz == 1:
                                before = low + jnp.where(first, 0.0, high)
                                before = pltpu.roll(before, nz - 1, 1)
                            else:
                                before = jnp.where(first, 0.0, low) + high
                            q = ((2 * sx + sy) * 2 + sz) * co
                            sig = 0.5 * jnp.tanh(0.5 * before) + 0.5
                            value = before * sig
                            vals[s, q : q + co, out] = value.astype(BF16)
                            slope = sig + value * (1.0 - sig)
                            grad = cots[s, q : q + co, out].astype(F32) * slope
                            if sz == 1:
                                grad = pltpu.roll(grad, 1, 1)
                            whole = grad.astype(BF16)
                            cut = jnp.where(first, 0.0, grad).astype(BF16)
                            ga[s, r, wide] = cut if sz == 0 else whole
                            gb[s, r, wide] = cut if sz == 1 else whole

    to_c = swap_matrix(ny, GROUP)
    copies = []
    for count, (i, sx, m, sy, sz) in enumerate(pairs):
        q = (2 * sx + sy) * 2 + sz
        mixed = jnp.concatenate(
            [
                jnp.concatenate(
                    [
                        vals[
                            slot[i],
                            q * co + k * GROUP : q * co + (k + 1) * GROUP,
                            y * nz : (y + 1) * nz,
                        ]
                        for y in range(ny)
                    ],
                    axis=0,
                )
                for k in range(split)
            ],
            axis=1,
        )
        moved = jnp.dot(to_c, mixed, preferred_element_type=F32).astype(BF16)
        for k in range(split):
            staged[count, k * GROUP : (k + 1) * GROUP] = moved[
                :, k * nz : (k + 1) * nz
            ].reshape(GROUP, ny, nz)
        copy = pltpu.make_async_copy(staged.at[count], act_out.at[q, :, m], sems.at[count])
        copy.start()
        copies.append(copy)

    nt = (((1,), (1,)), ((), ()))
    for part, (grads, get) in enumerate(((gb, block), (ga, rolled))):
        total = None
        for i in duals:
            term = lax.dot_general(
                grads[slot[i]], corners(get, i, 0, ny + 1), nt, preferred_element_type=F32
            )
            total = term if total is None else total + term
        wg_add(part, total)

    for i in duals:
        s = slot[i]
        for j0 in range(0, ny + 1, chunk):
            j1 = min(j0 + chunk, ny + 1)
            wide = slice(j0 * nz, j1 * nz)
            back = jnp.dot(wt[half:], ga[s, :, wide], preferred_element_type=F32)
            here = jnp.dot(wt[:half], gb[s, :, wide], preferred_element_type=F32)
            for j in range(j0, j1):
                cols = slice((j - j0) * nz, (j - j0 + 1) * nz)
                both = here[:, cols] + pltpu.roll(back[:, cols], nz - 1, 1)
                for ex in range(2):
                    for ey in range(2):
                        r = (2 * ex + ey) * ci
                        cell = (i - ex, j - ey)
                        ig_add(cell[0], cell[1], both[r : r + ci], cell not in started)
                        started.add(cell)

    for copy in copies:
        copy.wait()


def inner_kernel(dims, chunk, flat, ylo, yhi, w, wt, cot, act_out, wg, ig, *scratch):
    nx, ny, nz, ci, co = dims
    half = 4 * ci

    def block(x, y):
        if y == 0:
            return ylo[x - 1]
        if y == ny + 1:
            return yhi[x - 1]
        return flat[x - 1, :, (y - 1) * nz : y * nz]

    def wg_add(part, total):
        wg[:, part * half : (part + 1) * half] = total

    def ig_add(m, y, value, fresh):
        lanes = slice((y + 1) * nz, (y + 2) * nz)
        ig[m, :, lanes] = value if fresh else ig[m, :, lanes] + value

    brick_pass(
        dims, chunk, range(1, nx), block, cot, w, wt, act_out, wg_add, ig_add, scratch
    )


def outer_kernel(
    dims,
    chunk,
    core,
    flat,
    ylo,
    yhi,
    xlo,
    xhi,
    w,
    wt,
    cot,
    wg_in,
    ig_in,
    act_in,
    act_out,
    keep,
    send,
    own,
    yface,
    up,
    down,
    full,
    faces,
    *scratch,
):
    del act_in
    nx, ny, nz, ci, co = dims
    half = 4 * ci

    def block(x, y):
        lanes = slice(y * nz, (y + 1) * nz)
        if x == 0:
            return xlo[0, :, lanes]
        if x == nx + 1:
            return xhi[0, :, lanes]
        if y == 0:
            return ylo[x - 1]
        if y == ny + 1:
            return yhi[x - 1]
        return flat[x - 1, :, (y - 1) * nz : y * nz]

    def wg_add(part, total):
        total = total + wg_in[:, part * half : (part + 1) * half]
        for ex in range(2):
            for row in range(8):
                tx, ty, tz = row // 4, row // 2 % 2, row % 2
                index = ((tx * 2 + ty) * 2 + part) * 2 + tz
                full[ex, index] = total[
                    row * co : (row + 1) * co, ex * 2 * ci : (ex + 1) * 2 * ci
                ]

    def ig_add(m, y, value, fresh):
        lanes = slice((y + 1) * nz, (y + 2) * nz)
        if m < 0 or m >= nx:
            side = 0 if m < 0 else 1
            faces[side, :, lanes] = value if fresh else faces[side, :, lanes] + value
            return
        if y < 0 or y >= ny:
            side = 0 if y < 0 else 1
            base = ig_in[m, :, lanes] if fresh else yface[side, m]
            yface[side, m] = base + value
            return
        inner = slice(y * nz, (y + 1) * nz)
        base = ig_in[m, :, lanes] if fresh else own[m, :, inner]
        own[m, :, inner] = base + value

    for m in range(1, nx - 1):
        own[m] = ig_in[m, :, nz : (ny + 1) * nz]
        yface[0, m] = ig_in[m, :, :nz]
        yface[1, m] = ig_in[m, :, (ny + 1) * nz :]
    brick_pass(dims, chunk, (0, nx), block, cot, w, wt, act_out, wg_add, ig_add, scratch)
    c = core[0]
    keep[...] = full[c]
    send[...] = full[1 - c].astype(BF16)
    down[0] = faces[0].astype(BF16)
    up[0] = faces[1].astype(BF16)


def unpack_kernel(co, ci, core, mine, other, out, full):
    c = core[0]
    full[c] = mine[...].astype(F32)
    full[1 - c] = other[...].astype(F32)
    for ex in range(2):
        for tx in range(2):
            for ty in range(2):
                for ez in range(2):
                    for tz in range(2):
                        index = ((tx * 2 + ty) * 2 + ez) * 2 + tz
                        pair = full[ex, index]
                        for ey in range(2):
                            out[2 * ex + tx, 2 * ey + ty, 2 * ez + tz] = pair[
                                :, ey * ci : (ey + 1) * ci
                            ]


def neighbours(axis):
    count = lax.axis_size(axis)
    up = [(i, i + 1) for i in range(count - 1)]
    return up, [(b, a) for a, b in up]


def on_device(volume, kernel, cotangent):
    ci, nx, ny, nz = volume.shape
    co = kernel.shape[3]
    gx, gy = lax.axis_size("gx"), lax.axis_size("gy")
    gx_up, gx_down = neighbours("gx")
    gy_up, gy_down = neighbours("gy")
    cells = nx * gx * ny * gy * nz
    dims = (nx, ny, nz, ci, co)
    core = (lax.axis_index("gx") % 2).astype(jnp.int32).reshape(1)

    flat = volume.transpose(1, 0, 2, 3).reshape(nx, ci, ny * nz)
    ylo = lax.ppermute(flat[:, :, (ny - 1) * nz :], "gy", gy_up)
    yhi = lax.ppermute(flat[:, :, :nz], "gy", gy_down)
    top = jnp.concatenate([ylo[nx - 1 :], flat[nx - 1 :], yhi[nx - 1 :]], axis=2)
    low = jnp.concatenate([ylo[:1], flat[:1], yhi[:1]], axis=2)
    xlo = lax.ppermute(top, "gx", gx_up)
    xhi = lax.ppermute(low, "gx", gx_down)

    taps = kernel.reshape(2, 2, 2, 2, 2, 2, co, ci)
    w = taps.transpose(1, 3, 5, 6, 4, 0, 2, 7).reshape(8 * co, 8 * ci)
    wt = w.T
    cot = cotangent.reshape(8, co, nx, ny, nz)

    vmem = pl.BlockSpec(memory_space=pltpu.VMEM)
    smem = pl.BlockSpec(memory_space=pltpu.SMEM)
    anywhere = pl.BlockSpec(memory_space=pl.ANY)
    chunk = 4

    def scratch(duals, planes, pairs):
        return [
            pltpu.VMEM((planes, ci, (ny + 2) * nz), BF16),
            pltpu.VMEM((duals, 8 * co, (ny + 1) * nz), BF16),
            pltpu.VMEM((duals, 8 * co, (ny + 1) * nz), BF16),
            pltpu.VMEM((duals, 8 * co, ny * nz), BF16),
            pltpu.VMEM((duals, 8 * co, ny * nz), BF16),
            pltpu.VMEM((pairs, co, ny, nz), BF16),
            pltpu.SemaphoreType.DMA((pairs,)),
        ]

    params = pltpu.CompilerParams(vmem_limit_bytes=40 * 1024 * 1024)
    act, wg_part, ig_part = pl.pallas_call(
        functools.partial(inner_kernel, dims, chunk),
        out_shape=(
            jax.ShapeDtypeStruct(cot.shape, BF16),
            jax.ShapeDtypeStruct((8 * co, 8 * ci), F32),
            jax.ShapeDtypeStruct((nx, ci, (ny + 2) * nz), F32),
        ),
        in_specs=[vmem] * 6,
        out_specs=(anywhere, vmem, vmem),
        scratch_shapes=scratch(nx - 1, nx, 8 * (nx - 1)),
        compiler_params=params,
    )(flat, ylo, yhi, w, wt, cot)
    act, keep, send, own, yface, up, down = pl.pallas_call(
        functools.partial(outer_kernel, dims, chunk),
        out_shape=(
            jax.ShapeDtypeStruct(cot.shape, BF16),
            jax.ShapeDtypeStruct((16, co, 2 * ci), F32),
            jax.ShapeDtypeStruct((16, co, 2 * ci), BF16),
            jax.ShapeDtypeStruct((nx, ci, ny * nz), F32),
            jax.ShapeDtypeStruct((2, nx, ci, nz), F32),
            jax.ShapeDtypeStruct((1, ci, (ny + 2) * nz), BF16),
            jax.ShapeDtypeStruct((1, ci, (ny + 2) * nz), BF16),
        ),
        in_specs=[smem] + [vmem] * 10 + [anywhere],
        out_specs=(anywhere,) + (vmem,) * 6,
        input_output_aliases={11: 0},
        scratch_shapes=[
            pltpu.VMEM((2, 16, co, 2 * ci), F32),
            pltpu.VMEM((2, ci, (ny + 2) * nz), F32),
        ]
        + scratch(2, min(nx + 2, 4), 8),
        compiler_params=params,
    )(core, flat, ylo, yhi, xlo, xhi, w, wt, cot, wg_part, ig_part, act)

    scale = 1.0 / math.sqrt(cells)
    swap = [(i, i ^ 1) for i in range(gx)]
    pairs = gx // 2
    groups = [[2 * i + b for i in range(pairs)] for b in range(2)]
    piece = 16 * co // pairs
    half = keep + lax.ppermute(send, "gx", swap).astype(F32)
    shares = half.astype(BF16).reshape(pairs, piece, 2 * ci)
    shares = lax.all_to_all(shares, "gx", 0, 0, axis_index_groups=groups, tiled=True)
    part = jnp.sum(shares.astype(F32), axis=0).astype(BF16)
    rows = lax.all_to_all(
        jnp.broadcast_to(part[None], (gy,) + part.shape), "gy", 0, 0, tiled=True
    )
    total = (jnp.sum(rows.astype(F32), axis=0) * scale).astype(BF16)
    mine = lax.all_to_all(
        jnp.broadcast_to(total[None], (pairs,) + total.shape),
        "gx",
        0,
        0,
        axis_index_groups=groups,
        tiled=True,
    ).reshape(16, co, 2 * ci)
    other = lax.ppermute(mine, "gx", swap)
    weight_grad = pl.pallas_call(
        functools.partial(unpack_kernel, co, ci),
        out_shape=jax.ShapeDtypeStruct((4, 4, 4, co, ci), F32),
        in_specs=[smem, vmem, vmem],
        out_specs=vmem,
        scratch_shapes=[pltpu.VMEM((2, 16, co, 2 * ci), F32)],
    )(core, mine, other)

    from_low = lax.ppermute(up, "gx", gx_up).astype(F32)
    from_high = lax.ppermute(down, "gx", gx_down).astype(F32)

    def add_x(array, lanes):
        lead = (nx - 1,) + from_low[:, :, lanes].shape[1:]
        zero = jnp.zeros(lead, F32)
        return (
            array
            + jnp.concatenate([from_low[:, :, lanes], zero], axis=0)
            + jnp.concatenate([zero, from_high[:, :, lanes]], axis=0)
        )

    send_low = add_x(yface[0], slice(0, nz)).astype(BF16)
    send_high = add_x(yface[1], slice((ny + 1) * nz, None)).astype(BF16)
    y_low = lax.ppermute(send_high, "gy", gy_up).astype(F32)
    y_high = lax.ppermute(send_low, "gy", gy_down).astype(F32)
    gap = jnp.zeros((nx, ci, (ny - 1) * nz), F32)
    total_ig = (
        add_x(own, slice(nz, (ny + 1) * nz))
        + jnp.concatenate([y_low, gap], axis=2)
        + jnp.concatenate([gap, y_high], axis=2)
    )
    input_grad = total_ig.astype(BF16).reshape(nx, ci, ny, nz).transpose(1, 0, 2, 3)
    return act.reshape(cotangent.shape), input_grad, weight_grad


def solution(mesh):
    placed = (P(None, "gx", "gy", None), P(), P(None, None, None, None, "gx", "gy", None))
    return jax.shard_map(
        on_device,
        mesh=mesh,
        in_specs=placed,
        out_specs=(placed[2], placed[0], P()),
        check_vma=False,
    )
```

time: 90.1 us -> 72.5 us (0.80)
  local copies, waits for them, and re-layouts: 28.4 us -> 9.56 us
  waiting for transfers between devices: 13.3 us -> 7.03 us
  starting transfers between devices: 33.9 us -> 37.8 us
  Pallas kernels: 10.1 us -> 12.8 us
    unnamed x16 -> x17, local copies, waits for them, and re-layouts: 8.5 us -> 1.74 us
    reshape x3 -> x0, local copies, waits for them, and re-layouts: 6.7 us -> none  [the longest x1 4.18 us: on_device(): cotangent.reshape(8 * co, nx, ny, nz).transpose(1, 0, 2, 3)]
    transpose x5 -> x1, local copies, waits for them, and re-layouts: 7.44 us -> 0.83 us  [on_device(): total_ig.astype(BF16).reshape(nx, ci, ny, nz).transpose(1, 0, 2, 3)]
    all_to_all x2 -> x3, waiting for transfers between devices: 12.1 us -> 6.18 us  [the longest x1 3.57 us: on_device(): lax.all_to_all(jnp.broadcast_to(total[None], (pairs,) + total.shape), 'gx...]
    pallas_call x2 -> x3, Pallas kernels: 10.1 us -> 12.8 us  [the longest x1 7.14 us: on_device(): pl.pallas_call(functools.partial(outer_kernel, dims, chunk), out_shape=(j...]
    ppermute x6 -> x8, starting transfers between devices: 17.1 us -> 19.7 us  [the longest x1 4.96 us: on_device(): xlo = lax.ppermute(top, 'gx', gx_up)]
    another operation x2 -> x0, other arithmetic: 1.7 us -> none
    concatenate x0 -> x2, other arithmetic: none -> 1.48 us  [the longest x1 0.74 us: on_device(): top = jnp.concatenate([ylo[nx - 1:], flat[nx - 1:], yhi[nx - 1:]], axis=2)]
  transfers between devices with their start and end apart: 10 -> 13, of which waited for: 4 -> 4; matrix products, arithmetic and copies ran while one was open for 23% -> 13% of each run, Pallas kernels for 0% -> 5%
where the time goes in v3:
time: 72.5 us; the launch traced here: 71.4 us
  starting transfers between devices  37.8 us (52%)
  Pallas kernels  12.8 us (18%)
  local copies, waits for them, and re-layouts  9.56 us (13%)
  waiting for transfers between devices  7.03 us (10%)
  other arithmetic  3.22 us (4%)
  between operations  0.98 us (1%)
    pallas_call x1, Pallas kernels, on_device(): pl.pallas_call(functools.partial(outer_kernel, dims, chunk), out_shape=(j...  7.14 us
    all_to_all x1, starting transfers between devices, on_device(): lax.all_to_all(jnp.broadcast_to(part[None], (gy,) + part.shape), 'gy', 0,...  5.33 us
    ppermute x1, starting transfers between devices, on_device(): xlo = lax.ppermute(top, 'gx', gx_up)  4.96 us
    ppermute x1, starting transfers between devices, on_device(): ylo = lax.ppermute(flat[:, :, (ny - 1) * nz:], 'gy', gy_up)  4.66 us
    ppermute x1, starting transfers between devices, on_device(): from_low = lax.ppermute(up, 'gx', gx_up).astype(F32)  3.64 us
    all_to_all x1, waiting for transfers between devices, on_device(): lax.all_to_all(jnp.broadcast_to(total[None], (pairs,) + total.shape), 'gx...  3.57 us
    pallas_call x1, Pallas kernels, on_device(): pl.pallas_call(functools.partial(inner_kernel, dims, chunk), out_shape=(j...  3.54 us
    all_to_all x1, starting transfers between devices, on_device(): lax.all_to_all(shares, 'gx', 0, 0, axis_index_groups=groups, tiled=True)  3.51 us
  transfers between devices with their start and end apart: 13, of which 4 were waited for; matrix products, arithmetic and copies ran while one was open for 13% of the time, Pallas kernels for 5%

profile of v3, /device:TPU:1, one launch (start us, length us, event | category | flops | bytes accessed | tf_op | source)
XLA Modules:
  0.0 71.4 jit_solution(6126280181245785257)
XLA Ops:
  0.6 1.2 %reshape.49 = bf16[2,64,2048]{2,0,1:T(2,128)(2,1)S(1)} reshape(bf16[2,64,16,128]{3,2,0,1:T(8,128)(2,1)} %bitcast.49) | data formatting | bytes 1048576 | tf_op jit(solution)/shard_map/reshape | solution.py:319
  1.9 0.2 copy.20.flat
  2.1 1.3 %collective-permute-start.1 = (bf16[2,64,128]{2,1,0:T(8,128)(2,1)S(1)}, bf16[2,64,128]{2,1,0:T(8,128)(2,1)S(1)}, u32[]{:S(2)}, u32[]{:S(2)}) collective-permute-start(bf16[2,64,128]{2,1,0:T(8,128)(2,1)S(1)} %get-tuple-element.25), channel_id=1, source_target_pairs={{1,0},{2,1},{3,2},{5,4},{6,5},{7,6},{9,8},{10,9},{11,10},{13,12},{... | collective-permute-start | bytes 98312 | tf_op jit(solution)/shard_map/ppermute | solution.py:321
  3.4 4.7 %collective-permute-start = (bf16[2,64,128]{2,1,0:T(8,128)(2,1)S(1)}, bf16[2,64,128]{2,1,0:T(8,128)(2,1)S(1)}, u32[]{:S(2)}, u32[]{:S(2)}) collective-permute-start(bf16[2,64,128]{2,1,0:T(8,128)(2,1)S(1)} %get-tuple-element.26), channel_id=1, source_target_pairs={{0,1},{1,2},{2,3},{4,5},{5,6},{6,7},{8,9},{9,10},{10,11},{12,13},{... | collective-permute-start | bytes 98312 | tf_op jit(solution)/shard_map/ppermute | solution.py:320
  8.4 0.7 collective-permute-done.ylo
  9.0 0.7 %pad_maximum_fusion = bf16[1,64,2304]{2,1,0:T(8,128)(2,1)} fusion(bf16[1,64,128]{2,1,0:T(8,128)(2,1)S(1)} %get-tuple-element.36, bf16[1,64,2048]{2,1,0:T(8,128)(2,1)S(1)} %slice.58, bf16[1,64,128]{2,1,0:T(8,128)(2,1)S(1)} %get-tuple-element.34), kind=kLoop, calls=%fused_computation.3 | loop fusion | flops 884736 | bytes 589824 | tf_op jit(solution)/shard_map/concatenate | solution.py:322
  9.8 5.0 %collective-permute-start.2 = (bf16[1,64,2304]{2,1,0:T(8,128)(2,1)}, bf16[1,64,2304]{2,1,0:T(8,128)(2,1)S(1)}, u32[]{:S(2)}, u32[]{:S(2)}) collective-permute-start(bf16[1,64,2304]{2,1,0:T(8,128)(2,1)} %pad_maximum_fusion), channel_id=1, source_target_pairs={{0,4},{4,8},{8,12},{12,16},{16,20},{20,24},{24,28},{1,5},{5,9},{9,... | collective-permute-start | bytes 884744 | tf_op jit(solution)/shard_map/ppermute | solution.py:324
  14.7 0.7 %pad_maximum_fusion.1 = bf16[1,64,2304]{2,1,0:T(8,128)(2,1)} fusion(bf16[1,64,128]{2,1,0:T(8,128)(2,1)S(1)} %get-tuple-element.35, bf16[1,64,2048]{2,1,0:T(8,128)(2,1)S(1)} %slice.62, bf16[1,64,128]{2,1,0:T(8,128)(2,1)S(1)} %get-tuple-element.33), kind=kLoop, calls=%fused_computation.4 | loop fusion | flops 884736 | bytes 589824 | tf_op jit(solution)/shard_map/concatenate | solution.py:323
  15.5 1.9 %collective-permute-start.3 = (bf16[1,64,2304]{2,1,0:T(8,128)(2,1)}, bf16[1,64,2304]{2,1,0:T(8,128)(2,1)}, u32[]{:S(2)}, u32[]{:S(2)}) collective-permute-start(bf16[1,64,2304]{2,1,0:T(8,128)(2,1)} %pad_maximum_fusion.1), channel_id=1, source_target_pairs={{4,0},{8,4},{12,8},{16,12},{20,16},{24,20},{28,24},{5,1},{9,5},{13... | collective-permute-start | bytes 884744 | tf_op jit(solution)/shard_map/ppermute | solution.py:325
  17.4 2.4 %copy.24 = bf16[2,2,2,2,2,2,32,64]{7,2,0,4,6,5,3,1:T(2,128)(2,1)} copy(bf16[2,2,2,2,2,2,32,64]{7,6,5,4,3,2,1,0:T(8,128)(2,1)} %bitcast.57) | data formatting | bytes 524288 | tf_op jit(solution)/shard_map/reshape | solution.py:327
  19.8 1.4 %reshape.43.w = bf16[256,512]{1,0:T(8,128)(2,1)S(1)} reshape(bf16[2,2,2,32,2,2,2,64]{7,6,5,4,3,2,1,0:T(2,128)(2,1)} %bitcast.52) | data formatting | bytes 524288 | tf_op jit(solution)/shard_map/reshape | solution.py:328
  21.3 3.5 %shard_map.58 = (bf16[8,32,2,16,128]{4,3,2,1,0:T(8,128)(2,1)}, f32[256,512]{1,0:T(8,128)S(1)}, f32[2,64,2304]{2,1,0:T(8,128)S(1)}) custom-call(bf16[2,64,2048]{2,1,0:T(8,128)(2,1)S(1)} %copy.20.flat, bf16[2,64,128]{2,1,0:T(8,128)(2,1)S(1)} %collective-permute-done.ylo, bf16[2,64,128]{2,1,0:T(8,128)(2,1)S(1)} %collective-permute-done.1.yhi, ...), custom_call_target="tpu_custom_call" | custom-call | tf_op jit(solution)/shard_map/pallas_call | solution.py:349
  24.9 7.1 %shard_map.59 = (bf16[8,32,2,16,128]{4,3,2,1,0:T(8,128)(2,1)}, f32[16,32,128]{2,1,0:T(8,128)S(1)}, bf16[16,32,128]{2,1,0:T(8,128)(2,1)S(1)}, f32[2,64,2048]{2,1,...) custom-call(s32[1]{0:T(128)} %bitcast.core, ...), custom_call_target="tpu_custom_call", output_to_operand_aliasing={{0}: (11, {})} | custom-call | tf_op jit(solution)/shard_map/pallas_call | solution.py:361
  32.0 1.0 %copy-done.1 = f32[2,64,2048]{2,1,0:T(8,128)} copy-done((f32[2,64,2048]{2,1,0:T(8,128)}, f32[2,64,2048]{2,1,0:T(8,128)S(1)}, u32[]{:S(2)}) %copy-start.1) | copy-done | bytes 1048600
  33.0 3.6 %collective-permute-start.4 = (bf16[1,64,2304]{2,1,0:T(8,128)(2,1)}, bf16[1,64,2304]{2,1,0:T(8,128)(2,1)S(1)}, u32[]{:S(2)}, u32[]{:S(2)}) collective-permute-start(bf16[1,64,2304]{2,1,0:T(8,128)(2,1)} %get-tuple-element.18), channel_id=1, source_target_pairs={{0,4},{4,8},{8,12},{12,16},{16,20},{20,24},{24,28},{1,5},{5,9},{9,... | collective-permute-start | bytes 884744 | tf_op jit(solution)/shard_map/ppermute | solution.py:413
  36.7 0.7 add_convert_fusion.1
  37.4 3.5 %all-to-all-start = ((bf16[4,128,128]{2,1,0:T(8,128)(2,1)}), bf16[4,128,128]{2,1,0:T(8,128)(2,1)S(1)}, u32[]{:S(2)}, u32[]{:S(2)}) async-start(bf16[4,128,128]{2,1,0:T(8,128)(2,1)} %bitcast.10), calls=%async_computation | async-start | bytes 262144 | tf_op jit(solution)/shard_map/all_to_all | solution.py:390
  40.9 1.9 %collective-permute-start.5 = (bf16[1,64,2304]{2,1,0:T(8,128)(2,1)}, bf16[1,64,2304]{2,1,0:T(8,128)(2,1)S(1)}, u32[]{:S(2)}, u32[]{:S(2)}) collective-permute-start(bf16[1,64,2304]{2,1,0:T(8,128)(2,1)} %copy-done.4), channel_id=1, source_target_pairs={{4,0},{8,4},{12,8},{16,12},{20,16},{24,20},{28,24},{5,1},{9,5},{13... | collective-permute-start | bytes 884744 | tf_op jit(solution)/shard_map/ppermute | solution.py:414
  42.8 2.6 %all-to-all-done = bf16[4,128,128]{2,1,0:T(8,128)(2,1)S(1)} async-done(((bf16[4,128,128]{2,1,0:T(8,128)(2,1)}), bf16[4,128,128]{2,1,0:T(8,128)(2,1)S(1)}, u32[]{:S(2)}, u32[]{:S(2)}) %all-to-all-start) | async-done | bytes 131104 | tf_op jit(solution)/shard_map/all_to_all | solution.py:390
  45.4 0.7 broadcast_in_dim.4
  46.1 5.3 %all-to-all-start.1 = ((bf16[4,128,128]{2,1,0:T(8,128)(2,1)}), bf16[4,128,128]{2,1,0:T(8,128)(2,1)S(1)}, u32[]{:S(2)}, u32[]{:S(2)}) async-start(bf16[4,128,128]{2,1,0:T(8,128)(2,1)} %broadcast_in_dim.4), calls=%async_computation.1 | async-start | bytes 262144 | tf_op jit(solution)/shard_map/all_to_all | solution.py:392
  51.5 0.9 %fusion.3 = (bf16[2,64,128]{2,1,0:T(8,128)(2,1)S(1)}, bf16[2,64,128]{2,1,0:T(8,128)(2,1)S(1)}) fusion(f32[1,64,128]{2,1,0:T(8,128)S(1)} %get-tuple-element.29, f32[1,64,128]{2,1,0:T(8,128)S(1)} %get-tuple-element.27, f32[2,2,64,128]{3,2,1,0:T(8,128)} %copy-done.3, f32[1,64,128]{2,1,0:T(8,128)S(1)} %get-tuple-element.30, f32[1,64,128]{2,1,0:T(8,128)S(1)} %get-tuple-element.28), kind=kLoop, calls=%fused_computation.12 | loop fusion | flops 98304 | bytes 327680 | tf_op jit(solution)/shard_map/convert_element_type | solution.py:426
  52.4 3.4 %collective-permute-start.6 = (bf16[2,64,128]{2,1,0:T(8,128)(2,1)S(1)}, bf16[2,64,128]{2,1,0:T(8,128)(2,1)S(1)}, u32[]{:S(2)}, u32[]{:S(2)}) collective-permute-start(bf16[2,64,128]{2,1,0:T(8,128)(2,1)S(1)} %get-tuple-element.31), channel_id=1, source_target_pairs={{0,1},{1,2},{2,3},{4,5},{5,6},{6,7},{8,9},{9,10},{10,11},{12,13},{... | collective-permute-start | bytes 98312 | tf_op jit(solution)/shard_map/ppermute | solution.py:427
  55.7 1.3 %collective-permute-start.7 = (bf16[2,64,128]{2,1,0:T(8,128)(2,1)S(1)}, bf16[2,64,128]{2,1,0:T(8,128)(2,1)S(1)}, u32[]{:S(2)}, u32[]{:S(2)}) collective-permute-start(bf16[2,64,128]{2,1,0:T(8,128)(2,1)S(1)} %get-tuple-element.32), channel_id=1, source_target_pairs={{1,0},{2,1},{3,2},{5,4},{6,5},{7,6},{9,8},{10,9},{11,10},{13,12},{... | collective-permute-start | bytes 98312 | tf_op jit(solution)/shard_map/ppermute | solution.py:428
  57.2 0.7 broadcast_in_dim.5
  57.8 3.3 %all-to-all-start.2 = ((bf16[4,128,128]{2,1,0:T(8,128)(2,1)}), bf16[4,128,128]{2,1,0:T(8,128)(2,1)S(1)}, u32[]{:S(2)}, u32[]{:S(2)}) async-start(bf16[4,128,128]{2,1,0:T(8,128)(2,1)} %broadcast_in_dim.5), calls=%async_computation.2 | async-start | bytes 262144 | tf_op jit(solution)/shard_map/all_to_all | solution.py:396
  61.5 3.6 %all-to-all-done.2 = bf16[4,128,128]{2,1,0:T(8,128)(2,1)S(1)} async-done(((bf16[4,128,128]{2,1,0:T(8,128)(2,1)}), bf16[4,128,128]{2,1,0:T(8,128)(2,1)S(1)}, u32[]{:S(2)}, u32[]{:S(2)}) %all-to-all-start.2) | async-done | bytes 131104 | tf_op jit(solution)/shard_map/all_to_all | solution.py:396
  65.0 2.6 %collective-permute-start.9 = (bf16[16,32,128]{2,1,0:T(8,128)(2,1)S(1)}, bf16[16,32,128]{2,1,0:T(8,128)(2,1)S(1)}, u32[]{:S(2)}, u32[]{:S(2)}) collective-permute-start(bf16[16,32,128]{2,1,0:T(8,128)(2,1)S(1)} %bitcast.55), channel_id=1, source_target_pairs={{0,4},{4,0},{8,12},{12,8},{16,20},{20,16},{24,28},{28,24},{1,5},{5... | collective-permute-start | bytes 393224 | tf_op jit(solution)/shard_map/ppermute | solution.py:404
  67.6 0.8 %copy_bitcast_fusion = bf16[64,2,16,128]{3,2,1,0:T(8,128)(2,1)} fusion(bf16[2,64,16,128]{3,2,1,0:T(8,128)(2,1)S(1)} %bitcast.51), kind=kLoop, calls=%fused_computation.1 | loop fusion | bytes 1048576 | tf_op jit(solution)/shard_map/transpose | solution.py:435
  68.4 0.2 collective-permute-done.9.other
  68.6 0.6 copy-done.7
  69.2 2.2 %shard_map.60 = f32[4,4,4,32,64]{4,3,2,1,0:T(8,128)} custom-call(s32[1]{0:T(128)} %bitcast.core, bf16[16,32,128]{2,1,0:T(8,128)(2,1)} %bitcast.56, bf16[16,32,128]{2,1,0:T(8,128)(2,1)} %copy-done.7), custom_call_target="tpu_custom_call" | custom-call | tf_op jit(solution)/shard_map/pallas_call | solution.py:405
  (40 shorter events, 0.8 us)
Async XLA Ops:
  0.6 7.4 %copy-start.5 = (bf16[64,2,16,128]{3,2,1,0:T(8,128)(2,1)S(1)}, bf16[64,2,16,128]{3,2,1,0:T(8,128)(2,1)}, u32[]{:S(2)}) copy-start(bf16[64,2,16,128]{3,2,1,0:T(8,128)(2,1)} %param.3) | copy-start | bytes 1572868
  2.1 6.3 %collective-permute-start.1 = (bf16[2,64,128]{2,1,0:T(8,128)(2,1)S(1)}, bf16[2,64,128]{2,1,0:T(8,128)(2,1)S(1)}, u32[]{:S(2)}, u32[]{:S(2)}) collective-permute-start(bf16[2,64,128]{2,1,0:T(8,128)(2,1)S(1)} %get-tuple-element.25), channel_id=1, source_target_pairs={{1,0},{2,1},{3,2},{5,4},{6,5},{7,6},{9,8},{10,9},{11,10},{13,12},{... | collective-permute-start | bytes 98312 | tf_op jit(solution)/shard_map/ppermute | solution.py:321
  3.4 5.7 %collective-permute-start = (bf16[2,64,128]{2,1,0:T(8,128)(2,1)S(1)}, bf16[2,64,128]{2,1,0:T(8,128)(2,1)S(1)}, u32[]{:S(2)}, u32[]{:S(2)}) collective-permute-start(bf16[2,64,128]{2,1,0:T(8,128)(2,1)S(1)} %get-tuple-element.26), channel_id=1, source_target_pairs={{0,1},{1,2},{2,3},{4,5},{5,6},{6,7},{8,9},{9,10},{10,11},{12,13},{... | collective-permute-start | bytes 98312 | tf_op jit(solution)/shard_map/ppermute | solution.py:320
  8.2 13.1 %copy-start = (bf16[2,2,2,32,2,16,128]{6,5,4,3,2,1,0:T(8,128)(2,1)S(1)}, bf16[2,2,2,32,2,16,128]{6,5,4,3,2,1,0:T(8,128)(2,1)}, u32[]{:S(2)}) copy-start(bf16[2,2,2,32,2,16,128]{6,5,4,3,2,1,0:T(8,128)(2,1)} %param.5) | copy-start | bytes 6291460
  9.8 15.1 %collective-permute-start.2 = (bf16[1,64,2304]{2,1,0:T(8,128)(2,1)}, bf16[1,64,2304]{2,1,0:T(8,128)(2,1)S(1)}, u32[]{:S(2)}, u32[]{:S(2)}) collective-permute-start(bf16[1,64,2304]{2,1,0:T(8,128)(2,1)} %pad_maximum_fusion), channel_id=1, source_target_pairs={{0,4},{4,8},{8,12},{12,16},{16,20},{20,24},{24,28},{1,5},{5,9},{9,... | collective-permute-start | bytes 884744 | tf_op jit(solution)/shard_map/ppermute | solution.py:324
  15.5 9.4 %collective-permute-start.3 = (bf16[1,64,2304]{2,1,0:T(8,128)(2,1)}, bf16[1,64,2304]{2,1,0:T(8,128)(2,1)}, u32[]{:S(2)}, u32[]{:S(2)}) collective-permute-start(bf16[1,64,2304]{2,1,0:T(8,128)(2,1)} %pad_maximum_fusion.1), channel_id=1, source_target_pairs={{4,0},{8,4},{12,8},{16,12},{20,16},{24,20},{28,24},{5,1},{9,5},{13... | collective-permute-start | bytes 884744 | tf_op jit(solution)/shard_map/ppermute | solution.py:325
  32.0 1.0 %copy-start.1 = (f32[2,64,2048]{2,1,0:T(8,128)}, f32[2,64,2048]{2,1,0:T(8,128)S(1)}, u32[]{:S(2)}) copy-start(f32[2,64,2048]{2,1,0:T(8,128)S(1)} %get-tuple-element.17) | copy-start | bytes 3145732
  33.0 4.3 %copy-start.3 = (f32[2,2,64,128]{3,2,1,0:T(8,128)}, f32[2,2,64,128]{3,2,1,0:T(8,128)S(1)}, u32[]{:S(2)}) copy-start(f32[2,2,64,128]{3,2,1,0:T(8,128)S(1)} %get-tuple-element.20) | copy-start | bytes 393220
  33.0 4.3 %copy-start.4 = (bf16[1,64,2304]{2,1,0:T(8,128)(2,1)}, bf16[1,64,2304]{2,1,0:T(8,128)(2,1)S(1)}, u32[]{:S(2)}) copy-start(bf16[1,64,2304]{2,1,0:T(8,128)(2,1)S(1)} %get-tuple-element.19) | copy-start | bytes 884740
  33.0 3.7 %collective-permute-start.8 = (bf16[16,32,128]{2,1,0:T(8,128)(2,1)S(1)}, bf16[16,32,128]{2,1,0:T(8,128)(2,1)S(1)}, u32[]{:S(2)}, u32[]{:S(2)}) collective-permute-start(bf16[16,32,128]{2,1,0:T(8,128)(2,1)S(1)} %get-tuple-element.22), channel_id=1, source_target_pairs={{0,4},{4,0},{8,12},{12,8},{16,20},{20,16},{24,28},{28,24},{1,5},{5... | collective-permute-start | bytes 393224 | tf_op jit(solution)/shard_map/ppermute | solution.py:388
  33.0 18.4 %collective-permute-start.4 = (bf16[1,64,2304]{2,1,0:T(8,128)(2,1)}, bf16[1,64,2304]{2,1,0:T(8,128)(2,1)S(1)}, u32[]{:S(2)}, u32[]{:S(2)}) collective-permute-start(bf16[1,64,2304]{2,1,0:T(8,128)(2,1)} %get-tuple-element.18), channel_id=1, source_target_pairs={{0,4},{4,8},{8,12},{12,16},{16,20},{20,24},{24,28},{1,5},{5,9},{9,... | collective-permute-start | bytes 884744 | tf_op jit(solution)/shard_map/ppermute | solution.py:413
  37.4 23.8 %copy-start.2 = (f32[2,64,2048]{2,1,0:T(8,128)S(1)}, f32[2,64,2048]{2,1,0:T(8,128)}, u32[]{:S(2)}) copy-start(f32[2,64,2048]{2,1,0:T(8,128)} %copy-done.1) | copy-start | bytes 3145732
  37.4 8.0 %all-to-all-start = ((bf16[4,128,128]{2,1,0:T(8,128)(2,1)}), bf16[4,128,128]{2,1,0:T(8,128)(2,1)S(1)}, u32[]{:S(2)}, u32[]{:S(2)}) async-start(bf16[4,128,128]{2,1,0:T(8,128)(2,1)} %bitcast.10), calls=%async_computation | async-start | bytes 262144 | tf_op jit(solution)/shard_map/all_to_all | solution.py:390
  40.9 10.6 %collective-permute-start.5 = (bf16[1,64,2304]{2,1,0:T(8,128)(2,1)}, bf16[1,64,2304]{2,1,0:T(8,128)(2,1)S(1)}, u32[]{:S(2)}, u32[]{:S(2)}) collective-permute-start(bf16[1,64,2304]{2,1,0:T(8,128)(2,1)} %copy-done.4), channel_id=1, source_target_pairs={{4,0},{8,4},{12,8},{16,12},{20,16},{24,20},{28,24},{5,1},{9,5},{13... | collective-permute-start | bytes 884744 | tf_op jit(solution)/shard_map/ppermute | solution.py:414
  46.1 11.0 %all-to-all-start.1 = ((bf16[4,128,128]{2,1,0:T(8,128)(2,1)}), bf16[4,128,128]{2,1,0:T(8,128)(2,1)S(1)}, u32[]{:S(2)}, u32[]{:S(2)}) async-start(bf16[4,128,128]{2,1,0:T(8,128)(2,1)} %broadcast_in_dim.4), calls=%async_computation.1 | async-start | bytes 262144 | tf_op jit(solution)/shard_map/all_to_all | solution.py:392
  52.4 8.8 %collective-permute-start.6 = (bf16[2,64,128]{2,1,0:T(8,128)(2,1)S(1)}, bf16[2,64,128]{2,1,0:T(8,128)(2,1)S(1)}, u32[]{:S(2)}, u32[]{:S(2)}) collective-permute-start(bf16[2,64,128]{2,1,0:T(8,128)(2,1)S(1)} %get-tuple-element.31), channel_id=1, source_target_pairs={{0,1},{1,2},{2,3},{4,5},{5,6},{6,7},{8,9},{9,10},{10,11},{12,13},{... | collective-permute-start | bytes 98312 | tf_op jit(solution)/shard_map/ppermute | solution.py:427
  55.7 5.5 %collective-permute-start.7 = (bf16[2,64,128]{2,1,0:T(8,128)(2,1)S(1)}, bf16[2,64,128]{2,1,0:T(8,128)(2,1)S(1)}, u32[]{:S(2)}, u32[]{:S(2)}) collective-permute-start(bf16[2,64,128]{2,1,0:T(8,128)(2,1)S(1)} %get-tuple-element.32), channel_id=1, source_target_pairs={{1,0},{2,1},{3,2},{5,4},{6,5},{7,6},{9,8},{10,9},{11,10},{13,12},{... | collective-permute-start | bytes 98312 | tf_op jit(solution)/shard_map/ppermute | solution.py:428
  57.8 7.2 %all-to-all-start.2 = ((bf16[4,128,128]{2,1,0:T(8,128)(2,1)}), bf16[4,128,128]{2,1,0:T(8,128)(2,1)S(1)}, u32[]{:S(2)}, u32[]{:S(2)}) async-start(bf16[4,128,128]{2,1,0:T(8,128)(2,1)} %broadcast_in_dim.5), calls=%async_computation.2 | async-start | bytes 262144 | tf_op jit(solution)/shard_map/all_to_all | solution.py:396
  65.0 3.6 %copy-start.6 = (bf16[4,128,128]{2,1,0:T(8,128)(2,1)}, bf16[4,128,128]{2,1,0:T(8,128)(2,1)S(1)}, u32[]{:S(2)}) copy-start(bf16[4,128,128]{2,1,0:T(8,128)(2,1)S(1)} %all-to-all-done.2) | copy-start | bytes 393220
  65.0 3.6 %collective-permute-start.9 = (bf16[16,32,128]{2,1,0:T(8,128)(2,1)S(1)}, bf16[16,32,128]{2,1,0:T(8,128)(2,1)S(1)}, u32[]{:S(2)}, u32[]{:S(2)}) collective-permute-start(bf16[16,32,128]{2,1,0:T(8,128)(2,1)S(1)} %bitcast.55), channel_id=1, source_target_pairs={{0,4},{4,0},{8,12},{12,8},{16,20},{20,16},{24,28},{28,24},{1,5},{5... | collective-permute-start | bytes 393224 | tf_op jit(solution)/shard_map/ppermute | solution.py:404
  68.6 0.6 copy-start.7

commit v4 on v3

v4 whole, which is shorter than its diff:
```python
import functools
import math

import jax
import jax.numpy as jnp
from jax import lax
from jax.experimental import pallas as pl
from jax.experimental.pallas import tpu as pltpu
from jax.sharding import PartitionSpec as P

F32 = jnp.float32
BF16 = jnp.bfloat16
GROUP = 16


def swap_matrix(outer, inner):
    size = outer * inner
    row = lax.broadcasted_iota(jnp.int32, (size, size), 0)
    col = lax.broadcasted_iota(jnp.int32, (size, size), 1)
    return jnp.where(col == (row % outer) * inner + row // outer, 1.0, 0.0).astype(BF16)


def turn(matrix, pieces, nz):
    flat = [p.reshape(p.shape[0] * p.shape[1], nz) for p in pieces]
    moved = jnp.dot(matrix, jnp.concatenate(flat, axis=1), preferred_element_type=F32)
    return moved.astype(BF16)


def bring_plane(to_y, raw, ny, nz, put):
    for k in range(0, raw.count, 2):
        moved = turn(to_y, [raw(k), raw(k + 1)], nz)
        for y in range(ny):
            rows = slice(y * GROUP, (y + 1) * GROUP)
            put(k, y, moved[rows, :nz])
            put(k + 1, y, moved[rows, nz:])


class Tiles:
    def __init__(self, count, get):
        self.count, self.get = count, get

    def __call__(self, k):
        return self.get(k)


def columns_pass(dims, chunk, columns, block, rolled, w, wt, cot_at, put_value, wg_add, ig_add, ga, gb):
    nx, ny, nz, ci, co = dims
    half = 4 * ci
    first = lax.broadcasted_iota(jnp.int32, (co, nz), 1) == 0
    zeros = jnp.zeros((2 * co, nz), BF16)

    def corners(get, some):
        return jnp.concatenate(
            [
                jnp.concatenate([get(i + 1 - ex, j + 1 - ey) for i, j in some], axis=1)
                for ex in range(2)
                for ey in range(2)
            ],
            axis=0,
        )

    starts = range(0, len(columns), chunk)
    for c0 in starts:
        some = columns[c0 : c0 + chunk]
        back = jnp.dot(w[:, half:], corners(rolled, some), preferred_element_type=F32)
        here = jnp.dot(w[:, :half], corners(block, some), preferred_element_type=F32)
        for k, (i, j) in enumerate(some):
            cols = slice(k * nz, (k + 1) * nz)
            wide = slice((c0 + k) * nz, (c0 + k + 1) * nz)
            for tx in range(2):
                for ty in range(2):
                    sx, sy = 1 - tx, 1 - ty
                    m, n = i - sx, j - sy
                    base = (2 * tx + ty) * 2 * co
                    if not (0 <= m < nx and 0 <= n < ny):
                        ga[base : base + 2 * co, wide] = zeros
                        gb[base : base + 2 * co, wide] = zeros
                        continue
                    for tz in range(2):
                        sz = 1 - tz
                        r = slice(base + tz * co, base + (tz + 1) * co)
                        low, high = back[r, cols], here[r, cols]
                        if sz == 1:
                            before = low + jnp.where(first, 0.0, high)
                            before = pltpu.roll(before, nz - 1, 1)
                        else:
                            before = jnp.where(first, 0.0, low) + high
                        q = (2 * sx + sy) * 2 + sz
                        sig = 0.5 * jnp.tanh(0.5 * before) + 0.5
                        value = before * sig
                        put_value(q, m, n, value.astype(BF16))
                        slope = sig + value * (1.0 - sig)
                        grad = cot_at(q, m, n).astype(F32) * slope
                        if sz == 1:
                            grad = pltpu.roll(grad, 1, 1)
                        whole = grad.astype(BF16)
                        cut = jnp.where(first, 0.0, grad).astype(BF16)
                        ga[r, wide] = cut if sz == 0 else whole
                        gb[r, wide] = cut if sz == 1 else whole

    started = set()
    for c0 in starts:
        some = columns[c0 : c0 + chunk]
        wide = slice(c0 * nz, (c0 + len(some)) * nz)
        back = jnp.dot(wt[half:], ga[:, wide], preferred_element_type=F32)
        here = jnp.dot(wt[:half], gb[:, wide], preferred_element_type=F32)
        for k, (i, j) in enumerate(some):
            cols = slice(k * nz, (k + 1) * nz)
            both = here[:, cols] + pltpu.roll(back[:, cols], nz - 1, 1)
            for ex in range(2):
                for ey in range(2):
                    r = (2 * ex + ey) * ci
                    cell = (i - ex, j - ey)
                    ig_add(cell[0], cell[1], both[r : r + ci], cell not in started)
                    started.add(cell)

    nt = (((1,), (1,)), ((), ()))
    for part, (grads, get) in enumerate(((gb, block), (ga, rolled))):
        wg_add(
            part,
            lax.dot_general(grads[...], corners(get, columns), nt, preferred_element_type=F32),
        )
    return started


def edge_row(q, ny):
    return (ny - 1) if q // 2 % 2 else 0


def inner_kernel(
    dims, chunk, vol, taps, cot, flat, w, wt, vals, cot_edge, wg, ig, vm, ga, gb, cots
):
    nx, ny, nz, ci, co = dims
    half = 4 * ci
    to_y = swap_matrix(GROUP, ny)

    for tx in range(2):
        for ty in range(2):
            for tz in range(2):
                r = ((2 * tx + ty) * 2 + tz) * co
                for ez in range(2):
                    for ex in range(2):
                        pair = [taps[2 * ex + tx, 2 * ey + ty, 2 * ez + tz] for ey in range(2)]
                        c = (2 * ez + ex) * 2 * ci
                        w[r : r + co, c : c + 2 * ci] = jnp.concatenate(pair, axis=1)
    wt[...] = w[...].T

    for x in range(nx):

        def put(k, y, rows, x=x):
            r = slice(k * GROUP, (k + 1) * GROUP)
            lanes = slice(y * nz, (y + 1) * nz)
            flat[x, r, lanes] = rows
            vm[x, r, lanes] = pltpu.roll(rows.astype(F32), 1, 1).astype(BF16)

        tiles = Tiles(
            ci // GROUP, lambda k, x=x: vol[k * GROUP : (k + 1) * GROUP, x]
        )
        bring_plane(to_y, tiles, ny, nz, put)

    for i in range(1, nx):
        for q in range(8):
            m = i - q // 4

            def put(k, y, rows, i=i, q=q):
                r = slice(q * co + k * GROUP, q * co + (k + 1) * GROUP)
                cots[i - 1, r, y * nz : (y + 1) * nz] = rows
                if y == edge_row(q, ny):
                    cot_edge[i - 1, r] = rows

            tiles = Tiles(
                co // GROUP, lambda k, q=q, m=m: cot[q, k * GROUP : (k + 1) * GROUP, m]
            )
            bring_plane(to_y, tiles, ny, nz, put)

    def block(x, y):
        return flat[x - 1, :, (y - 1) * nz : y * nz]

    def rolled(x, y):
        return vm[x - 1, :, (y - 1) * nz : y * nz]

    def cot_at(q, m, n):
        return cots[m + q // 4 - 1, q * co : (q + 1) * co, n * nz : (n + 1) * nz]

    def put_value(q, m, n, value):
        vals[m + q // 4 - 1, q * co : (q + 1) * co, n * nz : (n + 1) * nz] = value

    def wg_add(part, total):
        wg[:, part * half : (part + 1) * half] = total

    def ig_add(m, y, value, fresh):
        lanes = slice(y * nz, (y + 1) * nz)
        ig[m, :, lanes] = value if fresh else ig[m, :, lanes] + value

    columns = [(i, j) for i in range(1, nx) for j in range(1, ny)]
    columns_pass(
        dims, chunk, columns, block, rolled, w, wt, cot_at, put_value, wg_add, ig_add, ga, gb
    )


def outer_kernel(
    dims,
    chunk,
    core,
    flat,
    xlo,
    xhi,
    ylo,
    yhi,
    w,
    wt,
    cot,
    vals_in,
    cot_edge,
    wg_in,
    ig_in,
    act_out,
    own_out,
    keep,
    send,
    yface,
    up,
    down,
    full,
    faces,
    own,
    xs,
    vm,
    ga,
    gb,
    cots,
    vals,
    val_edge,
    staged,
    sems,
):
    nx, ny, nz, ci, co = dims
    half = 4 * ci
    to_y = swap_matrix(GROUP, ny)
    to_c = swap_matrix(ny, GROUP)

    for side, plane in enumerate((xlo, xhi)):

        def put(k, y, rows, side=side):
            xs[side, k * GROUP : (k + 1) * GROUP, y * nz : (y + 1) * nz] = rows

        tiles = Tiles(
            ci // GROUP, lambda k, plane=plane: plane[k * GROUP : (k + 1) * GROUP, 0]
        )
        bring_plane(to_y, tiles, ny, nz, put)

    for side in range(2):
        for q in range(4 * side, 4 * side + 4):

            def put(k, y, rows, q=q):
                r = slice(q * co + k * GROUP, q * co + (k + 1) * GROUP)
                cots[r, y * nz : (y + 1) * nz] = rows

            tiles = Tiles(
                co // GROUP,
                lambda k, q=q, side=side: cot[
                    q, k * GROUP : (k + 1) * GROUP, side * (nx - 1)
                ],
            )
            bring_plane(to_y, tiles, ny, nz, put)

    def block(x, y):
        if y == 0:
            return ylo[x]
        if y == ny + 1:
            return yhi[x]
        lanes = slice((y - 1) * nz, y * nz)
        if x == 0:
            return xs[0, :, lanes]
        if x == nx + 1:
            return xs[1, :, lanes]
        return flat[x - 1, :, lanes]

    for x in range(nx + 2):
        for y in range(ny + 2):
            vm[x, :, y * nz : (y + 1) * nz] = pltpu.roll(block(x, y).astype(F32), 1, 1).astype(
                BF16
            )

    def rolled(x, y):
        return vm[x, :, y * nz : (y + 1) * nz]

    def inner(q, m):
        return 1 <= m + q // 4 < nx

    def cot_at(q, m, n):
        r = slice(q * co, (q + 1) * co)
        if inner(q, m):
            return cot_edge[m + q // 4 - 1, r]
        return cots[r, n * nz : (n + 1) * nz]

    def put_value(q, m, n, value):
        r = slice(q * co, (q + 1) * co)
        if inner(q, m):
            val_edge[m + q // 4 - 1, r] = value
        else:
            vals[r, n * nz : (n + 1) * nz] = value

    def wg_add(part, total):
        total = total + wg_in[:, part * half : (part + 1) * half]
        for ex in range(2):
            for row in range(8):
                tx, ty, tz = row // 4, row // 2 % 2, row % 2
                index = ((tx * 2 + ty) * 2 + part) * 2 + tz
                full[ex, index] = total[
                    row * co : (row + 1) * co, ex * 2 * ci : (ex + 1) * 2 * ci
                ]

    def ig_add(m, y, value, fresh):
        if m < 0 or m >= nx:
            side = 0 if m < 0 else 1
            lanes = slice((y + 1) * nz, (y + 2) * nz)
            faces[side, :, lanes] = value if fresh else faces[side, :, lanes] + value
        elif y < 0 or y >= ny:
            side = 0 if y < 0 else 1
            yface[side, m] = value if fresh else yface[side, m] + value
        else:
            lanes = slice(y * nz, (y + 1) * nz)
            own[m, :, lanes] = (ig_in if fresh else own)[m, :, lanes] + value

    columns = [(i, j) for i in (0, nx) for j in range(ny + 1)]
    columns += [(i, j) for i in range(1, nx) for j in (0, ny)]
    started = columns_pass(
        dims, chunk, columns, block, rolled, w, wt, cot_at, put_value, wg_add, ig_add, ga, gb
    )
    for m in range(nx):
        for y in range(ny):
            if (m, y) not in started:
                lanes = slice(y * nz, (y + 1) * nz)
                own[m, :, lanes] = ig_in[m, :, lanes]
    c = core[0]
    keep[...] = full[c]
    send[...] = full[1 - c].astype(BF16)
    down[0] = faces[0].astype(BF16)
    up[0] = faces[1].astype(BF16)
    copies = [pltpu.make_async_copy(own, own_out, sems.at[8 * nx])]
    copies[0].start()

    for m in range(nx):
        for q in range(8):
            tiles = []
            for k in range(co // GROUP):
                r = slice(q * co + k * GROUP, q * co + (k + 1) * GROUP)
                rows = []
                for y in range(ny):
                    lanes = slice(y * nz, (y + 1) * nz)
                    if not inner(q, m):
                        rows.append(vals[r, lanes])
                    elif y == edge_row(q, ny):
                        rows.append(val_edge[m + q // 4 - 1, r])
                    else:
                        rows.append(vals_in[m + q // 4 - 1, r, lanes])
                tiles.append(jnp.concatenate(rows, axis=0).reshape(ny, GROUP, nz))
            moved = turn(to_c, tiles, nz)
            spot = m * 8 + q
            for k in range(co // GROUP):
                staged[spot, k * GROUP : (k + 1) * GROUP] = moved[
                    :, k * nz : (k + 1) * nz
                ].reshape(GROUP, ny, nz)
            copy = pltpu.make_async_copy(staged.at[spot], act_out.at[q, :, m], sems.at[spot])
            copy.start()
            copies.append(copy)
    for copy in copies:
        copy.wait()


def unpack_kernel(co, ci, core, mine, other, out, full):
    c = core[0]
    full[c] = mine[...].astype(F32)
    full[1 - c] = other[...].astype(F32)
    for ex in range(2):
        for tx in range(2):
            for ty in range(2):
                for ez in range(2):
                    for tz in range(2):
                        index = ((tx * 2 + ty) * 2 + ez) * 2 + tz
                        pair = full[ex, index]
                        for ey in range(2):
                            out[2 * ex + tx, 2 * ey + ty, 2 * ez + tz] = pair[
                                :, ey * ci : (ey + 1) * ci
                            ]


def neighbours(axis):
    count = lax.axis_size(axis)
    up = [(i, i + 1) for i in range(count - 1)]
    return up, [(b, a) for a, b in up]


def on_device(volume, kernel, cotangent):
    ci, nx, ny, nz = volume.shape
    co = kernel.shape[3]
    gx, gy = lax.axis_size("gx"), lax.axis_size("gy")
    gx_up, gx_down = neighbours("gx")
    gy_up, gy_down = neighbours("gy")
    cells = nx * gx * ny * gy * nz
    dims = (nx, ny, nz, ci, co)
    core = (lax.axis_index("gx") % 2).astype(jnp.int32).reshape(1)

    xlo = lax.ppermute(volume[:, nx - 1 :], "gx", gx_up)
    xhi = lax.ppermute(volume[:, :1], "gx", gx_down)
    cot = cotangent.reshape(8, co, nx, ny, nz)

    vmem = pl.BlockSpec(memory_space=pltpu.VMEM)
    smem = pl.BlockSpec(memory_space=pltpu.SMEM)
    anywhere = pl.BlockSpec(memory_space=pl.ANY)
    params = pltpu.CompilerParams(vmem_limit_bytes=28 * 1024 * 1024)
    n_in = (nx - 1) * (ny - 1)
    n_out = 2 * (ny + 1) + 2 * (nx - 1)
    flat, w, wt, vals, cot_edge, wg_part, ig_part = pl.pallas_call(
        functools.partial(inner_kernel, dims, 5),
        out_shape=(
            jax.ShapeDtypeStruct((nx, ci, ny * nz), BF16),
            jax.ShapeDtypeStruct((8 * co, 8 * ci), BF16),
            jax.ShapeDtypeStruct((8 * ci, 8 * co), BF16),
            jax.ShapeDtypeStruct((nx - 1, 8 * co, ny * nz), BF16),
            jax.ShapeDtypeStruct((nx - 1, 8 * co, nz), BF16),
            jax.ShapeDtypeStruct((8 * co, 8 * ci), F32),
            jax.ShapeDtypeStruct((nx, ci, ny * nz), F32),
        ),
        in_specs=[vmem] * 3,
        out_specs=(vmem,) * 7,
        scratch_shapes=[
            pltpu.VMEM((nx, ci, ny * nz), BF16),
            pltpu.VMEM((8 * co, n_in * nz), BF16),
            pltpu.VMEM((8 * co, n_in * nz), BF16),
            pltpu.VMEM((nx - 1, 8 * co, ny * nz), BF16),
        ],
        compiler_params=params,
    )(volume, kernel, cot)

    def y_row(y):
        rows = jnp.concatenate([xlo[:, :, y], volume[:, :, y], xhi[:, :, y]], axis=1)
        return rows.transpose(1, 0, 2)

    ylo = lax.ppermute(y_row(ny - 1), "gy", gy_up)
    yhi = lax.ppermute(y_row(0), "gy", gy_down)
    act, own, keep, send, yface, up, down = pl.pallas_call(
        functools.partial(outer_kernel, dims, 4),
        out_shape=(
            jax.ShapeDtypeStruct(cot.shape, BF16),
            jax.ShapeDtypeStruct((nx, ci, ny * nz), F32),
            jax.ShapeDtypeStruct((16, co, 2 * ci), F32),
            jax.ShapeDtypeStruct((16, co, 2 * ci), BF16),
            jax.ShapeDtypeStruct((2, nx, ci, nz), F32),
            jax.ShapeDtypeStruct((1, ci, (ny + 2) * nz), BF16),
            jax.ShapeDtypeStruct((1, ci, (ny + 2) * nz), BF16),
        ),
        in_specs=[smem] + [vmem] * 12,
        out_specs=(anywhere, anywhere) + (vmem,) * 5,
        scratch_shapes=[
            pltpu.VMEM((2, 16, co, 2 * ci), F32),
            pltpu.VMEM((2, ci, (ny + 2) * nz), F32),
            pltpu.VMEM((nx, ci, ny * nz), F32),
            pltpu.VMEM((2, ci, ny * nz), BF16),
            pltpu.VMEM((nx + 2, ci, (ny + 2) * nz), BF16),
            pltpu.VMEM((8 * co, n_out * nz), BF16),
            pltpu.VMEM((8 * co, n_out * nz), BF16),
            pltpu.VMEM((8 * co, ny * nz), BF16),
            pltpu.VMEM((8 * co, ny * nz), BF16),
            pltpu.VMEM((nx - 1, 8 * co, nz), BF16),
            pltpu.VMEM((8 * nx, co, ny, nz), BF16),
            pltpu.SemaphoreType.DMA((8 * nx + 1,)),
        ],
        compiler_params=params,
    )(core, flat, xlo, xhi, ylo, yhi, w, wt, cot, vals, cot_edge, wg_part, ig_part)

    scale = 1.0 / math.sqrt(cells)
    place = lax.axis_index("gx")
    bits = [1 << b for b in range(1, gx.bit_length() - 1)]

    def trade(array, axis, count, distance):
        return lax.ppermute(array, axis, [(k, k ^ distance) for k in range(count)])

    part = (keep + trade(send, "gx", gx, 1).astype(F32)).reshape(16 * co, 2 * ci)
    for bit in bits:
        upper = (place & bit) != 0
        rows = part.shape[0] // 2
        kept = jnp.where(upper, part[rows:], part[:rows])
        sent = jnp.where(upper, part[:rows], part[rows:]).astype(BF16)
        part = kept + trade(sent, "gx", gx, bit).astype(F32)
    distance = 1
    while distance < gy:
        part = part + trade(part, "gy", gy, distance)
        distance *= 2
    total = (part * scale).astype(BF16)
    for bit in reversed(bits):
        upper = (place & bit) != 0
        others = trade(total, "gx", gx, bit)
        total = jnp.where(
            upper,
            jnp.concatenate([others, total], axis=0),
            jnp.concatenate([total, others], axis=0),
        )
    mine = total.reshape(16, co, 2 * ci)
    other = trade(mine, "gx", gx, 1)
    weight_grad = pl.pallas_call(
        functools.partial(unpack_kernel, co, ci),
        out_shape=jax.ShapeDtypeStruct((4, 4, 4, co, ci), F32),
        in_specs=[smem, vmem, vmem],
        out_specs=vmem,
        scratch_shapes=[pltpu.VMEM((2, 16, co, 2 * ci), F32)],
        compiler_params=pltpu.CompilerParams(vmem_limit_bytes=8 * 1024 * 1024),
    )(core, mine, other)

    from_low = lax.ppermute(up, "gx", gx_up).astype(F32)
    from_high = lax.ppermute(down, "gx", gx_down).astype(F32)

    def add_x(array, lanes):
        lead = (nx - 1,) + from_low[:, :, lanes].shape[1:]
        zero = jnp.zeros(lead, F32)
        return (
            array
            + jnp.concatenate([from_low[:, :, lanes], zero], axis=0)
            + jnp.concatenate([zero, from_high[:, :, lanes]], axis=0)
        )

    send_low = add_x(yface[0], slice(0, nz)).astype(BF16)
    send_high = add_x(yface[1], slice((ny + 1) * nz, None)).astype(BF16)
    y_low = lax.ppermute(send_high, "gy", gy_up).astype(F32)
    y_high = lax.ppermute(send_low, "gy", gy_down).astype(F32)
    gap = jnp.zeros((nx, ci, (ny - 1) * nz), F32)
    total_ig = (
        add_x(own, slice(nz, (ny + 1) * nz))
        + jnp.concatenate([y_low, gap], axis=2)
        + jnp.concatenate([gap, y_high], axis=2)
    )
    input_grad = total_ig.astype(BF16).reshape(nx, ci, ny, nz).transpose(1, 0, 2, 3)
    return act.reshape(cotangent.shape), input_grad, weight_grad


def solution(mesh):
    placed = (P(None, "gx", "gy", None), P(), P(None, None, None, None, "gx", "gy", None))
    return jax.shard_map(
        on_device,
        mesh=mesh,
        in_specs=placed,
        out_specs=(placed[2], placed[0], P()),
        check_vma=False,
    )
```

time: 72.5 us -> 74 us (1.021)
  waiting for transfers between devices: 7.03 us -> 18.3 us
  starting transfers between devices: 37.8 us -> 33.3 us
  other arithmetic: 3.22 us -> 0.37 us
  local copies, waits for them, and re-layouts: 9.56 us -> 8.27 us
  Pallas kernels: 12.8 us -> 11.9 us
    ppermute x6 -> x12, waiting for transfers between devices: 0.84 us -> 14.7 us  [the longest x8 9.11 us: trade(): return lax.ppermute(array, axis, [(k, k ^ distance) for k in range(count)])]
    all_to_all x3 -> x0, starting transfers between devices: 12.2 us -> none  [the longest x1 5.33 us: on_device(): lax.all_to_all(jnp.broadcast_to(part[None], (gy,) + part.shape), 'gy', 0,...]
    ppermute x6 -> x12, starting transfers between devices: 15.4 us -> 23.4 us  [the longest x8 12.5 us: trade(): return lax.ppermute(array, axis, [(k, k ^ distance) for k in range(count)])]
    all_to_all x3 -> x0, waiting for transfers between devices: 6.18 us -> none  [the longest x1 3.57 us: on_device(): lax.all_to_all(jnp.broadcast_to(total[None], (pairs,) + total.shape), 'gx...]
    reshape x5 -> x0, local copies, waits for them, and re-layouts: 5.27 us -> none  [the longest x1 2.38 us: on_device(): taps = kernel.reshape(2, 2, 2, 2, 2, 2, co, ci)]
    unnamed x17 -> x23, local copies, waits for them, and re-layouts: 1.74 us -> 5.67 us
    ppermute x1, waiting for transfers between devices: 0.01 us -> 3.04 us  [on_device(): y_high = lax.ppermute(send_low, 'gy', gy_down).astype(F32)]
    concatenate x2 -> x0, other arithmetic: 1.48 us -> none  [the longest x1 0.74 us: on_device(): top = jnp.concatenate([ylo[nx - 1:], flat[nx - 1:], yhi[nx - 1:]], axis=2)]
  transfers between devices with their start and end apart: 13 -> 16, of which waited for: 4 -> 9; matrix products, arithmetic and copies ran while one was open for 13% -> 2% of each run, Pallas kernels for 5% -> 4%
where the time goes in v4:
time: 74 us; the launch traced here: 73.1 us
  starting transfers between devices  33.3 us (45%)
  waiting for transfers between devices  18.3 us (25%)
  Pallas kernels  11.9 us (16%)
  local copies, waits for them, and re-layouts  8.27 us (11%)
  between operations  0.99 us (1%)
    ppermute x8, starting transfers between devices, trade(): return lax.ppermute(array, axis, [(k, k ^ distance) for k in range(count)])  12.5 us
    ppermute x8, waiting for transfers between devices, trade(): return lax.ppermute(array, axis, [(k, k ^ distance) for k in range(count)])  9.11 us
    pallas_call x1, Pallas kernels, on_device(): pl.pallas_call(functools.partial(outer_kernel, dims, 4), out_shape=(jax.S...  7.46 us
    unnamed x23, local copies, waits for them, and re-layouts  5.67 us
    ppermute x1, starting transfers between devices, on_device(): xlo = lax.ppermute(volume[:, nx - 1:], 'gx', gx_up)  4.51 us
    ppermute x1, waiting for transfers between devices, on_device(): xhi = lax.ppermute(volume[:, :1], 'gx', gx_down)  4.47 us
    ppermute x1, starting transfers between devices, on_device(): from_low = lax.ppermute(up, 'gx', gx_up).astype(F32)  3.64 us
    pallas_call x1, Pallas kernels, on_device(): pl.pallas_call(functools.partial(inner_kernel, dims, 5), out_shape=(jax.S...  3.21 us
  transfers between devices with their start and end apart: 16, of which 9 were waited for; matrix products, arithmetic and copies ran while one was open for 2% of the time, Pallas kernels for 4%

profile of v4, /device:TPU:1, one launch (start us, length us, event | category | flops | bytes accessed | tf_op | source)
XLA Modules:
  0.0 73.1 jit_solution(5851867592975807148)
XLA Ops:
  0.6 1.2 %fusion.5 = (bf16[64,1,16,128]{3,2,1,0:T(8,128)(2,1)S(1)}, bf16[64,1,16,128]{3,2,1,0:T(8,128)(2,1)S(1)}) fusion(bf16[64,2,16,128]{3,2,1,0:T(8,128)(2,1)} %vol.1), kind=kLoop, calls=%fused_computation.26 | loop fusion | bytes 1048576 | tf_op jit(solution)/shard_map/slice | solution.py:406
  1.9 4.5 %collective-permute-start = (bf16[64,1,16,128]{3,0,2,1:T(8,128)(2,1)S(1)}, bf16[64,1,16,128]{3,0,2,1:T(8,128)(2,1)S(1)}, u32[]{:S(2)}, u32[]{:S(2)}) collective-permute-start(bf16[64,1,16,128]{3,0,2,1:T(8,128)(2,1)S(1)} %copy.13), channel_id=1, source_target_pairs={{0,4},{4,8},{8,12},{12,16},{16,20},{20,24},{24,28},{1,5},{5,9},{9,... | collective-permute-start | bytes 786440 | tf_op jit(solution)/shard_map/ppermute | solution.py:405
  6.5 1.9 %collective-permute-start.1 = (bf16[64,1,16,128]{3,0,2,1:T(8,128)(2,1)S(1)}, bf16[64,1,16,128]{3,0,2,1:T(8,128)(2,1)S(1)}, u32[]{:S(2)}, u32[]{:S(2)}) collective-permute-start(bf16[64,1,16,128]{3,0,2,1:T(8,128)(2,1)S(1)} %copy.14), channel_id=1, source_target_pairs={{4,0},{8,4},{12,8},{16,12},{20,16},{24,20},{28,24},{5,1},{9,5},{13... | collective-permute-start | bytes 786440 | tf_op jit(solution)/shard_map/ppermute | solution.py:406
  8.6 1.1 %collective-permute-done = bf16[64,1,16,128]{3,0,2,1:T(8,128)(2,1)S(1)} collective-permute-done((bf16[64,1,16,128]{3,0,2,1:T(8,128)(2,1)S(1)}, bf16[64,1,16,128]{3,0,2,1:T(8,128)(2,1)S(1)}, u32[]{:S(2)}, u32[]{:S(2)}) %collective-permute-start) | collective-permute-done | bytes 262176 | tf_op jit(solution)/shard_map/ppermute | solution.py:405
  9.8 4.5 %collective-permute-done.1 = bf16[64,1,16,128]{3,0,2,1:T(8,128)(2,1)S(1)} collective-permute-done((bf16[64,1,16,128]{3,0,2,1:T(8,128)(2,1)S(1)}, bf16[64,1,16,128]{3,0,2,1:T(8,128)(2,1)S(1)}, u32[]{:S(2)}, u32[]{:S(2)}) %collective-permute-start.1) | collective-permute-done | bytes 262176 | tf_op jit(solution)/shard_map/ppermute | solution.py:406
  14.3 3.2 %collective-permute-start.2 = (bf16[4,64,128]{2,1,0:T(8,128)(2,1)S(1)}, bf16[4,64,128]{2,1,0:T(8,128)(2,1)S(1)}, u32[]{:S(2)}, u32[]{:S(2)}) collective-permute-start(bf16[4,64,128]{2,1,0:T(8,128)(2,1)S(1)} %maximum_bitcast_fusion), channel_id=1, source_target_pairs={{0,1},{1,2},{2,3},{4,5},{5,6},{6,7},{8,9},{9,10},{10,11},{12,13},{... | collective-permute-start | bytes 196616 | tf_op jit(solution)/shard_map/ppermute | solution.py:441
  17.5 1.3 %collective-permute-start.3 = (bf16[4,64,128]{2,1,0:T(8,128)(2,1)S(1)}, bf16[4,64,128]{2,1,0:T(8,128)(2,1)S(1)}, u32[]{:S(2)}, u32[]{:S(2)}) collective-permute-start(bf16[4,64,128]{2,1,0:T(8,128)(2,1)S(1)} %maximum_bitcast_fusion.1), channel_id=1, source_target_pairs={{1,0},{2,1},{3,2},{5,4},{6,5},{7,6},{9,8},{10,9},{11,10},{13,12},{... | collective-permute-start | bytes 196616 | tf_op jit(solution)/shard_map/ppermute | solution.py:442
  18.8 1.0 %copy-done.2 = bf16[4,4,4,32,64]{4,3,2,1,0:T(8,128)(2,1)S(1)} copy-done((bf16[4,4,4,32,64]{4,3,2,1,0:T(8,128)(2,1)S(1)}, bf16[4,4,4,32,64]{4,3,2,1,0:T(8,128)(2,1)}, u32[]{:S(2)}) %copy-start.2) | copy-done | bytes 262168
  19.9 3.2 %shard_map.58 = (bf16[2,64,2048]{2,1,0:T(8,128)(2,1)S(1)}, bf16[256,512]{1,0:T(8,128)(2,1)S(1)}, bf16[512,256]{1,0:T(8,128)(2,1)S(1)}, bf16[1,256,2048]{2,1,0:T(...) custom-call(bf16[64,2,16,128]{3,2,1,0:T(8,128)(2,1)S(1)} %copy-done.1, ...), custom_call_target="tpu_custom_call" | custom-call | tf_op jit(solution)/shard_map/pallas_call | solution.py:415
  23.4 0.6 copy-done.3
  24.1 0.6 copy-done.5
  24.7 0.8 %copy-done.4 = bf16[4,64,128]{2,1,0:T(8,128)(2,1)S(1)} copy-done((bf16[4,64,128]{2,1,0:T(8,128)(2,1)S(1)}, bf16[4,64,128]{2,1,0:T(8,128)(2,1)}, u32[]{:S(2)}) %copy-start.4) | copy-done | bytes 65560
  25.5 0.8 %copy-done.6 = bf16[4,64,128]{2,1,0:T(8,128)(2,1)S(1)} copy-done((bf16[4,64,128]{2,1,0:T(8,128)(2,1)S(1)}, bf16[4,64,128]{2,1,0:T(8,128)(2,1)}, u32[]{:S(2)}) %copy-start.6) | copy-done | bytes 65560
  26.4 7.5 %shard_map.59 = (bf16[8,32,2,16,128]{4,3,2,1,0:T(8,128)(2,1)}, f32[2,64,2048]{2,1,0:T(8,128)S(1)}, f32[16,32,128]{2,1,0:T(8,128)S(1)}, bf16[16,32,128]{2,1,0:T(8...) custom-call(s32[1]{0:T(128)} %bitcast.core, ...), custom_call_target="tpu_custom_call" | custom-call | tf_op jit(solution)/shard_map/pallas_call | solution.py:443
  33.9 0.7 copy-done.7
  34.6 0.7 copy-done.8
  35.3 1.6 %collective-permute-done.8 = bf16[16,32,128]{2,1,0:T(8,128)(2,1)S(1)} collective-permute-done((bf16[16,32,128]{2,1,0:T(8,128)(2,1)}, bf16[16,32,128]{2,1,0:T(8,128)(2,1)S(1)}, u32[]{:S(2)}, u32[]{:S(2)}) %collective-permute-start.8) | collective-permute-done | bytes 131104 | tf_op jit(solution)/shard_map/ppermute | solution.py:478
  36.9 2.2 %collective-permute-start.9 = (bf16[256,128]{1,0:T(8,128)(2,1)S(1)}, bf16[256,128]{1,0:T(8,128)(2,1)S(1)}, u32[]{:S(2)}, u32[]{:S(2)}) collective-permute-start(bf16[256,128]{1,0:T(8,128)(2,1)S(1)} %bitcast.55), channel_id=1, source_target_pairs={{0,8},{4,12},{8,0},{12,4},{16,24},{20,28},{24,16},{28,20},{1,9},{5... | collective-permute-start | bytes 196616 | tf_op jit(solution)/shard_map/ppermute | solution.py:478
  39.1 2.3 %collective-permute-done.9 = bf16[256,128]{1,0:T(8,128)(2,1)S(1)} collective-permute-done((bf16[256,128]{1,0:T(8,128)(2,1)S(1)}, bf16[256,128]{1,0:T(8,128)(2,1)S(1)}, u32[]{:S(2)}, u32[]{:S(2)}) %collective-permute-start.9) | collective-permute-done | bytes 65568 | tf_op jit(solution)/shard_map/ppermute | solution.py:478
  41.8 3.6 %collective-permute-start.4 = (bf16[1,64,2304]{2,1,0:T(8,128)(2,1)}, bf16[1,64,2304]{2,1,0:T(8,128)(2,1)S(1)}, u32[]{:S(2)}, u32[]{:S(2)}) collective-permute-start(bf16[1,64,2304]{2,1,0:T(8,128)(2,1)} %copy-done.8), channel_id=1, source_target_pairs={{0,4},{4,8},{8,12},{12,16},{16,20},{20,24},{24,28},{1,5},{5,9},{9,... | collective-permute-start | bytes 884744 | tf_op jit(solution)/shard_map/ppermute | solution.py:511
  45.5 1.9 %collective-permute-start.5 = (bf16[1,64,2304]{2,1,0:T(8,128)(2,1)}, bf16[1,64,2304]{2,1,0:T(8,128)(2,1)S(1)}, u32[]{:S(2)}, u32[]{:S(2)}) collective-permute-start(bf16[1,64,2304]{2,1,0:T(8,128)(2,1)} %copy-done.7), channel_id=1, source_target_pairs={{4,0},{8,4},{12,8},{16,12},{20,16},{24,20},{28,24},{5,1},{9,5},{13... | collective-permute-start | bytes 884744 | tf_op jit(solution)/shard_map/ppermute | solution.py:512
  47.5 2.1 %collective-permute-start.11 = (f32[128,128]{1,0:T(8,128)S(1)}, f32[128,128]{1,0:T(8,128)S(1)}, u32[]{:S(2)}, u32[]{:S(2)}) collective-permute-start(f32[128,128]{1,0:T(8,128)S(1)} %convert_add_fusion.1), channel_id=1, source_target_pairs={{0,1},{1,0},{2,3},{3,2},{4,5},{5,4},{6,7},{7,6},{8,9},{9,8},{10,11... | collective-permute-start | bytes 196616 | tf_op jit(solution)/shard_map/ppermute | solution.py:478
  49.6 1.7 %collective-permute-done.11 = f32[128,128]{1,0:T(8,128)S(1)} collective-permute-done((f32[128,128]{1,0:T(8,128)S(1)}, f32[128,128]{1,0:T(8,128)S(1)}, u32[]{:S(2)}, u32[]{:S(2)}) %collective-permute-start.11) | collective-permute-done | bytes 65568 | tf_op jit(solution)/shard_map/ppermute | solution.py:478
  51.3 2.5 %collective-permute-start.12 = (f32[128,128]{1,0:T(8,128)S(1)}, f32[128,128]{1,0:T(8,128)S(1)}, u32[]{:S(2)}, u32[]{:S(2)}) collective-permute-start(f32[128,128]{1,0:T(8,128)S(1)} %add.71), channel_id=1, source_target_pairs={{0,2},{1,3},{2,0},{3,1},{4,6},{5,7},{6,4},{7,5},{8,10},{9,11},{10,... | collective-permute-start | bytes 196616 | tf_op jit(solution)/shard_map/ppermute | solution.py:478
  53.8 0.6 collective-permute-done.5
  54.4 3.4 %collective-permute-done.12 = f32[128,128]{1,0:T(8,128)S(1)} collective-permute-done((f32[128,128]{1,0:T(8,128)S(1)}, f32[128,128]{1,0:T(8,128)S(1)}, u32[]{:S(2)}, u32[]{:S(2)}) %collective-permute-start.12) | collective-permute-done | bytes 65568 | tf_op jit(solution)/shard_map/ppermute | solution.py:478
  58.0 3.0 %collective-permute-start.6 = (bf16[2,64,128]{2,1,0:T(8,128)(2,1)S(1)}, bf16[2,64,128]{2,1,0:T(8,128)(2,1)S(1)}, u32[]{:S(2)}, u32[]{:S(2)}) collective-permute-start(bf16[2,64,128]{2,1,0:T(8,128)(2,1)S(1)} %get-tuple-element.43), channel_id=1, source_target_pairs={{0,1},{1,2},{2,3},{4,5},{5,6},{6,7},{8,9},{9,10},{10,11},{12,13},{... | collective-permute-start | bytes 98312 | tf_op jit(solution)/shard_map/ppermute | solution.py:525
  60.9 1.3 %collective-permute-start.7 = (bf16[2,64,128]{2,1,0:T(8,128)(2,1)S(1)}, bf16[2,64,128]{2,1,0:T(8,128)(2,1)S(1)}, u32[]{:S(2)}, u32[]{:S(2)}) collective-permute-start(bf16[2,64,128]{2,1,0:T(8,128)(2,1)S(1)} %get-tuple-element.44), channel_id=1, source_target_pairs={{1,0},{2,1},{3,2},{5,4},{6,5},{7,6},{9,8},{10,9},{11,10},{13,12},{... | collective-permute-start | bytes 98312 | tf_op jit(solution)/shard_map/ppermute | solution.py:526
  62.6 3.0 %collective-permute-done.7 = bf16[2,64,128]{2,1,0:T(8,128)(2,1)S(1)} collective-permute-done((bf16[2,64,128]{2,1,0:T(8,128)(2,1)S(1)}, bf16[2,64,128]{2,1,0:T(8,128)(2,1)S(1)}, u32[]{:S(2)}, u32[]{:S(2)}) %collective-permute-start.7) | collective-permute-done | bytes 32800 | tf_op jit(solution)/shard_map/ppermute | solution.py:526
  65.9 5.0 %collective-permute-start.15 = (bf16[16,32,128]{2,1,0:T(8,128)(2,1)S(1)}, bf16[16,32,128]{2,1,0:T(8,128)(2,1)S(1)}, u32[]{:S(2)}, u32[]{:S(2)}) collective-permute-start(bf16[16,32,128]{2,1,0:T(8,128)(2,1)S(1)} %bitcast.49), channel_id=1, source_target_pairs={{0,4},{4,0},{8,12},{12,8},{16,20},{20,16},{24,28},{28,24},{1,5},{5... | collective-permute-start | bytes 393224 | tf_op jit(solution)/shard_map/ppermute | solution.py:478
  70.9 0.8 %copy_bitcast_fusion = bf16[64,2,16,128]{3,2,1,0:T(8,128)(2,1)} fusion(bf16[2,64,16,128]{3,2,1,0:T(8,128)(2,1)S(1)} %bitcast.51), kind=kLoop, calls=%fused_computation.1 | loop fusion | bytes 1048576 | tf_op jit(solution)/shard_map/transpose | solution.py:533
  71.9 1.2 %shard_map.60 = f32[4,4,4,32,64]{4,3,2,1,0:T(8,128)} custom-call(s32[1]{0:T(128)} %bitcast.core, bf16[16,32,128]{2,1,0:T(8,128)(2,1)S(1)} %bitcast.50, bf16[16,32,128]{2,1,0:T(8,128)(2,1)S(1)} %collective-permute-done.15.other), custom_call_target="tpu_custom_call" | custom-call | tf_op jit(solution)/shard_map/pallas_call | solution.py:502
  (51 shorter events, 2.1 us)
Async XLA Ops:
  0.6 7.8 %copy-start.1 = (bf16[64,2,16,128]{3,2,1,0:T(8,128)(2,1)S(1)}, bf16[64,2,16,128]{3,2,1,0:T(8,128)(2,1)}, u32[]{:S(2)}) copy-start(bf16[64,2,16,128]{3,2,1,0:T(8,128)(2,1)} %vol.1) | copy-start | bytes 1572868
  0.6 18.2 %copy-start = (bf16[2,2,2,32,2,16,128]{6,5,4,3,2,1,0:T(8,128)(2,1)S(1)}, bf16[2,2,2,32,2,16,128]{6,5,4,3,2,1,0:T(8,128)(2,1)}, u32[]{:S(2)}) copy-start(bf16[2,2,2,32,2,16,128]{6,5,4,3,2,1,0:T(8,128)(2,1)} %param.5) | copy-start | bytes 6291460
  1.9 7.8 %collective-permute-start = (bf16[64,1,16,128]{3,0,2,1:T(8,128)(2,1)S(1)}, bf16[64,1,16,128]{3,0,2,1:T(8,128)(2,1)S(1)}, u32[]{:S(2)}, u32[]{:S(2)}) collective-permute-start(bf16[64,1,16,128]{3,0,2,1:T(8,128)(2,1)S(1)} %copy.13), channel_id=1, source_target_pairs={{0,4},{4,8},{8,12},{12,16},{16,20},{20,24},{24,28},{1,5},{5,9},{9,... | collective-permute-start | bytes 786440 | tf_op jit(solution)/shard_map/ppermute | solution.py:405
  6.5 7.7 %collective-permute-start.1 = (bf16[64,1,16,128]{3,0,2,1:T(8,128)(2,1)S(1)}, bf16[64,1,16,128]{3,0,2,1:T(8,128)(2,1)S(1)}, u32[]{:S(2)}, u32[]{:S(2)}) collective-permute-start(bf16[64,1,16,128]{3,0,2,1:T(8,128)(2,1)S(1)} %copy.14), channel_id=1, source_target_pairs={{4,0},{8,4},{12,8},{16,12},{20,16},{24,20},{28,24},{5,1},{9,5},{13... | collective-permute-start | bytes 786440 | tf_op jit(solution)/shard_map/ppermute | solution.py:406
  14.3 9.2 %collective-permute-start.2 = (bf16[4,64,128]{2,1,0:T(8,128)(2,1)S(1)}, bf16[4,64,128]{2,1,0:T(8,128)(2,1)S(1)}, u32[]{:S(2)}, u32[]{:S(2)}) collective-permute-start(bf16[4,64,128]{2,1,0:T(8,128)(2,1)S(1)} %maximum_bitcast_fusion), channel_id=1, source_target_pairs={{0,1},{1,2},{2,3},{4,5},{5,6},{6,7},{8,9},{9,10},{10,11},{12,13},{... | collective-permute-start | bytes 196616 | tf_op jit(solution)/shard_map/ppermute | solution.py:441
  17.5 6.6 %collective-permute-start.3 = (bf16[4,64,128]{2,1,0:T(8,128)(2,1)S(1)}, bf16[4,64,128]{2,1,0:T(8,128)(2,1)S(1)}, u32[]{:S(2)}, u32[]{:S(2)}) collective-permute-start(bf16[4,64,128]{2,1,0:T(8,128)(2,1)S(1)} %maximum_bitcast_fusion.1), channel_id=1, source_target_pairs={{1,0},{2,1},{3,2},{5,4},{6,5},{7,6},{9,8},{10,9},{11,10},{13,12},{... | collective-permute-start | bytes 196616 | tf_op jit(solution)/shard_map/ppermute | solution.py:442
  18.8 1.0 %copy-start.2 = (bf16[4,4,4,32,64]{4,3,2,1,0:T(8,128)(2,1)S(1)}, bf16[4,4,4,32,64]{4,3,2,1,0:T(8,128)(2,1)}, u32[]{:S(2)}) copy-start(bf16[4,4,4,32,64]{4,3,2,1,0:T(8,128)(2,1)} %taps.1) | copy-start | bytes 786436
  23.4 0.6 copy-start.3
  24.1 0.6 copy-start.5
  24.7 0.8 %copy-start.4 = (bf16[4,64,128]{2,1,0:T(8,128)(2,1)S(1)}, bf16[4,64,128]{2,1,0:T(8,128)(2,1)}, u32[]{:S(2)}) copy-start(bf16[4,64,128]{2,1,0:T(8,128)(2,1)} %copy-done.3) | copy-start | bytes 196612
  25.5 0.8 %copy-start.6 = (bf16[4,64,128]{2,1,0:T(8,128)(2,1)S(1)}, bf16[4,64,128]{2,1,0:T(8,128)(2,1)}, u32[]{:S(2)}) copy-start(bf16[4,64,128]{2,1,0:T(8,128)(2,1)} %copy-done.5) | copy-start | bytes 196612
  33.9 0.7 copy-start.7
  34.6 0.7 copy-start.8
  35.3 1.6 %collective-permute-start.8 = (bf16[16,32,128]{2,1,0:T(8,128)(2,1)}, bf16[16,32,128]{2,1,0:T(8,128)(2,1)S(1)}, u32[]{:S(2)}, u32[]{:S(2)}) collective-permute-start(bf16[16,32,128]{2,1,0:T(8,128)(2,1)} %get-tuple-element.30), channel_id=1, source_target_pairs={{0,4},{4,0},{8,12},{12,8},{16,20},{20,16},{24,28},{28,24},{1,5},{5... | collective-permute-start | bytes 393224 | tf_op jit(solution)/shard_map/ppermute | solution.py:478
  36.9 4.5 %collective-permute-start.9 = (bf16[256,128]{1,0:T(8,128)(2,1)S(1)}, bf16[256,128]{1,0:T(8,128)(2,1)S(1)}, u32[]{:S(2)}, u32[]{:S(2)}) collective-permute-start(bf16[256,128]{1,0:T(8,128)(2,1)S(1)} %bitcast.55), channel_id=1, source_target_pairs={{0,8},{4,12},{8,0},{12,4},{16,24},{20,28},{24,16},{28,20},{1,9},{5... | collective-permute-start | bytes 196616 | tf_op jit(solution)/shard_map/ppermute | solution.py:478
  41.4 6.0 %collective-permute-start.10 = (bf16[128,128]{1,0:T(8,128)(2,1)S(1)}, bf16[128,128]{1,0:T(8,128)(2,1)S(1)}, u32[]{:S(2)}, u32[]{:S(2)}) collective-permute-start(bf16[128,128]{1,0:T(8,128)(2,1)S(1)} %select_convert_fusion.1), channel_id=1, source_target_pairs={{0,16},{4,20},{8,24},{12,28},{16,0},{20,4},{24,8},{28,12},{1,17},{... | collective-permute-start | bytes 98312 | tf_op jit(solution)/shard_map/ppermute | solution.py:478
  41.8 12.0 %collective-permute-start.4 = (bf16[1,64,2304]{2,1,0:T(8,128)(2,1)}, bf16[1,64,2304]{2,1,0:T(8,128)(2,1)S(1)}, u32[]{:S(2)}, u32[]{:S(2)}) collective-permute-start(bf16[1,64,2304]{2,1,0:T(8,128)(2,1)} %copy-done.8), channel_id=1, source_target_pairs={{0,4},{4,8},{8,12},{12,16},{16,20},{20,24},{24,28},{1,5},{5,9},{9,... | collective-permute-start | bytes 884744 | tf_op jit(solution)/shard_map/ppermute | solution.py:511
  45.5 8.9 %collective-permute-start.5 = (bf16[1,64,2304]{2,1,0:T(8,128)(2,1)}, bf16[1,64,2304]{2,1,0:T(8,128)(2,1)S(1)}, u32[]{:S(2)}, u32[]{:S(2)}) collective-permute-start(bf16[1,64,2304]{2,1,0:T(8,128)(2,1)} %copy-done.7), channel_id=1, source_target_pairs={{4,0},{8,4},{12,8},{16,12},{20,16},{24,20},{28,24},{5,1},{9,5},{13... | collective-permute-start | bytes 884744 | tf_op jit(solution)/shard_map/ppermute | solution.py:512
  47.5 3.8 %collective-permute-start.11 = (f32[128,128]{1,0:T(8,128)S(1)}, f32[128,128]{1,0:T(8,128)S(1)}, u32[]{:S(2)}, u32[]{:S(2)}) collective-permute-start(f32[128,128]{1,0:T(8,128)S(1)} %convert_add_fusion.1), channel_id=1, source_target_pairs={{0,1},{1,0},{2,3},{3,2},{4,5},{5,4},{6,7},{7,6},{8,9},{9,8},{10,11... | collective-permute-start | bytes 196616 | tf_op jit(solution)/shard_map/ppermute | solution.py:478
  51.3 6.6 %collective-permute-start.12 = (f32[128,128]{1,0:T(8,128)S(1)}, f32[128,128]{1,0:T(8,128)S(1)}, u32[]{:S(2)}, u32[]{:S(2)}) collective-permute-start(f32[128,128]{1,0:T(8,128)S(1)} %add.71), channel_id=1, source_target_pairs={{0,2},{1,3},{2,0},{3,1},{4,6},{5,7},{6,4},{7,5},{8,10},{9,11},{10,... | collective-permute-start | bytes 196616 | tf_op jit(solution)/shard_map/ppermute | solution.py:478
  57.9 4.5 %collective-permute-start.13 = (bf16[128,128]{1,0:T(8,128)(2,1)S(1)}, bf16[128,128]{1,0:T(8,128)(2,1)S(1)}, u32[]{:S(2)}, u32[]{:S(2)}) collective-permute-start(bf16[128,128]{1,0:T(8,128)(2,1)S(1)} %multiply_convert_fusion), channel_id=1, source_target_pairs={{0,16},{4,20},{8,24},{12,28},{16,0},{20,4},{24,8},{28,12},{1,17},{... | collective-permute-start | bytes 98312 | tf_op jit(solution)/shard_map/ppermute | solution.py:478
  58.0 4.6 %collective-permute-start.6 = (bf16[2,64,128]{2,1,0:T(8,128)(2,1)S(1)}, bf16[2,64,128]{2,1,0:T(8,128)(2,1)S(1)}, u32[]{:S(2)}, u32[]{:S(2)}) collective-permute-start(bf16[2,64,128]{2,1,0:T(8,128)(2,1)S(1)} %get-tuple-element.43), channel_id=1, source_target_pairs={{0,1},{1,2},{2,3},{4,5},{5,6},{6,7},{8,9},{9,10},{10,11},{12,13},{... | collective-permute-start | bytes 98312 | tf_op jit(solution)/shard_map/ppermute | solution.py:525
  60.9 4.7 %collective-permute-start.7 = (bf16[2,64,128]{2,1,0:T(8,128)(2,1)S(1)}, bf16[2,64,128]{2,1,0:T(8,128)(2,1)S(1)}, u32[]{:S(2)}, u32[]{:S(2)}) collective-permute-start(bf16[2,64,128]{2,1,0:T(8,128)(2,1)S(1)} %get-tuple-element.44), channel_id=1, source_target_pairs={{1,0},{2,1},{3,2},{5,4},{6,5},{7,6},{9,8},{10,9},{11,10},{13,12},{... | collective-permute-start | bytes 98312 | tf_op jit(solution)/shard_map/ppermute | solution.py:526
  62.4 3.5 %collective-permute-start.14 = (bf16[256,128]{1,0:T(8,128)(2,1)S(1)}, bf16[256,128]{1,0:T(8,128)(2,1)S(1)}, u32[]{:S(2)}, u32[]{:S(2)}) collective-permute-start(bf16[256,128]{1,0:T(8,128)(2,1)S(1)} %maximum_select_fusion.1), channel_id=1, source_target_pairs={{0,8},{4,12},{8,0},{12,4},{16,24},{20,28},{24,16},{28,20},{1,9},{5... | collective-permute-start | bytes 196616 | tf_op jit(solution)/shard_map/ppermute | solution.py:478
  65.9 6.0 %collective-permute-start.15 = (bf16[16,32,128]{2,1,0:T(8,128)(2,1)S(1)}, bf16[16,32,128]{2,1,0:T(8,128)(2,1)S(1)}, u32[]{:S(2)}, u32[]{:S(2)}) collective-permute-start(bf16[16,32,128]{2,1,0:T(8,128)(2,1)S(1)} %bitcast.49), channel_id=1, source_target_pairs={{0,4},{4,0},{8,12},{12,8},{16,20},{20,16},{24,28},{28,24},{1,5},{5... | collective-permute-start | bytes 393224 | tf_op jit(solution)/shard_map/ppermute | solution.py:478

commit v5 on v4

--- a/solution.py
+++ b/solution.py
@@ -201,12 +201,11 @@
 def outer_kernel(
     dims,
     chunk,
-    core,
     flat,
-    xlo,
-    xhi,
-    ylo,
-    yhi,
+    xlo_in,
+    xhi_in,
+    ylo_in,
+    yhi_in,
     w,
     wt,
     cot,
@@ -216,14 +215,15 @@
     ig_in,
     act_out,
     own_out,
-    keep,
-    send,
+    up_out,
+    down_out,
+    wg,
     yface,
-    up,
-    down,
-    full,
+    sides,
     faces,
     own,
+    xraw,
+    yraw,
     xs,
     vm,
     ga,
@@ -238,16 +238,15 @@
     half = 4 * ci
     to_y = swap_matrix(GROUP, ny)
     to_c = swap_matrix(ny, GROUP)
-
-    for side, plane in enumerate((xlo, xhi)):
-
-        def put(k, y, rows, side=side):
-            xs[side, k * GROUP : (k + 1) * GROUP, y * nz : (y + 1) * nz] = rows
-
-        tiles = Tiles(
-            ci // GROUP, lambda k, plane=plane: plane[k * GROUP : (k + 1) * GROUP, 0]
-        )
-        bring_plane(to_y, tiles, ny, nz, put)
+    spots = 8 * nx
+    arriving = [
+        pltpu.make_async_copy(xlo_in, xraw.at[0], sems.at[spots]),
+        pltpu.make_async_copy(xhi_in, xraw.at[1], sems.at[spots + 1]),
+        pltpu.make_async_copy(ylo_in, yraw.at[0], sems.at[spots + 2]),
+        pltpu.make_async_copy(yhi_in, yraw.at[1], sems.at[spots + 3]),
+    ]
+    for copy in arriving:
+        copy.start()
 
     for side in range(2):
         for q in range(4 * side, 4 * side + 4):
@@ -264,11 +263,23 @@
             )
             bring_plane(to_y, tiles, ny, nz, put)
 
+    for copy in arriving:
+        copy.wait()
+    for side in range(2):
+
+        def put(k, y, rows, side=side):
+            xs[side, k * GROUP : (k + 1) * GROUP, y * nz : (y + 1) * nz] = rows
+
+        tiles = Tiles(
+            ci // GROUP, lambda k, side=side: xraw[side, k * GROUP : (k + 1) * GROUP, 0]
+        )
+        bring_plane(to_y, tiles, ny, nz, put)
+
     def block(x, y):
         if y == 0:
-            return ylo[x]
+            return yraw[0, x]
         if y == ny + 1:
-            return yhi[x]
+            return yraw[1, x]
         lanes = slice((y - 1) * nz, y * nz)
         if x == 0:
             return xs[0, :, lanes]
@@ -307,9 +318,9 @@
             for row in range(8):
                 tx, ty, tz = row // 4, row // 2 % 2, row % 2
                 index = ((tx * 2 + ty) * 2 + part) * 2 + tz
-                full[ex, index] = total[
+                wg[ex * 16 + index] = total[
                     row * co : (row + 1) * co, ex * 2 * ci : (ex + 1) * 2 * ci
-                ]
+                ].astype(BF16)
 
     def ig_add(m, y, value, fresh):
         if m < 0 or m >= nx:
@@ -333,13 +344,14 @@
             if (m, y) not in started:
                 lanes = slice(y * nz, (y + 1) * nz)
                 own[m, :, lanes] = ig_in[m, :, lanes]
-    c = core[0]
-    keep[...] = full[c]
-    send[...] = full[1 - c].astype(BF16)
-    down[0] = faces[0].astype(BF16)
-    up[0] = faces[1].astype(BF16)
-    copies = [pltpu.make_async_copy(own, own_out, sems.at[8 * nx])]
-    copies[0].start()
+    sides[...] = faces[...].astype(BF16)
+    copies = [
+        pltpu.make_async_copy(own, own_out, sems.at[spots]),
+        pltpu.make_async_copy(sides.at[0], down_out, sems.at[spots + 1]),
+        pltpu.make_async_copy(sides.at[1], up_out, sems.at[spots + 2]),
+    ]
+    for copy in copies:
+        copy.start()
 
     for m in range(nx):
         for q in range(8):
@@ -369,17 +381,14 @@
         copy.wait()
 
 
-def unpack_kernel(co, ci, core, mine, other, out, full):
-    c = core[0]
-    full[c] = mine[...].astype(F32)
-    full[1 - c] = other[...].astype(F32)
+def unpack_kernel(co, ci, packed, out):
     for ex in range(2):
         for tx in range(2):
             for ty in range(2):
                 for ez in range(2):
                     for tz in range(2):
-                        index = ((tx * 2 + ty) * 2 + ez) * 2 + tz
-                        pair = full[ex, index]
+                        index = (((ex * 2 + tx) * 2 + ty) * 2 + ez) * 2 + tz
+                        pair = packed[index].astype(F32)
                         for ey in range(2):
                             out[2 * ex + tx, 2 * ey + ty, 2 * ez + tz] = pair[
                                 :, ey * ci : (ey + 1) * ci
@@ -400,7 +409,6 @@
     gy_up, gy_down = neighbours("gy")
     cells = nx * gx * ny * gy * nz
     dims = (nx, ny, nz, ci, co)
-    core = (lax.axis_index("gx") % 2).astype(jnp.int32).reshape(1)
 
     xlo = lax.ppermute(volume[:, nx - 1 :], "gx", gx_up)
     xhi = lax.ppermute(volume[:, :1], "gx", gx_down)
@@ -435,28 +443,35 @@
     )(volume, kernel, cot)
 
     def y_row(y):
-        rows = jnp.concatenate([xlo[:, :, y], volume[:, :, y], xhi[:, :, y]], axis=1)
-        return rows.transpose(1, 0, 2)
+        return jnp.concatenate(
+            [
+                xlo[:, :, y].transpose(1, 0, 2),
+                flat[:, :, y * nz : (y + 1) * nz],
+                xhi[:, :, y].transpose(1, 0, 2),
+            ],
+            axis=0,
+        )
 
     ylo = lax.ppermute(y_row(ny - 1), "gy", gy_up)
     yhi = lax.ppermute(y_row(0), "gy", gy_down)
-    act, own, keep, send, yface, up, down = pl.pallas_call(
+    act, own, up, down, wg, yface = pl.pallas_call(
         functools.partial(outer_kernel, dims, 4),
         out_shape=(
             jax.ShapeDtypeStruct(cot.shape, BF16),
             jax.ShapeDtypeStruct((nx, ci, ny * nz), F32),
-            jax.ShapeDtypeStruct((16, co, 2 * ci), F32),
-            jax.ShapeDtypeStruct((16, co, 2 * ci), BF16),
+            jax.ShapeDtypeStruct((ci, (ny + 2) * nz), BF16),
+            jax.ShapeDtypeStruct((ci, (ny + 2) * nz), BF16),
+            jax.ShapeDtypeStruct((32, co, 2 * ci), BF16),
             jax.ShapeDtypeStruct((2, nx, ci, nz), F32),
-            jax.ShapeDtypeStruct((1, ci, (ny + 2) * nz), BF16),
-            jax.ShapeDtypeStruct((1, ci, (ny + 2) * nz), BF16),
         ),
-        in_specs=[smem] + [vmem] * 12,
-        out_specs=(anywhere, anywhere) + (vmem,) * 5,
+        in_specs=[vmem] + [anywhere] * 4 + [vmem] * 7,
+        out_specs=(anywhere,) * 4 + (vmem,) * 2,
         scratch_shapes=[
-            pltpu.VMEM((2, 16, co, 2 * ci), F32),
+            pltpu.VMEM((2, ci, (ny + 2) * nz), BF16),
             pltpu.VMEM((2, ci, (ny + 2) * nz), F32),
             pltpu.VMEM((nx, ci, ny * nz), F32),
+            pltpu.VMEM((2, ci, 1, ny, nz), BF16),
+            pltpu.VMEM((2, nx + 2, ci, nz), BF16),
             pltpu.VMEM((2, ci, ny * nz), BF16),
             pltpu.VMEM((nx + 2, ci, (ny + 2) * nz), BF16),
             pltpu.VMEM((8 * co, n_out * nz), BF16),
@@ -465,51 +480,28 @@
             pltpu.VMEM((8 * co, ny * nz), BF16),
             pltpu.VMEM((nx - 1, 8 * co, nz), BF16),
             pltpu.VMEM((8 * nx, co, ny, nz), BF16),
-            pltpu.SemaphoreType.DMA((8 * nx + 1,)),
+            pltpu.SemaphoreType.DMA((8 * nx + 4,)),
         ],
         compiler_params=params,
-    )(core, flat, xlo, xhi, ylo, yhi, w, wt, cot, vals, cot_edge, wg_part, ig_part)
+    )(flat, xlo, xhi, ylo, yhi, w, wt, cot, vals, cot_edge, wg_part, ig_part)
 
     scale = 1.0 / math.sqrt(cells)
-    place = lax.axis_index("gx")
-    bits = [1 << b for b in range(1, gx.bit_length() - 1)]
-
-    def trade(array, axis, count, distance):
-        return lax.ppermute(array, axis, [(k, k ^ distance) for k in range(count)])
-
-    part = (keep + trade(send, "gx", gx, 1).astype(F32)).reshape(16 * co, 2 * ci)
-    for bit in bits:
-        upper = (place & bit) != 0
-        rows = part.shape[0] // 2
-        kept = jnp.where(upper, part[rows:], part[:rows])
-        sent = jnp.where(upper, part[:rows], part[rows:]).astype(BF16)
-        part = kept + trade(sent, "gx", gx, bit).astype(F32)
-    distance = 1
-    while distance < gy:
-        part = part + trade(part, "gy", gy, distance)
-        distance *= 2
-    total = (part * scale).astype(BF16)
-    for bit in reversed(bits):
-        upper = (place & bit) != 0
-        others = trade(total, "gx", gx, bit)
-        total = jnp.where(
-            upper,
-            jnp.concatenate([others, total], axis=0),
-            jnp.concatenate([total, others], axis=0),
-        )
-    mine = total.reshape(16, co, 2 * ci)
-    other = trade(mine, "gx", gx, 1)
+    devices = gx * gy
+    shares = wg.reshape(devices, 32 * co // devices, 2 * ci)
+    shares = lax.all_to_all(shares, ("gx", "gy"), 0, 0, tiled=True)
+    piece = (jnp.sum(shares.astype(F32), axis=0) * scale).astype(BF16)
+    pieces = jnp.broadcast_to(piece[None], (devices,) + piece.shape)
+    pieces = lax.all_to_all(pieces, ("gx", "gy"), 0, 0, tiled=True)
     weight_grad = pl.pallas_call(
         functools.partial(unpack_kernel, co, ci),
         out_shape=jax.ShapeDtypeStruct((4, 4, 4, co, ci), F32),
-        in_specs=[smem, vmem, vmem],
+        in_specs=[vmem],
         out_specs=vmem,
-        scratch_shapes=[pltpu.VMEM((2, 16, co, 2 * ci), F32)],
         compiler_params=pltpu.CompilerParams(vmem_limit_bytes=8 * 1024 * 1024),
-    )(core, mine, other)
-
-    from_low = lax.ppermute(up, "gx", gx_up).astype(F32)
-    from_high = lax.ppermute(down, "gx", gx_down).astype(F32)
+    )(pieces.reshape(32, co, 2 * ci))
+
+    from_low = lax.ppermute(up, "gx", gx_up).astype(F32)[None]
+    from_high = lax.ppermute(down, "gx", gx_down).astype(F32)[None]
 
     def add_x(array, lanes):
         lead = (nx - 1,) + from_low[:, :, lanes].shape[1:]

time: 74 us -> 72.4 us (0.978)
  local copies, waits for them, and re-layouts: 8.27 us -> 5.58 us
  waiting for transfers between devices: 18.3 us -> 20.1 us
    ppermute x10 -> x2, starting transfers between devices: 18.1 us -> 7.45 us  [the longest x1 5.28 us: on_device(): from_low = lax.ppermute(up, 'gx', gx_up).astype(F32)[None]]
    all_to_all x0 -> x2, starting transfers between devices: none -> 9.44 us  [the longest x1 5.41 us: on_device(): pieces = lax.all_to_all(pieces, ('gx', 'gy'), 0, 0, tiled=True)]
    all_to_all x0 -> x2, waiting for transfers between devices: none -> 9.25 us  [the longest x1 9.24 us: on_device(): pieces = lax.all_to_all(pieces, ('gx', 'gy'), 0, 0, tiled=True)]
    ppermute x1, waiting for transfers between devices: 4.47 us -> 0.43 us  [on_device(): xhi = lax.ppermute(volume[:, :1], 'gx', gx_down)]
    ppermute x1, waiting for transfers between devices: 0.01 us -> 3.34 us  [on_device(): yhi = lax.ppermute(y_row(0), 'gy', gy_down)]
    unnamed x23 -> x9, local copies, waits for them, and re-layouts: 5.67 us -> 2.34 us
    ppermute x1, waiting for transfers between devices: 3.04 us -> 0.01 us  [on_device(): y_high = lax.ppermute(send_low, 'gy', gy_down).astype(F32)]
    ppermute x10 -> x2, waiting for transfers between devices: 9.69 us -> 7.07 us  [the longest x1 7.07 us: on_device(): from_high = lax.ppermute(down, 'gx', gx_down).astype(F32)[None]]
  transfers between devices with their start and end apart: 16 -> 10, of which waited for: 9 -> 4; matrix products, arithmetic and copies ran while one was open for 2% -> 3% of each run, Pallas kernels for 4% -> 4%
where the time goes in v5:
time: 72.4 us; the launch traced here: 71.9 us
  starting transfers between devices  32.6 us (45%)
  waiting for transfers between devices  20.1 us (28%)
  Pallas kernels  12.4 us (17%)
  local copies, waits for them, and re-layouts  5.58 us (8%)
  between operations  0.93 us (1%)
    all_to_all x1, waiting for transfers between devices, on_device(): pieces = lax.all_to_all(pieces, ('gx', 'gy'), 0, 0, tiled=True)  9.24 us
    pallas_call x1, Pallas kernels, on_device(): pl.pallas_call(functools.partial(outer_kernel, dims, 4), out_shape=(jax.S...  8.06 us
    ppermute x1, waiting for transfers between devices, on_device(): from_high = lax.ppermute(down, 'gx', gx_down).astype(F32)[None]  7.07 us
    all_to_all x1, starting transfers between devices, on_device(): pieces = lax.all_to_all(pieces, ('gx', 'gy'), 0, 0, tiled=True)  5.41 us
    ppermute x1, starting transfers between devices, on_device(): from_low = lax.ppermute(up, 'gx', gx_up).astype(F32)[None]  5.28 us
    ppermute x1, starting transfers between devices, on_device(): xlo = lax.ppermute(volume[:, nx - 1:], 'gx', gx_up)  4.51 us
    all_to_all x1, starting transfers between devices, on_device(): shares = lax.all_to_all(shares, ('gx', 'gy'), 0, 0, tiled=True)  4.03 us
    ppermute x1, starting transfers between devices, on_device(): y_low = lax.ppermute(send_high, 'gy', gy_up).astype(F32)  3.49 us
  transfers between devices with their start and end apart: 10, of which 4 were waited for; matrix products, arithmetic and copies ran while one was open for 3% of the time, Pallas kernels for 4%

profile of v5, /device:TPU:1, one launch (start us, length us, event | category | flops | bytes accessed | tf_op | source)
XLA Modules:
  0.0 71.9 jit_solution(11810756440040041093)
XLA Ops:
  0.6 1.2 %fusion.7 = (bf16[64,1,16,128]{3,2,1,0:T(8,128)(2,1)S(1)}, bf16[64,1,16,128]{3,2,1,0:T(8,128)(2,1)S(1)}) fusion(bf16[64,2,16,128]{3,2,1,0:T(8,128)(2,1)} %vol.1), kind=kLoop, calls=%fused_computation.21 | loop fusion | bytes 1048576 | tf_op jit(solution)/shard_map/slice | solution.py:414
  1.9 0.1 copy.11
  1.9 4.5 %collective-permute-start = (bf16[64,1,16,128]{3,0,2,1:T(8,128)(2,1)S(1)}, bf16[64,1,16,128]{3,0,2,1:T(8,128)(2,1)S(1)}, u32[]{:S(2)}, u32[]{:S(2)}) collective-permute-start(bf16[64,1,16,128]{3,0,2,1:T(8,128)(2,1)S(1)} %copy.11), channel_id=1, source_target_pairs={{0,4},{4,8},{8,12},{12,16},{16,20},{20,24},{24,28},{1,5},{5,9},{9,... | collective-permute-start | bytes 786440 | tf_op jit(solution)/shard_map/ppermute | solution.py:413
  6.5 0.1 copy.12
  6.5 1.9 %collective-permute-start.1 = (bf16[64,1,16,128]{3,0,2,1:T(8,128)(2,1)S(1)}, bf16[64,1,16,128]{3,0,2,1:T(8,128)(2,1)S(1)}, u32[]{:S(2)}, u32[]{:S(2)}) collective-permute-start(bf16[64,1,16,128]{3,0,2,1:T(8,128)(2,1)S(1)} %copy.12), channel_id=1, source_target_pairs={{4,0},{8,4},{12,8},{16,12},{20,16},{24,20},{28,24},{5,1},{9,5},{13... | collective-permute-start | bytes 786440 | tf_op jit(solution)/shard_map/ppermute | solution.py:414
  8.5 0.0 copy-start.1
  8.5 1.0 %copy-done.1 = bf16[64,2,16,128]{3,2,1,0:T(8,128)(2,1)S(1)} copy-done((bf16[64,2,16,128]{3,2,1,0:T(8,128)(2,1)S(1)}, bf16[64,2,16,128]{3,2,1,0:T(8,128)(2,1)}, u32[]{:S(2)}) %copy-start.1) | copy-done | bytes 524312
  9.5 1.0 %copy-done.2 = bf16[4,4,4,32,64]{4,3,2,1,0:T(8,128)(2,1)S(1)} copy-done((bf16[4,4,4,32,64]{4,3,2,1,0:T(8,128)(2,1)S(1)}, bf16[4,4,4,32,64]{4,3,2,1,0:T(8,128)(2,1)}, u32[]{:S(2)}) %copy-start.2) | copy-done | bytes 262168
  10.6 3.2 %shard_map.58 = (bf16[2,64,2048]{2,1,0:T(8,128)(2,1)S(1)}, bf16[256,512]{1,0:T(8,128)(2,1)S(1)}, bf16[512,256]{1,0:T(8,128)(2,1)S(1)}, bf16[1,256,2048]{2,1,0:T(...) custom-call(bf16[64,2,16,128]{3,2,1,0:T(8,128)(2,1)S(1)} %copy-done.1, ...), custom_call_target="tpu_custom_call" | custom-call | tf_op jit(solution)/shard_map/pallas_call | solution.py:423
  13.8 0.0 collective-permute-done
  13.8 0.4 collective-permute-done.1
  14.2 3.2 %collective-permute-start.2 = (bf16[4,64,128]{2,1,0:T(8,128)(2,1)S(1)}, bf16[4,64,128]{2,1,0:T(8,128)(2,1)S(1)}, u32[]{:S(2)}, u32[]{:S(2)}) collective-permute-start(bf16[4,64,128]{2,1,0:T(8,128)(2,1)S(1)} %pad_maximum_fusion), channel_id=1, source_target_pairs={{0,1},{1,2},{2,3},{4,5},{5,6},{6,7},{8,9},{9,10},{10,11},{12,13},{... | collective-permute-start | bytes 196616 | tf_op jit(solution)/shard_map/ppermute | solution.py:455
  17.5 1.3 %collective-permute-start.3 = (bf16[4,64,128]{2,1,0:T(8,128)(2,1)S(1)}, bf16[4,64,128]{2,1,0:T(8,128)(2,1)S(1)}, u32[]{:S(2)}, u32[]{:S(2)}) collective-permute-start(bf16[4,64,128]{2,1,0:T(8,128)(2,1)S(1)} %pad_maximum_fusion.1), channel_id=1, source_target_pairs={{1,0},{2,1},{3,2},{5,4},{6,5},{7,6},{9,8},{10,9},{11,10},{13,12},{... | collective-permute-start | bytes 196616 | tf_op jit(solution)/shard_map/ppermute | solution.py:456
  18.8 0.2 copy.8.xlo_in
  19.0 0.2 copy.9.xhi_in
  19.1 0.0 collective-permute-done.2.ylo_in
  19.1 3.3 %collective-permute-done.3.yhi_in = bf16[4,64,128]{2,1,0:T(8,128)(2,1)S(1)} collective-permute-done((bf16[4,64,128]{2,1,0:T(8,128)(2,1)S(1)}, bf16[4,64,128]{2,1,0:T(8,128)(2,1)S(1)}, u32[]{:S(2)}, u32[]{:S(2)}) %collective-permute-start.3) | collective-permute-done | bytes 65568 | tf_op jit(solution)/shard_map/ppermute | solution.py:456
  22.5 8.1 %shard_map.59 = (bf16[8,32,2,16,128]{4,3,2,1,0:T(8,128)(2,1)}, f32[2,64,2048]{2,1,0:T(8,128)S(1)}, bf16[64,2304]{1,0:T(8,128)(2,1)S(1)}, bf16[64,2304]{1,0:T(8,1...) custom-call(bf16[2,64,2048]{2,1,0:T(8,128)(2,1)S(1)} %get-tuple-element.16.flat, ...), custom_call_target="tpu_custom_call" | custom-call | tf_op jit(solution)/shard_map/pallas_call | solution.py:457
  30.5 5.3 %collective-permute-start.4 = (bf16[64,2304]{1,0:T(8,128)(2,1)S(1)}, bf16[64,2304]{1,0:T(8,128)(2,1)S(1)}, u32[]{:S(2)}, u32[]{:S(2)}) collective-permute-start(bf16[64,2304]{1,0:T(8,128)(2,1)S(1)} %get-tuple-element.25), channel_id=1, source_target_pairs={{0,4},{4,8},{8,12},{12,16},{16,20},{20,24},{24,28},{1,5},{5,9},{9,... | collective-permute-start | bytes 884744 | tf_op jit(solution)/shard_map/ppermute | solution.py:503
  35.8 4.0 %all-to-all-start = ((bf16[32,32,128]{2,1,0:T(8,128)(2,1)}), bf16[32,32,128]{2,1,0:T(8,128)(2,1)S(1)}, u32[]{:S(2)}, u32[]{:S(2)}) async-start(bf16[32,32,128]{2,1,0:T(8,128)(2,1)} %get-tuple-element.28), calls=%async_computation | async-start | bytes 524288 | tf_op jit(solution)/shard_map/all_to_all | solution.py:491
  39.9 2.2 %collective-permute-start.5 = (bf16[64,2304]{1,0:T(8,128)(2,1)S(1)}, bf16[64,2304]{1,0:T(8,128)(2,1)S(1)}, u32[]{:S(2)}, u32[]{:S(2)}) collective-permute-start(bf16[64,2304]{1,0:T(8,128)(2,1)S(1)} %get-tuple-element.26), channel_id=1, source_target_pairs={{4,0},{8,4},{12,8},{16,12},{20,16},{24,20},{28,24},{5,1},{9,5},{13... | collective-permute-start | bytes 884744 | tf_op jit(solution)/shard_map/ppermute | solution.py:504
  42.1 7.1 %collective-permute-done.5 = bf16[64,2304]{1,0:T(8,128)(2,1)S(1)} collective-permute-done((bf16[64,2304]{1,0:T(8,128)(2,1)S(1)}, bf16[64,2304]{1,0:T(8,128)(2,1)S(1)}, u32[]{:S(2)}, u32[]{:S(2)}) %collective-permute-start.5) | collective-permute-done | bytes 294944 | tf_op jit(solution)/shard_map/ppermute | solution.py:504
  49.4 3.5 %collective-permute-start.6 = (bf16[2,64,128]{2,1,0:T(8,128)(2,1)S(1)}, bf16[2,64,128]{2,1,0:T(8,128)(2,1)S(1)}, u32[]{:S(2)}, u32[]{:S(2)}) collective-permute-start(bf16[2,64,128]{2,1,0:T(8,128)(2,1)S(1)} %get-tuple-element.41), channel_id=1, source_target_pairs={{0,1},{1,2},{2,3},{4,5},{5,6},{6,7},{8,9},{9,10},{10,11},{12,13},{... | collective-permute-start | bytes 98312 | tf_op jit(solution)/shard_map/ppermute | solution.py:517
  52.9 1.3 %collective-permute-start.7 = (bf16[2,64,128]{2,1,0:T(8,128)(2,1)S(1)}, bf16[2,64,128]{2,1,0:T(8,128)(2,1)S(1)}, u32[]{:S(2)}, u32[]{:S(2)}) collective-permute-start(bf16[2,64,128]{2,1,0:T(8,128)(2,1)S(1)} %get-tuple-element.42), channel_id=1, source_target_pairs={{1,0},{2,1},{3,2},{5,4},{6,5},{7,6},{9,8},{10,9},{11,10},{13,12},{... | collective-permute-start | bytes 98312 | tf_op jit(solution)/shard_map/ppermute | solution.py:518
  54.2 0.7 %broadcast_in_dim.24 = bf16[32,32,128]{2,1,0:T(8,128)(2,1)} broadcast(bf16[32,128]{1,0:T(8,128)(2,1)S(1)} %multiply_convert_fusion), dimensions={1,2} | broadcast | bytes 270336 | tf_op jit(solution)/shard_map/broadcast_in_dim | solution.py:493
  55.0 5.4 %all-to-all-start.1 = ((bf16[32,32,128]{2,1,0:T(8,128)(2,1)}), bf16[32,32,128]{2,1,0:T(8,128)(2,1)S(1)}, u32[]{:S(2)}, u32[]{:S(2)}) async-start(bf16[32,32,128]{2,1,0:T(8,128)(2,1)} %broadcast_in_dim.24), calls=%async_computation.1 | async-start | bytes 524288 | tf_op jit(solution)/shard_map/all_to_all | solution.py:494
  60.4 0.0 collective-permute-done.7
  60.4 0.1 add_convert_fusion
  60.5 0.1 copy.13
  60.7 0.8 %copy_bitcast_fusion = bf16[64,2,16,128]{3,2,1,0:T(8,128)(2,1)} fusion(bf16[2,64,16,128]{3,2,1,0:T(8,128)(2,1)S(1)} %bitcast.40), kind=kLoop, calls=%fused_computation.1 | loop fusion | bytes 1048576 | tf_op jit(solution)/shard_map/transpose | solution.py:525
  61.5 9.2 %all-to-all-done.1.packed = bf16[32,32,128]{2,1,0:T(8,128)(2,1)S(1)} async-done(((bf16[32,32,128]{2,1,0:T(8,128)(2,1)}), bf16[32,32,128]{2,1,0:T(8,128)(2,1)S(1)}, u32[]{:S(2)}, u32[]{:S(2)}) %all-to-all-start.1) | async-done | bytes 262176 | tf_op jit(solution)/shard_map/all_to_all | solution.py:494
  70.7 1.1 %shard_map.60 = f32[4,4,4,32,64]{4,3,2,1,0:T(8,128)} custom-call(bf16[32,32,128]{2,1,0:T(8,128)(2,1)S(1)} %all-to-all-done.1.packed), custom_call_target="tpu_custom_call" | custom-call | tf_op jit(solution)/shard_map/pallas_call | solution.py:495
  (20 shorter events, 0.3 us)
Async XLA Ops:
  0.6 7.8 %copy-start = (bf16[2,2,2,32,2,16,128]{6,5,4,3,2,1,0:T(8,128)(2,1)S(1)}, bf16[2,2,2,32,2,16,128]{6,5,4,3,2,1,0:T(8,128)(2,1)}, u32[]{:S(2)}) copy-start(bf16[2,2,2,32,2,16,128]{6,5,4,3,2,1,0:T(8,128)(2,1)} %param.5) | copy-start | bytes 6291460
  1.9 11.8 %collective-permute-start = (bf16[64,1,16,128]{3,0,2,1:T(8,128)(2,1)S(1)}, bf16[64,1,16,128]{3,0,2,1:T(8,128)(2,1)S(1)}, u32[]{:S(2)}, u32[]{:S(2)}) collective-permute-start(bf16[64,1,16,128]{3,0,2,1:T(8,128)(2,1)S(1)} %copy.11), channel_id=1, source_target_pairs={{0,4},{4,8},{8,12},{12,16},{16,20},{20,24},{24,28},{1,5},{5,9},{9,... | collective-permute-start | bytes 786440 | tf_op jit(solution)/shard_map/ppermute | solution.py:413
  6.5 7.7 %collective-permute-start.1 = (bf16[64,1,16,128]{3,0,2,1:T(8,128)(2,1)S(1)}, bf16[64,1,16,128]{3,0,2,1:T(8,128)(2,1)S(1)}, u32[]{:S(2)}, u32[]{:S(2)}) collective-permute-start(bf16[64,1,16,128]{3,0,2,1:T(8,128)(2,1)S(1)} %copy.12), channel_id=1, source_target_pairs={{4,0},{8,4},{12,8},{16,12},{20,16},{24,20},{28,24},{5,1},{9,5},{13... | collective-permute-start | bytes 786440 | tf_op jit(solution)/shard_map/ppermute | solution.py:414
  8.5 1.0 %copy-start.1 = (bf16[64,2,16,128]{3,2,1,0:T(8,128)(2,1)S(1)}, bf16[64,2,16,128]{3,2,1,0:T(8,128)(2,1)}, u32[]{:S(2)}) copy-start(bf16[64,2,16,128]{3,2,1,0:T(8,128)(2,1)} %vol.1) | copy-start | bytes 1572868
  9.5 1.0 %copy-start.2 = (bf16[4,4,4,32,64]{4,3,2,1,0:T(8,128)(2,1)S(1)}, bf16[4,4,4,32,64]{4,3,2,1,0:T(8,128)(2,1)}, u32[]{:S(2)}) copy-start(bf16[4,4,4,32,64]{4,3,2,1,0:T(8,128)(2,1)} %taps.1) | copy-start | bytes 786436
  14.2 4.9 %collective-permute-start.2 = (bf16[4,64,128]{2,1,0:T(8,128)(2,1)S(1)}, bf16[4,64,128]{2,1,0:T(8,128)(2,1)S(1)}, u32[]{:S(2)}, u32[]{:S(2)}) collective-permute-start(bf16[4,64,128]{2,1,0:T(8,128)(2,1)S(1)} %pad_maximum_fusion), channel_id=1, source_target_pairs={{0,1},{1,2},{2,3},{4,5},{5,6},{6,7},{8,9},{9,10},{10,11},{12,13},{... | collective-permute-start | bytes 196616 | tf_op jit(solution)/shard_map/ppermute | solution.py:455
  17.5 5.0 %collective-permute-start.3 = (bf16[4,64,128]{2,1,0:T(8,128)(2,1)S(1)}, bf16[4,64,128]{2,1,0:T(8,128)(2,1)S(1)}, u32[]{:S(2)}, u32[]{:S(2)}) collective-permute-start(bf16[4,64,128]{2,1,0:T(8,128)(2,1)S(1)} %pad_maximum_fusion.1), channel_id=1, source_target_pairs={{1,0},{2,1},{3,2},{5,4},{6,5},{7,6},{9,8},{10,9},{11,10},{13,12},{... | collective-permute-start | bytes 196616 | tf_op jit(solution)/shard_map/ppermute | solution.py:456
  30.5 11.5 %collective-permute-start.4 = (bf16[64,2304]{1,0:T(8,128)(2,1)S(1)}, bf16[64,2304]{1,0:T(8,128)(2,1)S(1)}, u32[]{:S(2)}, u32[]{:S(2)}) collective-permute-start(bf16[64,2304]{1,0:T(8,128)(2,1)S(1)} %get-tuple-element.25), channel_id=1, source_target_pairs={{0,4},{4,8},{8,12},{12,16},{16,20},{20,24},{24,28},{1,5},{5,9},{9,... | collective-permute-start | bytes 884744 | tf_op jit(solution)/shard_map/ppermute | solution.py:503
  35.8 18.3 %all-to-all-start = ((bf16[32,32,128]{2,1,0:T(8,128)(2,1)}), bf16[32,32,128]{2,1,0:T(8,128)(2,1)S(1)}, u32[]{:S(2)}, u32[]{:S(2)}) async-start(bf16[32,32,128]{2,1,0:T(8,128)(2,1)} %get-tuple-element.28), calls=%async_computation | async-start | bytes 524288 | tf_op jit(solution)/shard_map/all_to_all | solution.py:491
  39.9 9.3 %collective-permute-start.5 = (bf16[64,2304]{1,0:T(8,128)(2,1)S(1)}, bf16[64,2304]{1,0:T(8,128)(2,1)S(1)}, u32[]{:S(2)}, u32[]{:S(2)}) collective-permute-start(bf16[64,2304]{1,0:T(8,128)(2,1)S(1)} %get-tuple-element.26), channel_id=1, source_target_pairs={{4,0},{8,4},{12,8},{16,12},{20,16},{24,20},{28,24},{5,1},{9,5},{13... | collective-permute-start | bytes 884744 | tf_op jit(solution)/shard_map/ppermute | solution.py:504
  49.4 11.0 %collective-permute-start.6 = (bf16[2,64,128]{2,1,0:T(8,128)(2,1)S(1)}, bf16[2,64,128]{2,1,0:T(8,128)(2,1)S(1)}, u32[]{:S(2)}, u32[]{:S(2)}) collective-permute-start(bf16[2,64,128]{2,1,0:T(8,128)(2,1)S(1)} %get-tuple-element.41), channel_id=1, source_target_pairs={{0,1},{1,2},{2,3},{4,5},{5,6},{6,7},{8,9},{9,10},{10,11},{12,13},{... | collective-permute-start | bytes 98312 | tf_op jit(solution)/shard_map/ppermute | solution.py:517
  52.9 7.5 %collective-permute-start.7 = (bf16[2,64,128]{2,1,0:T(8,128)(2,1)S(1)}, bf16[2,64,128]{2,1,0:T(8,128)(2,1)S(1)}, u32[]{:S(2)}, u32[]{:S(2)}) collective-permute-start(bf16[2,64,128]{2,1,0:T(8,128)(2,1)S(1)} %get-tuple-element.42), channel_id=1, source_target_pairs={{1,0},{2,1},{3,2},{5,4},{6,5},{7,6},{9,8},{10,9},{11,10},{13,12},{... | collective-permute-start | bytes 98312 | tf_op jit(solution)/shard_map/ppermute | solution.py:518
  55.0 15.8 %all-to-all-start.1 = ((bf16[32,32,128]{2,1,0:T(8,128)(2,1)}), bf16[32,32,128]{2,1,0:T(8,128)(2,1)S(1)}, u32[]{:S(2)}, u32[]{:S(2)}) async-start(bf16[32,32,128]{2,1,0:T(8,128)(2,1)} %broadcast_in_dim.24), calls=%async_computation.1 | async-start | bytes 524288 | tf_op jit(solution)/shard_map/all_to_all | solution.py:494

commit v6 on v5

--- a/solution.py
+++ b/solution.py
@@ -128,12 +128,53 @@
 
 
 def inner_kernel(
-    dims, chunk, vol, taps, cot, flat, w, wt, vals, cot_edge, wg, ig, vm, ga, gb, cots
+    dims,
+    chunk,
+    vol_in,
+    taps_in,
+    cot,
+    flat,
+    w,
+    wt,
+    vals,
+    cot_edge,
+    wg,
+    ig,
+    vol,
+    taps,
+    sems,
+    vm,
+    ga,
+    gb,
+    cots,
 ):
     nx, ny, nz, ci, co = dims
     half = 4 * ci
     to_y = swap_matrix(GROUP, ny)
-
+    arriving = [
+        pltpu.make_async_copy(vol_in, vol, sems.at[0]),
+        pltpu.make_async_copy(taps_in, taps, sems.at[1]),
+    ]
+    for copy in arriving:
+        copy.start()
+
+    for i in range(1, nx):
+        for q in range(8):
+            m = i - q // 4
+
+            def put(k, y, rows, i=i, q=q):
+                r = slice(q * co + k * GROUP, q * co + (k + 1) * GROUP)
+                cots[i - 1, r, y * nz : (y + 1) * nz] = rows
+                if y == edge_row(q, ny):
+                    cot_edge[i - 1, r] = rows
+
+            tiles = Tiles(
+                co // GROUP, lambda k, q=q, m=m: cot[q, k * GROUP : (k + 1) * GROUP, m]
+            )
+            bring_plane(to_y, tiles, ny, nz, put)
+
+    for copy in arriving:
+        copy.wait()
     for tx in range(2):
         for ty in range(2):
             for tz in range(2):
@@ -157,21 +198,6 @@
             ci // GROUP, lambda k, x=x: vol[k * GROUP : (k + 1) * GROUP, x]
         )
         bring_plane(to_y, tiles, ny, nz, put)
-
-    for i in range(1, nx):
-        for q in range(8):
-            m = i - q // 4
-
-            def put(k, y, rows, i=i, q=q):
-                r = slice(q * co + k * GROUP, q * co + (k + 1) * GROUP)
-                cots[i - 1, r, y * nz : (y + 1) * nz] = rows
-                if y == edge_row(q, ny):
-                    cot_edge[i - 1, r] = rows
-
-            tiles = Tiles(
-                co // GROUP, lambda k, q=q, m=m: cot[q, k * GROUP : (k + 1) * GROUP, m]
-            )
-            bring_plane(to_y, tiles, ny, nz, put)
 
     def block(x, y):
         return flat[x - 1, :, (y - 1) * nz : y * nz]
@@ -224,7 +250,6 @@
     own,
     xraw,
     yraw,
-    xs,
     vm,
     ga,
     gb,
@@ -265,27 +290,16 @@
 
     for copy in arriving:
         copy.wait()
-    for side in range(2):
-
-        def put(k, y, rows, side=side):
-            xs[side, k * GROUP : (k + 1) * GROUP, y * nz : (y + 1) * nz] = rows
-
-        tiles = Tiles(
-            ci // GROUP, lambda k, side=side: xraw[side, k * GROUP : (k + 1) * GROUP, 0]
-        )
-        bring_plane(to_y, tiles, ny, nz, put)
-
     def block(x, y):
         if y == 0:
             return yraw[0, x]
         if y == ny + 1:
             return yraw[1, x]
-        lanes = slice((y - 1) * nz, y * nz)
         if x == 0:
-            return xs[0, :, lanes]
+            return xraw[0, y - 1]
         if x == nx + 1:
-            return xs[1, :, lanes]
-        return flat[x - 1, :, lanes]
+            return xraw[1, y - 1]
+        return flat[x - 1, :, (y - 1) * nz : y * nz]
 
     for x in range(nx + 2):
         for y in range(ny + 2):
@@ -410,8 +424,8 @@
     cells = nx * gx * ny * gy * nz
     dims = (nx, ny, nz, ci, co)
 
-    xlo = lax.ppermute(volume[:, nx - 1 :], "gx", gx_up)
-    xhi = lax.ppermute(volume[:, :1], "gx", gx_down)
+    xlo = lax.ppermute(volume[:, nx - 1].transpose(1, 0, 2), "gx", gx_up)
+    xhi = lax.ppermute(volume[:, 0].transpose(1, 0, 2), "gx", gx_down)
     cot = cotangent.reshape(8, co, nx, ny, nz)
 
     vmem = pl.BlockSpec(memory_space=pltpu.VMEM)
@@ -431,9 +445,12 @@
             jax.ShapeDtypeStruct((8 * co, 8 * ci), F32),
             jax.ShapeDtypeStruct((nx, ci, ny * nz), F32),
         ),
-        in_specs=[vmem] * 3,
+        in_specs=[anywhere, anywhere, vmem],
         out_specs=(vmem,) * 7,
         scratch_shapes=[
+            pltpu.VMEM(volume.shape, BF16),
+            pltpu.VMEM(kernel.shape, BF16),
+            pltpu.SemaphoreType.DMA((2,)),
             pltpu.VMEM((nx, ci, ny * nz), BF16),
             pltpu.VMEM((8 * co, n_in * nz), BF16),
             pltpu.VMEM((8 * co, n_in * nz), BF16),
@@ -445,9 +462,9 @@
     def y_row(y):
         return jnp.concatenate(
             [
-                xlo[:, :, y].transpose(1, 0, 2),
+                xlo[y : y + 1],
                 flat[:, :, y * nz : (y + 1) * nz],
-                xhi[:, :, y].transpose(1, 0, 2),
+                xhi[y : y + 1],
             ],
             axis=0,
         )
@@ -470,9 +487,8 @@
             pltpu.VMEM((2, ci, (ny + 2) * nz), BF16),
             pltpu.VMEM((2, ci, (ny + 2) * nz), F32),
             pltpu.VMEM((nx, ci, ny * nz), F32),
-            pltpu.VMEM((2, ci, 1, ny, nz), BF16),
+            pltpu.VMEM((2, ny, ci, nz), BF16),
             pltpu.VMEM((2, nx + 2, ci, nz), BF16),
-            pltpu.VMEM((2, ci, ny * nz), BF16),
             pltpu.VMEM((nx + 2, ci, (ny + 2) * nz), BF16),
             pltpu.VMEM((8 * co, n_out * nz), BF16),
             pltpu.VMEM((8 * co, n_out * nz), BF16),
@@ -512,8 +528,9 @@
             + jnp.concatenate([zero, from_high[:, :, lanes]], axis=0)
         )
 
-    send_low = add_x(yface[0], slice(0, nz)).astype(BF16)
-    send_high = add_x(yface[1], slice((ny + 1) * nz, None)).astype(BF16)
+    later = 0.0 * piece[0, 0].astype(F32)
+    send_low = (add_x(yface[0], slice(0, nz)) + later).astype(BF16)
+    send_high = (add_x(yface[1], slice((ny + 1) * nz, None)) + later).astype(BF16)
     y_low = lax.ppermute(send_high, "gy", gy_up).astype(F32)
     y_high = lax.ppermute(send_low, "gy", gy_down).astype(F32)
     gap = jnp.zeros((nx, ci, (ny - 1) * nz), F32)

time: 72.4 us -> 74 us (1.022)
  waiting for transfers between devices: 20.1 us -> 21 us
    all_to_all x1, waiting for transfers between devices: 0.01 us -> 0.97 us  [on_device(): shares = lax.all_to_all(shares, ('gx', 'gy'), 0, 0, tiled=True)]
    ppermute x1, starting transfers between devices: 3.49 us -> 2.53 us  [on_device(): y_low = lax.ppermute(send_high, 'gy', gy_up).astype(F32)]
    slice x1 -> x4, local copies, waits for them, and re-layouts: 1.22 us -> 1.74 us  [the longest x1 1.22 us: on_device(): xhi = lax.ppermute(volume[:, 0].transpose(1, 0, 2), 'gx', gx_down)]
  transfers between devices with their start and end apart: 10 -> 10, of which waited for: 4 -> 4; matrix products, arithmetic and copies ran while one was open for 3% -> 3% of each run, Pallas kernels for 4% -> 5%
where the time goes in v6:
time: 74 us; the launch traced here: 73.4 us
  starting transfers between devices  32 us (43%)
  waiting for transfers between devices  21 us (28%)
  Pallas kernels  12.7 us (17%)
  local copies, waits for them, and re-layouts  5.74 us (8%)
  between operations  1.59 us (2%)
    all_to_all x1, waiting for transfers between devices, on_device(): pieces = lax.all_to_all(pieces, ('gx', 'gy'), 0, 0, tiled=True)  9.25 us
    pallas_call x1, Pallas kernels, on_device(): pl.pallas_call(functools.partial(outer_kernel, dims, 4), out_shape=(jax.S...  7.89 us
    ppermute x1, waiting for transfers between devices, on_device(): from_high = lax.ppermute(down, 'gx', gx_down).astype(F32)[None]  7.07 us
    all_to_all x1, starting transfers between devices, on_device(): pieces = lax.all_to_all(pieces, ('gx', 'gy'), 0, 0, tiled=True)  5.41 us
    ppermute x1, starting transfers between devices, on_device(): from_low = lax.ppermute(up, 'gx', gx_up).astype(F32)[None]  5.17 us
    all_to_all x1, starting transfers between devices, on_device(): shares = lax.all_to_all(shares, ('gx', 'gy'), 0, 0, tiled=True)  4.55 us
    ppermute x1, starting transfers between devices, on_device(): xlo = lax.ppermute(volume[:, nx - 1].transpose(1, 0, 2), 'gx', gx_up)  4.51 us
    pallas_call x1, Pallas kernels, on_device(): pl.pallas_call(functools.partial(inner_kernel, dims, 5), out_shape=(jax.S...  3.71 us
  transfers between devices with their start and end apart: 10, of which 4 were waited for; matrix products, arithmetic and copies ran while one was open for 3% of the time, Pallas kernels for 5%

profile of v6, /device:TPU:1, one launch (start us, length us, event | category | flops | bytes accessed | tf_op | source)
XLA Modules:
  0.0 73.4 jit_solution(15759750640057247330)
XLA Ops:
  0.6 1.2 %fusion.9 = (bf16[64,1,16,128]{3,2,1,0:T(8,128)(2,1)S(1)}, bf16[64,1,16,128]{3,2,1,0:T(8,128)(2,1)S(1)}) fusion(bf16[64,2,16,128]{3,2,1,0:T(8,128)(2,1)} %vol_in.1), kind=kLoop, calls=%fused_computation.21 | loop fusion | bytes 1048576 | tf_op jit(solution)/shard_map/slice | solution.py:428
  1.9 0.1 copy.16
  1.9 4.5 %collective-permute-start = (bf16[16,64,128]{2,1,0:T(8,128)(2,1)S(1)}, bf16[16,64,128]{2,1,0:T(8,128)(2,1)S(1)}, u32[]{:S(2)}, u32[]{:S(2)}) collective-permute-start(bf16[16,64,128]{2,1,0:T(8,128)(2,1)S(1)} %bitcast.49), channel_id=1, source_target_pairs={{0,4},{4,8},{8,12},{12,16},{16,20},{20,24},{24,28},{1,5},{5,9},{9,... | collective-permute-start | bytes 786440 | tf_op jit(solution)/shard_map/ppermute | solution.py:427
  6.5 0.1 copy.15
  6.5 1.9 %collective-permute-start.1 = (bf16[16,64,128]{2,1,0:T(8,128)(2,1)S(1)}, bf16[16,64,128]{2,1,0:T(8,128)(2,1)S(1)}, u32[]{:S(2)}, u32[]{:S(2)}) collective-permute-start(bf16[16,64,128]{2,1,0:T(8,128)(2,1)S(1)} %bitcast.50), channel_id=1, source_target_pairs={{4,0},{8,4},{12,8},{16,12},{20,16},{24,20},{28,24},{5,1},{9,5},{13... | collective-permute-start | bytes 786440 | tf_op jit(solution)/shard_map/ppermute | solution.py:428
  8.5 0.0 copy-start.1
  8.5 1.0 %copy-done.1 = bf16[64,2,16,128]{3,2,1,0:T(8,128)(2,1)S(1)} copy-done((bf16[64,2,16,128]{3,2,1,0:T(8,128)(2,1)S(1)}, bf16[64,2,16,128]{3,2,1,0:T(8,128)(2,1)}, u32[]{:S(2)}) %copy-start.1) | copy-done | bytes 524312
  9.5 1.0 %copy-done.2 = bf16[4,4,4,32,64]{4,3,2,1,0:T(8,128)(2,1)S(1)} copy-done((bf16[4,4,4,32,64]{4,3,2,1,0:T(8,128)(2,1)S(1)}, bf16[4,4,4,32,64]{4,3,2,1,0:T(8,128)(2,1)}, u32[]{:S(2)}) %copy-start.2) | copy-done | bytes 262168
  10.6 3.7 %shard_map.58 = (bf16[2,64,2048]{2,1,0:T(8,128)(2,1)S(1)}, bf16[256,512]{1,0:T(8,128)(2,1)S(1)}, bf16[512,256]{1,0:T(8,128)(2,1)S(1)}, bf16[1,256,2048]{2,1,0:T(...) custom-call(bf16[64,2,16,128]{3,2,1,0:T(8,128)(2,1)S(1)} %copy-done.1, ...), custom_call_target="tpu_custom_call" | custom-call | tf_op jit(solution)/shard_map/pallas_call | solution.py:437
  14.3 0.0 collective-permute-done.xlo_in
  14.3 0.0 collective-permute-done.1.xhi_in
  14.4 3.2 %collective-permute-start.2 = (bf16[4,64,128]{2,1,0:T(8,128)(2,1)S(1)}, bf16[4,64,128]{2,1,0:T(8,128)(2,1)S(1)}, u32[]{:S(2)}, u32[]{:S(2)}) collective-permute-start(bf16[4,64,128]{2,1,0:T(8,128)(2,1)S(1)} %pad_maximum_fusion), channel_id=1, source_target_pairs={{0,1},{1,2},{2,3},{4,5},{5,6},{6,7},{8,9},{9,10},{10,11},{12,13},{... | collective-permute-start | bytes 196616 | tf_op jit(solution)/shard_map/ppermute | solution.py:472
  17.6 1.3 %collective-permute-start.3 = (bf16[4,64,128]{2,1,0:T(8,128)(2,1)S(1)}, bf16[4,64,128]{2,1,0:T(8,128)(2,1)S(1)}, u32[]{:S(2)}, u32[]{:S(2)}) collective-permute-start(bf16[4,64,128]{2,1,0:T(8,128)(2,1)S(1)} %pad_maximum_fusion.1), channel_id=1, source_target_pairs={{1,0},{2,1},{3,2},{5,4},{6,5},{7,6},{9,8},{10,9},{11,10},{13,12},{... | collective-permute-start | bytes 196616 | tf_op jit(solution)/shard_map/ppermute | solution.py:473
  18.9 0.0 collective-permute-done.2.ylo_in
  18.9 3.7 %collective-permute-done.3.yhi_in = bf16[4,64,128]{2,1,0:T(8,128)(2,1)S(1)} collective-permute-done((bf16[4,64,128]{2,1,0:T(8,128)(2,1)S(1)}, bf16[4,64,128]{2,1,0:T(8,128)(2,1)S(1)}, u32[]{:S(2)}, u32[]{:S(2)}) %collective-permute-start.3) | collective-permute-done | bytes 65568 | tf_op jit(solution)/shard_map/ppermute | solution.py:473
  22.6 7.9 %shard_map.59 = (bf16[8,32,2,16,128]{4,3,2,1,0:T(8,128)(2,1)}, f32[2,64,2048]{2,1,0:T(8,128)S(1)}, bf16[64,2304]{1,0:T(8,128)(2,1)S(1)}, bf16[64,2304]{1,0:T(8,1...) custom-call(bf16[2,64,2048]{2,1,0:T(8,128)(2,1)S(1)} %get-tuple-element.16.flat, ...), custom_call_target="tpu_custom_call" | custom-call | tf_op jit(solution)/shard_map/pallas_call | solution.py:474
  30.5 5.2 %collective-permute-start.4 = (bf16[64,2304]{1,0:T(8,128)(2,1)S(1)}, bf16[64,2304]{1,0:T(8,128)(2,1)S(1)}, u32[]{:S(2)}, u32[]{:S(2)}) collective-permute-start(bf16[64,2304]{1,0:T(8,128)(2,1)S(1)} %get-tuple-element.25), channel_id=1, source_target_pairs={{0,4},{4,8},{8,12},{12,16},{16,20},{20,24},{24,28},{1,5},{5,9},{9,... | collective-permute-start | bytes 884744 | tf_op jit(solution)/shard_map/ppermute | solution.py:519
  35.7 4.5 %all-to-all-start = ((bf16[32,32,128]{2,1,0:T(8,128)(2,1)}), bf16[32,32,128]{2,1,0:T(8,128)(2,1)S(1)}, u32[]{:S(2)}, u32[]{:S(2)}) async-start(bf16[32,32,128]{2,1,0:T(8,128)(2,1)} %get-tuple-element.28), calls=%async_computation | async-start | bytes 524288 | tf_op jit(solution)/shard_map/all_to_all | solution.py:507
  40.2 2.2 %collective-permute-start.5 = (bf16[64,2304]{1,0:T(8,128)(2,1)S(1)}, bf16[64,2304]{1,0:T(8,128)(2,1)S(1)}, u32[]{:S(2)}, u32[]{:S(2)}) collective-permute-start(bf16[64,2304]{1,0:T(8,128)(2,1)S(1)} %get-tuple-element.26), channel_id=1, source_target_pairs={{4,0},{8,4},{12,8},{16,12},{20,16},{24,20},{28,24},{5,1},{9,5},{13... | collective-permute-start | bytes 884744 | tf_op jit(solution)/shard_map/ppermute | solution.py:520
  42.5 7.1 %collective-permute-done.5 = bf16[64,2304]{1,0:T(8,128)(2,1)S(1)} collective-permute-done((bf16[64,2304]{1,0:T(8,128)(2,1)S(1)}, bf16[64,2304]{1,0:T(8,128)(2,1)S(1)}, u32[]{:S(2)}, u32[]{:S(2)}) %collective-permute-start.5) | collective-permute-done | bytes 294944 | tf_op jit(solution)/shard_map/ppermute | solution.py:520
  49.6 1.0 %all-to-all-done = bf16[32,32,128]{2,1,0:T(8,128)(2,1)S(1)} async-done(((bf16[32,32,128]{2,1,0:T(8,128)(2,1)}), bf16[32,32,128]{2,1,0:T(8,128)(2,1)S(1)}, u32[]{:S(2)}, u32[]{:S(2)}) %all-to-all-start) | async-done | bytes 262176 | tf_op jit(solution)/shard_map/all_to_all | solution.py:507
  50.6 0.5 slice.76
  51.8 2.5 %collective-permute-start.6 = (bf16[2,64,128]{2,1,0:T(8,128)(2,1)S(1)}, bf16[2,64,128]{2,1,0:T(8,128)(2,1)S(1)}, u32[]{:S(2)}, u32[]{:S(2)}) collective-permute-start(bf16[2,64,128]{2,1,0:T(8,128)(2,1)S(1)} %get-tuple-element.41), channel_id=1, source_target_pairs={{0,1},{1,2},{2,3},{4,5},{5,6},{6,7},{8,9},{9,10},{10,11},{12,13},{... | collective-permute-start | bytes 98312 | tf_op jit(solution)/shard_map/ppermute | solution.py:534
  54.4 1.3 %collective-permute-start.7 = (bf16[2,64,128]{2,1,0:T(8,128)(2,1)S(1)}, bf16[2,64,128]{2,1,0:T(8,128)(2,1)S(1)}, u32[]{:S(2)}, u32[]{:S(2)}) collective-permute-start(bf16[2,64,128]{2,1,0:T(8,128)(2,1)S(1)} %get-tuple-element.42), channel_id=1, source_target_pairs={{1,0},{2,1},{3,2},{5,4},{6,5},{7,6},{9,8},{10,9},{11,10},{13,12},{... | collective-permute-start | bytes 98312 | tf_op jit(solution)/shard_map/ppermute | solution.py:535
  55.8 0.7 %broadcast_in_dim.24 = bf16[32,32,128]{2,1,0:T(8,128)(2,1)} broadcast(bf16[32,128]{1,0:T(8,128)(2,1)S(1)} %multiply_convert_fusion), dimensions={1,2} | broadcast | bytes 270336 | tf_op jit(solution)/shard_map/broadcast_in_dim | solution.py:509
  56.5 5.4 %all-to-all-start.1 = ((bf16[32,32,128]{2,1,0:T(8,128)(2,1)}), bf16[32,32,128]{2,1,0:T(8,128)(2,1)S(1)}, u32[]{:S(2)}, u32[]{:S(2)}) async-start(bf16[32,32,128]{2,1,0:T(8,128)(2,1)} %broadcast_in_dim.24), calls=%async_computation.1 | async-start | bytes 524288 | tf_op jit(solution)/shard_map/all_to_all | solution.py:510
  61.9 0.0 collective-permute-done.7
  61.9 0.1 add_convert_fusion
  62.1 0.1 copy.11
  62.2 0.8 %copy_bitcast_fusion = bf16[64,2,16,128]{3,2,1,0:T(8,128)(2,1)} fusion(bf16[2,64,16,128]{3,2,1,0:T(8,128)(2,1)S(1)} %bitcast.47), kind=kLoop, calls=%fused_computation.1 | loop fusion | bytes 1048576 | tf_op jit(solution)/shard_map/transpose | solution.py:542
  63.0 9.2 %all-to-all-done.1.packed = bf16[32,32,128]{2,1,0:T(8,128)(2,1)S(1)} async-done(((bf16[32,32,128]{2,1,0:T(8,128)(2,1)}), bf16[32,32,128]{2,1,0:T(8,128)(2,1)S(1)}, u32[]{:S(2)}, u32[]{:S(2)}) %all-to-all-start.1) | async-done | bytes 262176 | tf_op jit(solution)/shard_map/all_to_all | solution.py:510
  72.3 1.1 %shard_map.60 = f32[4,4,4,32,64]{4,3,2,1,0:T(8,128)} custom-call(bf16[32,32,128]{2,1,0:T(8,128)(2,1)S(1)} %all-to-all-done.1.packed), custom_call_target="tpu_custom_call" | custom-call | tf_op jit(solution)/shard_map/pallas_call | solution.py:511
  (19 shorter events, 0.3 us)
Async XLA Ops:
  0.6 7.8 %copy-start = (bf16[2,2,2,32,2,16,128]{6,5,4,3,2,1,0:T(8,128)(2,1)S(1)}, bf16[2,2,2,32,2,16,128]{6,5,4,3,2,1,0:T(8,128)(2,1)}, u32[]{:S(2)}) copy-start(bf16[2,2,2,32,2,16,128]{6,5,4,3,2,1,0:T(8,128)(2,1)} %param.5) | copy-start | bytes 6291460
  1.9 12.4 %collective-permute-start = (bf16[16,64,128]{2,1,0:T(8,128)(2,1)S(1)}, bf16[16,64,128]{2,1,0:T(8,128)(2,1)S(1)}, u32[]{:S(2)}, u32[]{:S(2)}) collective-permute-start(bf16[16,64,128]{2,1,0:T(8,128)(2,1)S(1)} %bitcast.49), channel_id=1, source_target_pairs={{0,4},{4,8},{8,12},{12,16},{16,20},{20,24},{24,28},{1,5},{5,9},{9,... | collective-permute-start | bytes 786440 | tf_op jit(solution)/shard_map/ppermute | solution.py:427
  6.5 7.8 %collective-permute-start.1 = (bf16[16,64,128]{2,1,0:T(8,128)(2,1)S(1)}, bf16[16,64,128]{2,1,0:T(8,128)(2,1)S(1)}, u32[]{:S(2)}, u32[]{:S(2)}) collective-permute-start(bf16[16,64,128]{2,1,0:T(8,128)(2,1)S(1)} %bitcast.50), channel_id=1, source_target_pairs={{4,0},{8,4},{12,8},{16,12},{20,16},{24,20},{28,24},{5,1},{9,5},{13... | collective-permute-start | bytes 786440 | tf_op jit(solution)/shard_map/ppermute | solution.py:428
  8.5 1.0 %copy-start.1 = (bf16[64,2,16,128]{3,2,1,0:T(8,128)(2,1)S(1)}, bf16[64,2,16,128]{3,2,1,0:T(8,128)(2,1)}, u32[]{:S(2)}) copy-start(bf16[64,2,16,128]{3,2,1,0:T(8,128)(2,1)} %vol_in.1) | copy-start | bytes 1572868
  9.5 1.0 %copy-start.2 = (bf16[4,4,4,32,64]{4,3,2,1,0:T(8,128)(2,1)S(1)}, bf16[4,4,4,32,64]{4,3,2,1,0:T(8,128)(2,1)}, u32[]{:S(2)}) copy-start(bf16[4,4,4,32,64]{4,3,2,1,0:T(8,128)(2,1)} %taps_in.1) | copy-start | bytes 786436
  14.4 4.5 %collective-permute-start.2 = (bf16[4,64,128]{2,1,0:T(8,128)(2,1)S(1)}, bf16[4,64,128]{2,1,0:T(8,128)(2,1)S(1)}, u32[]{:S(2)}, u32[]{:S(2)}) collective-permute-start(bf16[4,64,128]{2,1,0:T(8,128)(2,1)S(1)} %pad_maximum_fusion), channel_id=1, source_target_pairs={{0,1},{1,2},{2,3},{4,5},{5,6},{6,7},{8,9},{9,10},{10,11},{12,13},{... | collective-permute-start | bytes 196616 | tf_op jit(solution)/shard_map/ppermute | solution.py:472
  17.6 5.0 %collective-permute-start.3 = (bf16[4,64,128]{2,1,0:T(8,128)(2,1)S(1)}, bf16[4,64,128]{2,1,0:T(8,128)(2,1)S(1)}, u32[]{:S(2)}, u32[]{:S(2)}) collective-permute-start(bf16[4,64,128]{2,1,0:T(8,128)(2,1)S(1)} %pad_maximum_fusion.1), channel_id=1, source_target_pairs={{1,0},{2,1},{3,2},{5,4},{6,5},{7,6},{9,8},{10,9},{11,10},{13,12},{... | collective-permute-start | bytes 196616 | tf_op jit(solution)/shard_map/ppermute | solution.py:473
  30.5 11.9 %collective-permute-start.4 = (bf16[64,2304]{1,0:T(8,128)(2,1)S(1)}, bf16[64,2304]{1,0:T(8,128)(2,1)S(1)}, u32[]{:S(2)}, u32[]{:S(2)}) collective-permute-start(bf16[64,2304]{1,0:T(8,128)(2,1)S(1)} %get-tuple-element.25), channel_id=1, source_target_pairs={{0,4},{4,8},{8,12},{12,16},{16,20},{20,24},{24,28},{1,5},{5,9},{9,... | collective-permute-start | bytes 884744 | tf_op jit(solution)/shard_map/ppermute | solution.py:519
  35.7 14.9 %all-to-all-start = ((bf16[32,32,128]{2,1,0:T(8,128)(2,1)}), bf16[32,32,128]{2,1,0:T(8,128)(2,1)S(1)}, u32[]{:S(2)}, u32[]{:S(2)}) async-start(bf16[32,32,128]{2,1,0:T(8,128)(2,1)} %get-tuple-element.28), calls=%async_computation | async-start | bytes 524288 | tf_op jit(solution)/shard_map/all_to_all | solution.py:507
  40.2 9.3 %collective-permute-start.5 = (bf16[64,2304]{1,0:T(8,128)(2,1)S(1)}, bf16[64,2304]{1,0:T(8,128)(2,1)S(1)}, u32[]{:S(2)}, u32[]{:S(2)}) collective-permute-start(bf16[64,2304]{1,0:T(8,128)(2,1)S(1)} %get-tuple-element.26), channel_id=1, source_target_pairs={{4,0},{8,4},{12,8},{16,12},{20,16},{24,20},{28,24},{5,1},{9,5},{13... | collective-permute-start | bytes 884744 | tf_op jit(solution)/shard_map/ppermute | solution.py:520
  51.8 10.1 %collective-permute-start.6 = (bf16[2,64,128]{2,1,0:T(8,128)(2,1)S(1)}, bf16[2,64,128]{2,1,0:T(8,128)(2,1)S(1)}, u32[]{:S(2)}, u32[]{:S(2)}) collective-permute-start(bf16[2,64,128]{2,1,0:T(8,128)(2,1)S(1)} %get-tuple-element.41), channel_id=1, source_target_pairs={{0,1},{1,2},{2,3},{4,5},{5,6},{6,7},{8,9},{9,10},{10,11},{12,13},{... | collective-permute-start | bytes 98312 | tf_op jit(solution)/shard_map/ppermute | solution.py:534
  54.4 7.6 %collective-permute-start.7 = (bf16[2,64,128]{2,1,0:T(8,128)(2,1)S(1)}, bf16[2,64,128]{2,1,0:T(8,128)(2,1)S(1)}, u32[]{:S(2)}, u32[]{:S(2)}) collective-permute-start(bf16[2,64,128]{2,1,0:T(8,128)(2,1)S(1)} %get-tuple-element.42), channel_id=1, source_target_pairs={{1,0},{2,1},{3,2},{5,4},{6,5},{7,6},{9,8},{10,9},{11,10},{13,12},{... | collective-permute-start | bytes 98312 | tf_op jit(solution)/shard_map/ppermute | solution.py:535
  56.5 15.8 %all-to-all-start.1 = ((bf16[32,32,128]{2,1,0:T(8,128)(2,1)}), bf16[32,32,128]{2,1,0:T(8,128)(2,1)S(1)}, u32[]{:S(2)}, u32[]{:S(2)}) async-start(bf16[32,32,128]{2,1,0:T(8,128)(2,1)} %broadcast_in_dim.24), calls=%async_computation.1 | async-start | bytes 524288 | tf_op jit(solution)/shard_map/all_to_all | solution.py:510

commit v7 on v6

--- a/solution.py
+++ b/solution.py
@@ -43,7 +43,7 @@
         return self.get(k)
 
 
-def columns_pass(dims, chunk, columns, block, rolled, w, wt, cot_at, put_value, wg_add, ig_add, ga, gb):
+def columns_pass(dims, chunk, columns, block, rolled, w, cot_at, put_value, put_foreign, wg_add, ga, gb):
     nx, ny, nz, ci, co = dims
     half = 4 * ci
     first = lax.broadcasted_iota(jnp.int32, (co, nz), 1) == 0
@@ -75,6 +75,14 @@
                     if not (0 <= m < nx and 0 <= n < ny):
                         ga[base : base + 2 * co, wide] = zeros
                         gb[base : base + 2 * co, wide] = zeros
+                        r = slice(base, base + co)
+                        put_foreign(
+                            (i, j, tx, ty), 0, back[r, cols] + jnp.where(first, 0.0, here[r, cols])
+                        )
+                        r = slice(base + co, base + 2 * co)
+                        put_foreign(
+                            (i, j, tx, ty), 1, jnp.where(first, 0.0, back[r, cols]) + here[r, cols]
+                        )
                         continue
                     for tz in range(2):
                         sz = 1 - tz
@@ -98,29 +106,54 @@
                         ga[r, wide] = cut if sz == 0 else whole
                         gb[r, wide] = cut if sz == 1 else whole
 
-    started = set()
-    for c0 in starts:
-        some = columns[c0 : c0 + chunk]
-        wide = slice(c0 * nz, (c0 + len(some)) * nz)
-        back = jnp.dot(wt[half:], ga[:, wide], preferred_element_type=F32)
-        here = jnp.dot(wt[:half], gb[:, wide], preferred_element_type=F32)
-        for k, (i, j) in enumerate(some):
-            cols = slice(k * nz, (k + 1) * nz)
-            both = here[:, cols] + pltpu.roll(back[:, cols], nz - 1, 1)
-            for ex in range(2):
-                for ey in range(2):
-                    r = (2 * ex + ey) * ci
-                    cell = (i - ex, j - ey)
-                    ig_add(cell[0], cell[1], both[r : r + ci], cell not in started)
-                    started.add(cell)
-
     nt = (((1,), (1,)), ((), ()))
     for part, (grads, get) in enumerate(((gb, block), (ga, rolled))):
         wg_add(
             part,
             lax.dot_general(grads[...], corners(get, columns), nt, preferred_element_type=F32),
         )
+
+
+def input_pass(dims, chunk, columns, wt, cut_grads, ig_add):
+    nx, ny, nz, ci, co = dims
+    half = 4 * ci
+    started = set()
+    for c0 in range(0, len(columns), chunk):
+        some = columns[c0 : c0 + chunk]
+        left, right = cut_grads(c0, some)
+        back = jnp.dot(wt[half:], left, preferred_element_type=F32)
+        here = jnp.dot(wt[:half], right, preferred_element_type=F32)
+        for k, (i, j) in enumerate(some):
+            cols = slice(k * nz, (k + 1) * nz)
+            both = here[:, cols] + pltpu.roll(back[:, cols], nz - 1, 1)
+            for ex in range(2):
+                for ey in range(2):
+                    m, y = i - ex, j - ey
+                    if 0 <= m < nx and 0 <= y < ny:
+                        r = (2 * ex + ey) * ci
+                        ig_add(m, y, both[r : r + ci], (m, y) not in started)
+                        started.add((m, y))
     return started
+
+
+def outer_columns(nx, ny):
+    columns = [(i, j) for i in (0, nx) for j in range(ny + 1)]
+    return columns + [(i, j) for i in range(1, nx) for j in (0, ny)]
+
+
+def foreign_spots(nx, ny):
+    spots = {}
+    for i, j in outer_columns(nx, ny):
+        for tx in range(2):
+            for ty in range(2):
+                m, n = i - 1 + tx, j - 1 + ty
+                if not (0 <= m < nx and 0 <= n < ny):
+                    spots[i, j, tx, ty] = len(spots)
+    return spots
+
+
+def is_inner(q, m, nx):
+    return 1 <= m + q // 4 < nx
 
 
 def edge_row(q, ny):
@@ -136,9 +169,13 @@
     flat,
     w,
     wt,
-    vals,
+    vals_out,
     cot_edge,
     wg,
+    ig_out,
+    face_up,
+    face_down,
+    vals,
     ig,
     vol,
     taps,
@@ -155,7 +192,11 @@
         pltpu.make_async_copy(vol_in, vol, sems.at[0]),
         pltpu.make_async_copy(taps_in, taps, sems.at[1]),
     ]
-    for copy in arriving:
+    leaving = [
+        pltpu.make_async_copy(cot.at[4:, :, nx - 1], face_up, sems.at[2]),
+        pltpu.make_async_copy(cot.at[:4, :, 0], face_down, sems.at[3]),
+    ]
+    for copy in arriving + leaving:
         copy.start()
 
     for i in range(1, nx):
@@ -218,10 +259,21 @@
         lanes = slice(y * nz, (y + 1) * nz)
         ig[m, :, lanes] = value if fresh else ig[m, :, lanes] + value
 
+    def cut_grads(c0, some):
+        wide = slice(c0 * nz, (c0 + len(some)) * nz)
+        return ga[:, wide], gb[:, wide]
+
     columns = [(i, j) for i in range(1, nx) for j in range(1, ny)]
     columns_pass(
-        dims, chunk, columns, block, rolled, w, wt, cot_at, put_value, wg_add, ig_add, ga, gb
+        dims, chunk, columns, block, rolled, w, cot_at, put_value, None, wg_add, ga, gb
     )
+    input_pass(dims, chunk, columns, wt, cut_grads, ig_add)
+    leaving.append(pltpu.make_async_copy(vals, vals_out, sems.at[4]))
+    leaving.append(pltpu.make_async_copy(ig, ig_out, sems.at[5]))
+    for copy in leaving[2:]:
+        copy.start()
+    for copy in leaving:
+        copy.wait()
 
 
 def outer_kernel(
@@ -233,42 +285,34 @@
     ylo_in,
     yhi_in,
     w,
-    wt,
     cot,
-    vals_in,
     cot_edge,
     wg_in,
-    ig_in,
-    act_out,
-    own_out,
-    up_out,
-    down_out,
     wg,
-    yface,
-    sides,
-    faces,
-    own,
+    ga_out,
+    gb_out,
+    pre_out,
+    vals_out,
+    val_edge_out,
     xraw,
     yraw,
     vm,
     ga,
     gb,
+    pre,
     cots,
     vals,
     val_edge,
-    staged,
     sems,
 ):
     nx, ny, nz, ci, co = dims
     half = 4 * ci
     to_y = swap_matrix(GROUP, ny)
-    to_c = swap_matrix(ny, GROUP)
-    spots = 8 * nx
     arriving = [
-        pltpu.make_async_copy(xlo_in, xraw.at[0], sems.at[spots]),
-        pltpu.make_async_copy(xhi_in, xraw.at[1], sems.at[spots + 1]),
-        pltpu.make_async_copy(ylo_in, yraw.at[0], sems.at[spots + 2]),
-        pltpu.make_async_copy(yhi_in, yraw.at[1], sems.at[spots + 3]),
+        pltpu.make_async_copy(xlo_in.at[: ny * ci], xraw.at[0], sems.at[0]),
+        pltpu.make_async_copy(xhi_in.at[: ny * ci], xraw.at[1], sems.at[1]),
+        pltpu.make_async_copy(ylo_in.at[: (nx + 2) * ci], yraw.at[0], sems.at[2]),
+        pltpu.make_async_copy(yhi_in.at[: (nx + 2) * ci], yraw.at[1], sems.at[3]),
     ]
     for copy in arriving:
         copy.start()
@@ -290,15 +334,16 @@
 
     for copy in arriving:
         copy.wait()
+
     def block(x, y):
         if y == 0:
-            return yraw[0, x]
+            return yraw[0, x * ci : (x + 1) * ci]
         if y == ny + 1:
-            return yraw[1, x]
+            return yraw[1, x * ci : (x + 1) * ci]
         if x == 0:
-            return xraw[0, y - 1]
+            return xraw[0, (y - 1) * ci : y * ci]
         if x == nx + 1:
-            return xraw[1, y - 1]
+            return xraw[1, (y - 1) * ci : y * ci]
         return flat[x - 1, :, (y - 1) * nz : y * nz]
 
     for x in range(nx + 2):
@@ -310,23 +355,36 @@
     def rolled(x, y):
         return vm[x, :, y * nz : (y + 1) * nz]
 
-    def inner(q, m):
-        return 1 <= m + q // 4 < nx
-
     def cot_at(q, m, n):
         r = slice(q * co, (q + 1) * co)
-        if inner(q, m):
+        if is_inner(q, m, nx):
             return cot_edge[m + q // 4 - 1, r]
         return cots[r, n * nz : (n + 1) * nz]
 
     def put_value(q, m, n, value):
         r = slice(q * co, (q + 1) * co)
-        if inner(q, m):
+        if is_inner(q, m, nx):
             val_edge[m + q // 4 - 1, r] = value
         else:
             vals[r, n * nz : (n + 1) * nz] = value
 
+    spots = foreign_spots(nx, ny)
+
+    def put_foreign(key, tz, value):
+        pre[spots[key], tz * co : (tz + 1) * co] = value
+
+    leaving = []
+
+    def leave():
+        for k, (src, dst) in enumerate(
+            ((ga, ga_out), (gb, gb_out), (pre, pre_out), (vals, vals_out), (val_edge, val_edge_out))
+        ):
+            leaving.append(pltpu.make_async_copy(src, dst, sems.at[4 + k]))
+            leaving[-1].start()
+
     def wg_add(part, total):
+        if part == 0:
+            leave()
         total = total + wg_in[:, part * half : (part + 1) * half]
         for ex in range(2):
             for row in range(8):
@@ -336,36 +394,81 @@
                     row * co : (row + 1) * co, ex * 2 * ci : (ex + 1) * 2 * ci
                 ].astype(BF16)
 
-    def ig_add(m, y, value, fresh):
-        if m < 0 or m >= nx:
-            side = 0 if m < 0 else 1
-            lanes = slice((y + 1) * nz, (y + 2) * nz)
-            faces[side, :, lanes] = value if fresh else faces[side, :, lanes] + value
-        elif y < 0 or y >= ny:
-            side = 0 if y < 0 else 1
-            yface[side, m] = value if fresh else yface[side, m] + value
-        else:
-            lanes = slice(y * nz, (y + 1) * nz)
-            own[m, :, lanes] = (ig_in if fresh else own)[m, :, lanes] + value
-
-    columns = [(i, j) for i in (0, nx) for j in range(ny + 1)]
-    columns += [(i, j) for i in range(1, nx) for j in (0, ny)]
-    started = columns_pass(
-        dims, chunk, columns, block, rolled, w, wt, cot_at, put_value, wg_add, ig_add, ga, gb
+    columns_pass(
+        dims,
+        chunk,
+        outer_columns(nx, ny),
+        block,
+        rolled,
+        w,
+        cot_at,
+        put_value,
+        put_foreign,
+        wg_add,
+        ga,
+        gb,
     )
-    for m in range(nx):
-        for y in range(ny):
-            if (m, y) not in started:
-                lanes = slice(y * nz, (y + 1) * nz)
-                own[m, :, lanes] = ig_in[m, :, lanes]
-    sides[...] = faces[...].astype(BF16)
+    for copy in leaving:
+        copy.wait()
+
+
+def last_kernel(
+    dims,
+    chunk,
+    ga_in,
+    gb_in,
+    pre_in,
+    vals_in,
+    val_edge_in,
+    xlo_in,
+    xhi_in,
+    ylo_in,
+    yhi_in,
+    wt_in,
+    inner_vals_in,
+    ig_in,
+    act_out,
+    ig_out,
+    ga,
+    gb,
+    pre,
+    vals,
+    val_edge,
+    xraw,
+    yraw,
+    wt,
+    inner_vals,
+    ig,
+    cots,
+    staged,
+    ig_staged,
+    sems,
+):
+    nx, ny, nz, ci, co = dims
+    to_y = swap_matrix(GROUP, ny)
+    to_c = swap_matrix(ny, GROUP)
+    skip = (nx + 2) * ci
+    early = [(vals_in, vals), (val_edge_in, val_edge), (inner_vals_in, inner_vals)]
+    late = [
+        (xlo_in, xraw.at[0]),
+        (xhi_in, xraw.at[1]),
+        (ylo_in.at[skip:], yraw.at[0]),
+        (yhi_in.at[skip:], yraw.at[1]),
+        (ga_in, ga),
+        (gb_in, gb),
+        (pre_in, pre),
+        (wt_in, wt),
+        (ig_in, ig),
+    ]
     copies = [
-        pltpu.make_async_copy(own, own_out, sems.at[spots]),
-        pltpu.make_async_copy(sides.at[0], down_out, sems.at[spots + 1]),
-        pltpu.make_async_copy(sides.at[1], up_out, sems.at[spots + 2]),
+        pltpu.make_async_copy(src, dst, sems.at[k]) for k, (src, dst) in enumerate(early + late)
     ]
     for copy in copies:
         copy.start()
+    spot = len(copies)
+    for copy in copies[: len(early)]:
+        copy.wait()
+    leaving = []
 
     for m in range(nx):
         for q in range(8):
@@ -375,23 +478,111 @@
                 rows = []
                 for y in range(ny):
                     lanes = slice(y * nz, (y + 1) * nz)
-                    if not inner(q, m):
+                    if not is_inner(q, m, nx):
                         rows.append(vals[r, lanes])
                     elif y == edge_row(q, ny):
                         rows.append(val_edge[m + q // 4 - 1, r])
                     else:
-                        rows.append(vals_in[m + q // 4 - 1, r, lanes])
+                        rows.append(inner_vals[m + q // 4 - 1, r, lanes])
                 tiles.append(jnp.concatenate(rows, axis=0).reshape(ny, GROUP, nz))
             moved = turn(to_c, tiles, nz)
-            spot = m * 8 + q
+            index = m * 8 + q
             for k in range(co // GROUP):
-                staged[spot, k * GROUP : (k + 1) * GROUP] = moved[
+                staged[index, k * GROUP : (k + 1) * GROUP] = moved[
                     :, k * nz : (k + 1) * nz
                 ].reshape(GROUP, ny, nz)
-            copy = pltpu.make_async_copy(staged.at[spot], act_out.at[q, :, m], sems.at[spot])
-            copy.start()
-            copies.append(copy)
-    for copy in copies:
+            leaving.append(
+                pltpu.make_async_copy(
+                    staged.at[index], act_out.at[q, :, m], sems.at[spot + index]
+                )
+            )
+            leaving[-1].start()
+
+    for copy in copies[len(early) :]:
+        copy.wait()
+    for side in range(2):
+        for p in range(4):
+
+            def put(k, y, rows, side=side, p=p):
+                r = slice(p * co + k * GROUP, p * co + (k + 1) * GROUP)
+                cots[side, r, y * nz : (y + 1) * nz] = rows
+
+            tiles = Tiles(
+                co // GROUP,
+                lambda k, side=side, p=p: xraw[side, p, k * GROUP : (k + 1) * GROUP],
+            )
+            bring_plane(to_y, tiles, ny, nz, put)
+
+    spots = foreign_spots(nx, ny)
+    first = lax.broadcasted_iota(jnp.int32, (co, nz), 1) == 0
+    corner = 4 * co * nx
+
+    def foreign(i, j, tx, ty, tz):
+        sx, sy, sz = 1 - tx, 1 - ty, 1 - tz
+        m, n = i - sx, j - sy
+        if 0 <= n < ny:
+            side = 0 if m < 0 else 1
+            r = (2 * sy + sz) * co
+            cot = cots[side, r : r + co, n * nz : (n + 1) * nz]
+        else:
+            end = 0 if n < 0 else 1
+            if 0 <= m < nx:
+                r = ((m * 2 + sx) * 2 + sz) * co
+            else:
+                r = corner + ((0 if m < 0 else 2) + sz) * co
+            cot = yraw[end, r : r + co]
+        cot = cot.astype(F32)
+        if sz == 1:
+            cot = pltpu.roll(cot, 1, 1)
+        before = pre[spots[i, j, tx, ty], tz * co : (tz + 1) * co]
+        sig = 0.5 * jnp.tanh(0.5 * before) + 0.5
+        grad = cot * (sig + before * sig * (1.0 - sig))
+        whole = grad.astype(BF16)
+        cut = jnp.where(first, 0.0, grad).astype(BF16)
+        return (whole, cut) if sz == 1 else (cut, whole)
+
+    def cut_grads(c0, some):
+        lefts, rights = [], []
+        for k, (i, j) in enumerate(some):
+            wide = slice((c0 + k) * nz, (c0 + k + 1) * nz)
+            left, right = [], []
+            for tx in range(2):
+                for ty in range(2):
+                    base = (2 * tx + ty) * 2 * co
+                    if (i, j, tx, ty) in spots:
+                        for tz in range(2):
+                            one, two = foreign(i, j, tx, ty, tz)
+                            left.append(one)
+                            right.append(two)
+                    else:
+                        left.append(ga[base : base + 2 * co, wide])
+                        right.append(gb[base : base + 2 * co, wide])
+            lefts.append(jnp.concatenate(left, axis=0))
+            rights.append(jnp.concatenate(right, axis=0))
+        return jnp.concatenate(lefts, axis=1), jnp.concatenate(rights, axis=1)
+
+    def ig_add(m, y, value, fresh):
+        lanes = slice(y * nz, (y + 1) * nz)
+        ig[m, :, lanes] = ig[m, :, lanes] + value
+
+    input_pass(dims, chunk, outer_columns(nx, ny), wt, cut_grads, ig_add)
+    for m in range(nx):
+        for k in range(0, ci // GROUP, 2):
+            tiles = []
+            for h in range(2):
+                r = slice((k + h) * GROUP, (k + h + 1) * GROUP)
+                rows = [
+                    ig[m, r, y * nz : (y + 1) * nz].astype(BF16) for y in range(ny)
+                ]
+                tiles.append(jnp.concatenate(rows, axis=0).reshape(ny, GROUP, nz))
+            moved = turn(to_c, tiles, nz)
+            for h in range(2):
+                ig_staged[(k + h) * GROUP : (k + h + 1) * GROUP, m] = moved[
+                    :, h * nz : (h + 1) * nz
+                ].reshape(GROUP, ny, nz)
+    leaving.append(pltpu.make_async_copy(ig_staged, ig_out, sems.at[spot + 8 * nx]))
+    leaving[-1].start()
+    for copy in leaving:
         copy.wait()
 
 
@@ -424,9 +615,18 @@
     cells = nx * gx * ny * gy * nz
     dims = (nx, ny, nz, ci, co)
 
-    xlo = lax.ppermute(volume[:, nx - 1].transpose(1, 0, 2), "gx", gx_up)
-    xhi = lax.ppermute(volume[:, 0].transpose(1, 0, 2), "gx", gx_down)
     cot = cotangent.reshape(8, co, nx, ny, nz)
+
+    def corner(sx, sy):
+        m, n = (nx - 1) * sx, (ny - 1) * sy
+        return cotangent[sx, sy, :, :, m, n].reshape(2 * co, nz)
+
+    def x_message(sx):
+        plane = volume[:, (nx - 1) * sx].transpose(1, 0, 2).reshape(ny * ci, nz)
+        return jnp.concatenate([plane, corner(sx, 0), corner(sx, 1)], axis=0)
+
+    xlo = lax.ppermute(x_message(1), "gx", gx_up)
+    xhi = lax.ppermute(x_message(0), "gx", gx_down)
 
     vmem = pl.BlockSpec(memory_space=pltpu.VMEM)
     smem = pl.BlockSpec(memory_space=pltpu.SMEM)
@@ -434,7 +634,7 @@
     params = pltpu.CompilerParams(vmem_limit_bytes=28 * 1024 * 1024)
     n_in = (nx - 1) * (ny - 1)
     n_out = 2 * (ny + 1) + 2 * (nx - 1)
-    flat, w, wt, vals, cot_edge, wg_part, ig_part = pl.pallas_call(
+    flat, w, wt, vals, cot_edge, wg_part, ig_part, face_up, face_down = pl.pallas_call(
         functools.partial(inner_kernel, dims, 5),
         out_shape=(
             jax.ShapeDtypeStruct((nx, ci, ny * nz), BF16),
@@ -444,13 +644,17 @@
             jax.ShapeDtypeStruct((nx - 1, 8 * co, nz), BF16),
             jax.ShapeDtypeStruct((8 * co, 8 * ci), F32),
             jax.ShapeDtypeStruct((nx, ci, ny * nz), F32),
+            jax.ShapeDtypeStruct((4, co, ny, nz), BF16),
+            jax.ShapeDtypeStruct((4, co, ny, nz), BF16),
         ),
         in_specs=[anywhere, anywhere, vmem],
-        out_specs=(vmem,) * 7,
+        out_specs=(vmem,) * 3 + (anywhere,) + (vmem,) * 2 + (anywhere,) * 3,
         scratch_shapes=[
+            pltpu.VMEM((nx - 1, 8 * co, ny * nz), BF16),
+            pltpu.VMEM((nx, ci, ny * nz), F32),
             pltpu.VMEM(volume.shape, BF16),
             pltpu.VMEM(kernel.shape, BF16),
-            pltpu.SemaphoreType.DMA((2,)),
+            pltpu.SemaphoreType.DMA((6,)),
             pltpu.VMEM((nx, ci, ny * nz), BF16),
             pltpu.VMEM((8 * co, n_in * nz), BF16),
             pltpu.VMEM((8 * co, n_in * nz), BF16),
@@ -459,47 +663,74 @@
         compiler_params=params,
     )(volume, kernel, cot)
 
-    def y_row(y):
+    def y_message(sy):
+        y = (ny - 1) * sy
+        rows = slice(y * ci, (y + 1) * ci)
+        own = cotangent[:, sy, :, :, :, y].transpose(3, 0, 1, 2, 4).reshape(4 * co * nx, nz)
+        corner = slice((ny * ci + sy * 2 * co), (ny * ci + (sy + 1) * 2 * co))
         return jnp.concatenate(
             [
-                xlo[y : y + 1],
-                flat[:, :, y * nz : (y + 1) * nz],
-                xhi[y : y + 1],
+                xlo[rows],
+                flat[:, :, y * nz : (y + 1) * nz].reshape(nx * ci, nz),
+                xhi[rows],
+                own,
+                xlo[corner],
+                xhi[corner],
             ],
             axis=0,
         )
 
-    ylo = lax.ppermute(y_row(ny - 1), "gy", gy_up)
-    yhi = lax.ppermute(y_row(0), "gy", gy_down)
-    act, own, up, down, wg, yface = pl.pallas_call(
+    ylo = lax.ppermute(y_message(1), "gy", gy_up)
+    yhi = lax.ppermute(y_message(0), "gy", gy_down)
+    face_lo = lax.ppermute(face_up, "gx", gx_up)
+    face_hi = lax.ppermute(face_down, "gx", gx_down)
+    foreign = len(foreign_spots(nx, ny))
+    kept = (
+        jax.ShapeDtypeStruct((8 * co, n_out * nz), BF16),
+        jax.ShapeDtypeStruct((8 * co, n_out * nz), BF16),
+        jax.ShapeDtypeStruct((foreign, 2 * co, nz), F32),
+        jax.ShapeDtypeStruct((8 * co, ny * nz), BF16),
+        jax.ShapeDtypeStruct((nx - 1, 8 * co, nz), BF16),
+    )
+    held = [pltpu.VMEM(k.shape, k.dtype) for k in kept]
+    wg, *passed = pl.pallas_call(
         functools.partial(outer_kernel, dims, 4),
+        out_shape=(jax.ShapeDtypeStruct((32, co, 2 * ci), BF16),) + kept,
+        in_specs=[vmem] + [anywhere] * 4 + [vmem] * 4,
+        out_specs=(vmem,) + (anywhere,) * 5,
+        scratch_shapes=[
+            pltpu.VMEM((2, ny * ci, nz), BF16),
+            pltpu.VMEM((2, (nx + 2) * ci, nz), BF16),
+            pltpu.VMEM((nx + 2, ci, (ny + 2) * nz), BF16),
+        ]
+        + held[:3]
+        + [pltpu.VMEM((8 * co, ny * nz), BF16)]
+        + held[3:]
+        + [pltpu.SemaphoreType.DMA((9,))],
+        compiler_params=params,
+    )(flat, xlo, xhi, ylo, yhi, w, cot, cot_edge, wg_part)
+    act, input_grad = pl.pallas_call(
+        functools.partial(last_kernel, dims, 4),
         out_shape=(
             jax.ShapeDtypeStruct(cot.shape, BF16),
-            jax.ShapeDtypeStruct((nx, ci, ny * nz), F32),
-            jax.ShapeDtypeStruct((ci, (ny + 2) * nz), BF16),
-            jax.ShapeDtypeStruct((ci, (ny + 2) * nz), BF16),
-            jax.ShapeDtypeStruct((32, co, 2 * ci), BF16),
-            jax.ShapeDtypeStruct((2, nx, ci, nz), F32),
+            jax.ShapeDtypeStruct(volume.shape, BF16),
         ),
-        in_specs=[vmem] + [anywhere] * 4 + [vmem] * 7,
-        out_specs=(anywhere,) * 4 + (vmem,) * 2,
-        scratch_shapes=[
-            pltpu.VMEM((2, ci, (ny + 2) * nz), BF16),
-            pltpu.VMEM((2, ci, (ny + 2) * nz), F32),
+        in_specs=[anywhere] * 12,
+        out_specs=(anywhere,) * 2,
+        scratch_shapes=held
+        + [
+            pltpu.VMEM((2, 4, co, ny, nz), BF16),
+            pltpu.VMEM((2, 4 * co * nx + 4 * co, nz), BF16),
+            pltpu.VMEM((8 * ci, 8 * co), BF16),
+            pltpu.VMEM((nx - 1, 8 * co, ny * nz), BF16),
             pltpu.VMEM((nx, ci, ny * nz), F32),
-            pltpu.VMEM((2, ny, ci, nz), BF16),
-            pltpu.VMEM((2, nx + 2, ci, nz), BF16),
-            pltpu.VMEM((nx + 2, ci, (ny + 2) * nz), BF16),
-            pltpu.VMEM((8 * co, n_out * nz), BF16),
-            pltpu.VMEM((8 * co, n_out * nz), BF16),
-            pltpu.VMEM((8 * co, ny * nz), BF16),
-            pltpu.VMEM((8 * co, ny * nz), BF16),
-            pltpu.VMEM((nx - 1, 8 * co, nz), BF16),
+            pltpu.VMEM((2, 4 * co, ny * nz), BF16),
             pltpu.VMEM((8 * nx, co, ny, nz), BF16),
-            pltpu.SemaphoreType.DMA((8 * nx + 4,)),
+            pltpu.VMEM(volume.shape, BF16),
+            pltpu.SemaphoreType.DMA((13 + 8 * nx,)),
         ],
         compiler_params=params,
-    )(flat, xlo, xhi, ylo, yhi, w, wt, cot, vals, cot_edge, wg_part, ig_part)
+    )(*passed, face_lo, face_hi, ylo, yhi, wt, vals, ig_part)
 
     scale = 1.0 / math.sqrt(cells)
     devices = gx * gy
@@ -516,30 +747,6 @@
         compiler_params=pltpu.CompilerParams(vmem_limit_bytes=8 * 1024 * 1024),
     )(pieces.reshape(32, co, 2 * ci))
 
-    from_low = lax.ppermute(up, "gx", gx_up).astype(F32)[None]
-    from_high = lax.ppermute(down, "gx", gx_down).astype(F32)[None]
-
-    def add_x(array, lanes):
-        lead = (nx - 1,) + from_low[:, :, lanes].shape[1:]
-        zero = jnp.zeros(lead, F32)
-        return (
-            array
-            + jnp.concatenate([from_low[:, :, lanes], zero], axis=0)
-            + jnp.concatenate([zero, from_high[:, :, lanes]], axis=0)
-        )
-
-    later = 0.0 * piece[0, 0].astype(F32)
-    send_low = (add_x(yface[0], slice(0, nz)) + later).astype(BF16)
-    send_high = (add_x(yface[1], slice((ny + 1) * nz, None)) + later).astype(BF16)
-    y_low = lax.ppermute(send_high, "gy", gy_up).astype(F32)
-    y_high = lax.ppermute(send_low, "gy", gy_down).astype(F32)
-    gap = jnp.zeros((nx, ci, (ny - 1) * nz), F32)
-    total_ig = (
-        add_x(own, slice(nz, (ny + 1) * nz))
-        + jnp.concatenate([y_low, gap], axis=2)
-        + jnp.concatenate([gap, y_high], axis=2)
-    )
-    input_grad = total_ig.astype(BF16).reshape(nx, ci, ny, nz).transpose(1, 0, 2, 3)
     return act.reshape(cotangent.shape), input_grad, weight_grad
 
 

time: 74 us -> 79.8 us (1.078)
  local copies, waits for them, and re-layouts: 5.74 us -> 20.1 us
  waiting for transfers between devices: 21 us -> 10.9 us
  Pallas kernels: 12.7 us -> 17.3 us
  starting transfers between devices: 32 us -> 28.8 us
    unnamed x9 -> x54, local copies, waits for them, and re-layouts: 2.33 us -> 16.4 us
    all_to_all x1, waiting for transfers between devices: 9.25 us -> 0.01 us  [on_device(): pieces = lax.all_to_all(pieces, ('gx', 'gy'), 0, 0, tiled=True)]
    pallas_call x0 -> x1, Pallas kernels: none -> 5.37 us  [on_device(): pl.pallas_call(functools.partial(last_kernel, dims, 4), out_shape=(jax.Sh...]
    ppermute x8 -> x6, starting transfers between devices: 22.1 us -> 17.2 us  [the longest x1 4.51 us: on_device(): xlo = lax.ppermute(x_message(1), 'gx', gx_up)]
    ppermute x8 -> x6, waiting for transfers between devices: 10.8 us -> 5.98 us  [the longest x1 3.44 us: on_device(): face_hi = lax.ppermute(face_down, 'gx', gx_down)]
    all_to_all x1, waiting for transfers between devices: 0.97 us -> 4.91 us  [on_device(): shares = lax.all_to_all(shares, ('gx', 'gy'), 0, 0, tiled=True)]
    all_to_all x1, starting transfers between devices: 4.55 us -> 8.37 us  [on_device(): shares = lax.all_to_all(shares, ('gx', 'gy'), 0, 0, tiled=True)]
    all_to_all x1, starting transfers between devices: 5.41 us -> 3.23 us  [on_device(): pieces = lax.all_to_all(pieces, ('gx', 'gy'), 0, 0, tiled=True)]
  transfers between devices with their start and end apart: 10 -> 8, of which waited for: 4 -> 5; matrix products, arithmetic and copies ran while one was open for 3% -> 3% of each run, Pallas kernels for 5% -> 12%
where the time goes in v7:
time: 79.8 us; the launch traced here: 79 us
  starting transfers between devices  28.8 us (36%)
  local copies, waits for them, and re-layouts  20.1 us (25%)
  Pallas kernels  17.3 us (22%)
  waiting for transfers between devices  10.9 us (14%)
  other arithmetic  1.05 us (1%)
  between operations  0.98 us (1%)
    unnamed x54, local copies, waits for them, and re-layouts  16.4 us
    all_to_all x1, starting transfers between devices, on_device(): shares = lax.all_to_all(shares, ('gx', 'gy'), 0, 0, tiled=True)  8.37 us
    pallas_call x1, Pallas kernels, on_device(): pl.pallas_call(functools.partial(outer_kernel, dims, 4), out_shape=(jax.S...  5.87 us
    pallas_call x1, Pallas kernels, on_device(): pl.pallas_call(functools.partial(last_kernel, dims, 4), out_shape=(jax.Sh...  5.37 us
    all_to_all x1, waiting for transfers between devices, on_device(): shares = lax.all_to_all(shares, ('gx', 'gy'), 0, 0, tiled=True)  4.91 us
    ppermute x1, starting transfers between devices, on_device(): xlo = lax.ppermute(x_message(1), 'gx', gx_up)  4.51 us
    ppermute x1, starting transfers between devices, on_device(): ylo = lax.ppermute(y_message(1), 'gy', gy_up)  4 us
    pallas_call x1, Pallas kernels, on_device(): pl.pallas_call(functools.partial(inner_kernel, dims, 5), out_shape=(jax.S...  3.97 us
  transfers between devices with their start and end apart: 8, of which 5 were waited for; matrix products, arithmetic and copies ran while one was open for 3% of the time, Pallas kernels for 12%

profile of v7, /device:TPU:1, one launch (start us, length us, event | category | flops | bytes accessed | tf_op | source)
XLA Modules:
  0.0 79.0 jit_solution(16499011947787308786)
XLA Ops:
  0.6 1.4 %fusion.1 = (bf16[1,1,2,32,1,1,128]{6,5,4,3,2,1,0:T(2,128)(2,1)S(1)}, bf16[1,1,2,32,1,1,128]{6,5,4,3,2,1,0:T(2,128)(2,1)S(1)}, bf16[1,1,2,32,1,1,128]{6,5,4,3,2,...) fusion(bf16[2,2,2,32,2,16,128]{6,5,4,3,2,1,0:T(8,128)(2,1)} %param.5), kind=kLoop, calls=%fused_computation.19 | loop fusion | bytes 131072 | tf_op jit(solution)/shard_map/slice | solution.py:622
  2.1 1.2 %slice_bitcast_fusion = (bf16[16,64,128]{2,0,1:T(8,128)(2,1)S(1)}, bf16[16,64,128]{2,0,1:T(8,128)(2,1)S(1)}) fusion(bf16[64,2,16,128]{3,2,1,0:T(8,128)(2,1)} %vol_in.1), kind=kLoop, calls=%fused_computation.3 | loop fusion | bytes 1048576 | tf_op jit(solution)/shard_map/transpose | solution.py:625
  3.3 4.5 %collective-permute-start = (bf16[1152,128]{1,0:T(8,128)(2,1)S(1)}, bf16[1152,128]{1,0:T(8,128)(2,1)S(1)}, u32[]{:S(2)}, u32[]{:S(2)}) collective-permute-start(bf16[1152,128]{1,0:T(8,128)(2,1)S(1)} %pad_maximum_fusion), channel_id=1, source_target_pairs={{0,4},{4,8},{8,12},{12,16},{16,20},{20,24},{24,28},{1,5},{5,9},{9,... | collective-permute-start | bytes 884744 | tf_op jit(solution)/shard_map/ppermute | solution.py:628
  8.0 1.9 %collective-permute-start.1 = (bf16[1152,128]{1,0:T(8,128)(2,1)S(1)}, bf16[1152,128]{1,0:T(8,128)(2,1)S(1)}, u32[]{:S(2)}, u32[]{:S(2)}) collective-permute-start(bf16[1152,128]{1,0:T(8,128)(2,1)S(1)} %pad_maximum_fusion.1), channel_id=1, source_target_pairs={{4,0},{8,4},{12,8},{16,12},{20,16},{24,20},{28,24},{5,1},{9,5},{13... | collective-permute-start | bytes 884744 | tf_op jit(solution)/shard_map/ppermute | solution.py:629
  10.2 4.0 %shard_map.58 = (bf16[2,64,2048]{2,1,0:T(8,128)(2,1)S(1)}, bf16[256,512]{1,0:T(8,128)(2,1)S(1)}, bf16[512,256]{1,0:T(8,128)(2,1)S(1)}, bf16[1,256,2048]{2,1,0:T(...) custom-call(bf16[64,2,16,128]{3,2,1,0:T(8,128)(2,1)S(1)} %copy-done., ...), custom_call_target="tpu_custom_call" | custom-call | tf_op jit(solution)/shard_map/pallas_call | solution.py:637
  14.2 1.0 %copy-done.6 = f32[2,64,2048]{2,1,0:T(8,128)} copy-done((f32[2,64,2048]{2,1,0:T(8,128)}, f32[2,64,2048]{2,1,0:T(8,128)S(1)}, u32[]{:S(2)}) %copy-start.6) | copy-done | bytes 1048600
  15.1 0.8 %copy-done.21 = bf16[4,32,16,128]{3,2,1,0:T(8,128)(2,1)} copy-done((bf16[4,32,16,128]{3,2,1,0:T(8,128)(2,1)}, bf16[4,32,16,128]{3,2,1,0:T(8,128)(2,1)S(1)}, u32[]{:S(2)}) %copy-start.21) | copy-done | bytes 524312
  16.4 1.3 %collective-permute-start.3 = (bf16[640,128]{1,0:T(8,128)(2,1)S(1)}, bf16[640,128]{1,0:T(8,128)(2,1)S(1)}, u32[]{:S(2)}, u32[]{:S(2)}) collective-permute-start(bf16[640,128]{1,0:T(8,128)(2,1)S(1)} %get-tuple-element.47), channel_id=1, source_target_pairs={{1,0},{2,1},{3,2},{5,4},{6,5},{7,6},{9,8},{10,9},{11,10},{13,12},{... | collective-permute-start | bytes 491528 | tf_op jit(solution)/shard_map/ppermute | solution.py:684
  17.7 4.0 %collective-permute-start.2 = (bf16[640,128]{1,0:T(8,128)(2,1)S(1)}, bf16[640,128]{1,0:T(8,128)(2,1)S(1)}, u32[]{:S(2)}, u32[]{:S(2)}) collective-permute-start(bf16[640,128]{1,0:T(8,128)(2,1)S(1)} %get-tuple-element.48), channel_id=1, source_target_pairs={{0,1},{1,2},{2,3},{4,5},{5,6},{6,7},{8,9},{9,10},{10,11},{12,13},{... | collective-permute-start | bytes 491528 | tf_op jit(solution)/shard_map/ppermute | solution.py:683
  21.7 0.8 collective-permute-done.3.yhi_in
  22.4 1.5 %collective-permute-done.2.ylo_in = bf16[640,128]{1,0:T(8,128)(2,1)S(1)} collective-permute-done((bf16[640,128]{1,0:T(8,128)(2,1)S(1)}, bf16[640,128]{1,0:T(8,128)(2,1)S(1)}, u32[]{:S(2)}, u32[]{:S(2)}) %collective-permute-start.2) | collective-permute-done | bytes 163872 | tf_op jit(solution)/shard_map/ppermute | solution.py:683
  23.9 5.9 %shard_map.59 = (bf16[32,32,128]{2,1,0:T(8,128)(2,1)S(1)}, bf16[256,4608]{1,0:T(8,128)(2,1)S(1)}, bf16[256,4608]{1,0:T(8,128)(2,1)S(1)}, f32[76,64,128]{2,1,0:T(...) custom-call(bf16[2,64,2048]{2,1,0:T(8,128)(2,1)S(1)} %get-tuple-element.20.flat, ...), custom_call_target="tpu_custom_call" | custom-call | tf_op jit(solution)/shard_map/pallas_call | solution.py:696
  29.8 1.4 %copy-done.1 = bf16[256,4608]{1,0:T(8,128)(2,1)} copy-done((bf16[256,4608]{1,0:T(8,128)(2,1)}, bf16[256,4608]{1,0:T(8,128)(2,1)S(1)}, u32[]{:S(2)}) %copy-start.1) | copy-done | bytes 2359320
  31.2 1.4 %copy-done.3 = bf16[256,4608]{1,0:T(8,128)(2,1)} copy-done((bf16[256,4608]{1,0:T(8,128)(2,1)}, bf16[256,4608]{1,0:T(8,128)(2,1)S(1)}, u32[]{:S(2)}) %copy-start.3) | copy-done | bytes 2359320
  32.7 1.0 %copy-done.8 = bf16[256,2048]{1,0:T(8,128)(2,1)} copy-done((bf16[256,2048]{1,0:T(8,128)(2,1)}, bf16[256,2048]{1,0:T(8,128)(2,1)S(1)}, u32[]{:S(2)}) %copy-start.8) | copy-done | bytes 1048600
  35.0 8.4 %all-to-all-start = ((bf16[32,32,128]{2,1,0:T(8,128)(2,1)}), bf16[32,32,128]{2,1,0:T(8,128)(2,1)}, u32[]{:S(2)}, u32[]{:S(2)}) async-start(bf16[32,32,128]{2,1,0:T(8,128)(2,1)} %copy-done.17), calls=%async_computation | async-start | bytes 524288 | tf_op jit(solution)/shard_map/all_to_all | solution.py:738
  43.3 3.5 %collective-permute-start.4 = (bf16[4,32,16,128]{3,2,1,0:T(8,128)(2,1)}, bf16[4,32,16,128]{3,2,1,0:T(8,128)(2,1)}, u32[]{:S(2)}, u32[]{:S(2)}) collective-permute-start(bf16[4,32,16,128]{3,2,1,0:T(8,128)(2,1)} %copy-done.21), channel_id=1, source_target_pairs={{0,4},{4,8},{8,12},{12,16},{16,20},{20,24},{24,28},{1,5},{5,9},{9,... | collective-permute-start | bytes 1572872 | tf_op jit(solution)/shard_map/ppermute | solution.py:685
  46.9 1.9 %collective-permute-start.5 = (bf16[4,32,16,128]{3,2,1,0:T(8,128)(2,1)}, bf16[4,32,16,128]{3,2,1,0:T(8,128)(2,1)}, u32[]{:S(2)}, u32[]{:S(2)}) collective-permute-start(bf16[4,32,16,128]{3,2,1,0:T(8,128)(2,1)} %copy-done.20), channel_id=1, source_target_pairs={{4,0},{8,4},{12,8},{16,12},{20,16},{24,20},{28,24},{5,1},{9,5},{13... | collective-permute-start | bytes 1572872 | tf_op jit(solution)/shard_map/ppermute | solution.py:686
  48.8 4.9 %all-to-all-done = bf16[32,32,128]{2,1,0:T(8,128)(2,1)} async-done(((bf16[32,32,128]{2,1,0:T(8,128)(2,1)}), bf16[32,32,128]{2,1,0:T(8,128)(2,1)}, u32[]{:S(2)}, u32[]{:S(2)}) %all-to-all-start) | async-done | bytes 262176 | tf_op jit(solution)/shard_map/all_to_all | solution.py:738
  53.7 1.0 %convert_reduce_fusion = f32[32,128]{1,0:T(8,128)S(1)} fusion(bf16[32,32,128]{2,1,0:T(8,128)(2,1)} %all-to-all-done), kind=kLoop, calls=%fused_computation | loop fusion | flops 258048 | bytes 278528 | tf_op jit(solution)/shard_map/reduce_sum | solution.py:739
  55.5 3.2 %all-to-all-start.1 = ((bf16[32,32,128]{2,1,0:T(8,128)(2,1)}), bf16[32,32,128]{2,1,0:T(8,128)(2,1)}, u32[]{:S(2)}, u32[]{:S(2)}) async-start(bf16[32,32,128]{2,1,0:T(8,128)(2,1)} %broadcast_in_dim.2), calls=%async_computation.1 | async-start | bytes 524288 | tf_op jit(solution)/shard_map/all_to_all | solution.py:741
  58.7 3.4 %collective-permute-done.5.xhi_in = bf16[4,32,16,128]{3,2,1,0:T(8,128)(2,1)} collective-permute-done((bf16[4,32,16,128]{3,2,1,0:T(8,128)(2,1)}, bf16[4,32,16,128]{3,2,1,0:T(8,128)(2,1)}, u32[]{:S(2)}, u32[]{:S(2)}) %collective-permute-start.5) | collective-permute-done | bytes 524320 | tf_op jit(solution)/shard_map/ppermute | solution.py:686
  62.2 1.7 %copy-done.2 = bf16[256,4608]{1,0:T(8,128)(2,1)S(1)} copy-done((bf16[256,4608]{1,0:T(8,128)(2,1)S(1)}, bf16[256,4608]{1,0:T(8,128)(2,1)}, u32[]{:S(2)}) %copy-start.2) | copy-done | bytes 2359320
  63.8 1.7 %copy-done.4 = bf16[256,4608]{1,0:T(8,128)(2,1)S(1)} copy-done((bf16[256,4608]{1,0:T(8,128)(2,1)S(1)}, bf16[256,4608]{1,0:T(8,128)(2,1)}, u32[]{:S(2)}) %copy-start.4) | copy-done | bytes 2359320
  65.5 1.2 %copy-done.7 = f32[2,64,2048]{2,1,0:T(8,128)S(1)} copy-done((f32[2,64,2048]{2,1,0:T(8,128)S(1)}, f32[2,64,2048]{2,1,0:T(8,128)}, u32[]{:S(2)}) %copy-start.7) | copy-done | bytes 1048600
  66.7 1.2 %copy-done.9 = bf16[256,2048]{1,0:T(8,128)(2,1)S(1)} copy-done((bf16[256,2048]{1,0:T(8,128)(2,1)S(1)}, bf16[256,2048]{1,0:T(8,128)(2,1)}, u32[]{:S(2)}) %copy-start.9) | copy-done | bytes 1048600
  68.0 0.9 %copy-done.11 = bf16[640,128]{1,0:T(8,128)(2,1)S(1)} copy-done((bf16[640,128]{1,0:T(8,128)(2,1)S(1)}, bf16[640,128]{1,0:T(8,128)(2,1)}, u32[]{:S(2)}) %copy-start.11) | copy-done | bytes 163864
  68.9 0.9 %copy-done.13 = bf16[640,128]{1,0:T(8,128)(2,1)S(1)} copy-done((bf16[640,128]{1,0:T(8,128)(2,1)S(1)}, bf16[640,128]{1,0:T(8,128)(2,1)}, u32[]{:S(2)}) %copy-start.13) | copy-done | bytes 163864
  69.8 0.9 %copy-done.16 = bf16[512,256]{1,0:T(8,128)(2,1)S(1)} copy-done((bf16[512,256]{1,0:T(8,128)(2,1)S(1)}, bf16[512,256]{1,0:T(8,128)(2,1)}, u32[]{:S(2)}) %copy-start.16) | copy-done | bytes 262168
  70.7 0.8 %copy-done.19 = bf16[1,256,128]{2,1,0:T(8,128)(2,1)S(1)} copy-done((bf16[1,256,128]{2,1,0:T(8,128)(2,1)S(1)}, bf16[1,256,128]{2,1,0:T(8,128)(2,1)}, u32[]{:S(2)}) %copy-start.19) | copy-done | bytes 65560
  71.6 5.4 %shard_map.60 = (bf16[8,32,2,16,128]{4,3,2,1,0:T(8,128)(2,1)}, bf16[64,2,16,128]{3,2,1,0:T(8,128)(2,1)}) custom-call(bf16[256,4608]{1,0:T(8,128)(2,1)S(1)} %copy-done.2, bf16[256,4608]{1,0:T(8,128)(2,1)S(1)} %copy-done.4, f32[76,64,128]{2,1,0:T(8,128)S(1)} %get-tuple-element.26.pre_in, bf16[256,2048]{1,0:T(8,128)(2,1)S(1)} %copy-done.9, ...), custom_call_target="tpu_custom_call" | custom-call | tf_op jit(solution)/shard_map/pallas_call | solution.py:712
  77.0 2.1 %shard_map.61 = f32[4,4,4,32,64]{4,3,2,1,0:T(8,128)} custom-call(bf16[32,32,128]{2,1,0:T(8,128)(2,1)} %all-to-all-done.1.packed), custom_call_target="tpu_custom_call" | custom-call | tf_op jit(solution)/shard_map/pallas_call | solution.py:742
  (56 shorter events, 3.0 us)
Async XLA Ops:
  0.6 9.3 %copy-start = (bf16[2,2,2,32,2,16,128]{6,5,4,3,2,1,0:T(8,128)(2,1)S(1)}, bf16[2,2,2,32,2,16,128]{6,5,4,3,2,1,0:T(8,128)(2,1)}, u32[]{:S(2)}) copy-start(bf16[2,2,2,32,2,16,128]{6,5,4,3,2,1,0:T(8,128)(2,1)} %param.5) | copy-start | bytes 6291460
  2.0 8.1 %copy-start.5 = (bf16[64,2,16,128]{3,2,1,0:T(8,128)(2,1)S(1)}, bf16[64,2,16,128]{3,2,1,0:T(8,128)(2,1)}, u32[]{:S(2)}) copy-start(bf16[64,2,16,128]{3,2,1,0:T(8,128)(2,1)} %vol_in.1) | copy-start | bytes 1572868
  2.0 8.1 %copy-start.14 = (bf16[4,4,4,32,64]{4,3,2,1,0:T(8,128)(2,1)S(1)}, bf16[4,4,4,32,64]{4,3,2,1,0:T(8,128)(2,1)}, u32[]{:S(2)}) copy-start(bf16[4,4,4,32,64]{4,3,2,1,0:T(8,128)(2,1)} %taps_in.1) | copy-start | bytes 786436
  3.3 12.6 %collective-permute-start = (bf16[1152,128]{1,0:T(8,128)(2,1)S(1)}, bf16[1152,128]{1,0:T(8,128)(2,1)S(1)}, u32[]{:S(2)}, u32[]{:S(2)}) collective-permute-start(bf16[1152,128]{1,0:T(8,128)(2,1)S(1)} %pad_maximum_fusion), channel_id=1, source_target_pairs={{0,4},{4,8},{8,12},{12,16},{16,20},{20,24},{24,28},{1,5},{5,9},{9,... | collective-permute-start | bytes 884744 | tf_op jit(solution)/shard_map/ppermute | solution.py:628
  8.0 8.3 %collective-permute-start.1 = (bf16[1152,128]{1,0:T(8,128)(2,1)S(1)}, bf16[1152,128]{1,0:T(8,128)(2,1)S(1)}, u32[]{:S(2)}, u32[]{:S(2)}) collective-permute-start(bf16[1152,128]{1,0:T(8,128)(2,1)S(1)} %pad_maximum_fusion.1), channel_id=1, source_target_pairs={{4,0},{8,4},{12,8},{16,12},{20,16},{24,20},{28,24},{5,1},{9,5},{13... | collective-permute-start | bytes 884744 | tf_op jit(solution)/shard_map/ppermute | solution.py:629
  14.2 1.0 %copy-start.6 = (f32[2,64,2048]{2,1,0:T(8,128)}, f32[2,64,2048]{2,1,0:T(8,128)S(1)}, u32[]{:S(2)}) copy-start(f32[2,64,2048]{2,1,0:T(8,128)S(1)} %get-tuple-element.33.ig_in) | copy-start | bytes 3145732
  15.1 0.8 %copy-start.21 = (bf16[4,32,16,128]{3,2,1,0:T(8,128)(2,1)}, bf16[4,32,16,128]{3,2,1,0:T(8,128)(2,1)S(1)}, u32[]{:S(2)}) copy-start(bf16[4,32,16,128]{3,2,1,0:T(8,128)(2,1)S(1)} %get-tuple-element.29) | copy-start | bytes 1572868
  15.9 8.0 %copy-start.20 = (bf16[4,32,16,128]{3,2,1,0:T(8,128)(2,1)}, bf16[4,32,16,128]{3,2,1,0:T(8,128)(2,1)S(1)}, u32[]{:S(2)}) copy-start(bf16[4,32,16,128]{3,2,1,0:T(8,128)(2,1)S(1)} %get-tuple-element.30) | copy-start | bytes 1572868
  15.9 13.9 %copy-start.15 = (bf16[512,256]{1,0:T(8,128)(2,1)}, bf16[512,256]{1,0:T(8,128)(2,1)S(1)}, u32[]{:S(2)}) copy-start(bf16[512,256]{1,0:T(8,128)(2,1)S(1)} %get-tuple-element.31.wt_in) | copy-start | bytes 786436
  16.4 6.1 %collective-permute-start.3 = (bf16[640,128]{1,0:T(8,128)(2,1)S(1)}, bf16[640,128]{1,0:T(8,128)(2,1)S(1)}, u32[]{:S(2)}, u32[]{:S(2)}) collective-permute-start(bf16[640,128]{1,0:T(8,128)(2,1)S(1)} %get-tuple-element.47), channel_id=1, source_target_pairs={{1,0},{2,1},{3,2},{5,4},{6,5},{7,6},{9,8},{10,9},{11,10},{13,12},{... | collective-permute-start | bytes 491528 | tf_op jit(solution)/shard_map/ppermute | solution.py:684
  17.7 6.2 %collective-permute-start.2 = (bf16[640,128]{1,0:T(8,128)(2,1)S(1)}, bf16[640,128]{1,0:T(8,128)(2,1)S(1)}, u32[]{:S(2)}, u32[]{:S(2)}) collective-permute-start(bf16[640,128]{1,0:T(8,128)(2,1)S(1)} %get-tuple-element.48), channel_id=1, source_target_pairs={{0,1},{1,2},{2,3},{4,5},{5,6},{6,7},{8,9},{9,10},{10,11},{12,13},{... | collective-permute-start | bytes 491528 | tf_op jit(solution)/shard_map/ppermute | solution.py:683
  22.4 7.4 %copy-start.10 = (bf16[640,128]{1,0:T(8,128)(2,1)}, bf16[640,128]{1,0:T(8,128)(2,1)S(1)}, u32[]{:S(2)}) copy-start(bf16[640,128]{1,0:T(8,128)(2,1)S(1)} %collective-permute-done.3.yhi_in) | copy-start | bytes 491524
  23.9 5.9 %copy-start.12 = (bf16[640,128]{1,0:T(8,128)(2,1)}, bf16[640,128]{1,0:T(8,128)(2,1)S(1)}, u32[]{:S(2)}) copy-start(bf16[640,128]{1,0:T(8,128)(2,1)S(1)} %collective-permute-done.2.ylo_in) | copy-start | bytes 491524
  29.8 1.4 %copy-start.1 = (bf16[256,4608]{1,0:T(8,128)(2,1)}, bf16[256,4608]{1,0:T(8,128)(2,1)S(1)}, u32[]{:S(2)}) copy-start(bf16[256,4608]{1,0:T(8,128)(2,1)S(1)} %get-tuple-element.24.ga_in) | copy-start | bytes 7077892
  31.2 1.4 %copy-start.3 = (bf16[256,4608]{1,0:T(8,128)(2,1)}, bf16[256,4608]{1,0:T(8,128)(2,1)S(1)}, u32[]{:S(2)}) copy-start(bf16[256,4608]{1,0:T(8,128)(2,1)S(1)} %get-tuple-element.25.gb_in) | copy-start | bytes 7077892
  32.7 1.0 %copy-start.8 = (bf16[256,2048]{1,0:T(8,128)(2,1)}, bf16[256,2048]{1,0:T(8,128)(2,1)S(1)}, u32[]{:S(2)}) copy-start(bf16[256,2048]{1,0:T(8,128)(2,1)S(1)} %get-tuple-element.27.vals_in) | copy-start | bytes 3145732
  33.6 0.7 copy-start.17
  34.3 0.6 copy-start.18
  35.0 18.8 %all-to-all-start = ((bf16[32,32,128]{2,1,0:T(8,128)(2,1)}), bf16[32,32,128]{2,1,0:T(8,128)(2,1)}, u32[]{:S(2)}, u32[]{:S(2)}) async-start(bf16[32,32,128]{2,1,0:T(8,128)(2,1)} %copy-done.17), calls=%async_computation | async-start | bytes 524288 | tf_op jit(solution)/shard_map/all_to_all | solution.py:738
  43.3 15.4 %collective-permute-start.4 = (bf16[4,32,16,128]{3,2,1,0:T(8,128)(2,1)}, bf16[4,32,16,128]{3,2,1,0:T(8,128)(2,1)}, u32[]{:S(2)}, u32[]{:S(2)}) collective-permute-start(bf16[4,32,16,128]{3,2,1,0:T(8,128)(2,1)} %copy-done.21), channel_id=1, source_target_pairs={{0,4},{4,8},{8,12},{12,16},{16,20},{20,24},{24,28},{1,5},{5,9},{9,... | collective-permute-start | bytes 1572872 | tf_op jit(solution)/shard_map/ppermute | solution.py:685
  46.9 15.3 %collective-permute-start.5 = (bf16[4,32,16,128]{3,2,1,0:T(8,128)(2,1)}, bf16[4,32,16,128]{3,2,1,0:T(8,128)(2,1)}, u32[]{:S(2)}, u32[]{:S(2)}) collective-permute-start(bf16[4,32,16,128]{3,2,1,0:T(8,128)(2,1)} %copy-done.20), channel_id=1, source_target_pairs={{4,0},{8,4},{12,8},{16,12},{20,16},{24,20},{28,24},{5,1},{9,5},{13... | collective-permute-start | bytes 1572872 | tf_op jit(solution)/shard_map/ppermute | solution.py:686
  55.5 21.5 %all-to-all-start.1 = ((bf16[32,32,128]{2,1,0:T(8,128)(2,1)}), bf16[32,32,128]{2,1,0:T(8,128)(2,1)}, u32[]{:S(2)}, u32[]{:S(2)}) async-start(bf16[32,32,128]{2,1,0:T(8,128)(2,1)} %broadcast_in_dim.2), calls=%async_computation.1 | async-start | bytes 524288 | tf_op jit(solution)/shard_map/all_to_all | solution.py:741
  62.2 1.7 %copy-start.2 = (bf16[256,4608]{1,0:T(8,128)(2,1)S(1)}, bf16[256,4608]{1,0:T(8,128)(2,1)}, u32[]{:S(2)}) copy-start(bf16[256,4608]{1,0:T(8,128)(2,1)} %copy-done.1) | copy-start | bytes 7077892
  63.8 1.7 %copy-start.4 = (bf16[256,4608]{1,0:T(8,128)(2,1)S(1)}, bf16[256,4608]{1,0:T(8,128)(2,1)}, u32[]{:S(2)}) copy-start(bf16[256,4608]{1,0:T(8,128)(2,1)} %copy-done.3) | copy-start | bytes 7077892
  65.5 1.2 %copy-start.7 = (f32[2,64,2048]{2,1,0:T(8,128)S(1)}, f32[2,64,2048]{2,1,0:T(8,128)}, u32[]{:S(2)}) copy-start(f32[2,64,2048]{2,1,0:T(8,128)} %copy-done.6) | copy-start | bytes 3145732
  66.7 1.2 %copy-start.9 = (bf16[256,2048]{1,0:T(8,128)(2,1)S(1)}, bf16[256,2048]{1,0:T(8,128)(2,1)}, u32[]{:S(2)}) copy-start(bf16[256,2048]{1,0:T(8,128)(2,1)} %copy-done.8) | copy-start | bytes 3145732
  68.0 0.9 %copy-start.11 = (bf16[640,128]{1,0:T(8,128)(2,1)S(1)}, bf16[640,128]{1,0:T(8,128)(2,1)}, u32[]{:S(2)}) copy-start(bf16[640,128]{1,0:T(8,128)(2,1)} %copy-done.10) | copy-start | bytes 491524
  68.9 0.9 %copy-start.13 = (bf16[640,128]{1,0:T(8,128)(2,1)S(1)}, bf16[640,128]{1,0:T(8,128)(2,1)}, u32[]{:S(2)}) copy-start(bf16[640,128]{1,0:T(8,128)(2,1)} %copy-done.12) | copy-start | bytes 491524
  69.8 0.9 %copy-start.16 = (bf16[512,256]{1,0:T(8,128)(2,1)S(1)}, bf16[512,256]{1,0:T(8,128)(2,1)}, u32[]{:S(2)}) copy-start(bf16[512,256]{1,0:T(8,128)(2,1)} %copy-done.15) | copy-start | bytes 786436
  70.7 0.8 %copy-start.19 = (bf16[1,256,128]{2,1,0:T(8,128)(2,1)S(1)}, bf16[1,256,128]{2,1,0:T(8,128)(2,1)}, u32[]{:S(2)}) copy-start(bf16[1,256,128]{2,1,0:T(8,128)(2,1)} %copy-done.18) | copy-start | bytes 196612

commit v8 on v7

--- a/solution.py
+++ b/solution.py
@@ -43,21 +43,22 @@
         return self.get(k)
 
 
-def columns_pass(dims, chunk, columns, block, rolled, w, cot_at, put_value, put_foreign, wg_add, ga, gb):
+def corners(get, some):
+    return jnp.concatenate(
+        [
+            jnp.concatenate([get(i + 1 - ex, j + 1 - ey) for i, j in some], axis=1)
+            for ex in range(2)
+            for ey in range(2)
+        ],
+        axis=0,
+    )
+
+
+def forward_pass(dims, chunk, columns, block, rolled, w, cot_at, put_value, put_foreign, ga, gb):
     nx, ny, nz, ci, co = dims
     half = 4 * ci
     first = lax.broadcasted_iota(jnp.int32, (co, nz), 1) == 0
     zeros = jnp.zeros((2 * co, nz), BF16)
-
-    def corners(get, some):
-        return jnp.concatenate(
-            [
-                jnp.concatenate([get(i + 1 - ex, j + 1 - ey) for i, j in some], axis=1)
-                for ex in range(2)
-                for ey in range(2)
-            ],
-            axis=0,
-        )
 
     starts = range(0, len(columns), chunk)
     for c0 in starts:
@@ -106,6 +107,8 @@
                         ga[r, wide] = cut if sz == 0 else whole
                         gb[r, wide] = cut if sz == 1 else whole
 
+
+def weight_pass(columns, block, rolled, ga, gb, wg_add):
     nt = (((1,), (1,)), ((), ()))
     for part, (grads, get) in enumerate(((gb, block), (ga, rolled))):
         wg_add(
@@ -169,14 +172,12 @@
     flat,
     w,
     wt,
-    vals_out,
+    vals,
     cot_edge,
     wg,
-    ig_out,
+    ig,
     face_up,
     face_down,
-    vals,
-    ig,
     vol,
     taps,
     sems,
@@ -264,14 +265,9 @@
         return ga[:, wide], gb[:, wide]
 
     columns = [(i, j) for i in range(1, nx) for j in range(1, ny)]
-    columns_pass(
-        dims, chunk, columns, block, rolled, w, cot_at, put_value, None, wg_add, ga, gb
-    )
+    forward_pass(dims, chunk, columns, block, rolled, w, cot_at, put_value, None, ga, gb)
+    weight_pass(columns, block, rolled, ga, gb, wg_add)
     input_pass(dims, chunk, columns, wt, cut_grads, ig_add)
-    leaving.append(pltpu.make_async_copy(vals, vals_out, sems.at[4]))
-    leaving.append(pltpu.make_async_copy(ig, ig_out, sems.at[5]))
-    for copy in leaving[2:]:
-        copy.start()
     for copy in leaving:
         copy.wait()
 
@@ -287,26 +283,19 @@
     w,
     cot,
     cot_edge,
-    wg_in,
-    wg,
-    ga_out,
-    gb_out,
-    pre_out,
-    vals_out,
-    val_edge_out,
-    xraw,
-    yraw,
-    vm,
     ga,
     gb,
     pre,
-    cots,
     vals,
     val_edge,
+    plain,
+    vm,
+    xraw,
+    yraw,
+    cots,
     sems,
 ):
     nx, ny, nz, ci, co = dims
-    half = 4 * ci
     to_y = swap_matrix(GROUP, ny)
     arriving = [
         pltpu.make_async_copy(xlo_in.at[: ny * ci], xraw.at[0], sems.at[0]),
@@ -348,9 +337,9 @@
 
     for x in range(nx + 2):
         for y in range(ny + 2):
-            vm[x, :, y * nz : (y + 1) * nz] = pltpu.roll(block(x, y).astype(F32), 1, 1).astype(
-                BF16
-            )
+            lanes = slice(y * nz, (y + 1) * nz)
+            plain[x, :, lanes] = block(x, y)
+            vm[x, :, lanes] = pltpu.roll(block(x, y).astype(F32), 1, 1).astype(BF16)
 
     def rolled(x, y):
         return vm[x, :, y * nz : (y + 1) * nz]
@@ -373,28 +362,7 @@
     def put_foreign(key, tz, value):
         pre[spots[key], tz * co : (tz + 1) * co] = value
 
-    leaving = []
-
-    def leave():
-        for k, (src, dst) in enumerate(
-            ((ga, ga_out), (gb, gb_out), (pre, pre_out), (vals, vals_out), (val_edge, val_edge_out))
-        ):
-            leaving.append(pltpu.make_async_copy(src, dst, sems.at[4 + k]))
-            leaving[-1].start()
-
-    def wg_add(part, total):
-        if part == 0:
-            leave()
-        total = total + wg_in[:, part * half : (part + 1) * half]
-        for ex in range(2):
-            for row in range(8):
-                tx, ty, tz = row // 4, row // 2 % 2, row % 2
-                index = ((tx * 2 + ty) * 2 + part) * 2 + tz
-                wg[ex * 16 + index] = total[
-                    row * co : (row + 1) * co, ex * 2 * ci : (ex + 1) * 2 * ci
-                ].astype(BF16)
-
-    columns_pass(
+    forward_pass(
         dims,
         chunk,
         outer_columns(nx, ny),
@@ -404,40 +372,55 @@
         cot_at,
         put_value,
         put_foreign,
-        wg_add,
         ga,
         gb,
     )
-    for copy in leaving:
-        copy.wait()
+
+
+def weight_kernel(dims, plain, vm, ga, gb, wg_in, face_lo, face_hi, wg):
+    del face_lo, face_hi
+    nx, ny, nz, ci, co = dims
+    half = 4 * ci
+
+    def wg_add(part, total):
+        total = total + wg_in[:, part * half : (part + 1) * half]
+        for ex in range(2):
+            for row in range(8):
+                tx, ty, tz = row // 4, row // 2 % 2, row % 2
+                index = ((tx * 2 + ty) * 2 + part) * 2 + tz
+                wg[ex * 16 + index] = total[
+                    row * co : (row + 1) * co, ex * 2 * ci : (ex + 1) * 2 * ci
+                ].astype(BF16)
+
+    weight_pass(
+        outer_columns(nx, ny),
+        lambda x, y: plain[x, :, y * nz : (y + 1) * nz],
+        lambda x, y: vm[x, :, y * nz : (y + 1) * nz],
+        ga,
+        gb,
+        wg_add,
+    )
 
 
 def last_kernel(
     dims,
     chunk,
-    ga_in,
-    gb_in,
-    pre_in,
-    vals_in,
-    val_edge_in,
-    xlo_in,
-    xhi_in,
-    ylo_in,
-    yhi_in,
-    wt_in,
-    inner_vals_in,
-    ig_in,
-    act_out,
-    ig_out,
     ga,
     gb,
     pre,
     vals,
     val_edge,
+    xlo_in,
+    xhi_in,
+    ylo_in,
+    yhi_in,
+    wt,
+    inner_vals,
+    ig_in,
+    act_out,
+    ig_out,
     xraw,
     yraw,
-    wt,
-    inner_vals,
     ig,
     cots,
     staged,
@@ -448,26 +431,16 @@
     to_y = swap_matrix(GROUP, ny)
     to_c = swap_matrix(ny, GROUP)
     skip = (nx + 2) * ci
-    early = [(vals_in, vals), (val_edge_in, val_edge), (inner_vals_in, inner_vals)]
     late = [
         (xlo_in, xraw.at[0]),
         (xhi_in, xraw.at[1]),
         (ylo_in.at[skip:], yraw.at[0]),
         (yhi_in.at[skip:], yraw.at[1]),
-        (ga_in, ga),
-        (gb_in, gb),
-        (pre_in, pre),
-        (wt_in, wt),
-        (ig_in, ig),
     ]
-    copies = [
-        pltpu.make_async_copy(src, dst, sems.at[k]) for k, (src, dst) in enumerate(early + late)
-    ]
+    copies = [pltpu.make_async_copy(src, dst, sems.at[k]) for k, (src, dst) in enumerate(late)]
     for copy in copies:
         copy.start()
     spot = len(copies)
-    for copy in copies[: len(early)]:
-        copy.wait()
     leaving = []
 
     for m in range(nx):
@@ -498,7 +471,7 @@
             )
             leaving[-1].start()
 
-    for copy in copies[len(early) :]:
+    for copy in copies:
         copy.wait()
     for side in range(2):
         for p in range(4):
@@ -563,9 +536,14 @@
 
     def ig_add(m, y, value, fresh):
         lanes = slice(y * nz, (y + 1) * nz)
-        ig[m, :, lanes] = ig[m, :, lanes] + value
-
-    input_pass(dims, chunk, outer_columns(nx, ny), wt, cut_grads, ig_add)
+        ig[m, :, lanes] = (ig_in if fresh else ig)[m, :, lanes] + value
+
+    started = input_pass(dims, chunk, outer_columns(nx, ny), wt, cut_grads, ig_add)
+    for m in range(nx):
+        for y in range(ny):
+            if (m, y) not in started:
+                lanes = slice(y * nz, (y + 1) * nz)
+                ig[m, :, lanes] = ig_in[m, :, lanes]
     for m in range(nx):
         for k in range(0, ci // GROUP, 2):
             tiles = []
@@ -600,6 +578,14 @@
                             ]
 
 
+def held(shape, dtype):
+    return pltpu.VMEM(shape, dtype)
+
+
+def hold(array):
+    return pltpu.with_memory_space_constraint(array, pltpu.VMEM)
+
+
 def neighbours(axis):
     count = lax.axis_size(axis)
     up = [(i, i + 1) for i in range(count - 1)]
@@ -631,7 +617,7 @@
     vmem = pl.BlockSpec(memory_space=pltpu.VMEM)
     smem = pl.BlockSpec(memory_space=pltpu.SMEM)
     anywhere = pl.BlockSpec(memory_space=pl.ANY)
-    params = pltpu.CompilerParams(vmem_limit_bytes=28 * 1024 * 1024)
+    params = pltpu.CompilerParams(vmem_limit_bytes=24 * 1024 * 1024)
     n_in = (nx - 1) * (ny - 1)
     n_out = 2 * (ny + 1) + 2 * (nx - 1)
     flat, w, wt, vals, cot_edge, wg_part, ig_part, face_up, face_down = pl.pallas_call(
@@ -640,21 +626,19 @@
             jax.ShapeDtypeStruct((nx, ci, ny * nz), BF16),
             jax.ShapeDtypeStruct((8 * co, 8 * ci), BF16),
             jax.ShapeDtypeStruct((8 * ci, 8 * co), BF16),
-            jax.ShapeDtypeStruct((nx - 1, 8 * co, ny * nz), BF16),
+            held((nx - 1, 8 * co, ny * nz), BF16),
             jax.ShapeDtypeStruct((nx - 1, 8 * co, nz), BF16),
-            jax.ShapeDtypeStruct((8 * co, 8 * ci), F32),
-            jax.ShapeDtypeStruct((nx, ci, ny * nz), F32),
+            held((8 * co, 8 * ci), F32),
+            held((nx, ci, ny * nz), F32),
             jax.ShapeDtypeStruct((4, co, ny, nz), BF16),
             jax.ShapeDtypeStruct((4, co, ny, nz), BF16),
         ),
         in_specs=[anywhere, anywhere, vmem],
-        out_specs=(vmem,) * 3 + (anywhere,) + (vmem,) * 2 + (anywhere,) * 3,
+        out_specs=(vmem,) * 7 + (anywhere,) * 2,
         scratch_shapes=[
-            pltpu.VMEM((nx - 1, 8 * co, ny * nz), BF16),
-            pltpu.VMEM((nx, ci, ny * nz), F32),
             pltpu.VMEM(volume.shape, BF16),
             pltpu.VMEM(kernel.shape, BF16),
-            pltpu.SemaphoreType.DMA((6,)),
+            pltpu.SemaphoreType.DMA((4,)),
             pltpu.VMEM((nx, ci, ny * nz), BF16),
             pltpu.VMEM((8 * co, n_in * nz), BF16),
             pltpu.VMEM((8 * co, n_in * nz), BF16),
@@ -685,52 +669,54 @@
     face_lo = lax.ppermute(face_up, "gx", gx_up)
     face_hi = lax.ppermute(face_down, "gx", gx_down)
     foreign = len(foreign_spots(nx, ny))
-    kept = (
-        jax.ShapeDtypeStruct((8 * co, n_out * nz), BF16),
-        jax.ShapeDtypeStruct((8 * co, n_out * nz), BF16),
-        jax.ShapeDtypeStruct((foreign, 2 * co, nz), F32),
-        jax.ShapeDtypeStruct((8 * co, ny * nz), BF16),
-        jax.ShapeDtypeStruct((nx - 1, 8 * co, nz), BF16),
-    )
-    held = [pltpu.VMEM(k.shape, k.dtype) for k in kept]
-    wg, *passed = pl.pallas_call(
+    *passed, plain, vm = pl.pallas_call(
         functools.partial(outer_kernel, dims, 4),
-        out_shape=(jax.ShapeDtypeStruct((32, co, 2 * ci), BF16),) + kept,
-        in_specs=[vmem] + [anywhere] * 4 + [vmem] * 4,
-        out_specs=(vmem,) + (anywhere,) * 5,
+        out_shape=(
+            held((8 * co, n_out * nz), BF16),
+            held((8 * co, n_out * nz), BF16),
+            held((foreign, 2 * co, nz), F32),
+            held((8 * co, ny * nz), BF16),
+            held((nx - 1, 8 * co, nz), BF16),
+            held((nx + 2, ci, (ny + 2) * nz), BF16),
+            held((nx + 2, ci, (ny + 2) * nz), BF16),
+        ),
+        in_specs=[vmem] + [anywhere] * 4 + [vmem] * 3,
+        out_specs=(vmem,) * 7,
         scratch_shapes=[
             pltpu.VMEM((2, ny * ci, nz), BF16),
             pltpu.VMEM((2, (nx + 2) * ci, nz), BF16),
-            pltpu.VMEM((nx + 2, ci, (ny + 2) * nz), BF16),
-        ]
-        + held[:3]
-        + [pltpu.VMEM((8 * co, ny * nz), BF16)]
-        + held[3:]
-        + [pltpu.SemaphoreType.DMA((9,))],
+            pltpu.VMEM((8 * co, ny * nz), BF16),
+            pltpu.SemaphoreType.DMA((4,)),
+        ],
         compiler_params=params,
-    )(flat, xlo, xhi, ylo, yhi, w, cot, cot_edge, wg_part)
+    )(flat, xlo, xhi, ylo, yhi, w, cot, cot_edge)
+    passed = [hold(p) for p in passed]
+    wg = pl.pallas_call(
+        functools.partial(weight_kernel, dims),
+        out_shape=jax.ShapeDtypeStruct((32, co, 2 * ci), BF16),
+        in_specs=[vmem] * 5 + [anywhere] * 2,
+        out_specs=vmem,
+        compiler_params=params,
+    )(hold(plain), hold(vm), passed[0], passed[1], hold(wg_part), face_lo, face_hi)
     act, input_grad = pl.pallas_call(
         functools.partial(last_kernel, dims, 4),
         out_shape=(
             jax.ShapeDtypeStruct(cot.shape, BF16),
             jax.ShapeDtypeStruct(volume.shape, BF16),
         ),
-        in_specs=[anywhere] * 12,
+        in_specs=[vmem] * 5 + [anywhere] * 4 + [vmem] * 3,
         out_specs=(anywhere,) * 2,
-        scratch_shapes=held
-        + [
+        scratch_shapes=[
             pltpu.VMEM((2, 4, co, ny, nz), BF16),
             pltpu.VMEM((2, 4 * co * nx + 4 * co, nz), BF16),
-            pltpu.VMEM((8 * ci, 8 * co), BF16),
-            pltpu.VMEM((nx - 1, 8 * co, ny * nz), BF16),
             pltpu.VMEM((nx, ci, ny * nz), F32),
             pltpu.VMEM((2, 4 * co, ny * nz), BF16),
             pltpu.VMEM((8 * nx, co, ny, nz), BF16),
             pltpu.VMEM(volume.shape, BF16),
-            pltpu.SemaphoreType.DMA((13 + 8 * nx,)),
+            pltpu.SemaphoreType.DMA((5 + 8 * nx,)),
         ],
         compiler_params=params,
-    )(*passed, face_lo, face_hi, ylo, yhi, wt, vals, ig_part)
+    )(*passed, face_lo, face_hi, ylo, yhi, wt, hold(vals), hold(ig_part))
 
     scale = 1.0 / math.sqrt(cells)
     devices = gx * gy

time: 79.8 us -> 76 us (0.952)
  blocking collectives: 0 us -> 18.6 us
  starting transfers between devices: 28.8 us -> 20.5 us
  waiting for transfers between devices: 10.9 us -> 2.92 us
  local copies, waits for them, and re-layouts: 20.1 us -> 16.9 us
  Pallas kernels: 17.3 us -> 15 us
  other arithmetic: 1.05 us -> 0.1 us
    all_to_all x0 -> x1, blocking collectives: none -> 18.6 us  [on_device(): shares = lax.all_to_all(shares, ('gx', 'gy'), 0, 0, tiled=True)]
    all_to_all x1 -> x0, starting transfers between devices: 8.37 us -> none  [on_device(): shares = lax.all_to_all(shares, ('gx', 'gy'), 0, 0, tiled=True)]
    all_to_all x1 -> x0, waiting for transfers between devices: 4.91 us -> none  [on_device(): shares = lax.all_to_all(shares, ('gx', 'gy'), 0, 0, tiled=True)]
    ppermute x1, waiting for transfers between devices: 3.44 us -> 0.01 us  [on_device(): face_hi = lax.ppermute(face_down, 'gx', gx_down)]
    unnamed x54 -> x48, local copies, waits for them, and re-layouts: 16.4 us -> 13.3 us
    pallas_call x1 -> x2, Pallas kernels: 5.87 us -> 4.75 us  [the longest x1 3.34 us: on_device(): pl.pallas_call(functools.partial(outer_kernel, dims, 4), out_shape=(held(...]
    pallas_call x1, Pallas kernels: 5.37 us -> 4.41 us  [on_device(): pl.pallas_call(functools.partial(last_kernel, dims, 4), out_shape=(jax.Sh...]
    reduce_sum x1, other arithmetic: 1 us -> 0.05 us  [on_device(): piece = (jnp.sum(shares.astype(F32), axis=0) * scale).astype(BF16)]
  transfers between devices with their start and end apart: 8 -> 7, of which waited for: 5 -> 2; matrix products, arithmetic and copies ran while one was open for 3% -> 1% of each run, Pallas kernels for 12% -> 15%
where the time goes in v8:
time: 76 us; the launch traced here: 75.1 us
  starting transfers between devices  20.5 us (27%)
  blocking collectives  18.6 us (24%)
  local copies, waits for them, and re-layouts  16.9 us (22%)
  Pallas kernels  15 us (20%)
  waiting for transfers between devices  2.92 us (4%)
  between operations  1 us (1%)
    all_to_all x1, blocking collectives, on_device(): shares = lax.all_to_all(shares, ('gx', 'gy'), 0, 0, tiled=True)  18.6 us
    unnamed x48, local copies, waits for them, and re-layouts  13.3 us
    ppermute x1, starting transfers between devices, on_device(): xlo = lax.ppermute(x_message(1), 'gx', gx_up)  4.51 us
    pallas_call x1, Pallas kernels, on_device(): pl.pallas_call(functools.partial(last_kernel, dims, 4), out_shape=(jax.Sh...  4.41 us
    ppermute x1, starting transfers between devices, on_device(): ylo = lax.ppermute(y_message(1), 'gy', gy_up)  4 us
    pallas_call x1, Pallas kernels, on_device(): pl.pallas_call(functools.partial(inner_kernel, dims, 5), out_shape=(jax.S...  3.82 us
    ppermute x1, starting transfers between devices, on_device(): face_lo = lax.ppermute(face_up, 'gx', gx_up)  3.63 us
    pallas_call x1, Pallas kernels, on_device(): pl.pallas_call(functools.partial(outer_kernel, dims, 4), out_shape=(held(...  3.34 us
  transfers between devices with their start and end apart: 7, of which 2 were waited for; matrix products, arithmetic and copies ran while one was open for 1% of the time, Pallas kernels for 15%

profile of v8, /device:TPU:1, one launch (start us, length us, event | category | flops | bytes accessed | tf_op | source)
XLA Modules:
  0.0 75.1 jit_solution(4835500850447491023)
XLA Ops:
  0.7 1.4 %fusion.1 = (bf16[1,1,2,32,1,1,128]{6,5,4,3,2,1,0:T(2,128)(2,1)S(1)}, bf16[1,1,2,32,1,1,128]{6,5,4,3,2,1,0:T(2,128)(2,1)S(1)}, bf16[1,1,2,32,1,1,128]{6,5,4,3,2,...) fusion(bf16[2,2,2,32,2,16,128]{6,5,4,3,2,1,0:T(8,128)(2,1)} %param.5), kind=kLoop, calls=%fused_computation.19 | loop fusion | bytes 131072 | tf_op jit(solution)/shard_map/slice | solution.py:608
  2.1 1.1 %slice_bitcast_fusion = (bf16[16,64,128]{2,0,1:T(8,128)(2,1)S(1)}, bf16[16,64,128]{2,0,1:T(8,128)(2,1)S(1)}) fusion(bf16[64,2,16,128]{3,2,1,0:T(8,128)(2,1)} %vol_in.1), kind=kLoop, calls=%fused_computation.3 | loop fusion | bytes 1048576 | tf_op jit(solution)/shard_map/transpose | solution.py:611
  3.1 0.1 copy.10
  3.2 4.5 %collective-permute-start = (bf16[1152,128]{1,0:T(8,128)(2,1)S(1)}, bf16[1152,128]{1,0:T(8,128)(2,1)S(1)}, u32[]{:S(2)}, u32[]{:S(2)}) collective-permute-start(bf16[1152,128]{1,0:T(8,128)(2,1)S(1)} %pad_maximum_fusion), channel_id=1, source_target_pairs={{0,4},{4,8},{8,12},{12,16},{16,20},{20,24},{24,28},{1,5},{5,9},{9,... | collective-permute-start | bytes 884744 | tf_op jit(solution)/shard_map/ppermute | solution.py:614
  7.8 0.1 copy.13
  7.9 1.9 %collective-permute-start.1 = (bf16[1152,128]{1,0:T(8,128)(2,1)S(1)}, bf16[1152,128]{1,0:T(8,128)(2,1)S(1)}, u32[]{:S(2)}, u32[]{:S(2)}) collective-permute-start(bf16[1152,128]{1,0:T(8,128)(2,1)S(1)} %pad_maximum_fusion.1), channel_id=1, source_target_pairs={{4,0},{8,4},{12,8},{16,12},{20,16},{24,20},{28,24},{5,1},{9,5},{13... | collective-permute-start | bytes 884744 | tf_op jit(solution)/shard_map/ppermute | solution.py:615
  9.8 3.8 %shard_map.58 = (bf16[2,64,2048]{2,1,0:T(8,128)(2,1)S(1)}, bf16[256,512]{1,0:T(8,128)(2,1)S(1)}, bf16[512,256]{1,0:T(8,128)(2,1)S(1)}, bf16[1,256,2048]{2,1,0:T(...) custom-call(bf16[64,2,16,128]{3,2,1,0:T(8,128)(2,1)S(1)} %copy-done., ...), custom_call_target="tpu_custom_call" | custom-call | tf_op jit(solution)/shard_map/pallas_call | solution.py:623
  13.7 1.0 %copy-done.8 = f32[2,64,2048]{2,1,0:T(8,128)} copy-done((f32[2,64,2048]{2,1,0:T(8,128)}, f32[2,64,2048]{2,1,0:T(8,128)S(1)}, u32[]{:S(2)}) %copy-start.8) | copy-done | bytes 1048600
  14.7 3.6 %collective-permute-start.4 = (bf16[4,32,16,128]{3,2,1,0:T(8,128)(2,1)S(1)}, bf16[4,32,16,128]{3,2,1,0:T(8,128)(2,1)S(1)}, u32[]{:S(2)}, u32[]{:S(2)}) collective-permute-start(bf16[4,32,16,128]{3,2,1,0:T(8,128)(2,1)S(1)} %get-tuple-element.29), channel_id=1, source_target_pairs={{0,4},{4,8},{8,12},{12,16},{16,20},{20,24},{24,28},{1,5},{5,9},{9,... | collective-permute-start | bytes 1572872 | tf_op jit(solution)/shard_map/ppermute | solution.py:669
  18.3 1.9 %collective-permute-start.5 = (bf16[4,32,16,128]{3,2,1,0:T(8,128)(2,1)S(1)}, bf16[4,32,16,128]{3,2,1,0:T(8,128)(2,1)S(1)}, u32[]{:S(2)}, u32[]{:S(2)}) collective-permute-start(bf16[4,32,16,128]{3,2,1,0:T(8,128)(2,1)S(1)} %get-tuple-element.30), channel_id=1, source_target_pairs={{4,0},{8,4},{12,8},{16,12},{20,16},{24,20},{28,24},{5,1},{9,5},{13... | collective-permute-start | bytes 1572872 | tf_op jit(solution)/shard_map/ppermute | solution.py:670
  20.2 0.2 fusion
  20.7 1.3 %collective-permute-start.3 = (bf16[640,128]{1,0:T(8,128)(2,1)S(1)}, bf16[640,128]{1,0:T(8,128)(2,1)S(1)}, u32[]{:S(2)}, u32[]{:S(2)}) collective-permute-start(bf16[640,128]{1,0:T(8,128)(2,1)S(1)} %get-tuple-element.49), channel_id=1, source_target_pairs={{1,0},{2,1},{3,2},{5,4},{6,5},{7,6},{9,8},{10,9},{11,10},{13,12},{... | collective-permute-start | bytes 491528 | tf_op jit(solution)/shard_map/ppermute | solution.py:668
  22.0 4.0 %collective-permute-start.2 = (bf16[640,128]{1,0:T(8,128)(2,1)S(1)}, bf16[640,128]{1,0:T(8,128)(2,1)S(1)}, u32[]{:S(2)}, u32[]{:S(2)}) collective-permute-start(bf16[640,128]{1,0:T(8,128)(2,1)S(1)} %get-tuple-element.50), channel_id=1, source_target_pairs={{0,1},{1,2},{2,3},{4,5},{5,6},{6,7},{8,9},{9,10},{10,11},{12,13},{... | collective-permute-start | bytes 491528 | tf_op jit(solution)/shard_map/ppermute | solution.py:667
  26.0 1.2 %collective-permute-done.3.yhi_in = bf16[640,128]{1,0:T(8,128)(2,1)S(1)} collective-permute-done((bf16[640,128]{1,0:T(8,128)(2,1)S(1)}, bf16[640,128]{1,0:T(8,128)(2,1)S(1)}, u32[]{:S(2)}, u32[]{:S(2)}) %collective-permute-start.3) | collective-permute-done | bytes 163872 | tf_op jit(solution)/shard_map/ppermute | solution.py:668
  27.1 1.8 %collective-permute-done.2.ylo_in = bf16[640,128]{1,0:T(8,128)(2,1)S(1)} collective-permute-done((bf16[640,128]{1,0:T(8,128)(2,1)S(1)}, bf16[640,128]{1,0:T(8,128)(2,1)S(1)}, u32[]{:S(2)}, u32[]{:S(2)}) %collective-permute-start.2) | collective-permute-done | bytes 163872 | tf_op jit(solution)/shard_map/ppermute | solution.py:667
  28.9 3.3 %shard_map.59 = (bf16[256,4608]{1,0:T(8,128)(2,1)S(1)}, bf16[256,4608]{1,0:T(8,128)(2,1)S(1)}, f32[76,64,128]{2,1,0:T(8,128)S(1)}, bf16[256,2048]{1,0:T(8,128)(2...) custom-call(bf16[2,64,2048]{2,1,0:T(8,128)(2,1)S(1)} %get-tuple-elemen, ...), custom_call_target="tpu_custom_call" | custom-call | tf_op jit(solution)/shard_map/pallas_call | solution.py:672
  32.2 1.5 %copy-done.3 = f32[76,64,128]{2,1,0:T(8,128)} copy-done((f32[76,64,128]{2,1,0:T(8,128)}, f32[76,64,128]{2,1,0:T(8,128)S(1)}, u32[]{:S(2)}) %copy-start.3) | copy-done | bytes 2490392
  33.7 1.0 %copy-done.10 = bf16[256,2048]{1,0:T(8,128)(2,1)} copy-done((bf16[256,2048]{1,0:T(8,128)(2,1)}, bf16[256,2048]{1,0:T(8,128)(2,1)S(1)}, u32[]{:S(2)}) %copy-start.10) | copy-done | bytes 1048600
  34.7 1.4 %shard_map.61 = bf16[32,32,128]{2,1,0:T(8,128)(2,1)S(1)} custom-call(bf16[4,64,2304]{2,1,0:T(8,128)(2,1)S(1)} %get-tuple-element.36.plain, bf16[4,64,2304]{2,1,0:T(8,128)(2,1)S(1)} %get-tuple-element.37.vm, bf16[256,4608]{1,0:T(8,128)(2,1)S(1)} %get-tuple-element.24.ga, bf16[256,4608]{1,0:T(8,128)(2,1)S(1)} %get-tuple-element.25.gb, ...), custom_call_target="tpu_custom_call" | custom-call | tf_op jit(solution)/shard_map/pallas_call | solution.py:694
  36.1 18.6 %all_to_all.10 = bf16[32,32,128]{2,1,0:T(8,128)(2,1)S(1)} all-to-all(bf16[32,32,128]{2,1,0:T(8,128)(2,1)S(1)} %shard_map.61), channel_id=1, replica_groups=mesh['gx'=8,'gy'=4] {'gx','gy'}, dimensions={0} | all-to-all | bytes 524288 | tf_op jit(solution)/shard_map/all_to_all | solution.py:724
  54.8 0.7 broadcast_in_dim.2
  55.5 3.2 %all-to-all-start.1 = ((bf16[32,32,128]{2,1,0:T(8,128)(2,1)}), bf16[32,32,128]{2,1,0:T(8,128)(2,1)}, u32[]{:S(2)}, u32[]{:S(2)}) async-start(bf16[32,32,128]{2,1,0:T(8,128)(2,1)} %broadcast_in_dim.2), calls=%async_computation.1 | async-start | bytes 524288 | tf_op jit(solution)/shard_map/all_to_all | solution.py:727
  58.8 1.7 %copy-done.2 = bf16[256,4608]{1,0:T(8,128)(2,1)S(1)} copy-done((bf16[256,4608]{1,0:T(8,128)(2,1)S(1)}, bf16[256,4608]{1,0:T(8,128)(2,1)}, u32[]{:S(2)}) %copy-start.2) | copy-done | bytes 2359320
  60.4 1.7 %copy-done.4 = f32[76,64,128]{2,1,0:T(8,128)S(1)} copy-done((f32[76,64,128]{2,1,0:T(8,128)S(1)}, f32[76,64,128]{2,1,0:T(8,128)}, u32[]{:S(2)}) %copy-start.4) | copy-done | bytes 2490392
  62.1 1.2 %copy-done.7 = bf16[1,256,2048]{2,1,0:T(8,128)(2,1)S(1)} copy-done((bf16[1,256,2048]{2,1,0:T(8,128)(2,1)S(1)}, bf16[1,256,2048]{2,1,0:T(8,128)(2,1)}, u32[]{:S(2)}) %copy-start.7) | copy-done | bytes 1048600
  63.4 1.2 %copy-done.9 = f32[2,64,2048]{2,1,0:T(8,128)S(1)} copy-done((f32[2,64,2048]{2,1,0:T(8,128)S(1)}, f32[2,64,2048]{2,1,0:T(8,128)}, u32[]{:S(2)}) %copy-start.9) | copy-done | bytes 1048600
  64.6 1.2 %copy-done.11 = bf16[256,2048]{1,0:T(8,128)(2,1)S(1)} copy-done((bf16[256,2048]{1,0:T(8,128)(2,1)S(1)}, bf16[256,2048]{1,0:T(8,128)(2,1)}, u32[]{:S(2)}) %copy-start.11) | copy-done | bytes 1048600
  65.8 0.9 %copy-done.13 = bf16[640,128]{1,0:T(8,128)(2,1)S(1)} copy-done((bf16[640,128]{1,0:T(8,128)(2,1)S(1)}, bf16[640,128]{1,0:T(8,128)(2,1)}, u32[]{:S(2)}) %copy-start.13) | copy-done | bytes 163864
  66.7 0.9 %copy-done.15 = bf16[640,128]{1,0:T(8,128)(2,1)S(1)} copy-done((bf16[640,128]{1,0:T(8,128)(2,1)S(1)}, bf16[640,128]{1,0:T(8,128)(2,1)}, u32[]{:S(2)}) %copy-start.15) | copy-done | bytes 163864
  67.7 0.9 %copy-done.18 = bf16[512,256]{1,0:T(8,128)(2,1)S(1)} copy-done((bf16[512,256]{1,0:T(8,128)(2,1)S(1)}, bf16[512,256]{1,0:T(8,128)(2,1)}, u32[]{:S(2)}) %copy-start.18) | copy-done | bytes 262168
  68.6 4.4 %shard_map.60 = (bf16[8,32,2,16,128]{4,3,2,1,0:T(8,128)(2,1)}, bf16[64,2,16,128]{3,2,1,0:T(8,128)(2,1)}) custom-call(bf16[256,4608]{1,0:T(8,128)(2,1)S(1)} %get-tuple-element.24.ga, bf16[256,4608]{1,0:T(8,128)(2,1)S(1)} %copy-done.2, f32[76,64,128]{2,1,0:T(8,128)S(1)} %copy-done.4, bf16[256,2048]{1,0:T(8,128)(2,1)S(1)} %copy-done.11, ...), custom_call_target="tpu_custom_call" | custom-call | tf_op jit(solution)/shard_map/pallas_call | solution.py:701
  73.0 2.1 %shard_map.62 = f32[4,4,4,32,64]{4,3,2,1,0:T(8,128)} custom-call(bf16[32,32,128]{2,1,0:T(8,128)(2,1)} %all-to-all-done.1.packed), custom_call_target="tpu_custom_call" | custom-call | tf_op jit(solution)/shard_map/pallas_call | solution.py:728
  (50 shorter events, 0.3 us)
Async XLA Ops:
  0.6 9.2 %copy-start = (bf16[2,2,2,32,2,16,128]{6,5,4,3,2,1,0:T(8,128)(2,1)S(1)}, bf16[2,2,2,32,2,16,128]{6,5,4,3,2,1,0:T(8,128)(2,1)}, u32[]{:S(2)}) copy-start(bf16[2,2,2,32,2,16,128]{6,5,4,3,2,1,0:T(8,128)(2,1)} %param.5) | copy-start | bytes 6291460
  0.6 9.2 %copy-start.5 = (bf16[64,2,16,128]{3,2,1,0:T(8,128)(2,1)S(1)}, bf16[64,2,16,128]{3,2,1,0:T(8,128)(2,1)}, u32[]{:S(2)}) copy-start(bf16[64,2,16,128]{3,2,1,0:T(8,128)(2,1)} %vol_in.1) | copy-start | bytes 1572868
  0.7 9.2 %copy-start.16 = (bf16[4,4,4,32,64]{4,3,2,1,0:T(8,128)(2,1)S(1)}, bf16[4,4,4,32,64]{4,3,2,1,0:T(8,128)(2,1)}, u32[]{:S(2)}) copy-start(bf16[4,4,4,32,64]{4,3,2,1,0:T(8,128)(2,1)} %taps_in.1) | copy-start | bytes 786436
  3.2 17.3 %collective-permute-start = (bf16[1152,128]{1,0:T(8,128)(2,1)S(1)}, bf16[1152,128]{1,0:T(8,128)(2,1)S(1)}, u32[]{:S(2)}, u32[]{:S(2)}) collective-permute-start(bf16[1152,128]{1,0:T(8,128)(2,1)S(1)} %pad_maximum_fusion), channel_id=1, source_target_pairs={{0,4},{4,8},{8,12},{12,16},{16,20},{20,24},{24,28},{1,5},{5,9},{9,... | collective-permute-start | bytes 884744 | tf_op jit(solution)/shard_map/ppermute | solution.py:614
  7.9 12.7 %collective-permute-start.1 = (bf16[1152,128]{1,0:T(8,128)(2,1)S(1)}, bf16[1152,128]{1,0:T(8,128)(2,1)S(1)}, u32[]{:S(2)}, u32[]{:S(2)}) collective-permute-start(bf16[1152,128]{1,0:T(8,128)(2,1)S(1)} %pad_maximum_fusion.1), channel_id=1, source_target_pairs={{4,0},{8,4},{12,8},{16,12},{20,16},{24,20},{28,24},{5,1},{9,5},{13... | collective-permute-start | bytes 884744 | tf_op jit(solution)/shard_map/ppermute | solution.py:615
  13.7 1.0 %copy-start.8 = (f32[2,64,2048]{2,1,0:T(8,128)}, f32[2,64,2048]{2,1,0:T(8,128)S(1)}, u32[]{:S(2)}) copy-start(f32[2,64,2048]{2,1,0:T(8,128)S(1)} %get-tuple-element.33.ig_in) | copy-start | bytes 3145732
  14.7 14.2 %copy-start.6 = (bf16[1,256,2048]{2,1,0:T(8,128)(2,1)}, bf16[1,256,2048]{2,1,0:T(8,128)(2,1)S(1)}, u32[]{:S(2)}) copy-start(bf16[1,256,2048]{2,1,0:T(8,128)(2,1)S(1)} %get-tuple-element.32.inner_vals) | copy-start | bytes 3145732
  14.7 14.2 %copy-start.17 = (bf16[512,256]{1,0:T(8,128)(2,1)}, bf16[512,256]{1,0:T(8,128)(2,1)S(1)}, u32[]{:S(2)}) copy-start(bf16[512,256]{1,0:T(8,128)(2,1)S(1)} %get-tuple-element.31.wt) | copy-start | bytes 786436
  14.7 20.0 %collective-permute-start.4 = (bf16[4,32,16,128]{3,2,1,0:T(8,128)(2,1)S(1)}, bf16[4,32,16,128]{3,2,1,0:T(8,128)(2,1)S(1)}, u32[]{:S(2)}, u32[]{:S(2)}) collective-permute-start(bf16[4,32,16,128]{3,2,1,0:T(8,128)(2,1)S(1)} %get-tuple-element.29), channel_id=1, source_target_pairs={{0,4},{4,8},{8,12},{12,16},{16,20},{20,24},{24,28},{1,5},{5,9},{9,... | collective-permute-start | bytes 1572872 | tf_op jit(solution)/shard_map/ppermute | solution.py:669
  18.3 16.4 %collective-permute-start.5 = (bf16[4,32,16,128]{3,2,1,0:T(8,128)(2,1)S(1)}, bf16[4,32,16,128]{3,2,1,0:T(8,128)(2,1)S(1)}, u32[]{:S(2)}, u32[]{:S(2)}) collective-permute-start(bf16[4,32,16,128]{3,2,1,0:T(8,128)(2,1)S(1)} %get-tuple-element.30), channel_id=1, source_target_pairs={{4,0},{8,4},{12,8},{16,12},{20,16},{24,20},{28,24},{5,1},{9,5},{13... | collective-permute-start | bytes 1572872 | tf_op jit(solution)/shard_map/ppermute | solution.py:670
  20.7 6.5 %collective-permute-start.3 = (bf16[640,128]{1,0:T(8,128)(2,1)S(1)}, bf16[640,128]{1,0:T(8,128)(2,1)S(1)}, u32[]{:S(2)}, u32[]{:S(2)}) collective-permute-start(bf16[640,128]{1,0:T(8,128)(2,1)S(1)} %get-tuple-element.49), channel_id=1, source_target_pairs={{1,0},{2,1},{3,2},{5,4},{6,5},{7,6},{9,8},{10,9},{11,10},{13,12},{... | collective-permute-start | bytes 491528 | tf_op jit(solution)/shard_map/ppermute | solution.py:668
  22.0 6.9 %collective-permute-start.2 = (bf16[640,128]{1,0:T(8,128)(2,1)S(1)}, bf16[640,128]{1,0:T(8,128)(2,1)S(1)}, u32[]{:S(2)}, u32[]{:S(2)}) collective-permute-start(bf16[640,128]{1,0:T(8,128)(2,1)S(1)} %get-tuple-element.50), channel_id=1, source_target_pairs={{0,1},{1,2},{2,3},{4,5},{5,6},{6,7},{8,9},{9,10},{10,11},{12,13},{... | collective-permute-start | bytes 491528 | tf_op jit(solution)/shard_map/ppermute | solution.py:667
  27.1 9.0 %copy-start.12 = (bf16[640,128]{1,0:T(8,128)(2,1)}, bf16[640,128]{1,0:T(8,128)(2,1)S(1)}, u32[]{:S(2)}) copy-start(bf16[640,128]{1,0:T(8,128)(2,1)S(1)} %collective-permute-done.3.yhi_in) | copy-start | bytes 491524
  28.9 7.2 %copy-start.14 = (bf16[640,128]{1,0:T(8,128)(2,1)}, bf16[640,128]{1,0:T(8,128)(2,1)S(1)}, u32[]{:S(2)}) copy-start(bf16[640,128]{1,0:T(8,128)(2,1)S(1)} %collective-permute-done.2.ylo_in) | copy-start | bytes 491524
  32.2 1.5 %copy-start.3 = (f32[76,64,128]{2,1,0:T(8,128)}, f32[76,64,128]{2,1,0:T(8,128)S(1)}, u32[]{:S(2)}) copy-start(f32[76,64,128]{2,1,0:T(8,128)S(1)} %get-tuple-element.26.pre) | copy-start | bytes 7471108
  33.7 1.0 %copy-start.10 = (bf16[256,2048]{1,0:T(8,128)(2,1)}, bf16[256,2048]{1,0:T(8,128)(2,1)S(1)}, u32[]{:S(2)}) copy-start(bf16[256,2048]{1,0:T(8,128)(2,1)S(1)} %get-tuple-element.27.vals) | copy-start | bytes 3145732
  34.7 1.5 %copy-start.1 = (bf16[256,4608]{1,0:T(8,128)(2,1)}, bf16[256,4608]{1,0:T(8,128)(2,1)S(1)}, u32[]{:S(2)}) copy-start(bf16[256,4608]{1,0:T(8,128)(2,1)S(1)} %get-tuple-element.25.gb) | copy-start | bytes 7077892
  55.5 17.5 %all-to-all-start.1 = ((bf16[32,32,128]{2,1,0:T(8,128)(2,1)}), bf16[32,32,128]{2,1,0:T(8,128)(2,1)}, u32[]{:S(2)}, u32[]{:S(2)}) async-start(bf16[32,32,128]{2,1,0:T(8,128)(2,1)} %broadcast_in_dim.2), calls=%async_computation.1 | async-start | bytes 524288 | tf_op jit(solution)/shard_map/all_to_all | solution.py:727
  58.8 1.7 %copy-start.2 = (bf16[256,4608]{1,0:T(8,128)(2,1)S(1)}, bf16[256,4608]{1,0:T(8,128)(2,1)}, u32[]{:S(2)}) copy-start(bf16[256,4608]{1,0:T(8,128)(2,1)} %copy-done.1) | copy-start | bytes 7077892
  60.4 1.7 %copy-start.4 = (f32[76,64,128]{2,1,0:T(8,128)S(1)}, f32[76,64,128]{2,1,0:T(8,128)}, u32[]{:S(2)}) copy-start(f32[76,64,128]{2,1,0:T(8,128)} %copy-done.3) | copy-start | bytes 7471108
  62.1 1.2 %copy-start.7 = (bf16[1,256,2048]{2,1,0:T(8,128)(2,1)S(1)}, bf16[1,256,2048]{2,1,0:T(8,128)(2,1)}, u32[]{:S(2)}) copy-start(bf16[1,256,2048]{2,1,0:T(8,128)(2,1)} %copy-done.6) | copy-start | bytes 3145732
  63.4 1.2 %copy-start.9 = (f32[2,64,2048]{2,1,0:T(8,128)S(1)}, f32[2,64,2048]{2,1,0:T(8,128)}, u32[]{:S(2)}) copy-start(f32[2,64,2048]{2,1,0:T(8,128)} %copy-done.8) | copy-start | bytes 3145732
  64.6 1.2 %copy-start.11 = (bf16[256,2048]{1,0:T(8,128)(2,1)S(1)}, bf16[256,2048]{1,0:T(8,128)(2,1)}, u32[]{:S(2)}) copy-start(bf16[256,2048]{1,0:T(8,128)(2,1)} %copy-done.10) | copy-start | bytes 3145732
  65.8 0.9 %copy-start.13 = (bf16[640,128]{1,0:T(8,128)(2,1)S(1)}, bf16[640,128]{1,0:T(8,128)(2,1)}, u32[]{:S(2)}) copy-start(bf16[640,128]{1,0:T(8,128)(2,1)} %copy-done.12) | copy-start | bytes 491524
  66.7 0.9 %copy-start.15 = (bf16[640,128]{1,0:T(8,128)(2,1)S(1)}, bf16[640,128]{1,0:T(8,128)(2,1)}, u32[]{:S(2)}) copy-start(bf16[640,128]{1,0:T(8,128)(2,1)} %copy-done.14) | copy-start | bytes 491524
  67.7 0.9 %copy-start.18 = (bf16[512,256]{1,0:T(8,128)(2,1)S(1)}, bf16[512,256]{1,0:T(8,128)(2,1)}, u32[]{:S(2)}) copy-start(bf16[512,256]{1,0:T(8,128)(2,1)} %copy-done.17) | copy-start | bytes 786436

commit v9 on v8

--- a/solution.py
+++ b/solution.py
@@ -54,7 +54,7 @@
     )
 
 
-def forward_pass(dims, chunk, columns, block, rolled, w, cot_at, put_value, put_foreign, ga, gb):
+def forward_pass(dims, chunk, columns, block, rolled, w, cot_at, put_value, put_foreign, ga, gb, base_column=0):
     nx, ny, nz, ci, co = dims
     half = 4 * ci
     first = lax.broadcasted_iota(jnp.int32, (co, nz), 1) == 0
@@ -67,7 +67,8 @@
         here = jnp.dot(w[:, :half], corners(block, some), preferred_element_type=F32)
         for k, (i, j) in enumerate(some):
             cols = slice(k * nz, (k + 1) * nz)
-            wide = slice((c0 + k) * nz, (c0 + k + 1) * nz)
+            at = base_column + c0 + k
+            wide = slice(at * nz, (at + 1) * nz)
             for tx in range(2):
                 for ty in range(2):
                     sx, sy = 1 - tx, 1 - ty
@@ -171,13 +172,16 @@
     cot,
     flat,
     w,
+    wt_out,
+    vals_out,
+    cot_edge,
+    wg,
+    ig_out,
+    face_up,
+    face_down,
     wt,
     vals,
-    cot_edge,
-    wg,
     ig,
-    face_up,
-    face_down,
     vol,
     taps,
     sems,
@@ -227,6 +231,8 @@
                         c = (2 * ez + ex) * 2 * ci
                         w[r : r + co, c : c + 2 * ci] = jnp.concatenate(pair, axis=1)
     wt[...] = w[...].T
+    leaving.append(pltpu.make_async_copy(wt, wt_out, sems.at[4]))
+    leaving[-1].start()
 
     for x in range(nx):
 
@@ -266,8 +272,12 @@
 
     columns = [(i, j) for i in range(1, nx) for j in range(1, ny)]
     forward_pass(dims, chunk, columns, block, rolled, w, cot_at, put_value, None, ga, gb)
+    leaving.append(pltpu.make_async_copy(vals, vals_out, sems.at[5]))
+    leaving[-1].start()
+    input_pass(dims, chunk, columns, wt, cut_grads, ig_add)
+    leaving.append(pltpu.make_async_copy(ig, ig_out, sems.at[6]))
+    leaving[-1].start()
     weight_pass(columns, block, rolled, ga, gb, wg_add)
-    input_pass(dims, chunk, columns, wt, cut_grads, ig_add)
     for copy in leaving:
         copy.wait()
 
@@ -283,13 +293,16 @@
     w,
     cot,
     cot_edge,
+    pre_out,
+    vals_out,
+    val_edge_out,
     ga,
     gb,
+    plain,
+    vm,
     pre,
     vals,
     val_edge,
-    plain,
-    vm,
     xraw,
     yraw,
     cots,
@@ -362,23 +375,42 @@
     def put_foreign(key, tz, value):
         pre[spots[key], tz * co : (tz + 1) * co] = value
 
-    forward_pass(
-        dims,
-        chunk,
-        outer_columns(nx, ny),
-        block,
-        rolled,
-        w,
-        cot_at,
-        put_value,
-        put_foreign,
-        ga,
-        gb,
-    )
-
-
-def weight_kernel(dims, plain, vm, ga, gb, wg_in, face_lo, face_hi, wg):
+    leaving = []
+
+    def leave(src, dst):
+        leaving.append(pltpu.make_async_copy(src, dst, sems.at[4 + len(leaving)]))
+        leaving[-1].start()
+
+    columns = outer_columns(nx, ny)
+    sent = 0
+    for k, i in enumerate((0, nx, None)):
+        c0 = k * (ny + 1)
+        some = columns[c0 : c0 + ny + 1] if k < 2 else columns[c0:]
+        forward_pass(
+            dims, chunk, some, block, rolled, w, cot_at, put_value, put_foreign, ga, gb, c0
+        )
+        upto = sent + sum(spot[:2] in some for spot in spots)
+        leave(pre.at[sent:upto], pre_out.at[sent:upto])
+        sent = upto
+        if k < 2:
+            rows = pl.ds(4 * k * co, 4 * co)
+            leave(vals.at[rows], vals_out.at[rows])
+        else:
+            leave(val_edge, val_edge_out)
+    for copy in leaving:
+        copy.wait()
+
+
+def weight_kernel(
+    dims, plain, vm, ga, gb, wg_in, face_lo, face_hi, wg, ga_out, gb_out, sems
+):
     del face_lo, face_hi
+    leaving = [
+        pltpu.make_async_copy(ga, ga_out, sems.at[0]),
+        pltpu.make_async_copy(gb, gb_out, sems.at[1]),
+    ]
+    for copy in leaving:
+        copy.start()
     nx, ny, nz, ci, co = dims
     half = 4 * ci
 
@@ -400,27 +432,36 @@
         gb,
         wg_add,
     )
+    for copy in leaving:
+        copy.wait()
 
 
 def last_kernel(
     dims,
     chunk,
+    ga_in,
+    gb_in,
+    pre_in,
+    vals_in,
+    val_edge_in,
+    xlo_in,
+    xhi_in,
+    ylo_in,
+    yhi_in,
+    wt_in,
+    inner_vals_in,
+    ig_in,
+    act_out,
+    ig_out,
     ga,
     gb,
     pre,
     vals,
     val_edge,
-    xlo_in,
-    xhi_in,
-    ylo_in,
-    yhi_in,
+    xraw,
+    yraw,
     wt,
     inner_vals,
-    ig_in,
-    act_out,
-    ig_out,
-    xraw,
-    yraw,
     ig,
     cots,
     staged,
@@ -431,16 +472,26 @@
     to_y = swap_matrix(GROUP, ny)
     to_c = swap_matrix(ny, GROUP)
     skip = (nx + 2) * ci
+    early = [(vals_in, vals), (val_edge_in, val_edge), (inner_vals_in, inner_vals)]
     late = [
         (xlo_in, xraw.at[0]),
         (xhi_in, xraw.at[1]),
         (ylo_in.at[skip:], yraw.at[0]),
         (yhi_in.at[skip:], yraw.at[1]),
+        (ga_in, ga),
+        (gb_in, gb),
+        (pre_in, pre),
+        (wt_in, wt),
+        (ig_in, ig),
     ]
-    copies = [pltpu.make_async_copy(src, dst, sems.at[k]) for k, (src, dst) in enumerate(late)]
+    copies = [
+        pltpu.make_async_copy(src, dst, sems.at[k]) for k, (src, dst) in enumerate(early + late)
+    ]
     for copy in copies:
         copy.start()
     spot = len(copies)
+    for copy in copies[: len(early)]:
+        copy.wait()
     leaving = []
 
     for m in range(nx):
@@ -471,7 +522,7 @@
             )
             leaving[-1].start()
 
-    for copy in copies:
+    for copy in copies[len(early) :]:
         copy.wait()
     for side in range(2):
         for p in range(4):
@@ -536,14 +587,9 @@
 
     def ig_add(m, y, value, fresh):
         lanes = slice(y * nz, (y + 1) * nz)
-        ig[m, :, lanes] = (ig_in if fresh else ig)[m, :, lanes] + value
-
-    started = input_pass(dims, chunk, outer_columns(nx, ny), wt, cut_grads, ig_add)
-    for m in range(nx):
-        for y in range(ny):
-            if (m, y) not in started:
-                lanes = slice(y * nz, (y + 1) * nz)
-                ig[m, :, lanes] = ig_in[m, :, lanes]
+        ig[m, :, lanes] = ig[m, :, lanes] + value
+
+    input_pass(dims, chunk, outer_columns(nx, ny), wt, cut_grads, ig_add)
     for m in range(nx):
         for k in range(0, ci // GROUP, 2):
             tiles = []
@@ -578,12 +624,12 @@
                             ]
 
 
-def held(shape, dtype):
-    return pltpu.VMEM(shape, dtype)
-
-
-def hold(array):
-    return pltpu.with_memory_space_constraint(array, pltpu.VMEM)
+def far(shape, dtype):
+    return pltpu.HBM(shape, dtype)
+
+
+def stay(array):
+    return pltpu.with_memory_space_constraint(array, pltpu.HBM)
 
 
 def neighbours(axis):
@@ -617,28 +663,32 @@
     vmem = pl.BlockSpec(memory_space=pltpu.VMEM)
     smem = pl.BlockSpec(memory_space=pltpu.SMEM)
     anywhere = pl.BlockSpec(memory_space=pl.ANY)
+    hbm = pl.BlockSpec(memory_space=pltpu.HBM)
     params = pltpu.CompilerParams(vmem_limit_bytes=24 * 1024 * 1024)
     n_in = (nx - 1) * (ny - 1)
     n_out = 2 * (ny + 1) + 2 * (nx - 1)
-    flat, w, wt, vals, cot_edge, wg_part, ig_part, face_up, face_down = pl.pallas_call(
+    flat, w, wt, inner_vals, cot_edge, wg_part, ig_part, face_up, face_down = pl.pallas_call(
         functools.partial(inner_kernel, dims, 5),
         out_shape=(
             jax.ShapeDtypeStruct((nx, ci, ny * nz), BF16),
             jax.ShapeDtypeStruct((8 * co, 8 * ci), BF16),
-            jax.ShapeDtypeStruct((8 * ci, 8 * co), BF16),
-            held((nx - 1, 8 * co, ny * nz), BF16),
+            far((8 * ci, 8 * co), BF16),
+            far((nx - 1, 8 * co, ny * nz), BF16),
             jax.ShapeDtypeStruct((nx - 1, 8 * co, nz), BF16),
-            held((8 * co, 8 * ci), F32),
-            held((nx, ci, ny * nz), F32),
-            jax.ShapeDtypeStruct((4, co, ny, nz), BF16),
-            jax.ShapeDtypeStruct((4, co, ny, nz), BF16),
+            jax.ShapeDtypeStruct((8 * co, 8 * ci), F32),
+            far((nx, ci, ny * nz), F32),
+            far((4, co, ny, nz), BF16),
+            far((4, co, ny, nz), BF16),
         ),
         in_specs=[anywhere, anywhere, vmem],
-        out_specs=(vmem,) * 7 + (anywhere,) * 2,
+        out_specs=(vmem, vmem, hbm, hbm, vmem, vmem, hbm, hbm, hbm),
         scratch_shapes=[
+            pltpu.VMEM((8 * ci, 8 * co), BF16),
+            pltpu.VMEM((nx - 1, 8 * co, ny * nz), BF16),
+            pltpu.VMEM((nx, ci, ny * nz), F32),
             pltpu.VMEM(volume.shape, BF16),
             pltpu.VMEM(kernel.shape, BF16),
-            pltpu.SemaphoreType.DMA((4,)),
+            pltpu.SemaphoreType.DMA((7,)),
             pltpu.VMEM((nx, ci, ny * nz), BF16),
             pltpu.VMEM((8 * co, n_in * nz), BF16),
             pltpu.VMEM((8 * co, n_in * nz), BF16),
@@ -669,54 +719,73 @@
     face_lo = lax.ppermute(face_up, "gx", gx_up)
     face_hi = lax.ppermute(face_down, "gx", gx_down)
     foreign = len(foreign_spots(nx, ny))
-    *passed, plain, vm = pl.pallas_call(
+    pre_shape = (foreign, 2 * co, nz)
+    pre, vals, val_edge, ga, gb, plain, vm = pl.pallas_call(
         functools.partial(outer_kernel, dims, 4),
         out_shape=(
-            held((8 * co, n_out * nz), BF16),
-            held((8 * co, n_out * nz), BF16),
-            held((foreign, 2 * co, nz), F32),
-            held((8 * co, ny * nz), BF16),
-            held((nx - 1, 8 * co, nz), BF16),
-            held((nx + 2, ci, (ny + 2) * nz), BF16),
-            held((nx + 2, ci, (ny + 2) * nz), BF16),
+            far(pre_shape, F32),
+            far((8 * co, ny * nz), BF16),
+            far((nx - 1, 8 * co, nz), BF16),
+            jax.ShapeDtypeStruct((8 * co, n_out * nz), BF16),
+            jax.ShapeDtypeStruct((8 * co, n_out * nz), BF16),
+            jax.ShapeDtypeStruct((nx + 2, ci, (ny + 2) * nz), BF16),
+            jax.ShapeDtypeStruct((nx + 2, ci, (ny + 2) * nz), BF16),
         ),
         in_specs=[vmem] + [anywhere] * 4 + [vmem] * 3,
-        out_specs=(vmem,) * 7,
+        out_specs=(hbm,) * 3 + (vmem,) * 4,
         scratch_shapes=[
+            pltpu.VMEM(pre_shape, F32),
+            pltpu.VMEM((8 * co, ny * nz), BF16),
+            pltpu.VMEM((nx - 1, 8 * co, nz), BF16),
             pltpu.VMEM((2, ny * ci, nz), BF16),
             pltpu.VMEM((2, (nx + 2) * ci, nz), BF16),
             pltpu.VMEM((8 * co, ny * nz), BF16),
-            pltpu.SemaphoreType.DMA((4,)),
+            pltpu.SemaphoreType.DMA((10,)),
         ],
         compiler_params=params,
     )(flat, xlo, xhi, ylo, yhi, w, cot, cot_edge)
-    passed = [hold(p) for p in passed]
-    wg = pl.pallas_call(
+    wg, ga, gb = pl.pallas_call(
         functools.partial(weight_kernel, dims),
-        out_shape=jax.ShapeDtypeStruct((32, co, 2 * ci), BF16),
+        out_shape=(
+            jax.ShapeDtypeStruct((32, co, 2 * ci), BF16),
+            far((8 * co, n_out * nz), BF16),
+            far((8 * co, n_out * nz), BF16),
+        ),
         in_specs=[vmem] * 5 + [anywhere] * 2,
-        out_specs=vmem,
+        out_specs=(vmem, hbm, hbm),
+        scratch_shapes=[pltpu.SemaphoreType.DMA((2,))],
         compiler_params=params,
-    )(hold(plain), hold(vm), passed[0], passed[1], hold(wg_part), face_lo, face_hi)
+    )(plain, vm, ga, gb, wg_part, face_lo, face_hi)
+    passed = [
+        stay(array)
+        for array in (ga, gb, pre, vals, val_edge, face_lo, face_hi, ylo, yhi, wt, inner_vals, ig_part)
+    ]
     act, input_grad = pl.pallas_call(
         functools.partial(last_kernel, dims, 4),
         out_shape=(
             jax.ShapeDtypeStruct(cot.shape, BF16),
             jax.ShapeDtypeStruct(volume.shape, BF16),
         ),
-        in_specs=[vmem] * 5 + [anywhere] * 4 + [vmem] * 3,
+        in_specs=[hbm] * 12,
         out_specs=(anywhere,) * 2,
         scratch_shapes=[
+            pltpu.VMEM((8 * co, n_out * nz), BF16),
+            pltpu.VMEM((8 * co, n_out * nz), BF16),
+            pltpu.VMEM(pre_shape, F32),
+            pltpu.VMEM((8 * co, ny * nz), BF16),
+            pltpu.VMEM((nx - 1, 8 * co, nz), BF16),
             pltpu.VMEM((2, 4, co, ny, nz), BF16),
             pltpu.VMEM((2, 4 * co * nx + 4 * co, nz), BF16),
+            pltpu.VMEM((8 * ci, 8 * co), BF16),
+            pltpu.VMEM((nx - 1, 8 * co, ny * nz), BF16),
             pltpu.VMEM((nx, ci, ny * nz), F32),
             pltpu.VMEM((2, 4 * co, ny * nz), BF16),
             pltpu.VMEM((8 * nx, co, ny, nz), BF16),
             pltpu.VMEM(volume.shape, BF16),
-            pltpu.SemaphoreType.DMA((5 + 8 * nx,)),
+            pltpu.SemaphoreType.DMA((13 + 8 * nx,)),
         ],
         compiler_params=params,
-    )(*passed, face_lo, face_hi, ylo, yhi, wt, hold(vals), hold(ig_part))
+    )(*passed)
 
     scale = 1.0 / math.sqrt(cells)
     devices = gx * gy

time: 76 us -> 69.6 us (0.916)
  local copies, waits for them, and re-layouts: 16.9 us -> 3.92 us
  Pallas kernels: 15 us -> 21.1 us
  waiting for transfers between devices: 2.92 us -> 4.72 us
    unnamed x48 -> x24, local copies, waits for them, and re-layouts: 13.3 us -> 0.33 us
    pallas_call x1, Pallas kernels: 4.41 us -> 8.52 us  [on_device(): pl.pallas_call(functools.partial(last_kernel, dims, 4), out_shape=(jax.Sh...]
    pallas_call x2, Pallas kernels: 4.75 us -> 6.95 us  [the longest x1 4.71 us: on_device(): pl.pallas_call(functools.partial(outer_kernel, dims, 4), out_shape=(far(p...]
    all_to_all x1, waiting for transfers between devices: 0.01 us -> 1.81 us  [on_device(): pieces = lax.all_to_all(pieces, ('gx', 'gy'), 0, 0, tiled=True)]
    pallas_call x1, Pallas kernels: 2.06 us -> 1.11 us  [on_device(): pl.pallas_call(functools.partial(unpack_kernel, co, ci), out_shape=jax.Sh...]
  transfers between devices with their start and end apart: 7 -> 7, of which waited for: 2 -> 3; matrix products, arithmetic and copies ran while one was open for 1% -> 1% of each run, Pallas kernels for 15% -> 26%
where the time goes in v9:
time: 69.6 us; the launch traced here: 69.3 us
  Pallas kernels  21.1 us (30%)
  starting transfers between devices  19.9 us (29%)
  blocking collectives  18.6 us (27%)
  waiting for transfers between devices  4.72 us (7%)
  local copies, waits for them, and re-layouts  3.92 us (6%)
  between operations  0.97 us (1%)
    all_to_all x1, blocking collectives, on_device(): shares = lax.all_to_all(shares, ('gx', 'gy'), 0, 0, tiled=True)  18.6 us
    pallas_call x1, Pallas kernels, on_device(): pl.pallas_call(functools.partial(last_kernel, dims, 4), out_shape=(jax.Sh...  8.52 us
    pallas_call x1, Pallas kernels, on_device(): pl.pallas_call(functools.partial(outer_kernel, dims, 4), out_shape=(far(p...  4.71 us
    ppermute x1, starting transfers between devices, on_device(): xlo = lax.ppermute(x_message(1), 'gx', gx_up)  4.51 us
    pallas_call x1, Pallas kernels, on_device(): pl.pallas_call(functools.partial(inner_kernel, dims, 5), out_shape=(jax.S...  4.49 us
    ppermute x1, starting transfers between devices, on_device(): ylo = lax.ppermute(y_message(1), 'gy', gy_up)  4 us
    ppermute x1, starting transfers between devices, on_device(): face_lo = lax.ppermute(face_up, 'gx', gx_up)  3.64 us
    all_to_all x1, starting transfers between devices, on_device(): pieces = lax.all_to_all(pieces, ('gx', 'gy'), 0, 0, tiled=True)  2.58 us
  transfers between devices with their start and end apart: 7, of which 3 were waited for; matrix products, arithmetic and copies ran while one was open for 1% of the time, Pallas kernels for 26%

profile of v9, /device:TPU:1, one launch (start us, length us, event | category | flops | bytes accessed | tf_op | source)
XLA Modules:
  0.0 69.3 jit_solution(3528031144791084692)
XLA Ops:
  0.6 0.0 copy-start.3
  0.7 1.4 %fusion.1 = (bf16[1,1,2,32,1,1,128]{6,5,4,3,2,1,0:T(2,128)(2,1)S(1)}, bf16[1,1,2,32,1,1,128]{6,5,4,3,2,1,0:T(2,128)(2,1)S(1)}, bf16[1,1,2,32,1,1,128]{6,5,4,3,2,...) fusion(bf16[2,2,2,32,2,16,128]{6,5,4,3,2,1,0:T(8,128)(2,1)} %param.5), kind=kLoop, calls=%fused_computation.19 | loop fusion | bytes 131072 | tf_op jit(solution)/shard_map/slice | solution.py:654
  2.1 1.1 %slice_bitcast_fusion = (bf16[16,64,128]{2,0,1:T(8,128)(2,1)S(1)}, bf16[16,64,128]{2,0,1:T(8,128)(2,1)S(1)}) fusion(bf16[64,2,16,128]{3,2,1,0:T(8,128)(2,1)} %vol_in.1), kind=kLoop, calls=%fused_computation.3 | loop fusion | bytes 1048576 | tf_op jit(solution)/shard_map/transpose | solution.py:657
  3.1 0.1 copy.10
  3.2 4.5 %collective-permute-start = (bf16[1152,128]{1,0:T(8,128)(2,1)S(1)}, bf16[1152,128]{1,0:T(8,128)(2,1)S(1)}, u32[]{:S(2)}, u32[]{:S(2)}) collective-permute-start(bf16[1152,128]{1,0:T(8,128)(2,1)S(1)} %pad_maximum_fusion), channel_id=1, source_target_pairs={{0,4},{4,8},{8,12},{12,16},{16,20},{20,24},{24,28},{1,5},{5,9},{9,... | collective-permute-start | bytes 884744 | tf_op jit(solution)/shard_map/ppermute | solution.py:660
  7.8 0.1 copy.13
  7.9 1.9 %collective-permute-start.1 = (bf16[1152,128]{1,0:T(8,128)(2,1)S(1)}, bf16[1152,128]{1,0:T(8,128)(2,1)S(1)}, u32[]{:S(2)}, u32[]{:S(2)}) collective-permute-start(bf16[1152,128]{1,0:T(8,128)(2,1)S(1)} %pad_maximum_fusion.1), channel_id=1, source_target_pairs={{4,0},{8,4},{12,8},{16,12},{20,16},{24,20},{28,24},{5,1},{9,5},{13... | collective-permute-start | bytes 884744 | tf_op jit(solution)/shard_map/ppermute | solution.py:661
  9.8 4.5 %shard_map.58 = (bf16[2,64,2048]{2,1,0:T(8,128)(2,1)S(1)}, bf16[256,512]{1,0:T(8,128)(2,1)S(1)}, bf16[512,256]{1,0:T(8,128)(2,1)}, bf16[1,256,2048]{2,1,0:T(8,12...) custom-call(bf16[64,2,16,128]{3,2,1,0:T(8,128)(2,1)S(1)} %copy-done., ...), custom_call_target="tpu_custom_call" | custom-call | tf_op jit(solution)/shard_map/pallas_call | solution.py:670
  14.3 3.6 %collective-permute-start.4 = (bf16[4,32,16,128]{3,2,1,0:T(8,128)(2,1)}, bf16[4,32,16,128]{3,2,1,0:T(8,128)(2,1)S(1)}, u32[]{:S(2)}, u32[]{:S(2)}) collective-permute-start(bf16[4,32,16,128]{3,2,1,0:T(8,128)(2,1)} %get-tuple-element.32), channel_id=1, source_target_pairs={{0,4},{4,8},{8,12},{12,16},{16,20},{20,24},{24,28},{1,5},{5,9},{9,... | collective-permute-start | bytes 1572872 | tf_op jit(solution)/shard_map/ppermute | solution.py:719
  18.0 1.9 %collective-permute-start.5 = (bf16[4,32,16,128]{3,2,1,0:T(8,128)(2,1)}, bf16[4,32,16,128]{3,2,1,0:T(8,128)(2,1)S(1)}, u32[]{:S(2)}, u32[]{:S(2)}) collective-permute-start(bf16[4,32,16,128]{3,2,1,0:T(8,128)(2,1)} %get-tuple-element.33), channel_id=1, source_target_pairs={{4,0},{8,4},{12,8},{16,12},{20,16},{24,20},{28,24},{5,1},{9,5},{13... | collective-permute-start | bytes 1572872 | tf_op jit(solution)/shard_map/ppermute | solution.py:720
  19.9 0.2 fusion
  20.2 0.0 collective-permute-done.xlo_in
  20.2 0.0 collective-permute-done.1.xhi_in
  20.3 1.3 %collective-permute-start.3 = (bf16[640,128]{1,0:T(8,128)(2,1)S(1)}, bf16[640,128]{1,0:T(8,128)(2,1)S(1)}, u32[]{:S(2)}, u32[]{:S(2)}) collective-permute-start(bf16[640,128]{1,0:T(8,128)(2,1)S(1)} %get-tuple-element.55), channel_id=1, source_target_pairs={{1,0},{2,1},{3,2},{5,4},{6,5},{7,6},{9,8},{10,9},{11,10},{13,12},{... | collective-permute-start | bytes 491528 | tf_op jit(solution)/shard_map/ppermute | solution.py:718
  21.6 4.0 %collective-permute-start.2 = (bf16[640,128]{1,0:T(8,128)(2,1)S(1)}, bf16[640,128]{1,0:T(8,128)(2,1)S(1)}, u32[]{:S(2)}, u32[]{:S(2)}) collective-permute-start(bf16[640,128]{1,0:T(8,128)(2,1)S(1)} %get-tuple-element.56), channel_id=1, source_target_pairs={{0,1},{1,2},{2,3},{4,5},{5,6},{6,7},{8,9},{9,10},{10,11},{12,13},{... | collective-permute-start | bytes 491528 | tf_op jit(solution)/shard_map/ppermute | solution.py:717
  25.6 1.2 %collective-permute-done.3.yhi_in = bf16[640,128]{1,0:T(8,128)(2,1)S(1)} collective-permute-done((bf16[640,128]{1,0:T(8,128)(2,1)S(1)}, bf16[640,128]{1,0:T(8,128)(2,1)S(1)}, u32[]{:S(2)}, u32[]{:S(2)}) %collective-permute-start.3) | collective-permute-done | bytes 163872 | tf_op jit(solution)/shard_map/ppermute | solution.py:718
  26.8 1.8 %collective-permute-done.2.ylo_in = bf16[640,128]{1,0:T(8,128)(2,1)S(1)} collective-permute-done((bf16[640,128]{1,0:T(8,128)(2,1)S(1)}, bf16[640,128]{1,0:T(8,128)(2,1)S(1)}, u32[]{:S(2)}, u32[]{:S(2)}) %collective-permute-start.2) | collective-permute-done | bytes 163872 | tf_op jit(solution)/shard_map/ppermute | solution.py:717
  28.6 4.7 %shard_map.59 = (f32[76,64,128]{2,1,0:T(8,128)}, bf16[256,2048]{1,0:T(8,128)(2,1)}, bf16[1,256,128]{2,1,0:T(8,128)(2,1)}, bf16[256,4608]{1,0:T(8,128)(2,1)S(1)},...) custom-call(bf16[2,64,2048]{2,1,0:T(8,128)(2,1)S(1)} %get-tuple-element.24.flat, ...), custom_call_target="tpu_custom_call" | custom-call | tf_op jit(solution)/shard_map/pallas_call | solution.py:723
  33.3 0.0 collective-permute-done.4.face_lo.xlo_in
  33.3 0.0 copy-start.1
  33.3 0.0 collective-permute-done.5.face_hi.xhi_in
  33.3 2.2 %shard_map.60 = (bf16[32,32,128]{2,1,0:T(8,128)(2,1)S(1)}, bf16[256,4608]{1,0:T(8,128)(2,1)}, bf16[256,4608]{1,0:T(8,128)(2,1)}) custom-call(bf16[4,64,2304]{2,1,0:T(8,128)(2,1)S(1)} %get-tuple-element.27.plain, bf16[4,64,2304]{2,1,0:T(8,128)(2,1)S(1)} %get-tuple-element.28.vm, bf16[256,4608]{1,0:T(8,128)(2,1)S(1)} %get-tuple-element.29.ga, ...), custom_call_target="tpu_custom_call" | custom-call | tf_op jit(solution)/shard_map/pallas_call | solution.py:747
  35.6 0.0 copy-done.4
  35.6 0.0 copy-done.5
  35.6 0.1 copy-done.1
  35.7 0.1 copy-done.2
  35.8 18.6 %all_to_all.10 = bf16[32,32,128]{2,1,0:T(8,128)(2,1)S(1)} all-to-all(bf16[32,32,128]{2,1,0:T(8,128)(2,1)S(1)} %get-tuple-element.44), channel_id=1, replica_groups=mesh['gx'=8,'gy'=4] {'gx','gy'}, dimensions={0} | all-to-all | bytes 524288 | tf_op jit(solution)/shard_map/all_to_all | solution.py:793
  54.5 0.8 %broadcast_in_dim.2 = bf16[32,32,128]{2,1,0:T(8,128)(2,1)} broadcast(bf16[32,128]{1,0:T(8,128)(2,1)S(1)} %multiply_convert_fusion), dimensions={1,2} | broadcast | bytes 270336 | tf_op jit(solution)/shard_map/broadcast_in_dim | solution.py:795
  55.2 2.6 %all-to-all-start.1 = ((bf16[32,32,128]{2,1,0:T(8,128)(2,1)}), bf16[32,32,128]{2,1,0:T(8,128)(2,1)S(1)}, u32[]{:S(2)}, u32[]{:S(2)}) async-start(bf16[32,32,128]{2,1,0:T(8,128)(2,1)} %broadcast_in_dim.2), calls=%async_computation.1 | async-start | bytes 524288 | tf_op jit(solution)/shard_map/all_to_all | solution.py:796
  57.8 8.5 %shard_map.61 = (bf16[8,32,2,16,128]{4,3,2,1,0:T(8,128)(2,1)}, bf16[64,2,16,128]{3,2,1,0:T(8,128)(2,1)}) custom-call(bf16[256,4608]{1,0:T(8,128)(2,1)} %get-tuple-element.34.ga_in, bf16[256,4608]{1,0:T(8,128)(2,1)} %get-tuple-element.35.gb_in, f32[76,64,128]{2,1,0:T(8,128)} %get-tuple-element.36.pre_in, bf16[256,2048]{1,0:T(8,128)(2,1)} %get-tuple-element.37.vals_in, ...), custom_call_target="tpu_custom_call" | custom-call | tf_op jit(solution)/shard_map/pallas_call | solution.py:763
  66.3 1.8 %all-to-all-done.1.packed = bf16[32,32,128]{2,1,0:T(8,128)(2,1)S(1)} async-done(((bf16[32,32,128]{2,1,0:T(8,128)(2,1)}), bf16[32,32,128]{2,1,0:T(8,128)(2,1)S(1)}, u32[]{:S(2)}, u32[]{:S(2)}) %all-to-all-start.1) | async-done | bytes 262176 | tf_op jit(solution)/shard_map/all_to_all | solution.py:796
  68.1 1.1 %shard_map.62 = f32[4,4,4,32,64]{4,3,2,1,0:T(8,128)} custom-call(bf16[32,32,128]{2,1,0:T(8,128)(2,1)S(1)} %all-to-all-done.1.packed), custom_call_target="tpu_custom_call" | custom-call | tf_op jit(solution)/shard_map/pallas_call | solution.py:797
  (26 shorter events, 0.3 us)
Async XLA Ops:
  0.6 9.2 %copy-start = (bf16[2,2,2,32,2,16,128]{6,5,4,3,2,1,0:T(8,128)(2,1)S(1)}, bf16[2,2,2,32,2,16,128]{6,5,4,3,2,1,0:T(8,128)(2,1)}, u32[]{:S(2)}) copy-start(bf16[2,2,2,32,2,16,128]{6,5,4,3,2,1,0:T(8,128)(2,1)} %param.5) | copy-start | bytes 6291460
  0.6 9.2 %copy-start.3 = (bf16[64,2,16,128]{3,2,1,0:T(8,128)(2,1)S(1)}, bf16[64,2,16,128]{3,2,1,0:T(8,128)(2,1)}, u32[]{:S(2)}) copy-start(bf16[64,2,16,128]{3,2,1,0:T(8,128)(2,1)} %vol_in.1) | copy-start | bytes 1572868
  0.7 9.2 %copy-start.6 = (bf16[4,4,4,32,64]{4,3,2,1,0:T(8,128)(2,1)S(1)}, bf16[4,4,4,32,64]{4,3,2,1,0:T(8,128)(2,1)}, u32[]{:S(2)}) copy-start(bf16[4,4,4,32,64]{4,3,2,1,0:T(8,128)(2,1)} %taps_in.1) | copy-start | bytes 786436
  3.2 17.0 %collective-permute-start = (bf16[1152,128]{1,0:T(8,128)(2,1)S(1)}, bf16[1152,128]{1,0:T(8,128)(2,1)S(1)}, u32[]{:S(2)}, u32[]{:S(2)}) collective-permute-start(bf16[1152,128]{1,0:T(8,128)(2,1)S(1)} %pad_maximum_fusion), channel_id=1, source_target_pairs={{0,4},{4,8},{8,12},{12,16},{16,20},{20,24},{24,28},{1,5},{5,9},{9,... | collective-permute-start | bytes 884744 | tf_op jit(solution)/shard_map/ppermute | solution.py:660
  7.9 12.4 %collective-permute-start.1 = (bf16[1152,128]{1,0:T(8,128)(2,1)S(1)}, bf16[1152,128]{1,0:T(8,128)(2,1)S(1)}, u32[]{:S(2)}, u32[]{:S(2)}) collective-permute-start(bf16[1152,128]{1,0:T(8,128)(2,1)S(1)} %pad_maximum_fusion.1), channel_id=1, source_target_pairs={{4,0},{8,4},{12,8},{16,12},{20,16},{24,20},{28,24},{5,1},{9,5},{13... | collective-permute-start | bytes 884744 | tf_op jit(solution)/shard_map/ppermute | solution.py:661
  14.3 18.9 %collective-permute-start.4 = (bf16[4,32,16,128]{3,2,1,0:T(8,128)(2,1)}, bf16[4,32,16,128]{3,2,1,0:T(8,128)(2,1)S(1)}, u32[]{:S(2)}, u32[]{:S(2)}) collective-permute-start(bf16[4,32,16,128]{3,2,1,0:T(8,128)(2,1)} %get-tuple-element.32), channel_id=1, source_target_pairs={{0,4},{4,8},{8,12},{12,16},{16,20},{20,24},{24,28},{1,5},{5,9},{9,... | collective-permute-start | bytes 1572872 | tf_op jit(solution)/shard_map/ppermute | solution.py:719
  18.0 15.3 %collective-permute-start.5 = (bf16[4,32,16,128]{3,2,1,0:T(8,128)(2,1)}, bf16[4,32,16,128]{3,2,1,0:T(8,128)(2,1)S(1)}, u32[]{:S(2)}, u32[]{:S(2)}) collective-permute-start(bf16[4,32,16,128]{3,2,1,0:T(8,128)(2,1)} %get-tuple-element.33), channel_id=1, source_target_pairs={{4,0},{8,4},{12,8},{16,12},{20,16},{24,20},{28,24},{5,1},{9,5},{13... | collective-permute-start | bytes 1572872 | tf_op jit(solution)/shard_map/ppermute | solution.py:720
  20.3 6.5 %collective-permute-start.3 = (bf16[640,128]{1,0:T(8,128)(2,1)S(1)}, bf16[640,128]{1,0:T(8,128)(2,1)S(1)}, u32[]{:S(2)}, u32[]{:S(2)}) collective-permute-start(bf16[640,128]{1,0:T(8,128)(2,1)S(1)} %get-tuple-element.55), channel_id=1, source_target_pairs={{1,0},{2,1},{3,2},{5,4},{6,5},{7,6},{9,8},{10,9},{11,10},{13,12},{... | collective-permute-start | bytes 491528 | tf_op jit(solution)/shard_map/ppermute | solution.py:718
  21.6 6.9 %collective-permute-start.2 = (bf16[640,128]{1,0:T(8,128)(2,1)S(1)}, bf16[640,128]{1,0:T(8,128)(2,1)S(1)}, u32[]{:S(2)}, u32[]{:S(2)}) collective-permute-start(bf16[640,128]{1,0:T(8,128)(2,1)S(1)} %get-tuple-element.56), channel_id=1, source_target_pairs={{0,1},{1,2},{2,3},{4,5},{5,6},{6,7},{8,9},{9,10},{10,11},{12,13},{... | collective-permute-start | bytes 491528 | tf_op jit(solution)/shard_map/ppermute | solution.py:717
  26.8 8.8 %copy-start.4 = (bf16[640,128]{1,0:T(8,128)(2,1)}, bf16[640,128]{1,0:T(8,128)(2,1)S(1)}, u32[]{:S(2)}) copy-start(bf16[640,128]{1,0:T(8,128)(2,1)S(1)} %collective-permute-done.3.yhi_in) | copy-start | bytes 491524
  28.6 7.0 %copy-start.5 = (bf16[640,128]{1,0:T(8,128)(2,1)}, bf16[640,128]{1,0:T(8,128)(2,1)S(1)}, u32[]{:S(2)}) copy-start(bf16[640,128]{1,0:T(8,128)(2,1)S(1)} %collective-permute-done.2.ylo_in) | copy-start | bytes 491524
  33.3 2.4 %copy-start.1 = (bf16[4,32,16,128]{3,2,1,0:T(8,128)(2,1)}, bf16[4,32,16,128]{3,2,1,0:T(8,128)(2,1)S(1)}, u32[]{:S(2)}) copy-start(bf16[4,32,16,128]{3,2,1,0:T(8,128)(2,1)S(1)} %collective-permute-done.4.face_lo.xlo_in) | copy-start | bytes 1572868
  33.3 2.5 %copy-start.2 = (bf16[4,32,16,128]{3,2,1,0:T(8,128)(2,1)}, bf16[4,32,16,128]{3,2,1,0:T(8,128)(2,1)S(1)}, u32[]{:S(2)}) copy-start(bf16[4,32,16,128]{3,2,1,0:T(8,128)(2,1)S(1)} %collective-permute-done.5.face_hi.xhi_in) | copy-start | bytes 1572868
  55.2 12.9 %all-to-all-start.1 = ((bf16[32,32,128]{2,1,0:T(8,128)(2,1)}), bf16[32,32,128]{2,1,0:T(8,128)(2,1)S(1)}, u32[]{:S(2)}, u32[]{:S(2)}) async-start(bf16[32,32,128]{2,1,0:T(8,128)(2,1)} %broadcast_in_dim.2), calls=%async_computation.1 | async-start | bytes 524288 | tf_op jit(solution)/shard_map/all_to_all | solution.py:796

commit v10 on v9

--- a/solution.py
+++ b/solution.py
@@ -293,12 +293,15 @@
     w,
     cot,
     cot_edge,
+    wg_in,
     pre_out,
     vals_out,
     val_edge_out,
+    ga_out,
+    gb_out,
+    wg,
     ga,
     gb,
-    plain,
     vm,
     pre,
     vals,
@@ -351,7 +354,6 @@
     for x in range(nx + 2):
         for y in range(ny + 2):
             lanes = slice(y * nz, (y + 1) * nz)
-            plain[x, :, lanes] = block(x, y)
             vm[x, :, lanes] = pltpu.roll(block(x, y).astype(F32), 1, 1).astype(BF16)
 
     def rolled(x, y):
@@ -397,25 +399,11 @@
             leave(vals.at[rows], vals_out.at[rows])
         else:
             leave(val_edge, val_edge_out)
-    for copy in leaving:
-        copy.wait()
-
-
-def weight_kernel(
-    dims, plain, vm, ga, gb, wg_in, face_lo, face_hi, wg, ga_out, gb_out, sems
-):
-    del face_lo, face_hi
-    leaving = [
-        pltpu.make_async_copy(ga, ga_out, sems.at[0]),
-        pltpu.make_async_copy(gb, gb_out, sems.at[1]),
-    ]
-    for copy in leaving:
-        copy.start()
-    nx, ny, nz, ci, co = dims
-    half = 4 * ci
+    leave(ga, ga_out)
+    leave(gb, gb_out)
 
     def wg_add(part, total):
-        total = total + wg_in[:, part * half : (part + 1) * half]
+        total = total + wg_in[:, part * 4 * ci : (part + 1) * 4 * ci]
         for ex in range(2):
             for row in range(8):
                 tx, ty, tz = row // 4, row // 2 % 2, row % 2
@@ -424,14 +412,7 @@
                     row * co : (row + 1) * co, ex * 2 * ci : (ex + 1) * 2 * ci
                 ].astype(BF16)
 
-    weight_pass(
-        outer_columns(nx, ny),
-        lambda x, y: plain[x, :, y * nz : (y + 1) * nz],
-        lambda x, y: vm[x, :, y * nz : (y + 1) * nz],
-        ga,
-        gb,
-        wg_add,
-    )
+    weight_pass(columns, block, rolled, ga, gb, wg_add)
     for copy in leaving:
         copy.wait()
 
@@ -720,42 +701,32 @@
     face_hi = lax.ppermute(face_down, "gx", gx_down)
     foreign = len(foreign_spots(nx, ny))
     pre_shape = (foreign, 2 * co, nz)
-    pre, vals, val_edge, ga, gb, plain, vm = pl.pallas_call(
+    pre, vals, val_edge, ga, gb, wg = pl.pallas_call(
         functools.partial(outer_kernel, dims, 4),
         out_shape=(
             far(pre_shape, F32),
             far((8 * co, ny * nz), BF16),
             far((nx - 1, 8 * co, nz), BF16),
-            jax.ShapeDtypeStruct((8 * co, n_out * nz), BF16),
-            jax.ShapeDtypeStruct((8 * co, n_out * nz), BF16),
-            jax.ShapeDtypeStruct((nx + 2, ci, (ny + 2) * nz), BF16),
-            jax.ShapeDtypeStruct((nx + 2, ci, (ny + 2) * nz), BF16),
+            far((8 * co, n_out * nz), BF16),
+            far((8 * co, n_out * nz), BF16),
+            jax.ShapeDtypeStruct((32, co, 2 * ci), BF16),
         ),
-        in_specs=[vmem] + [anywhere] * 4 + [vmem] * 3,
-        out_specs=(hbm,) * 3 + (vmem,) * 4,
+        in_specs=[vmem] + [anywhere] * 4 + [vmem] * 4,
+        out_specs=(hbm,) * 5 + (vmem,),
         scratch_shapes=[
+            pltpu.VMEM((8 * co, n_out * nz), BF16),
+            pltpu.VMEM((8 * co, n_out * nz), BF16),
+            pltpu.VMEM((nx + 2, ci, (ny + 2) * nz), BF16),
             pltpu.VMEM(pre_shape, F32),
             pltpu.VMEM((8 * co, ny * nz), BF16),
             pltpu.VMEM((nx - 1, 8 * co, nz), BF16),
             pltpu.VMEM((2, ny * ci, nz), BF16),
             pltpu.VMEM((2, (nx + 2) * ci, nz), BF16),
             pltpu.VMEM((8 * co, ny * nz), BF16),
-            pltpu.SemaphoreType.DMA((10,)),
+            pltpu.SemaphoreType.DMA((12,)),
         ],
         compiler_params=params,
-    )(flat, xlo, xhi, ylo, yhi, w, cot, cot_edge)
-    wg, ga, gb = pl.pallas_call(
-        functools.partial(weight_kernel, dims),
-        out_shape=(
-            jax.ShapeDtypeStruct((32, co, 2 * ci), BF16),
-            far((8 * co, n_out * nz), BF16),
-            far((8 * co, n_out * nz), BF16),
-        ),
-        in_specs=[vmem] * 5 + [anywhere] * 2,
-        out_specs=(vmem, hbm, hbm),
-        scratch_shapes=[pltpu.SemaphoreType.DMA((2,))],
-        compiler_params=params,
-    )(plain, vm, ga, gb, wg_part, face_lo, face_hi)
+    )(flat, xlo, xhi, ylo, yhi, w, cot, cot_edge, wg_part)
     passed = [
         stay(array)
         for array in (ga, gb, pre, vals, val_edge, face_lo, face_hi, ylo, yhi, wt, inner_vals, ig_part)

time: 69.6 us -> 68.6 us (0.986)
  blocking collectives: 18.6 us -> 0 us
  waiting for transfers between devices: 4.72 us -> 14.4 us
  starting transfers between devices: 19.9 us -> 27.2 us
    all_to_all x1 -> x0, blocking collectives: 18.6 us -> none  [on_device(): shares = lax.all_to_all(shares, ('gx', 'gy'), 0, 0, tiled=True)]
    all_to_all x0 -> x1, starting transfers between devices: none -> 7.44 us  [on_device(): shares = lax.all_to_all(shares, ('gx', 'gy'), 0, 0, tiled=True)]
    ppermute x1, waiting for transfers between devices: 0.01 us -> 5.8 us  [on_device(): face_hi = lax.ppermute(face_down, 'gx', gx_down)]
    all_to_all x0 -> x1, waiting for transfers between devices: none -> 4.85 us  [on_device(): shares = lax.all_to_all(shares, ('gx', 'gy'), 0, 0, tiled=True)]
    pallas_call x1 -> x0, Pallas kernels: 2.24 us -> none  [on_device(): pl.pallas_call(functools.partial(weight_kernel, dims), out_shape=(jax.Sha...]
    pallas_call x1, Pallas kernels: 4.71 us -> 6.75 us  [on_device(): pl.pallas_call(functools.partial(outer_kernel, dims, 4), out_shape=(far(p...]
    all_to_all x1, waiting for transfers between devices: 1.81 us -> 0.01 us  [on_device(): pieces = lax.all_to_all(pieces, ('gx', 'gy'), 0, 0, tiled=True)]
    ppermute x1, waiting for transfers between devices: 0.01 us -> 1.54 us  [on_device(): xhi = lax.ppermute(x_message(0), 'gx', gx_down)]
  transfers between devices with their start and end apart: 7 -> 8, of which waited for: 3 -> 5; matrix products, arithmetic and copies ran while one was open for 1% -> 2% of each run, Pallas kernels for 26% -> 19%
where the time goes in v10:
time: 68.6 us; the launch traced here: 68.2 us
  starting transfers between devices  27.2 us (40%)
  Pallas kernels  20.9 us (30%)
  waiting for transfers between devices  14.4 us (21%)
  local copies, waits for them, and re-layouts  4.6 us (7%)
  between operations  0.97 us (1%)
    pallas_call x1, Pallas kernels, on_device(): pl.pallas_call(functools.partial(last_kernel, dims, 4), out_shape=(jax.Sh...  8.52 us
    all_to_all x1, starting transfers between devices, on_device(): shares = lax.all_to_all(shares, ('gx', 'gy'), 0, 0, tiled=True)  7.44 us
    pallas_call x1, Pallas kernels, on_device(): pl.pallas_call(functools.partial(outer_kernel, dims, 4), out_shape=(far(p...  6.75 us
    ppermute x1, waiting for transfers between devices, on_device(): face_hi = lax.ppermute(face_down, 'gx', gx_down)  5.8 us
    all_to_all x1, waiting for transfers between devices, on_device(): shares = lax.all_to_all(shares, ('gx', 'gy'), 0, 0, tiled=True)  4.85 us
    ppermute x1, starting transfers between devices, on_device(): xlo = lax.ppermute(x_message(1), 'gx', gx_up)  4.51 us
    pallas_call x1, Pallas kernels, on_device(): pl.pallas_call(functools.partial(inner_kernel, dims, 5), out_shape=(jax.S...  4.49 us
    ppermute x1, starting transfers between devices, on_device(): ylo = lax.ppermute(y_message(1), 'gy', gy_up)  4 us
  transfers between devices with their start and end apart: 8, of which 5 were waited for; matrix products, arithmetic and copies ran while one was open for 2% of the time, Pallas kernels for 19%

profile of v10, /device:TPU:1, one launch (start us, length us, event | category | flops | bytes accessed | tf_op | source)
XLA Modules:
  0.0 68.2 jit_solution(17300512491352739656)
XLA Ops:
  0.6 1.4 %fusion.1 = (bf16[1,1,2,32,1,1,128]{6,5,4,3,2,1,0:T(2,128)(2,1)S(1)}, bf16[1,1,2,32,1,1,128]{6,5,4,3,2,1,0:T(2,128)(2,1)S(1)}, bf16[1,1,2,32,1,1,128]{6,5,4,3,2,...) fusion(bf16[2,2,2,32,2,16,128]{6,5,4,3,2,1,0:T(8,128)(2,1)} %param.5), kind=kLoop, calls=%fused_computation.19 | loop fusion | bytes 131072 | tf_op jit(solution)/shard_map/slice | solution.py:635
  2.0 0.0 copy-start.1
  2.0 0.0 copy-start.4
  2.1 1.2 %slice_bitcast_fusion = (bf16[16,64,128]{2,0,1:T(8,128)(2,1)S(1)}, bf16[16,64,128]{2,0,1:T(8,128)(2,1)S(1)}) fusion(bf16[64,2,16,128]{3,2,1,0:T(8,128)(2,1)} %vol_in.1), kind=kLoop, calls=%fused_computation.3 | loop fusion | bytes 1048576 | tf_op jit(solution)/shard_map/transpose | solution.py:638
  3.2 0.1 copy.10
  3.3 4.5 %collective-permute-start = (bf16[1152,128]{1,0:T(8,128)(2,1)S(1)}, bf16[1152,128]{1,0:T(8,128)(2,1)S(1)}, u32[]{:S(2)}, u32[]{:S(2)}) collective-permute-start(bf16[1152,128]{1,0:T(8,128)(2,1)S(1)} %pad_maximum_fusion), channel_id=1, source_target_pairs={{0,4},{4,8},{8,12},{12,16},{16,20},{20,24},{24,28},{1,5},{5,9},{9,... | collective-permute-start | bytes 884744 | tf_op jit(solution)/shard_map/ppermute | solution.py:641
  7.9 0.1 copy.13
  8.0 1.9 %collective-permute-start.1 = (bf16[1152,128]{1,0:T(8,128)(2,1)S(1)}, bf16[1152,128]{1,0:T(8,128)(2,1)S(1)}, u32[]{:S(2)}, u32[]{:S(2)}) collective-permute-start(bf16[1152,128]{1,0:T(8,128)(2,1)S(1)} %pad_maximum_fusion.1), channel_id=1, source_target_pairs={{4,0},{8,4},{12,8},{16,12},{20,16},{24,20},{28,24},{5,1},{9,5},{13... | collective-permute-start | bytes 884744 | tf_op jit(solution)/shard_map/ppermute | solution.py:642
  9.9 0.2 fusion
  10.2 0.0 copy-done.1
  10.2 0.0 copy-done.4
  10.2 4.5 %shard_map.58 = (bf16[2,64,2048]{2,1,0:T(8,128)(2,1)S(1)}, bf16[256,512]{1,0:T(8,128)(2,1)S(1)}, bf16[512,256]{1,0:T(8,128)(2,1)}, bf16[1,256,2048]{2,1,0:T(8,12...) custom-call(bf16[64,2,16,128]{3,2,1,0:T(8,128)(2,1)S(1)} %copy-done., ...), custom_call_target="tpu_custom_call" | custom-call | tf_op jit(solution)/shard_map/pallas_call | solution.py:651
  14.7 0.0 collective-permute-done.xlo_in
  14.7 1.5 %collective-permute-done.1.xhi_in = bf16[1152,128]{1,0:T(8,128)(2,1)S(1)} collective-permute-done((bf16[1152,128]{1,0:T(8,128)(2,1)S(1)}, bf16[1152,128]{1,0:T(8,128)(2,1)S(1)}, u32[]{:S(2)}, u32[]{:S(2)}) %collective-permute-start.1) | collective-permute-done | bytes 294944 | tf_op jit(solution)/shard_map/ppermute | solution.py:642
  16.4 1.3 %collective-permute-start.3 = (bf16[640,128]{1,0:T(8,128)(2,1)S(1)}, bf16[640,128]{1,0:T(8,128)(2,1)S(1)}, u32[]{:S(2)}, u32[]{:S(2)}) collective-permute-start(bf16[640,128]{1,0:T(8,128)(2,1)S(1)} %get-tuple-element.47), channel_id=1, source_target_pairs={{1,0},{2,1},{3,2},{5,4},{6,5},{7,6},{9,8},{10,9},{11,10},{13,12},{... | collective-permute-start | bytes 491528 | tf_op jit(solution)/shard_map/ppermute | solution.py:699
  17.7 4.0 %collective-permute-start.2 = (bf16[640,128]{1,0:T(8,128)(2,1)S(1)}, bf16[640,128]{1,0:T(8,128)(2,1)S(1)}, u32[]{:S(2)}, u32[]{:S(2)}) collective-permute-start(bf16[640,128]{1,0:T(8,128)(2,1)S(1)} %get-tuple-element.48), channel_id=1, source_target_pairs={{0,1},{1,2},{2,3},{4,5},{5,6},{6,7},{8,9},{9,10},{10,11},{12,13},{... | collective-permute-start | bytes 491528 | tf_op jit(solution)/shard_map/ppermute | solution.py:698
  21.7 0.8 %collective-permute-done.3.yhi_in = bf16[640,128]{1,0:T(8,128)(2,1)S(1)} collective-permute-done((bf16[640,128]{1,0:T(8,128)(2,1)S(1)}, bf16[640,128]{1,0:T(8,128)(2,1)S(1)}, u32[]{:S(2)}, u32[]{:S(2)}) %collective-permute-start.3) | collective-permute-done | bytes 163872 | tf_op jit(solution)/shard_map/ppermute | solution.py:699
  22.4 1.5 %collective-permute-done.2.ylo_in = bf16[640,128]{1,0:T(8,128)(2,1)S(1)} collective-permute-done((bf16[640,128]{1,0:T(8,128)(2,1)S(1)}, bf16[640,128]{1,0:T(8,128)(2,1)S(1)}, u32[]{:S(2)}, u32[]{:S(2)}) %collective-permute-start.2) | collective-permute-done | bytes 163872 | tf_op jit(solution)/shard_map/ppermute | solution.py:698
  23.9 6.8 %shard_map.59 = (f32[76,64,128]{2,1,0:T(8,128)}, bf16[256,2048]{1,0:T(8,128)(2,1)}, bf16[1,256,128]{2,1,0:T(8,128)(2,1)}, bf16[256,4608]{1,0:T(8,128)(2,1)}, bf1...) custom-call(bf16[2,64,2048]{2,1,0:T(8,128)(2,1)S(1)} %get-tuple-element.20.flat, ...), custom_call_target="tpu_custom_call" | custom-call | tf_op jit(solution)/shard_map/pallas_call | solution.py:704
  30.7 7.4 %all-to-all-start = ((bf16[32,32,128]{2,1,0:T(8,128)(2,1)}), bf16[32,32,128]{2,1,0:T(8,128)(2,1)S(1)}, u32[]{:S(2)}, u32[]{:S(2)}) async-start(bf16[32,32,128]{2,1,0:T(8,128)(2,1)} %get-tuple-element.36), calls=%async_computation | async-start | bytes 524288 | tf_op jit(solution)/shard_map/all_to_all | solution.py:764
  38.1 0.0 copy-done.8
  38.2 3.5 %collective-permute-start.4 = (bf16[4,32,16,128]{3,2,1,0:T(8,128)(2,1)S(1)}, bf16[4,32,16,128]{3,2,1,0:T(8,128)(2,1)S(1)}, u32[]{:S(2)}, u32[]{:S(2)}) collective-permute-start(bf16[4,32,16,128]{3,2,1,0:T(8,128)(2,1)S(1)} %copy-done.8), channel_id=1, source_target_pairs={{0,4},{4,8},{8,12},{12,16},{16,20},{20,24},{24,28},{1,5},{5,9},{9,... | collective-permute-start | bytes 1572872 | tf_op jit(solution)/shard_map/ppermute | solution.py:700
  41.7 1.9 %collective-permute-start.5 = (bf16[4,32,16,128]{3,2,1,0:T(8,128)(2,1)S(1)}, bf16[4,32,16,128]{3,2,1,0:T(8,128)(2,1)S(1)}, u32[]{:S(2)}, u32[]{:S(2)}) collective-permute-start(bf16[4,32,16,128]{3,2,1,0:T(8,128)(2,1)S(1)} %copy-done.7), channel_id=1, source_target_pairs={{4,0},{8,4},{12,8},{16,12},{20,16},{24,20},{28,24},{5,1},{9,5},{13... | collective-permute-start | bytes 1572872 | tf_op jit(solution)/shard_map/ppermute | solution.py:701
  43.6 4.8 %all-to-all-done = bf16[32,32,128]{2,1,0:T(8,128)(2,1)S(1)} async-done(((bf16[32,32,128]{2,1,0:T(8,128)(2,1)}), bf16[32,32,128]{2,1,0:T(8,128)(2,1)S(1)}, u32[]{:S(2)}, u32[]{:S(2)}) %all-to-all-start) | async-done | bytes 262176 | tf_op jit(solution)/shard_map/all_to_all | solution.py:764
  48.6 0.7 %broadcast_in_dim.2 = bf16[32,32,128]{2,1,0:T(8,128)(2,1)} broadcast(bf16[32,128]{1,0:T(8,128)(2,1)S(1)} %multiply_convert_fusion), dimensions={1,2} | broadcast | bytes 270336 | tf_op jit(solution)/shard_map/broadcast_in_dim | solution.py:766
  49.3 2.6 %all-to-all-start.1 = ((bf16[32,32,128]{2,1,0:T(8,128)(2,1)}), bf16[32,32,128]{2,1,0:T(8,128)(2,1)S(1)}, u32[]{:S(2)}, u32[]{:S(2)}) async-start(bf16[32,32,128]{2,1,0:T(8,128)(2,1)} %broadcast_in_dim.2), calls=%async_computation.1 | async-start | bytes 524288 | tf_op jit(solution)/shard_map/all_to_all | solution.py:767
  51.9 0.0 collective-permute-done.4.xlo_in
  51.9 5.8 %collective-permute-done.5.xhi_in = bf16[4,32,16,128]{3,2,1,0:T(8,128)(2,1)S(1)} collective-permute-done((bf16[4,32,16,128]{3,2,1,0:T(8,128)(2,1)S(1)}, bf16[4,32,16,128]{3,2,1,0:T(8,128)(2,1)S(1)}, u32[]{:S(2)}, u32[]{:S(2)}) %collective-permute-start.5) | collective-permute-done | bytes 524320 | tf_op jit(solution)/shard_map/ppermute | solution.py:701
  57.7 0.8 %copy-done.6 = bf16[4,32,16,128]{3,2,1,0:T(8,128)(2,1)} copy-done((bf16[4,32,16,128]{3,2,1,0:T(8,128)(2,1)}, bf16[4,32,16,128]{3,2,1,0:T(8,128)(2,1)S(1)}, u32[]{:S(2)}) %copy-start.6) | copy-done | bytes 524312
  58.5 8.5 %shard_map.60 = (bf16[8,32,2,16,128]{4,3,2,1,0:T(8,128)(2,1)}, bf16[64,2,16,128]{3,2,1,0:T(8,128)(2,1)}) custom-call(bf16[256,4608]{1,0:T(8,128)(2,1)} %get-tuple-element.24.ga_in, bf16[256,4608]{1,0:T(8,128)(2,1)} %get-tuple-element.25.gb_in, f32[76,64,128]{2,1,0:T(8,128)} %get-tuple-element.26.pre_in, bf16[256,2048]{1,0:T(8,128)(2,1)} %get-tuple-element.27.vals_in, ...), custom_call_target="tpu_custom_call" | custom-call | tf_op jit(solution)/shard_map/pallas_call | solution.py:734
  67.1 0.0 all-to-all-done.1.packed
  67.1 1.1 %shard_map.61 = f32[4,4,4,32,64]{4,3,2,1,0:T(8,128)} custom-call(bf16[32,32,128]{2,1,0:T(8,128)(2,1)S(1)} %all-to-all-done.1.packed), custom_call_target="tpu_custom_call" | custom-call | tf_op jit(solution)/shard_map/pallas_call | solution.py:768
  (30 shorter events, 0.3 us)
Async XLA Ops:
  0.6 9.3 %copy-start = (bf16[2,2,2,32,2,16,128]{6,5,4,3,2,1,0:T(8,128)(2,1)S(1)}, bf16[2,2,2,32,2,16,128]{6,5,4,3,2,1,0:T(8,128)(2,1)}, u32[]{:S(2)}) copy-start(bf16[2,2,2,32,2,16,128]{6,5,4,3,2,1,0:T(8,128)(2,1)} %param.5) | copy-start | bytes 6291460
  2.0 8.1 %copy-start.1 = (bf16[64,2,16,128]{3,2,1,0:T(8,128)(2,1)S(1)}, bf16[64,2,16,128]{3,2,1,0:T(8,128)(2,1)}, u32[]{:S(2)}) copy-start(bf16[64,2,16,128]{3,2,1,0:T(8,128)(2,1)} %vol_in.1) | copy-start | bytes 1572868
  2.0 8.1 %copy-start.4 = (bf16[4,4,4,32,64]{4,3,2,1,0:T(8,128)(2,1)S(1)}, bf16[4,4,4,32,64]{4,3,2,1,0:T(8,128)(2,1)}, u32[]{:S(2)}) copy-start(bf16[4,4,4,32,64]{4,3,2,1,0:T(8,128)(2,1)} %taps_in.1) | copy-start | bytes 786436
  3.3 11.4 %collective-permute-start = (bf16[1152,128]{1,0:T(8,128)(2,1)S(1)}, bf16[1152,128]{1,0:T(8,128)(2,1)S(1)}, u32[]{:S(2)}, u32[]{:S(2)}) collective-permute-start(bf16[1152,128]{1,0:T(8,128)(2,1)S(1)} %pad_maximum_fusion), channel_id=1, source_target_pairs={{0,4},{4,8},{8,12},{12,16},{16,20},{20,24},{24,28},{1,5},{5,9},{9,... | collective-permute-start | bytes 884744 | tf_op jit(solution)/shard_map/ppermute | solution.py:641
  8.0 8.3 %collective-permute-start.1 = (bf16[1152,128]{1,0:T(8,128)(2,1)S(1)}, bf16[1152,128]{1,0:T(8,128)(2,1)S(1)}, u32[]{:S(2)}, u32[]{:S(2)}) collective-permute-start(bf16[1152,128]{1,0:T(8,128)(2,1)S(1)} %pad_maximum_fusion.1), channel_id=1, source_target_pairs={{4,0},{8,4},{12,8},{16,12},{20,16},{24,20},{28,24},{5,1},{9,5},{13... | collective-permute-start | bytes 884744 | tf_op jit(solution)/shard_map/ppermute | solution.py:642
  16.4 6.1 %collective-permute-start.3 = (bf16[640,128]{1,0:T(8,128)(2,1)S(1)}, bf16[640,128]{1,0:T(8,128)(2,1)S(1)}, u32[]{:S(2)}, u32[]{:S(2)}) collective-permute-start(bf16[640,128]{1,0:T(8,128)(2,1)S(1)} %get-tuple-element.47), channel_id=1, source_target_pairs={{1,0},{2,1},{3,2},{5,4},{6,5},{7,6},{9,8},{10,9},{11,10},{13,12},{... | collective-permute-start | bytes 491528 | tf_op jit(solution)/shard_map/ppermute | solution.py:699
  17.7 6.2 %collective-permute-start.2 = (bf16[640,128]{1,0:T(8,128)(2,1)S(1)}, bf16[640,128]{1,0:T(8,128)(2,1)S(1)}, u32[]{:S(2)}, u32[]{:S(2)}) collective-permute-start(bf16[640,128]{1,0:T(8,128)(2,1)S(1)} %get-tuple-element.48), channel_id=1, source_target_pairs={{0,1},{1,2},{2,3},{4,5},{5,6},{6,7},{8,9},{9,10},{10,11},{12,13},{... | collective-permute-start | bytes 491528 | tf_op jit(solution)/shard_map/ppermute | solution.py:698
  22.4 8.2 %copy-start.2 = (bf16[640,128]{1,0:T(8,128)(2,1)}, bf16[640,128]{1,0:T(8,128)(2,1)S(1)}, u32[]{:S(2)}) copy-start(bf16[640,128]{1,0:T(8,128)(2,1)S(1)} %collective-permute-done.3.yhi_in) | copy-start | bytes 491524
  23.9 6.8 %copy-start.3 = (bf16[640,128]{1,0:T(8,128)(2,1)}, bf16[640,128]{1,0:T(8,128)(2,1)S(1)}, u32[]{:S(2)}) copy-start(bf16[640,128]{1,0:T(8,128)(2,1)S(1)} %collective-permute-done.2.ylo_in) | copy-start | bytes 491524
  23.9 14.2 %copy-start.8 = (bf16[4,32,16,128]{3,2,1,0:T(8,128)(2,1)S(1)}, bf16[4,32,16,128]{3,2,1,0:T(8,128)(2,1)}, u32[]{:S(2)}) copy-start(bf16[4,32,16,128]{3,2,1,0:T(8,128)(2,1)} %get-tuple-element.29) | copy-start | bytes 1572868
  23.9 17.8 %copy-start.7 = (bf16[4,32,16,128]{3,2,1,0:T(8,128)(2,1)S(1)}, bf16[4,32,16,128]{3,2,1,0:T(8,128)(2,1)}, u32[]{:S(2)}) copy-start(bf16[4,32,16,128]{3,2,1,0:T(8,128)(2,1)} %get-tuple-element.30) | copy-start | bytes 1572868
  30.7 17.8 %all-to-all-start = ((bf16[32,32,128]{2,1,0:T(8,128)(2,1)}), bf16[32,32,128]{2,1,0:T(8,128)(2,1)S(1)}, u32[]{:S(2)}, u32[]{:S(2)}) async-start(bf16[32,32,128]{2,1,0:T(8,128)(2,1)} %get-tuple-element.36), calls=%async_computation | async-start | bytes 524288 | tf_op jit(solution)/shard_map/all_to_all | solution.py:764
  38.2 13.7 %collective-permute-start.4 = (bf16[4,32,16,128]{3,2,1,0:T(8,128)(2,1)S(1)}, bf16[4,32,16,128]{3,2,1,0:T(8,128)(2,1)S(1)}, u32[]{:S(2)}, u32[]{:S(2)}) collective-permute-start(bf16[4,32,16,128]{3,2,1,0:T(8,128)(2,1)S(1)} %copy-done.8), channel_id=1, source_target_pairs={{0,4},{4,8},{8,12},{12,16},{16,20},{20,24},{24,28},{1,5},{5,9},{9,... | collective-permute-start | bytes 1572872 | tf_op jit(solution)/shard_map/ppermute | solution.py:700
  41.7 16.0 %collective-permute-start.5 = (bf16[4,32,16,128]{3,2,1,0:T(8,128)(2,1)S(1)}, bf16[4,32,16,128]{3,2,1,0:T(8,128)(2,1)S(1)}, u32[]{:S(2)}, u32[]{:S(2)}) collective-permute-start(bf16[4,32,16,128]{3,2,1,0:T(8,128)(2,1)S(1)} %copy-done.7), channel_id=1, source_target_pairs={{4,0},{8,4},{12,8},{16,12},{20,16},{24,20},{28,24},{5,1},{9,5},{13... | collective-permute-start | bytes 1572872 | tf_op jit(solution)/shard_map/ppermute | solution.py:701
  49.3 17.8 %all-to-all-start.1 = ((bf16[32,32,128]{2,1,0:T(8,128)(2,1)}), bf16[32,32,128]{2,1,0:T(8,128)(2,1)S(1)}, u32[]{:S(2)}, u32[]{:S(2)}) async-start(bf16[32,32,128]{2,1,0:T(8,128)(2,1)} %broadcast_in_dim.2), calls=%async_computation.1 | async-start | bytes 524288 | tf_op jit(solution)/shard_map/all_to_all | solution.py:767
  51.9 5.8 %copy-start.5 = (bf16[4,32,16,128]{3,2,1,0:T(8,128)(2,1)}, bf16[4,32,16,128]{3,2,1,0:T(8,128)(2,1)S(1)}, u32[]{:S(2)}) copy-start(bf16[4,32,16,128]{3,2,1,0:T(8,128)(2,1)S(1)} %collective-permute-done.4.xlo_in) | copy-start | bytes 1572868
  57.7 0.8 %copy-start.6 = (bf16[4,32,16,128]{3,2,1,0:T(8,128)(2,1)}, bf16[4,32,16,128]{3,2,1,0:T(8,128)(2,1)S(1)}, u32[]{:S(2)}) copy-start(bf16[4,32,16,128]{3,2,1,0:T(8,128)(2,1)S(1)} %collective-permute-done.5.xhi_in) | copy-start | bytes 1572868

commit v11 on v10

--- a/solution.py
+++ b/solution.py
@@ -729,15 +729,16 @@
     )(flat, xlo, xhi, ylo, yhi, w, cot, cot_edge, wg_part)
     passed = [
         stay(array)
-        for array in (ga, gb, pre, vals, val_edge, face_lo, face_hi, ylo, yhi, wt, inner_vals, ig_part)
+        for array in (ga, gb, pre, vals, val_edge, ylo, yhi, wt, inner_vals, ig_part)
     ]
+    passed[5:5] = [face_lo, face_hi]
     act, input_grad = pl.pallas_call(
         functools.partial(last_kernel, dims, 4),
         out_shape=(
             jax.ShapeDtypeStruct(cot.shape, BF16),
             jax.ShapeDtypeStruct(volume.shape, BF16),
         ),
-        in_specs=[hbm] * 12,
+        in_specs=[hbm] * 5 + [anywhere] * 2 + [hbm] * 5,
         out_specs=(anywhere,) * 2,
         scratch_shapes=[
             pltpu.VMEM((8 * co, n_out * nz), BF16),

time: 68.6 us -> 67.5 us (0.984)
  local copies, waits for them, and re-layouts: 4.6 us -> 3.78 us
    unnamed x28 -> x24, local copies, waits for them, and re-layouts: 0.94 us -> 0.12 us
where the time goes in v11:
time: 67.5 us; the launch traced here: 67.1 us
  starting transfers between devices  27.2 us (40%)
  Pallas kernels  20.6 us (31%)
  waiting for transfers between devices  14.4 us (21%)
  local copies, waits for them, and re-layouts  3.78 us (6%)
  between operations  0.96 us (1%)
    pallas_call x1, Pallas kernels, on_device(): pl.pallas_call(functools.partial(last_kernel, dims, 4), out_shape=(jax.Sh...  8.27 us
    all_to_all x1, starting transfers between devices, on_device(): shares = lax.all_to_all(shares, ('gx', 'gy'), 0, 0, tiled=True)  7.44 us
    pallas_call x1, Pallas kernels, on_device(): pl.pallas_call(functools.partial(outer_kernel, dims, 4), out_shape=(far(p...  6.76 us
    ppermute x1, waiting for transfers between devices, on_device(): face_hi = lax.ppermute(face_down, 'gx', gx_down)  5.81 us
    all_to_all x1, waiting for transfers between devices, on_device(): shares = lax.all_to_all(shares, ('gx', 'gy'), 0, 0, tiled=True)  4.85 us
    ppermute x1, starting transfers between devices, on_device(): xlo = lax.ppermute(x_message(1), 'gx', gx_up)  4.51 us
    pallas_call x1, Pallas kernels, on_device(): pl.pallas_call(functools.partial(inner_kernel, dims, 5), out_shape=(jax.S...  4.48 us
    ppermute x1, starting transfers between devices, on_device(): ylo = lax.ppermute(y_message(1), 'gy', gy_up)  4 us
  transfers between devices with their start and end apart: 8, of which 5 were waited for; matrix products, arithmetic and copies ran while one was open for 2% of the time, Pallas kernels for 19%

profile of v11, /device:TPU:1, one launch (start us, length us, event | category | flops | bytes accessed | tf_op | source)
XLA Modules:
  0.0 67.1 jit_solution(12266199479025157701)
XLA Ops:
  0.6 0.0 copy-start
  0.6 1.4 %fusion.1 = (bf16[1,1,2,32,1,1,128]{6,5,4,3,2,1,0:T(2,128)(2,1)S(1)}, bf16[1,1,2,32,1,1,128]{6,5,4,3,2,1,0:T(2,128)(2,1)S(1)}, bf16[1,1,2,32,1,1,128]{6,5,4,3,2,...) fusion(bf16[2,2,2,32,2,16,128]{6,5,4,3,2,1,0:T(8,128)(2,1)} %param.5), kind=kLoop, calls=%fused_computation.19 | loop fusion | bytes 131072 | tf_op jit(solution)/shard_map/slice | solution.py:635
  2.0 0.0 copy-start.1
  2.0 0.0 copy-start.4
  2.1 1.2 %slice_bitcast_fusion = (bf16[16,64,128]{2,0,1:T(8,128)(2,1)S(1)}, bf16[16,64,128]{2,0,1:T(8,128)(2,1)S(1)}) fusion(bf16[64,2,16,128]{3,2,1,0:T(8,128)(2,1)} %vol_in.1), kind=kLoop, calls=%fused_computation.3 | loop fusion | bytes 1048576 | tf_op jit(solution)/shard_map/transpose | solution.py:638
  3.2 0.1 copy.10
  3.3 4.5 %collective-permute-start = (bf16[1152,128]{1,0:T(8,128)(2,1)S(1)}, bf16[1152,128]{1,0:T(8,128)(2,1)S(1)}, u32[]{:S(2)}, u32[]{:S(2)}) collective-permute-start(bf16[1152,128]{1,0:T(8,128)(2,1)S(1)} %pad_maximum_fusion), channel_id=1, source_target_pairs={{0,4},{4,8},{8,12},{12,16},{16,20},{20,24},{24,28},{1,5},{5,9},{9,... | collective-permute-start | bytes 884744 | tf_op jit(solution)/shard_map/ppermute | solution.py:641
  7.9 0.1 copy.13
  8.0 1.9 %collective-permute-start.1 = (bf16[1152,128]{1,0:T(8,128)(2,1)S(1)}, bf16[1152,128]{1,0:T(8,128)(2,1)S(1)}, u32[]{:S(2)}, u32[]{:S(2)}) collective-permute-start(bf16[1152,128]{1,0:T(8,128)(2,1)S(1)} %pad_maximum_fusion.1), channel_id=1, source_target_pairs={{4,0},{8,4},{12,8},{16,12},{20,16},{24,20},{28,24},{5,1},{9,5},{13... | collective-permute-start | bytes 884744 | tf_op jit(solution)/shard_map/ppermute | solution.py:642
  9.9 0.0 copy-done
  9.9 0.2 fusion
  10.2 0.0 copy-done.1
  10.2 0.0 copy-done.4
  10.2 4.5 %shard_map.58 = (bf16[2,64,2048]{2,1,0:T(8,128)(2,1)S(1)}, bf16[256,512]{1,0:T(8,128)(2,1)S(1)}, bf16[512,256]{1,0:T(8,128)(2,1)}, bf16[1,256,2048]{2,1,0:T(8,12...) custom-call(bf16[64,2,16,128]{3,2,1,0:T(8,128)(2,1)S(1)} %copy-done., ...), custom_call_target="tpu_custom_call" | custom-call | tf_op jit(solution)/shard_map/pallas_call | solution.py:651
  14.7 0.0 collective-permute-done.xlo_in
  14.7 1.6 %collective-permute-done.1.xhi_in = bf16[1152,128]{1,0:T(8,128)(2,1)S(1)} collective-permute-done((bf16[1152,128]{1,0:T(8,128)(2,1)S(1)}, bf16[1152,128]{1,0:T(8,128)(2,1)S(1)}, u32[]{:S(2)}, u32[]{:S(2)}) %collective-permute-start.1) | collective-permute-done | bytes 294944 | tf_op jit(solution)/shard_map/ppermute | solution.py:642
  16.4 1.3 %collective-permute-start.3 = (bf16[640,128]{1,0:T(8,128)(2,1)S(1)}, bf16[640,128]{1,0:T(8,128)(2,1)S(1)}, u32[]{:S(2)}, u32[]{:S(2)}) collective-permute-start(bf16[640,128]{1,0:T(8,128)(2,1)S(1)} %get-tuple-element.47), channel_id=1, source_target_pairs={{1,0},{2,1},{3,2},{5,4},{6,5},{7,6},{9,8},{10,9},{11,10},{13,12},{... | collective-permute-start | bytes 491528 | tf_op jit(solution)/shard_map/ppermute | solution.py:699
  17.7 4.0 %collective-permute-start.2 = (bf16[640,128]{1,0:T(8,128)(2,1)S(1)}, bf16[640,128]{1,0:T(8,128)(2,1)S(1)}, u32[]{:S(2)}, u32[]{:S(2)}) collective-permute-start(bf16[640,128]{1,0:T(8,128)(2,1)S(1)} %get-tuple-element.48), channel_id=1, source_target_pairs={{0,1},{1,2},{2,3},{4,5},{5,6},{6,7},{8,9},{9,10},{10,11},{12,13},{... | collective-permute-start | bytes 491528 | tf_op jit(solution)/shard_map/ppermute | solution.py:698
  21.7 0.8 %collective-permute-done.3.yhi_in = bf16[640,128]{1,0:T(8,128)(2,1)S(1)} collective-permute-done((bf16[640,128]{1,0:T(8,128)(2,1)S(1)}, bf16[640,128]{1,0:T(8,128)(2,1)S(1)}, u32[]{:S(2)}, u32[]{:S(2)}) %collective-permute-start.3) | collective-permute-done | bytes 163872 | tf_op jit(solution)/shard_map/ppermute | solution.py:699
  22.4 1.5 %collective-permute-done.2.ylo_in = bf16[640,128]{1,0:T(8,128)(2,1)S(1)} collective-permute-done((bf16[640,128]{1,0:T(8,128)(2,1)S(1)}, bf16[640,128]{1,0:T(8,128)(2,1)S(1)}, u32[]{:S(2)}, u32[]{:S(2)}) %collective-permute-start.2) | collective-permute-done | bytes 163872 | tf_op jit(solution)/shard_map/ppermute | solution.py:698
  23.9 6.8 %shard_map.59 = (f32[76,64,128]{2,1,0:T(8,128)}, bf16[256,2048]{1,0:T(8,128)(2,1)}, bf16[1,256,128]{2,1,0:T(8,128)(2,1)}, bf16[256,4608]{1,0:T(8,128)(2,1)}, bf1...) custom-call(bf16[2,64,2048]{2,1,0:T(8,128)(2,1)S(1)} %get-tuple-element.20.flat, ...), custom_call_target="tpu_custom_call" | custom-call | tf_op jit(solution)/shard_map/pallas_call | solution.py:704
  30.7 7.4 %all-to-all-start = ((bf16[32,32,128]{2,1,0:T(8,128)(2,1)}), bf16[32,32,128]{2,1,0:T(8,128)(2,1)S(1)}, u32[]{:S(2)}, u32[]{:S(2)}) async-start(bf16[32,32,128]{2,1,0:T(8,128)(2,1)} %get-tuple-element.36), calls=%async_computation | async-start | bytes 524288 | tf_op jit(solution)/shard_map/all_to_all | solution.py:765
  38.2 3.5 %collective-permute-start.4 = (bf16[4,32,16,128]{3,2,1,0:T(8,128)(2,1)S(1)}, bf16[4,32,16,128]{3,2,1,0:T(8,128)(2,1)S(1)}, u32[]{:S(2)}, u32[]{:S(2)}) collective-permute-start(bf16[4,32,16,128]{3,2,1,0:T(8,128)(2,1)S(1)} %copy-done.6), channel_id=1, source_target_pairs={{0,4},{4,8},{8,12},{12,16},{16,20},{20,24},{24,28},{1,5},{5,9},{9,... | collective-permute-start | bytes 1572872 | tf_op jit(solution)/shard_map/ppermute | solution.py:700
  41.7 1.9 %collective-permute-start.5 = (bf16[4,32,16,128]{3,2,1,0:T(8,128)(2,1)S(1)}, bf16[4,32,16,128]{3,2,1,0:T(8,128)(2,1)S(1)}, u32[]{:S(2)}, u32[]{:S(2)}) collective-permute-start(bf16[4,32,16,128]{3,2,1,0:T(8,128)(2,1)S(1)} %copy-done.5), channel_id=1, source_target_pairs={{4,0},{8,4},{12,8},{16,12},{20,16},{24,20},{28,24},{5,1},{9,5},{13... | collective-permute-start | bytes 1572872 | tf_op jit(solution)/shard_map/ppermute | solution.py:701
  43.6 4.8 %all-to-all-done = bf16[32,32,128]{2,1,0:T(8,128)(2,1)S(1)} async-done(((bf16[32,32,128]{2,1,0:T(8,128)(2,1)}), bf16[32,32,128]{2,1,0:T(8,128)(2,1)S(1)}, u32[]{:S(2)}, u32[]{:S(2)}) %all-to-all-start) | async-done | bytes 262176 | tf_op jit(solution)/shard_map/all_to_all | solution.py:765
  48.6 0.7 %broadcast_in_dim.2 = bf16[32,32,128]{2,1,0:T(8,128)(2,1)} broadcast(bf16[32,128]{1,0:T(8,128)(2,1)S(1)} %multiply_convert_fusion), dimensions={1,2} | broadcast | bytes 270336 | tf_op jit(solution)/shard_map/broadcast_in_dim | solution.py:767
  49.3 2.6 %all-to-all-start.1 = ((bf16[32,32,128]{2,1,0:T(8,128)(2,1)}), bf16[32,32,128]{2,1,0:T(8,128)(2,1)S(1)}, u32[]{:S(2)}, u32[]{:S(2)}) async-start(bf16[32,32,128]{2,1,0:T(8,128)(2,1)} %broadcast_in_dim.2), calls=%async_computation.1 | async-start | bytes 524288 | tf_op jit(solution)/shard_map/all_to_all | solution.py:768
  51.9 0.0 collective-permute-done.4.xlo_in
  51.9 5.8 %collective-permute-done.5.xhi_in = bf16[4,32,16,128]{3,2,1,0:T(8,128)(2,1)S(1)} collective-permute-done((bf16[4,32,16,128]{3,2,1,0:T(8,128)(2,1)S(1)}, bf16[4,32,16,128]{3,2,1,0:T(8,128)(2,1)S(1)}, u32[]{:S(2)}, u32[]{:S(2)}) %collective-permute-start.5) | collective-permute-done | bytes 524320 | tf_op jit(solution)/shard_map/ppermute | solution.py:701
  57.7 8.3 %shard_map.60 = (bf16[8,32,2,16,128]{4,3,2,1,0:T(8,128)(2,1)}, bf16[64,2,16,128]{3,2,1,0:T(8,128)(2,1)}) custom-call(bf16[256,4608]{1,0:T(8,128)(2,1)} %get-tuple-element.24.ga_in, bf16[256,4608]{1,0:T(8,128)(2,1)} %get-tuple-element.25.gb_in, f32[76,64,128]{2,1,0:T(8,128)} %get-tuple-element.26.pre_in, bf16[256,2048]{1,0:T(8,128)(2,1)} %get-tuple-element.27.vals_in, ...), custom_call_target="tpu_custom_call" | custom-call | tf_op jit(solution)/shard_map/pallas_call | solution.py:735
  66.0 0.0 all-to-all-done.1.packed
  66.0 1.1 %shard_map.61 = f32[4,4,4,32,64]{4,3,2,1,0:T(8,128)} custom-call(bf16[32,32,128]{2,1,0:T(8,128)(2,1)S(1)} %all-to-all-done.1.packed), custom_call_target="tpu_custom_call" | custom-call | tf_op jit(solution)/shard_map/pallas_call | solution.py:769
  (26 shorter events, 0.3 us)
Async XLA Ops:
  0.6 9.3 %copy-start = (bf16[2,2,2,32,2,16,128]{6,5,4,3,2,1,0:T(8,128)(2,1)S(1)}, bf16[2,2,2,32,2,16,128]{6,5,4,3,2,1,0:T(8,128)(2,1)}, u32[]{:S(2)}) copy-start(bf16[2,2,2,32,2,16,128]{6,5,4,3,2,1,0:T(8,128)(2,1)} %param.5) | copy-start | bytes 6291460
  2.0 8.1 %copy-start.1 = (bf16[64,2,16,128]{3,2,1,0:T(8,128)(2,1)S(1)}, bf16[64,2,16,128]{3,2,1,0:T(8,128)(2,1)}, u32[]{:S(2)}) copy-start(bf16[64,2,16,128]{3,2,1,0:T(8,128)(2,1)} %vol_in.1) | copy-start | bytes 1572868
  2.0 8.1 %copy-start.4 = (bf16[4,4,4,32,64]{4,3,2,1,0:T(8,128)(2,1)S(1)}, bf16[4,4,4,32,64]{4,3,2,1,0:T(8,128)(2,1)}, u32[]{:S(2)}) copy-start(bf16[4,4,4,32,64]{4,3,2,1,0:T(8,128)(2,1)} %taps_in.1) | copy-start | bytes 786436
  3.3 11.4 %collective-permute-start = (bf16[1152,128]{1,0:T(8,128)(2,1)S(1)}, bf16[1152,128]{1,0:T(8,128)(2,1)S(1)}, u32[]{:S(2)}, u32[]{:S(2)}) collective-permute-start(bf16[1152,128]{1,0:T(8,128)(2,1)S(1)} %pad_maximum_fusion), channel_id=1, source_target_pairs={{0,4},{4,8},{8,12},{12,16},{16,20},{20,24},{24,28},{1,5},{5,9},{9,... | collective-permute-start | bytes 884744 | tf_op jit(solution)/shard_map/ppermute | solution.py:641
  8.0 8.3 %collective-permute-start.1 = (bf16[1152,128]{1,0:T(8,128)(2,1)S(1)}, bf16[1152,128]{1,0:T(8,128)(2,1)S(1)}, u32[]{:S(2)}, u32[]{:S(2)}) collective-permute-start(bf16[1152,128]{1,0:T(8,128)(2,1)S(1)} %pad_maximum_fusion.1), channel_id=1, source_target_pairs={{4,0},{8,4},{12,8},{16,12},{20,16},{24,20},{28,24},{5,1},{9,5},{13... | collective-permute-start | bytes 884744 | tf_op jit(solution)/shard_map/ppermute | solution.py:642
  16.4 6.1 %collective-permute-start.3 = (bf16[640,128]{1,0:T(8,128)(2,1)S(1)}, bf16[640,128]{1,0:T(8,128)(2,1)S(1)}, u32[]{:S(2)}, u32[]{:S(2)}) collective-permute-start(bf16[640,128]{1,0:T(8,128)(2,1)S(1)} %get-tuple-element.47), channel_id=1, source_target_pairs={{1,0},{2,1},{3,2},{5,4},{6,5},{7,6},{9,8},{10,9},{11,10},{13,12},{... | collective-permute-start | bytes 491528 | tf_op jit(solution)/shard_map/ppermute | solution.py:699
  17.7 6.2 %collective-permute-start.2 = (bf16[640,128]{1,0:T(8,128)(2,1)S(1)}, bf16[640,128]{1,0:T(8,128)(2,1)S(1)}, u32[]{:S(2)}, u32[]{:S(2)}) collective-permute-start(bf16[640,128]{1,0:T(8,128)(2,1)S(1)} %get-tuple-element.48), channel_id=1, source_target_pairs={{0,1},{1,2},{2,3},{4,5},{5,6},{6,7},{8,9},{9,10},{10,11},{12,13},{... | collective-permute-start | bytes 491528 | tf_op jit(solution)/shard_map/ppermute | solution.py:698
  22.4 8.3 %copy-start.2 = (bf16[640,128]{1,0:T(8,128)(2,1)}, bf16[640,128]{1,0:T(8,128)(2,1)S(1)}, u32[]{:S(2)}) copy-start(bf16[640,128]{1,0:T(8,128)(2,1)S(1)} %collective-permute-done.3.yhi_in) | copy-start | bytes 491524
  23.9 6.8 %copy-start.3 = (bf16[640,128]{1,0:T(8,128)(2,1)}, bf16[640,128]{1,0:T(8,128)(2,1)S(1)}, u32[]{:S(2)}) copy-start(bf16[640,128]{1,0:T(8,128)(2,1)S(1)} %collective-permute-done.2.ylo_in) | copy-start | bytes 491524
  23.9 14.2 %copy-start.6 = (bf16[4,32,16,128]{3,2,1,0:T(8,128)(2,1)S(1)}, bf16[4,32,16,128]{3,2,1,0:T(8,128)(2,1)}, u32[]{:S(2)}) copy-start(bf16[4,32,16,128]{3,2,1,0:T(8,128)(2,1)} %get-tuple-element.29) | copy-start | bytes 1572868
  23.9 17.8 %copy-start.5 = (bf16[4,32,16,128]{3,2,1,0:T(8,128)(2,1)S(1)}, bf16[4,32,16,128]{3,2,1,0:T(8,128)(2,1)}, u32[]{:S(2)}) copy-start(bf16[4,32,16,128]{3,2,1,0:T(8,128)(2,1)} %get-tuple-element.30) | copy-start | bytes 1572868
  30.7 17.8 %all-to-all-start = ((bf16[32,32,128]{2,1,0:T(8,128)(2,1)}), bf16[32,32,128]{2,1,0:T(8,128)(2,1)S(1)}, u32[]{:S(2)}, u32[]{:S(2)}) async-start(bf16[32,32,128]{2,1,0:T(8,128)(2,1)} %get-tuple-element.36), calls=%async_computation | async-start | bytes 524288 | tf_op jit(solution)/shard_map/all_to_all | solution.py:765
  38.2 13.7 %collective-permute-start.4 = (bf16[4,32,16,128]{3,2,1,0:T(8,128)(2,1)S(1)}, bf16[4,32,16,128]{3,2,1,0:T(8,128)(2,1)S(1)}, u32[]{:S(2)}, u32[]{:S(2)}) collective-permute-start(bf16[4,32,16,128]{3,2,1,0:T(8,128)(2,1)S(1)} %copy-done.6), channel_id=1, source_target_pairs={{0,4},{4,8},{8,12},{12,16},{16,20},{20,24},{24,28},{1,5},{5,9},{9,... | collective-permute-start | bytes 1572872 | tf_op jit(solution)/shard_map/ppermute | solution.py:700
  41.7 16.0 %collective-permute-start.5 = (bf16[4,32,16,128]{3,2,1,0:T(8,128)(2,1)S(1)}, bf16[4,32,16,128]{3,2,1,0:T(8,128)(2,1)S(1)}, u32[]{:S(2)}, u32[]{:S(2)}) collective-permute-start(bf16[4,32,16,128]{3,2,1,0:T(8,128)(2,1)S(1)} %copy-done.5), channel_id=1, source_target_pairs={{4,0},{8,4},{12,8},{16,12},{20,16},{24,20},{28,24},{5,1},{9,5},{13... | collective-permute-start | bytes 1572872 | tf_op jit(solution)/shard_map/ppermute | solution.py:701
  49.3 16.7 %all-to-all-start.1 = ((bf16[32,32,128]{2,1,0:T(8,128)(2,1)}), bf16[32,32,128]{2,1,0:T(8,128)(2,1)S(1)}, u32[]{:S(2)}, u32[]{:S(2)}) async-start(bf16[32,32,128]{2,1,0:T(8,128)(2,1)} %broadcast_in_dim.2), calls=%async_computation.1 | async-start | bytes 524288 | tf_op jit(solution)/shard_map/all_to_all | solution.py:768
